TPU v7x, 32 devices: a whole 2x2x4 slice. The times are simulated.
32 devices in a mesh: group: 2 (over core), cuts: 4 (over y, x), sub: 4 (over z).
Axes of the slice: x: 2, y: 2, z: 4, core: 2. Of those that a mesh axis runs over, the one named last changes fastest.
Arguments:
- disp_now: float32 [2, 3, 128, 1089], P('group', None, ('cuts', 'sub')), may hold values from -6 to 6
- disp_prev: float32 [2, 3, 128, 1089], P('group', None, ('cuts', 'sub')), may hold values from -6 to 6
- memory_init: float32 [2, 3, 5, 125, 2048], P('group', None, None, None, ('cuts', 'sub')), may hold values from -6 to 6
- density: float32 [128, 1089], P(('cuts', 'sub')), may hold values from 0.8 to 1.6
- lame_lambda: float32 [125, 2048], P(None, ('cuts', 'sub')), may hold values from 0.4 to 1.6
- shear_mu: float32 [125, 2048], P(None, ('cuts', 'sub')), may hold values from 0.4 to 1.2
- sls_decay: float32 [3, 2048], P(None, ('cuts', 'sub')), may hold values from 0.3 to 0.98
- owner_map: int32 [32, 64, 1], P(('cuts', 'sub')), may hold values from 0 to 3; in each aligned block of 64 rows (0 to 63, 64 to 127, ..., all dimensions but the last counted through in order) at most 32 rows name the same one
Outputs:
- disp_final: float32 [2, 3, 128, 1089], P('group', None, ('cuts', 'sub'))
- kernels: float32 [2, 4096, 250], P('group', ('cuts', 'sub'))
Inputs may be any that keep to these rules, and one draw needn't show every extreme that they name: `owner_map`: among the 64 elements of one slab, no sub-slice owns more than 32; in some slab one owns exactly 32.
All inputs are finite; a program needn't handle non-finite values.
Results may differ from a plain program's by a relative error of at most 0.0004.
The roundings to bfloat16 on the way count: a program that leaves them out, or rounds other values in their place, can miss the bound.
Values may be sent and summed in bfloat16 or wider, within the bound.
No kernel may reach another device: no remote copies, remote signals or barrier semaphores. Data moves between devices by JAX's collectives and lax.ppermute only.
A program may use at most 64 MiB of HBM per device.

v0:
```python
import math

import jax
import jax.numpy as jnp
import numpy as np
from jax import lax
from jax.experimental import pallas as pl
from jax.experimental.pallas import tpu as pltpu
from jax.sharding import PartitionSpec as P

STEPS = 3
EY = 8
EZ = 8
LANES = 128
SIDE = 33
FACE = SIDE * SIDE
BLOCKS = 26
ROWS = 8 * BLOCKS
WIDE = 64 * BLOCKS
JUMP = 4 * SIDE
WINDOW = 256

time_step = 0.03
step_square = 0.0009
relax_strength = (0.12, 0.08, 0.05)

F32 = jnp.float32
BF16 = jnp.bfloat16


def gll_tables():
    root_value = math.sqrt(3.0 / 7.0)
    points = [-1.0, -root_value, 0.0, root_value, 1.0]
    weights = [0.1, 49.0 / 90.0, 32.0 / 45.0, 49.0 / 90.0, 0.1]
    derivative = np.zeros((5, 5))
    for p in range(5):
        for a in range(5):
            accum = 0.0
            for m in range(5):
                if m != a:
                    factor = 1.0 / (points[a] - points[m])
                    for k in range(5):
                        if k != a and k != m:
                            factor = factor * (points[p] - points[k]) / (points[a] - points[k])
                    accum = accum + factor
            derivative[p, a] = accum
    return derivative.astype(np.float32).astype(np.float64), np.array(weights).astype(np.float32).astype(np.float64)


def node(a, b, d):
    return a * 25 + b * 5 + d


def place(a, b, d):
    return (b * 5 + d) * 8 + a


def make_tables():
    derivative, weights = gll_tables()
    grad = np.zeros((3 * 128, ROWS))
    force = np.zeros((ROWS, 3 * 128))
    for a in range(5):
        for b in range(5):
            for d in range(5):
                for m in range(5):
                    grad[node(a, b, d), place(m, b, d)] = derivative[a, m]
                    grad[128 + node(a, b, d), place(a, m, d)] = derivative[b, m]
                    grad[256 + node(a, b, d), place(a, b, m)] = derivative[d, m]
                    row = place(a, b, d)
                    force[row, node(m, b, d)] = -derivative[m, a] * weights[m] * weights[b] * weights[d]
                    force[row, 128 + node(a, m, d)] = -derivative[m, b] * weights[a] * weights[m] * weights[d]
                    force[row, 256 + node(a, b, m)] = -derivative[m, d] * weights[a] * weights[b] * weights[m]
    face = np.zeros((64, 3 * 128))
    face[0:25] = force[0:200:8]
    face[32:57] = force[4:200:8]
    spread = np.zeros((WINDOW, WIDE), np.float32)
    collect = np.zeros((WIDE, WINDOW), np.float32)
    line = np.zeros(SIDE)
    for e in range(8):
        line[4 * e : 4 * e + 5] += weights
    layer = np.array([2 * weights[0], weights[1], weights[2], weights[3], 2 * weights[0], 1.0, 1.0, 1.0])
    mass = np.ones((ROWS, LANES), np.float32)
    for b in range(5):
        for d in range(5):
            for ey in range(8):
                for ez in range(8):
                    column = (b * 5 + d) * 64 + ey * 8 + ez
                    spot = b * SIDE + 4 * ez + d
                    spread[spot, column] = 1.0
                    if d < 4 or ez == 7:
                        collect[column, spot] = 1.0
                    for slab in range(2):
                        at = (b * 5 + d) * 8
                        mass[at : at + 8, slab * 64 + ey * 8 + ez] = layer * line[4 * ey + b] * line[4 * ez + d]
    return grad, force, face, spread, collect, mass


def cut_table(table):
    value = table.astype(np.float32)
    pieces = []
    for _ in range(3):
        piece = value.astype(jnp.bfloat16)
        pieces.append(piece)
        value = value - piece.astype(np.float32)
    return np.stack(pieces)


GRAD, FORCE, FACES, SPREAD, COLLECT, MASS = make_tables()


def cut(value):
    high = value.astype(BF16)
    rest = value - high.astype(F32)
    middle = rest.astype(BF16)
    low = (rest - middle.astype(F32)).astype(BF16)
    return high, middle, low


def dot(left, right):
    return jnp.dot(left, right, preferred_element_type=F32)


def dot_six(table, value):
    high, middle, low = cut(value)
    small = dot(table[2], high) + dot(table[1], middle) + dot(table[0], low)
    return dot(table[0], high) + (dot(table[0], middle) + dot(table[1], high) + small)


def lanes_of(shape):
    return lax.broadcasted_iota(jnp.int32, shape, len(shape) - 1)


def rolled(value, shift, axis):
    return pltpu.roll(value, shift % value.shape[axis], axis)


def window_rows(value, window_ref):
    for ey in range(EY):
        width = min(WINDOW, FACE - JUMP * ey)
        if width < WINDOW:
            window_ref[ey] = jnp.zeros(window_ref.shape[1:], F32)
        window_ref[ey, :, 0:width] = value[:, JUMP * ey : JUMP * ey + width]
    return window_ref[...].reshape(-1, WINDOW)


def to_columns(value, window_ref, spread_ref):
    rows = value.shape[0]
    high, middle, low = cut(window_rows(value, window_ref))
    spread = spread_ref[...]
    wide = dot(high, spread) + dot(middle, spread) + dot(low, spread)
    own = (lanes_of((rows, WIDE)) // 8) % 8
    picked = wide[0:rows]
    for ey in range(1, EY):
        picked = jnp.where(own == ey, wide[ey * rows : (ey + 1) * rows], picked)
    return picked


def assembled(blocks):
    lane = lanes_of((8, LANES))
    blocks = dict(blocks)
    for shift, at, pairs in (
        (1, lane % 8, [((b, 0), (b, 4)) for b in range(5)]),
        (8, (lane // 8) % 8, [((0, d), (4, d)) for d in range(5)]),
    ):
        for c in range(3):
            for near, far in pairs:
                first, last = blocks[(c,) + near], blocks[(c,) + far]
                blocks[(c,) + near] = first + jnp.where(at > 0, rolled(last, shift, 1), 0.0)
                blocks[(c,) + far] = last + jnp.where(at < 7, rolled(first, -shift, 1), 0.0)
    return blocks


def block_rows(b, d):
    return slice((b * 5 + d) * 8, (b * 5 + d) * 8 + 8)


def beside(value):
    return jnp.concatenate([value[0], value[1], value[2]], axis=1)


def prologue_kernel(
    index_ref, now_ref, prev_ref, density_ref, memory_ref, decay_ref, owner_col_ref, owner_row_ref, spread_ref, mass_ref,
    u_ref, p_ref, scale_ref, m1_ref, m2_ref, m3_ref, select_ref, window_ref,
):
    rows = jnp.concatenate([now_ref[0].reshape(24, FACE), prev_ref[0].reshape(24, FACE), density_ref[...]], axis=0)
    columns = to_columns(rows, window_ref, spread_ref)
    lane = lanes_of((8, LANES))
    for group in range(7):
        for pair in range(BLOCKS // 2):
            tile = columns[8 * group : 8 * group + 8, LANES * pair : LANES * pair + LANES]
            swapped = rolled(tile, 64, 1)
            even = jnp.where(lane < 64, tile, rolled(swapped, 4, 0))
            odd = jnp.where(lane < 64, swapped, rolled(tile, 4, 0))
            for block, value in ((2 * pair, even), (2 * pair + 1, odd)):
                at = slice(8 * block, 8 * block + 8)
                if group < 3:
                    u_ref[group, at, :] = value
                elif group < 6:
                    p_ref[group - 3, at, :] = value
                elif block < 25:
                    scale_ref[at, :] = step_square / (value * mass_ref[at, :])
                else:
                    scale_ref[at, :] = jnp.zeros((8, LANES), F32)
    decays = [decay_ref[l : l + 1, :] for l in range(3)]
    for part in range(5):
        terms = [decays[l] * memory_ref[0, l, part] for l in range(3)]
        m1_ref[part] = terms[0] + terms[1] + terms[2]
        terms = [decays[l] * terms[l] for l in range(3)]
        m2_ref[part] = terms[0] + terms[1] + terms[2]
        terms = [decays[l] * terms[l] for l in range(3)]
        m3_ref[part] = terms[0] + terms[1] + terms[2]
    owner_row = owner_row_ref[...]
    earlier = lax.broadcasted_iota(jnp.int32, (LANES, LANES), 0)
    later = lax.broadcasted_iota(jnp.int32, (LANES, LANES), 1)
    ahead = (owner_col_ref[...] == owner_row) & (earlier < later) & ((earlier // 64) == (later // 64))
    rank = jnp.sum(jnp.where(ahead, 1.0, 0.0), axis=0, keepdims=True).astype(jnp.int32)
    total = select_ref.shape[0]
    subs = index_ref[2]
    slots = total // subs
    slot = lax.broadcasted_iota(jnp.int32, (total, LANES), 0)
    toward = (slot // slots) ^ index_ref[0]
    wanted = (lanes_of((1, LANES)) // 64) * (slots // 2) + rank
    chosen = (owner_row == toward) & (wanted == slot % slots)
    select_ref[...] = jnp.where(chosen, 1.0, 0.0).astype(BF16)


def rim_kernel(rim_ref, u_in, p_in, scale_in, spread_ref, mass_ref, u_ref, p_ref, scale_ref, low_ref, window_ref, rows_ref):
    columns = to_columns(rim_ref[...], window_ref, spread_ref)
    for pair in range(BLOCKS // 2):
        tile = columns[:, LANES * pair : LANES * pair + LANES]
        rows_ref[16 * pair : 16 * pair + 8, :] = rolled(tile, 64, 1)
        rows_ref[16 * pair + 8 : 16 * pair + 16, :] = tile
    u_ref[...] = u_in[...]
    p_ref[...] = p_in[...]
    scale_ref[...] = scale_in[...]
    upper = lanes_of((25, LANES)) >= 64
    last = pl.ds(4, 25, stride=8)
    for c in range(3):
        u_ref[c, last, :] = jnp.where(upper, rows_ref[pl.ds(c, 25, stride=8), :], u_ref[c, last, :])
        p_ref[c, last, :] = jnp.where(upper, rows_ref[pl.ds(3 + c, 25, stride=8), :], p_ref[c, last, :])
    rim = step_square / (rows_ref[pl.ds(6, 25, stride=8), :] * mass_ref[last, :])
    scale_ref[last, :] = jnp.where(upper, rim, scale_ref[last, :])
    low_ref[...] = u_ref[...].astype(BF16)


def strains(grad, rows):
    def at(direction, c):
        return grad[direction * 128 + rows.start : direction * 128 + rows.stop, c * LANES : (c + 1) * LANES]

    return [
        at(0, 0),
        at(1, 1),
        at(2, 2),
        0.5 * (at(1, 0) + at(0, 1)),
        0.5 * (at(2, 0) + at(0, 2)),
        0.5 * (at(2, 1) + at(1, 2)),
    ]


CHUNKS = [slice(0, 32), slice(32, 64), slice(64, 96), slice(96, 125)]


def pack_face(face, upper):
    parts = [face[:, c * LANES : (c + 1) * LANES] for c in range(3)]
    lower_lane = lanes_of((16, LANES)) < 64
    lower_lanes = lanes_of((32, LANES)) < 64
    if upper:
        first = jnp.where(lower_lanes, rolled(parts[0], 64, 1), parts[1])
        second = jnp.where(lower_lane, rolled(parts[2][0:16], 64, 1), parts[2][16:32])
    else:
        first = jnp.where(lower_lanes, parts[0], rolled(parts[1], 64, 1))
        second = jnp.where(lower_lane, parts[2][0:16], rolled(parts[2][16:32], 64, 1))
    return jnp.concatenate([first, second], axis=0)


def step_kernel(step, *refs):
    u_ref, lame_ref, mu_ref, m_ref, decay_ref, grad_table, face_table = refs[0:7]
    older = refs[7 : 7 + step]
    refs = refs[7 + step :]
    strain_ref, sigma_ref, first_ref, last_ref = refs[0:4]
    keep_ref = refs[4] if step < STEPS - 1 else None
    grad_ref = refs[-1]
    grad_ref[...] = dot_six(grad_table, beside(u_ref))
    for block in range(9):
        sigma_ref[(block // 3) * 128 + 120 : (block // 3) * 128 + 128, (block % 3) * LANES : (block % 3) * LANES + LANES] = (
            jnp.zeros((8, LANES), F32)
        )
    decays = [decay_ref[l : l + 1, :] for l in range(3)]
    shares = [(1.0 - decays[l]) * relax_strength[l] for l in range(3)]
    factors = []
    for _ in range(step + 1):
        factors.append(shares[0] + shares[1] + shares[2])
        shares = [decays[l] * shares[l] for l in range(3)]
    for rows in CHUNKS:
        strain = strains(grad_ref, rows)
        for part in range(6):
            strain_ref[part, rows, :] = strain[part]
        lame = lame_ref[rows, :]
        twice_mu = 2.0 * mu_ref[rows, :]
        trace = strain[0] + strain[1] + strain[2]
        third = trace * (1.0 / 3.0)
        pulls = [twice_mu * s for s in strain]
        pull_third = twice_mu * third
        fresh = [pulls[0] - pull_third, pulls[1] - pull_third, pulls[3], pulls[4], pulls[5]]
        relax = []
        for part in range(5):
            value = m_ref[part, rows, :] + factors[0] * fresh[part]
            for back in range(step):
                value = value + factors[back + 1] * older[step - 1 - back][part, rows, :]
            relax.append(value)
            if keep_ref is not None:
                keep_ref[part, rows, :] = fresh[part]
        bulk = lame * trace
        xx = bulk + pulls[0] - relax[0]
        yy = bulk + pulls[1] - relax[1]
        zz = bulk + pulls[2] + relax[0] + relax[1]
        xy = pulls[3] - relax[2]
        xz = pulls[4] - relax[3]
        yz = pulls[5] - relax[4]
        for direction, values in enumerate(((xx, xy, xz), (xy, yy, yz), (xz, yz, zz))):
            for c in range(3):
                sigma_ref[direction * 128 + rows.start : direction * 128 + rows.stop, c * LANES : (c + 1) * LANES] = values[c]
    faces = dot_six(face_table, sigma_ref[...])
    first_ref[...] = pack_face(faces[0:32], False)
    last_ref[...] = pack_face(faces[32:64], True)


def rest_kernel(sigma_ref, u_ref, p_ref, scale_ref, force_table, next_ref):
    force = dot_six(force_table, sigma_ref[...])
    blocks = {}
    for c in range(3):
        for b in range(5):
            for d in range(5):
                blocks[(c, b, d)] = force[block_rows(b, d), c * LANES : (c + 1) * LANES]
    blocks = assembled(blocks)
    lane = lanes_of((8, LANES))
    sub = lax.broadcasted_iota(jnp.int32, (8, LANES), 0)
    inner = ((sub == 4) & (lane < 64)) | ((sub == 0) & (lane >= 64))
    for c in range(3):
        for b in range(5):
            for d in range(5):
                value = blocks[(c, b, d)]
                value = value + jnp.where(inner, rolled(rolled(value, 4, 0), 64, 1), 0.0)
                at = block_rows(b, d)
                next_ref[c, at, :] = 2.0 * u_ref[c, at, :] - p_ref[c, at, :] + scale_ref[at, :] * value
        next_ref[c, 200:208, :] = jnp.zeros((8, LANES), F32)


def add_faces(from_before, from_after, partial_ref, scale_ref, u_ref, delta_ref):
    delta_ref[...] = jnp.zeros(delta_ref.shape, F32)
    lower = lanes_of((25, LANES)) < 64
    if from_before is not None:
        packed = from_before[...]
        turned = rolled(packed, 64, 1)
        values = [packed[0:32], turned[0:32], jnp.concatenate([packed[32:48], turned[32:48]], axis=0)]
        for c in range(3):
            delta_ref[c, pl.ds(0, 25, stride=8), :] = jnp.where(lower, values[c][0:25], 0.0)
    if from_after is not None:
        packed = from_after[...]
        turned = rolled(packed, 64, 1)
        values = [turned[0:32], packed[0:32], jnp.concatenate([turned[32:48], packed[32:48]], axis=0)]
        for c in range(3):
            delta_ref[c, pl.ds(4, 25, stride=8), :] = jnp.where(lower, 0.0, values[c][0:25])
    blocks = {}
    for c in range(3):
        for b in range(5):
            for d in range(5):
                blocks[(c, b, d)] = delta_ref[c, block_rows(b, d), :]
    blocks = assembled(blocks)
    for c in range(3):
        for b in range(5):
            for d in range(5):
                at = block_rows(b, d)
                u_ref[c, at, :] = partial_ref[c, at, :] + scale_ref[at, :] * blocks[(c, b, d)]
        u_ref[c, 200:208, :] = jnp.zeros((8, LANES), F32)


def update_kernel(before_ref, after_ref, partial_ref, scale_ref, u_ref, low_ref, delta_ref):
    add_faces(before_ref, after_ref, partial_ref, scale_ref, u_ref, delta_ref)
    low_ref[...] = u_ref[...].astype(BF16)


def parts_kernel(index_ref, strain_ref, low_ref, far_ref, lame_ref, mu_ref, select_ref, grad_table, *refs):
    out_refs, (grad_ref, kernel_ref) = refs[:-2], refs[-2:]
    forward = jnp.where(index_ref[1] == 0, beside(low_ref), beside(far_ref))
    grad_ref[...] = dot(grad_table[0], forward) + (dot(grad_table[1], forward) + dot(grad_table[2], forward))
    for rows in CHUNKS:
        far = strains(grad_ref, rows)
        own = [strain_ref[part, rows, :] for part in range(6)]
        trace_own = own[0] + own[1] + own[2]
        trace_far = far[0] + far[1] + far[2]
        third_own, third_far = trace_own * (1.0 / 3.0), trace_far * (1.0 / 3.0)
        twice_mu = 2.0 * mu_ref[rows, :]
        kappa = lame_ref[rows, :] + twice_mu * (1.0 / 3.0)
        kernel_ref[rows, :] = time_step * kappa * trace_far * trace_own
        product = (
            (own[0] - third_own) * (far[0] - third_far)
            + (own[1] - third_own) * (far[1] - third_far)
            + (own[2] - third_own) * (far[2] - third_far)
            + 2.0 * (own[3] * far[3] + own[4] * far[4] + own[5] * far[5])
        )
        kernel_ref[125 + rows.start : 125 + rows.stop, :] = time_step * twice_mu * product
    kernel_ref[250:256, :] = jnp.zeros((6, LANES), F32)
    outgoing = lax.dot_general(
        select_ref[...], kernel_ref[...].astype(BF16), (((1,), (1,)), ((), ())), preferred_element_type=F32
    ).astype(BF16)
    slots = out_refs[0].shape[0]
    for k, ref in enumerate(out_refs):
        ref[...] = outgoing[k * slots : (k + 1) * slots]


def sum_kernel(index_ref, *refs):
    in_refs, out_ref = refs[:-1], refs[-1]
    subs = len(in_refs) // STEPS
    slots = in_refs[0].shape[0]
    for k in range(subs):
        value = in_refs[k][...].astype(F32) + in_refs[subs + k][...].astype(F32) + in_refs[2 * subs + k][...].astype(F32)
        start = pl.multiple_of((index_ref[0] ^ k) * slots, 16)
        out_ref[0, pl.ds(start, slots), :] = value[:, 0:250]


def finish_kernel(before_ref, partial_ref, scale_ref, collect_ref, out_ref, u_ref, delta_ref):
    add_faces(before_ref, None, partial_ref, scale_ref, u_ref, delta_ref)
    lane = lanes_of((8, LANES))
    sub = lax.broadcasted_iota(jnp.int32, (8, LANES), 0)
    tiles = []
    for c in range(3):
        row = []
        for pair in range(BLOCKS // 2):
            even = u_ref[c, 16 * pair : 16 * pair + 8, :]
            odd = u_ref[c, 16 * pair + 8 : 16 * pair + 16, :]
            low = jnp.where(sub < 4, even, rolled(rolled(even, 64, 1), 4, 0))
            high = jnp.where(sub < 4, rolled(odd, 64, 1), rolled(odd, 4, 0))
            row.append(jnp.where(lane < 64, low, high))
        tiles.append(jnp.concatenate(row, axis=1))
    columns = jnp.concatenate(tiles, axis=0)
    own = (lanes_of((24, WIDE)) // 8) % 8
    spread = jnp.concatenate([jnp.where(own == ey, columns, 0.0) for ey in range(EY)], axis=0)
    high, middle, low = cut(spread)
    collect = collect_ref[...]
    windows = dot(high, collect) + dot(middle, collect) + dot(low, collect)
    for ey in range(EY):
        width = JUMP if ey < EY - 1 else JUMP + SIDE
        for c in range(3):
            out_ref[0, c, :, JUMP * ey : JUMP * ey + width] = windows[24 * ey + 8 * c : 24 * ey + 8 * c + 8, 0:width]


VMEM = pl.BlockSpec(memory_space=pltpu.VMEM)
SMEM = pl.BlockSpec(memory_space=pltpu.SMEM)


def shaped(*shape, dtype=F32):
    return jax.ShapeDtypeStruct(shape, dtype)


def call(kernel, name, outs, scratch, *args, scalars=0, micros=1):
    return pl.pallas_call(
        kernel,
        name=name,
        out_shape=outs,
        in_specs=[SMEM] * scalars + [VMEM] * (len(args) - scalars),
        out_specs=jax.tree.map(lambda _: VMEM, outs),
        scratch_shapes=scratch,
        compiler_params=pltpu.CompilerParams(vmem_limit_bytes=32 * 1024 * 1024),
        cost_estimate=pl.CostEstimate(flops=0, bytes_accessed=micros * 3000000, transcendentals=0),
    )(*args)


def passed_along(value, axis, steps):
    count = lax.axis_size(axis)
    return lax.ppermute(value, axis, [(source, (source + steps) % count) for source in range(count)])


def per_device(disp_now, disp_prev, memory_init, density, lame_lambda, shear_mu, sls_decay, owner_map):
    ring = ("cuts", "sub")
    subs = lax.axis_size("sub")
    groups = lax.axis_size("group")
    slots = 2 * EY * EZ * 2 // subs
    index = jnp.stack([lax.axis_index("sub"), lax.axis_index("group"), jnp.int32(subs)]).astype(jnp.int32)

    rim = jnp.concatenate(
        [disp_now[0, :, 0, :], disp_prev[0, :, 0, :], density[0:1, :], jnp.ones((1, FACE), F32)], axis=0
    )
    rim = passed_along(rim, ring, -1)

    grad_table = jnp.asarray(cut_table(GRAD))
    force_table = jnp.asarray(cut_table(FORCE))
    face_table = jnp.asarray(cut_table(FACES))
    spread = jnp.asarray(SPREAD, BF16)
    collect = jnp.asarray(COLLECT, BF16)
    mass = jnp.asarray(MASS)

    state = shaped(3, ROWS, LANES)
    state_low = shaped(3, ROWS, LANES, dtype=BF16)
    scale_shape = shaped(ROWS, LANES)
    five = shaped(5, 125, LANES)
    u, p, scale, m1, m2, m3, select = call(
        prologue_kernel, "prologue",
        [state, state, scale_shape, five, five, five, shaped(subs * slots, LANES, dtype=BF16)],
        [pltpu.VMEM((8, 56, WINDOW), F32)],
        index, disp_now, disp_prev, density, memory_init, sls_decay,
        owner_map.reshape(2 * EY * EZ, 1), owner_map.reshape(1, 2 * EY * EZ), spread, mass,
        scalars=1, micros=3,
    )
    u, p, scale, low = call(
        rim_kernel, "rim", [state, state, scale_shape, state_low],
        [pltpu.VMEM((8, 8, WINDOW), F32), pltpu.VMEM((ROWS, LANES), F32)],
        rim, u, p, scale, spread, mass,
    )
    memories = (m1, m2, m3)
    kept = []
    parts = []
    for step in range(STEPS):
        far = None
        for k in range(1, groups):
            moved = passed_along(low, "group", k)
            far = moved if far is None else jnp.where(lax.axis_index("group") == k, moved, far)
        outs = [shaped(6, 125, LANES), shaped(384, 384), shaped(48, LANES), shaped(48, LANES)]
        if step < STEPS - 1:
            outs.append(five)
        results = call(
            lambda *refs, step=step: step_kernel(step, *refs), "step", outs, [pltpu.VMEM((384, 384), F32)],
            u, lame_lambda, shear_mu, memories[step], sls_decay, grad_table, face_table, *kept,
        )
        strain, sigma, first, last = results[0:4]
        kept.extend(results[4:])
        from_before = passed_along(last, ring, 1)
        if step < STEPS - 1:
            from_after = passed_along(first, ring, -1)
        partial = call(rest_kernel, "rest", state, [], sigma, u, p, scale, force_table)
        sent = call(
            parts_kernel, "parts", [shaped(slots, WINDOW, dtype=BF16)] * subs,
            [pltpu.VMEM((384, 384), F32), pltpu.VMEM((256, LANES), F32)],
            index, strain, low, far, lame_lambda, shear_mu, select, grad_table, scalars=1,
        )
        parts.append(sent[0])
        for k in range(1, subs):
            parts.append(lax.ppermute(sent[k], "sub", [(j, j ^ k) for j in range(subs)]))
        p = u
        if step < STEPS - 1:
            u, low = call(
                update_kernel, "update", [state, state_low], [pltpu.VMEM((3, ROWS, LANES), F32)],
                from_before, from_after, partial, scale,
            )
    final = call(
        finish_kernel, "finish", shaped(1, 3, 8, FACE),
        [pltpu.VMEM((3, ROWS, LANES), F32), pltpu.VMEM((3, ROWS, LANES), F32)],
        from_before, partial, scale, collect,
    )
    kernels = call(sum_kernel, "sum", shaped(1, subs * slots, 250), [], index, *parts, scalars=1)
    return final, kernels


def solution(mesh):
    in_specs = (
        P("group", None, ("cuts", "sub"), None),
        P("group", None, ("cuts", "sub"), None),
        P("group", None, None, None, ("cuts", "sub")),
        P(("cuts", "sub"), None),
        P(None, ("cuts", "sub")),
        P(None, ("cuts", "sub")),
        P(None, ("cuts", "sub")),
        P(("cuts", "sub"), None, None),
    )
    out_specs = (P("group", None, ("cuts", "sub"), None), P("group", ("cuts", "sub"), None))
    return jax.shard_map(
        per_device, mesh=mesh, in_specs=in_specs, out_specs=out_specs, check_vma=False
    )
```

profile of v0, /device:TPU:0, one launch (start us, length us, event | category | flops | bytes accessed | tf_op | source)
XLA Modules:
  0.0 65.4 jit_solution(17717685634573470683)
XLA Ops:
  2.1 6.9 %collective-permute-start = (f32[8,1089]{1,0:T(8,128)S(1)}, f32[8,1089]{1,0:T(8,128)S(1)}, u32[]{:S(2)}, u32[]{:S(2)}) collective-permute-start(f32[8,1089]{1,0:T(8,128)S(1)} %maximum_maximum_fusion), channel_id=1, source_target_pairs={{0,15},{1,0},{2,1},{3,2},{4,3},{5,4},{6,5},{7,6},{8,7},{9,8},{10,9... | collective-permute-start | bytes 104552 | tf_op jit(solution)/shard_map/ppermute | solution.py:471
  11.3 1.4 %copy.18.memory_ref = f32[1,3,5,125,128]{4,3,2,1,0:T(8,128)S(1)} copy(f32[1,3,5,125,128]{4,0,3,2,1:T(1,128)} %param.16) | data formatting | bytes 1920000 | tf_op args[2]
  12.7 4.9 %prologue.1 = (f32[3,208,128]{2,1,0:T(8,128)S(1)}, f32[3,208,128]{2,1,0:T(8,128)S(1)}, f32[208,128]{1,0:T(8,128)S(1)}, f32[5,125,128]{2,1,0:T(8,128)S(1)}, f32[5...) custom-call(s32[3]{0:T(128)S(1)} %pad_add_fusion.index_ref, ...), custom_call_target="tpu_custom_call" | custom-call | bytes 9000000 | tf_op jit(solution)/shard_map/prologue/pallas_call | solution.py:457
  18.7 1.4 %step.3 = (f32[6,125,128]{2,1,0:T(8,128)S(1)}, f32[384,384]{1,0:T(8,128)S(1)}, f32[48,128]{1,0:T(8,128)S(1)}, f32[48,128]{1,0:T(8,128)S(1)}, f32[5,125,128]{2,1,0:T(8,128)S(1)}) custom-call(f32[3,208,128]{2,1,0:T(8,128)S(1)} %get-tuple-element.45.refs_0_.u_ref.p_ref, f32[125,128]{1,0:T(8,128)S(1)} %copy-done.3, f32[125,128]{1,0:T(8,128)S(1)} %copy-done.4, ...), custom_call_target="tpu_custom_call" | custom-call | bytes 3000000 | tf_op jit(solution)/shard_map/step/pallas_call | solution.py:457
  20.2 5.6 %collective-permute-start.2 = (f32[48,128]{1,0:T(8,128)S(1)}, f32[48,128]{1,0:T(8,128)S(1)}, u32[]{:S(2)}, u32[]{:S(2)}) collective-permute-start(f32[48,128]{1,0:T(8,128)S(1)} %get-tuple-element.48), channel_id=1, source_target_pairs={{0,15},{1,0},{2,1},{3,2},{4,3},{5,4},{6,5},{7,6},{8,7},{9,8},{10,9... | collective-permute-start | bytes 73736 | tf_op jit(solution)/shard_map/ppermute | solution.py:471
  25.8 1.1 %rest.3.partial_ref = f32[3,208,128]{2,1,0:T(8,128)S(1)} custom-call(f32[384,384]{1,0:T(8,128)S(1)} %get-tuple-element.49.sigma_ref, f32[3,208,128]{2,1,0:T(8,128)S(1)} %get-tuple-element.45.refs_0_.u_ref.p_ref, f32[3,208,128]{2,1,0:T(8,128)S(1)} %get-tuple-element.50.p_ref, f32[208,128]{1,0:T(8,128)S(1)} %get-tuple-element.51.scale_ref, ...), custom_call_target="tpu_custom_call" | custom-call | bytes 3000000 | tf_op jit(solution)/shard_map/rest/pallas_call | solution.py:457
  27.9 1.4 %step.4 = (f32[6,125,128]{2,1,0:T(8,128)S(1)}, f32[384,384]{1,0:T(8,128)S(1)}, f32[48,128]{1,0:T(8,128)S(1)}, f32[48,128]{1,0:T(8,128)S(1)}, f32[5,125,128]{2,1,0:T(8,128)S(1)}) custom-call(f32[3,208,128]{2,1,0:T(8,128)S(1)} %get-tuple-element.52.refs_0_.u_ref.p_ref, f32[125,128]{1,0:T(8,128)S(1)} %copy-done.3, f32[125,128]{1,0:T(8,128)S(1)} %copy-done.4, ...), custom_call_target="tpu_custom_call" | custom-call | bytes 3000000 | tf_op jit(solution)/shard_map/step/pallas_call | solution.py:457
  29.3 5.8 %collective-permute-start.4 = (f32[48,128]{1,0:T(8,128)S(1)}, f32[48,128]{1,0:T(8,128)S(1)}, u32[]{:S(2)}, u32[]{:S(2)}) collective-permute-start(f32[48,128]{1,0:T(8,128)S(1)} %get-tuple-element.56), channel_id=1, source_target_pairs={{0,15},{1,0},{2,1},{3,2},{4,3},{5,4},{6,5},{7,6},{8,7},{9,8},{10,9... | collective-permute-start | bytes 73736 | tf_op jit(solution)/shard_map/ppermute | solution.py:471
  35.7 1.1 %rest.4.partial_ref = f32[3,208,128]{2,1,0:T(8,128)S(1)} custom-call(f32[384,384]{1,0:T(8,128)S(1)} %get-tuple-element.57.sigma_ref, f32[3,208,128]{2,1,0:T(8,128)S(1)} %get-tuple-element.52.refs_0_.u_ref.p_ref, f32[3,208,128]{2,1,0:T(8,128)S(1)} %get-tuple-element.45.refs_0_.u_ref.p_ref, f32[208,128]{1,0:T(8,128)S(1)} %get-tuple-element.51.scale_ref, ...), custom_call_target="tpu_custom_call" | custom-call | bytes 3000000 | tf_op jit(solution)/shard_map/rest/pallas_call | solution.py:457
  37.1 1.3 %parts.3 = (bf16[64,256]{1,0:T(8,128)(2,1)S(1)}, bf16[64,256]{1,0:T(8,128)(2,1)S(1)}, bf16[64,256]{1,0:T(8,128)(2,1)S(1)}, bf16[64,256]{1,0:T(8,128)(2,1)S(1)}) custom-call(s32[3]{0:T(128)S(1)} %pad_add_fusion.index_ref, f32[6,125,128]{2,1,0:T(8,128)S(1)} %get-tuple-element.63.strain_ref, bf16[3,208,128]{2,1,0:T(8,128)(2,1)S(1)} %get-tuple-element.64.low_ref, ...), custom_call_target="tpu_custom_call" | custom-call | bytes 3000000 | tf_op jit(solution)/shard_map/parts/pallas_call | solution.py:457
  38.5 1.8 %collective-permute-start.8 = (bf16[64,256]{1,0:T(8,128)(2,1)S(1)}, bf16[64,256]{1,0:T(8,128)(2,1)S(1)}, u32[]{:S(2)}, u32[]{:S(2)}) collective-permute-start(bf16[64,256]{1,0:T(8,128)(2,1)S(1)} %get-tuple-element.68), channel_id=1, source_target_pairs={{0,2},{1,3},{2,0},{3,1},{4,6},{5,7},{6,4},{7,5},{8,10},{9,11},{10,... | collective-permute-start | bytes 98312 | tf_op jit(solution)/shard_map/ppermute | solution.py:538
  40.3 2.6 %collective-permute-start.9 = (bf16[64,256]{1,0:T(8,128)(2,1)S(1)}, bf16[64,256]{1,0:T(8,128)(2,1)S(1)}, u32[]{:S(2)}, u32[]{:S(2)}) collective-permute-start(bf16[64,256]{1,0:T(8,128)(2,1)S(1)} %get-tuple-element.69), channel_id=1, source_target_pairs={{0,3},{1,2},{2,1},{3,0},{4,7},{5,6},{6,5},{7,4},{8,11},{9,10},{10,... | collective-permute-start | bytes 98312 | tf_op jit(solution)/shard_map/ppermute | solution.py:538
  42.9 1.3 %parts.4 = (bf16[64,256]{1,0:T(8,128)(2,1)S(1)}, bf16[64,256]{1,0:T(8,128)(2,1)S(1)}, bf16[64,256]{1,0:T(8,128)(2,1)S(1)}, bf16[64,256]{1,0:T(8,128)(2,1)S(1)}) custom-call(s32[3]{0:T(128)S(1)} %pad_add_fusion.index_ref, f32[6,125,128]{2,1,0:T(8,128)S(1)} %get-tuple-element.70.strain_ref, bf16[3,208,128]{2,1,0:T(8,128)(2,1)S(1)} %get-tuple-element.71.low_ref, ...), custom_call_target="tpu_custom_call" | custom-call | bytes 3000000 | tf_op jit(solution)/shard_map/parts/pallas_call | solution.py:457
  44.2 2.0 %step.5 = (f32[6,125,128]{2,1,0:T(8,128)S(1)}, f32[384,384]{1,0:T(8,128)S(1)}, f32[48,128]{1,0:T(8,128)}, f32[48,128]{1,0:T(8,128)S(1)}) custom-call(f32[3,208,128]{2,1,0:T(8,128)S(1)} %get-tuple-element.58.refs_0_.u_ref, f32[125,128]{1,0:T(8,128)S(1)} %copy-done.3, f32[125,128]{1,0:T(8,128)S(1)} %copy-done.4, f32[5,125,128]{2,1,0:T(8,128)S(1)} %get-tuple-element.59.refs_3_, ...), custom_call_target="tpu_custom_call" | custom-call | bytes 3000000 | tf_op jit(solution)/shard_map/step/pallas_call | solution.py:457
  46.2 2.0 %collective-permute-start.5 = (f32[48,128]{1,0:T(8,128)S(1)}, f32[48,128]{1,0:T(8,128)S(1)}, u32[]{:S(2)}, u32[]{:S(2)}) collective-permute-start(f32[48,128]{1,0:T(8,128)S(1)} %get-tuple-element.61), channel_id=1, source_target_pairs={{0,1},{1,2},{2,3},{3,4},{4,5},{5,6},{6,7},{7,8},{8,9},{9,10},{10,1... | collective-permute-start | bytes 73736 | tf_op jit(solution)/shard_map/ppermute | solution.py:471
  48.2 1.3 %parts.5 = (bf16[64,256]{1,0:T(8,128)(2,1)S(1)}, bf16[64,256]{1,0:T(8,128)(2,1)S(1)}, bf16[64,256]{1,0:T(8,128)(2,1)S(1)}, bf16[64,256]{1,0:T(8,128)(2,1)S(1)}) custom-call(s32[3]{0:T(128)S(1)} %pad_add_fusion.index_ref, f32[6,125,128]{2,1,0:T(8,128)S(1)} %get-tuple-element.76.strain_ref, bf16[3,208,128]{2,1,0:T(8,128)(2,1)S(1)} %get-tuple-element.77.low_ref, ...), custom_call_target="tpu_custom_call" | custom-call | bytes 3000000 | tf_op jit(solution)/shard_map/parts/pallas_call | solution.py:457
  49.5 4.3 %collective-permute-done.5.before_ref = f32[48,128]{1,0:T(8,128)S(1)} collective-permute-done((f32[48,128]{1,0:T(8,128)S(1)}, f32[48,128]{1,0:T(8,128)S(1)}, u32[]{:S(2)}, u32[]{:S(2)}) %collective-permute-start.5) | collective-permute-done | bytes 24608 | tf_op jit(solution)/shard_map/ppermute | solution.py:471
  54.4 2.9 %collective-permute-start.15 = (bf16[64,256]{1,0:T(8,128)(2,1)S(1)}, bf16[64,256]{1,0:T(8,128)(2,1)S(1)}, u32[]{:S(2)}, u32[]{:S(2)}) collective-permute-start(bf16[64,256]{1,0:T(8,128)(2,1)S(1)} %get-tuple-element.79), channel_id=1, source_target_pairs={{0,1},{1,0},{2,3},{3,2},{4,5},{5,4},{6,7},{7,6},{8,9},{9,8},{10,11... | collective-permute-start | bytes 98312 | tf_op jit(solution)/shard_map/ppermute | solution.py:538
  57.4 0.9 %collective-permute-start.16 = (bf16[64,256]{1,0:T(8,128)(2,1)S(1)}, bf16[64,256]{1,0:T(8,128)(2,1)S(1)}, u32[]{:S(2)}, u32[]{:S(2)}) collective-permute-start(bf16[64,256]{1,0:T(8,128)(2,1)S(1)} %get-tuple-element.80), channel_id=1, source_target_pairs={{0,2},{1,3},{2,0},{3,1},{4,6},{5,7},{6,4},{7,5},{8,10},{9,11},{10,... | collective-permute-start | bytes 98312 | tf_op jit(solution)/shard_map/ppermute | solution.py:538
  58.3 1.5 %collective-permute-start.17 = (bf16[64,256]{1,0:T(8,128)(2,1)S(1)}, bf16[64,256]{1,0:T(8,128)(2,1)S(1)}, u32[]{:S(2)}, u32[]{:S(2)}) collective-permute-start(bf16[64,256]{1,0:T(8,128)(2,1)S(1)} %get-tuple-element.81), channel_id=1, source_target_pairs={{0,3},{1,2},{2,1},{3,0},{4,7},{5,6},{6,5},{7,4},{8,11},{9,10},{10,... | collective-permute-start | bytes 98312 | tf_op jit(solution)/shard_map/ppermute | solution.py:538
  59.8 1.1 %rest.5.partial_ref = f32[3,208,128]{2,1,0:T(8,128)S(1)} custom-call(f32[384,384]{1,0:T(8,128)S(1)} %get-tuple-element.62.sigma_ref, f32[3,208,128]{2,1,0:T(8,128)S(1)} %get-tuple-element.58.refs_0_.u_ref, f32[3,208,128]{2,1,0:T(8,128)S(1)} %get-tuple-element.52.refs_0_.u_ref.p_ref, f32[208,128]{1,0:T(8,128)S(1)} %get-tuple-element.51.scale_ref, ...), custom_call_target="tpu_custom_call" | custom-call | bytes 3000000 | tf_op jit(solution)/shard_map/rest/pallas_call | solution.py:457
  60.9 1.8 %finish.1 = f32[1,3,8,1089]{3,2,1,0:T(8,128)} custom-call(f32[48,128]{1,0:T(8,128)S(1)} %collective-permute-done.5.before_ref, f32[3,208,128]{2,1,0:T(8,128)S(1)} %rest.5.partial_ref, f32[208,128]{1,0:T(8,128)S(1)} %get-tuple-element.51.scale_ref, bf16[1664,256]{1,0:T(8,128)(2,1)S(1)} %copy-done.6), custom_call_target="tpu_custom_call" | custom-call | bytes 3000000 | tf_op jit(solution)/shard_map/finish/pallas_call | solution.py:457
  62.8 1.2 %collective-permute-done.17.refs_11_ = bf16[64,256]{1,0:T(8,128)(2,1)S(1)} collective-permute-done((bf16[64,256]{1,0:T(8,128)(2,1)S(1)}, bf16[64,256]{1,0:T(8,128)(2,1)S(1)}, u32[]{:S(2)}, u32[]{:S(2)}) %collective-permute-start.17) | collective-permute-done | bytes 32800 | tf_op jit(solution)/shard_map/ppermute | solution.py:538
  64.6 0.8 %copy.20 = f32[1,256,250]{1,0,2:T(1,128)} copy(f32[1,256,250]{2,1,0:T(8,128)S(1)} %sum.1) | data formatting | bytes 512000
  (69 shorter events, 8.1 us)
Async XLA Ops:
  2.1 15.5 %collective-permute-start = (f32[8,1089]{1,0:T(8,128)S(1)}, f32[8,1089]{1,0:T(8,128)S(1)}, u32[]{:S(2)}, u32[]{:S(2)}) collective-permute-start(f32[8,1089]{1,0:T(8,128)S(1)} %maximum_maximum_fusion), channel_id=1, source_target_pairs={{0,15},{1,0},{2,1},{3,2},{4,3},{5,4},{6,5},{7,6},{8,7},{9,8},{10,9... | collective-permute-start | bytes 104552 | tf_op jit(solution)/shard_map/ppermute | solution.py:471
  11.2 1.4 %copy-start.2 = (bf16[256,1664]{1,0:T(8,128)(2,1)S(1)}, bf16[256,1664]{1,0:T(8,128)(2,1)}, u32[]{:S(2)}) copy-start(bf16[256,1664]{1,0:T(8,128)(2,1)} %constant.29.clone.spread_ref) | copy-start | bytes 2555908
  11.2 1.5 %copy-start.8 = (f32[1,3,8,1089]{3,2,1,0:T(8,128)S(1)}, f32[1,3,8,1089]{3,2,1,0:T(8,128)}, u32[]{:S(2)}) copy-start(f32[1,3,8,1089]{3,2,1,0:T(8,128)} %prev_ref.1) | copy-start | bytes 313636
  11.3 1.5 %copy-start.9 = (f32[1,3,8,1089]{3,2,1,0:T(8,128)S(1)}, f32[1,3,8,1089]{3,2,1,0:T(8,128)}, u32[]{:S(2)}) copy-start(f32[1,3,8,1089]{3,2,1,0:T(8,128)} %now_ref.1) | copy-start | bytes 313636
  11.3 1.5 %copy-start.10 = (f32[8,1089]{1,0:T(8,128)S(1)}, f32[8,1089]{1,0:T(8,128)}, u32[]{:S(2)}) copy-start(f32[8,1089]{1,0:T(8,128)} %density_ref.1) | copy-start | bytes 104548
  11.3 1.5 %copy-start.11 = (f32[3,128]{1,0:T(4,128)S(1)}, f32[3,128]{1,0:T(4,128)}, u32[]{:S(2)}) copy-start(f32[3,128]{1,0:T(4,128)} %refs_4_.5) | copy-start | bytes 4612
  18.7 7.1 %copy-start.1 = (bf16[3,208,384]{2,1,0:T(8,128)(2,1)S(1)}, bf16[3,208,384]{2,1,0:T(8,128)(2,1)}, u32[]{:S(2)}) copy-start(bf16[3,208,384]{2,1,0:T(8,128)(2,1)} %constant.27.clone.force_table) | copy-start | bytes 1437700
  20.1 7.5 %collective-permute-start.1 = (f32[48,128]{1,0:T(8,128)S(1)}, f32[48,128]{1,0:T(8,128)S(1)}, u32[]{:S(2)}, u32[]{:S(2)}) collective-permute-start(f32[48,128]{1,0:T(8,128)S(1)} %get-tuple-element.47), channel_id=1, source_target_pairs={{0,1},{1,2},{2,3},{3,4},{4,5},{5,6},{6,7},{7,8},{8,9},{9,10},{10,1... | collective-permute-start | bytes 73736 | tf_op jit(solution)/shard_map/ppermute | solution.py:471
  20.2 7.4 %collective-permute-start.2 = (f32[48,128]{1,0:T(8,128)S(1)}, f32[48,128]{1,0:T(8,128)S(1)}, u32[]{:S(2)}, u32[]{:S(2)}) collective-permute-start(f32[48,128]{1,0:T(8,128)S(1)} %get-tuple-element.48), channel_id=1, source_target_pairs={{0,15},{1,0},{2,1},{3,2},{4,3},{5,4},{6,5},{7,6},{8,7},{9,8},{10,9... | collective-permute-start | bytes 73736 | tf_op jit(solution)/shard_map/ppermute | solution.py:471
  29.3 7.5 %collective-permute-start.3 = (f32[48,128]{1,0:T(8,128)S(1)}, f32[48,128]{1,0:T(8,128)S(1)}, u32[]{:S(2)}, u32[]{:S(2)}) collective-permute-start(f32[48,128]{1,0:T(8,128)S(1)} %get-tuple-element.55), channel_id=1, source_target_pairs={{0,1},{1,2},{2,3},{3,4},{4,5},{5,6},{6,7},{7,8},{8,9},{9,10},{10,1... | collective-permute-start | bytes 73736 | tf_op jit(solution)/shard_map/ppermute | solution.py:471
  29.3 7.4 %collective-permute-start.4 = (f32[48,128]{1,0:T(8,128)S(1)}, f32[48,128]{1,0:T(8,128)S(1)}, u32[]{:S(2)}, u32[]{:S(2)}) collective-permute-start(f32[48,128]{1,0:T(8,128)S(1)} %get-tuple-element.56), channel_id=1, source_target_pairs={{0,15},{1,0},{2,1},{3,2},{4,3},{5,4},{6,5},{7,6},{8,7},{9,8},{10,9... | collective-permute-start | bytes 73736 | tf_op jit(solution)/shard_map/ppermute | solution.py:471
  35.2 1.9 %collective-permute-start.6 = (bf16[3,208,128]{2,1,0:T(8,128)(2,1)S(1)}, bf16[3,208,128]{2,1,0:T(8,128)(2,1)S(1)}, u32[]{:S(2)}, u32[]{:S(2)}) collective-permute-start(bf16[3,208,128]{2,1,0:T(8,128)(2,1)S(1)} %get-tuple-element.64.low_ref), channel_id=1, source_target_pairs={{0,16},{16,0},{1,17},{17,1},{2,18},{18,2},{3,19},{19,3},{4,20},{20... | collective-permute-start | bytes 479240 | tf_op jit(solution)/shard_map/ppermute | solution.py:471
  35.2 7.7 %collective-permute-start.10 = (bf16[3,208,128]{2,1,0:T(8,128)(2,1)S(1)}, bf16[3,208,128]{2,1,0:T(8,128)(2,1)S(1)}, u32[]{:S(2)}, u32[]{:S(2)}) collective-permute-start(bf16[3,208,128]{2,1,0:T(8,128)(2,1)S(1)} %get-tuple-element.71.low_ref), channel_id=1, source_target_pairs={{0,16},{16,0},{1,17},{17,1},{2,18},{18,2},{3,19},{19,3},{4,20},{20... | collective-permute-start | bytes 479240 | tf_op jit(solution)/shard_map/ppermute | solution.py:471
  37.0 9.2 %collective-permute-start.14 = (bf16[3,208,128]{2,1,0:T(8,128)(2,1)S(1)}, bf16[3,208,128]{2,1,0:T(8,128)(2,1)S(1)}, u32[]{:S(2)}, u32[]{:S(2)}) collective-permute-start(bf16[3,208,128]{2,1,0:T(8,128)(2,1)S(1)} %get-tuple-element.77.low_ref), channel_id=1, source_target_pairs={{0,16},{16,0},{1,17},{17,1},{2,18},{18,2},{3,19},{19,3},{4,20},{20... | collective-permute-start | bytes 479240 | tf_op jit(solution)/shard_map/ppermute | solution.py:471
  38.4 15.4 %collective-permute-start.7 = (bf16[64,256]{1,0:T(8,128)(2,1)S(1)}, bf16[64,256]{1,0:T(8,128)(2,1)S(1)}, u32[]{:S(2)}, u32[]{:S(2)}) collective-permute-start(bf16[64,256]{1,0:T(8,128)(2,1)S(1)} %get-tuple-element.67), channel_id=1, source_target_pairs={{0,1},{1,0},{2,3},{3,2},{4,5},{5,4},{6,7},{7,6},{8,9},{9,8},{10,11... | collective-permute-start | bytes 98312 | tf_op jit(solution)/shard_map/ppermute | solution.py:538
  38.5 16.0 %collective-permute-start.8 = (bf16[64,256]{1,0:T(8,128)(2,1)S(1)}, bf16[64,256]{1,0:T(8,128)(2,1)S(1)}, u32[]{:S(2)}, u32[]{:S(2)}) collective-permute-start(bf16[64,256]{1,0:T(8,128)(2,1)S(1)} %get-tuple-element.68), channel_id=1, source_target_pairs={{0,2},{1,3},{2,0},{3,1},{4,6},{5,7},{6,4},{7,5},{8,10},{9,11},{10,... | collective-permute-start | bytes 98312 | tf_op jit(solution)/shard_map/ppermute | solution.py:538
  40.3 17.0 %collective-permute-start.9 = (bf16[64,256]{1,0:T(8,128)(2,1)S(1)}, bf16[64,256]{1,0:T(8,128)(2,1)S(1)}, u32[]{:S(2)}, u32[]{:S(2)}) collective-permute-start(bf16[64,256]{1,0:T(8,128)(2,1)S(1)} %get-tuple-element.69), channel_id=1, source_target_pairs={{0,3},{1,2},{2,1},{3,0},{4,7},{5,6},{6,5},{7,4},{8,11},{9,10},{10,... | collective-permute-start | bytes 98312 | tf_op jit(solution)/shard_map/ppermute | solution.py:538
  44.1 14.1 %collective-permute-start.11 = (bf16[64,256]{1,0:T(8,128)(2,1)S(1)}, bf16[64,256]{1,0:T(8,128)(2,1)S(1)}, u32[]{:S(2)}, u32[]{:S(2)}) collective-permute-start(bf16[64,256]{1,0:T(8,128)(2,1)S(1)} %get-tuple-element.73), channel_id=1, source_target_pairs={{0,1},{1,0},{2,3},{3,2},{4,5},{5,4},{6,7},{7,6},{8,9},{9,8},{10,11... | collective-permute-start | bytes 98312 | tf_op jit(solution)/shard_map/ppermute | solution.py:538
  46.2 7.6 %collective-permute-start.5 = (f32[48,128]{1,0:T(8,128)S(1)}, f32[48,128]{1,0:T(8,128)S(1)}, u32[]{:S(2)}, u32[]{:S(2)}) collective-permute-start(f32[48,128]{1,0:T(8,128)S(1)} %get-tuple-element.61), channel_id=1, source_target_pairs={{0,1},{1,2},{2,3},{3,4},{4,5},{5,6},{6,7},{7,8},{8,9},{9,10},{10,1... | collective-permute-start | bytes 73736 | tf_op jit(solution)/shard_map/ppermute | solution.py:471
  53.9 8.9 %collective-permute-start.12 = (bf16[64,256]{1,0:T(8,128)(2,1)S(1)}, bf16[64,256]{1,0:T(8,128)(2,1)S(1)}, u32[]{:S(2)}, u32[]{:S(2)}) collective-permute-start(bf16[64,256]{1,0:T(8,128)(2,1)S(1)} %get-tuple-element.74), channel_id=1, source_target_pairs={{0,2},{1,3},{2,0},{3,1},{4,6},{5,7},{6,4},{7,5},{8,10},{9,11},{10,... | collective-permute-start | bytes 98312 | tf_op jit(solution)/shard_map/ppermute | solution.py:538
  53.9 8.9 %collective-permute-start.13 = (bf16[64,256]{1,0:T(8,128)(2,1)S(1)}, bf16[64,256]{1,0:T(8,128)(2,1)S(1)}, u32[]{:S(2)}, u32[]{:S(2)}) collective-permute-start(bf16[64,256]{1,0:T(8,128)(2,1)S(1)} %get-tuple-element.75), channel_id=1, source_target_pairs={{0,3},{1,2},{2,1},{3,0},{4,7},{5,6},{6,5},{7,4},{8,11},{9,10},{10,... | collective-permute-start | bytes 98312 | tf_op jit(solution)/shard_map/ppermute | solution.py:538
  54.4 8.3 %collective-permute-start.15 = (bf16[64,256]{1,0:T(8,128)(2,1)S(1)}, bf16[64,256]{1,0:T(8,128)(2,1)S(1)}, u32[]{:S(2)}, u32[]{:S(2)}) collective-permute-start(bf16[64,256]{1,0:T(8,128)(2,1)S(1)} %get-tuple-element.79), channel_id=1, source_target_pairs={{0,1},{1,0},{2,3},{3,2},{4,5},{5,4},{6,7},{7,6},{8,9},{9,8},{10,11... | collective-permute-start | bytes 98312 | tf_op jit(solution)/shard_map/ppermute | solution.py:538
  57.4 5.4 %collective-permute-start.16 = (bf16[64,256]{1,0:T(8,128)(2,1)S(1)}, bf16[64,256]{1,0:T(8,128)(2,1)S(1)}, u32[]{:S(2)}, u32[]{:S(2)}) collective-permute-start(bf16[64,256]{1,0:T(8,128)(2,1)S(1)} %get-tuple-element.80), channel_id=1, source_target_pairs={{0,2},{1,3},{2,0},{3,1},{4,6},{5,7},{6,4},{7,5},{8,10},{9,11},{10,... | collective-permute-start | bytes 98312 | tf_op jit(solution)/shard_map/ppermute | solution.py:538
  58.3 5.7 %collective-permute-start.17 = (bf16[64,256]{1,0:T(8,128)(2,1)S(1)}, bf16[64,256]{1,0:T(8,128)(2,1)S(1)}, u32[]{:S(2)}, u32[]{:S(2)}) collective-permute-start(bf16[64,256]{1,0:T(8,128)(2,1)S(1)} %get-tuple-element.81), channel_id=1, source_target_pairs={{0,3},{1,2},{2,1},{3,0},{4,7},{5,6},{6,5},{7,4},{8,11},{9,10},{10,... | collective-permute-start | bytes 98312 | tf_op jit(solution)/shard_map/ppermute | solution.py:538
  (10 other events, 9.7 us)
where the time goes:
time: 65.7 us; the launch traced here: 65.4 us
  starting transfers between devices  31.5 us (48%)
  Pallas kernels  20.2 us (31%)
  waiting for transfers between devices  6.3 us (10%)
  local copies, waits for them, and re-layouts  5.6 us (9%)
  between operations  0.94 us (1%)
  other arithmetic  0.81 us (1%)
    ppermute x9, starting transfers between devices, passed_along(): lax.ppermute(value, axis, [(source, (source + steps) % count) for source...  21.1 us
    pallas_call x15, Pallas kernels, call(): pl.pallas_call(kernel, name=name, out_shape=outs, in_specs=[SMEM] * scala...  20.2 us
    ppermute x9, starting transfers between devices, per_device(): lax.ppermute(sent[k], 'sub', [(j, j ^ k) for j in range(subs)])  10.4 us
    ppermute x9, waiting for transfers between devices, passed_along(): lax.ppermute(value, axis, [(source, (source + steps) % count) for source...  5.08 us
    unnamed x29, local copies, waits for them, and re-layouts  3.98 us
  transfers between devices with their start and end apart: 18, of which 3 were waited for; matrix products, arithmetic and copies ran while one was open for 4% of the time, Pallas kernels for 24%

commit v1 on v0

--- a/solution.py
+++ b/solution.py
@@ -178,9 +178,26 @@
     return jnp.concatenate([value[0], value[1], value[2]], axis=1)
 
 
+def gather_kernel(now_ref, prev_ref, density_ref, rim_ref):
+    for c in range(3):
+        rim_ref[c : c + 1, :] = now_ref[0, c, 0:1, :]
+        rim_ref[3 + c : 4 + c, :] = prev_ref[0, c, 0:1, :]
+    rim_ref[6:7, :] = density_ref[0:1, :]
+    rim_ref[7:8, :] = density_ref[0:1, :]
+
+
+def weighted_memory(memory_ref, decays, part, power):
+    value = 0.0
+    for l in range(3):
+        factor = decays[l]
+        for _ in range(power - 1):
+            factor = factor * decays[l]
+        value = value + factor * memory_ref[l, part, :, 0, :]
+    return value
+
+
 def prologue_kernel(
-    index_ref, now_ref, prev_ref, density_ref, memory_ref, decay_ref, owner_col_ref, owner_row_ref, spread_ref, mass_ref,
-    u_ref, p_ref, scale_ref, m1_ref, m2_ref, m3_ref, select_ref, window_ref,
+    now_ref, prev_ref, density_ref, memory_ref, decay_ref, spread_ref, mass_ref, u_ref, p_ref, scale_ref, m1_ref, window_ref
 ):
     rows = jnp.concatenate([now_ref[0].reshape(24, FACE), prev_ref[0].reshape(24, FACE), density_ref[...]], axis=0)
     columns = to_columns(rows, window_ref, spread_ref)
@@ -203,24 +220,26 @@
                     scale_ref[at, :] = jnp.zeros((8, LANES), F32)
     decays = [decay_ref[l : l + 1, :] for l in range(3)]
     for part in range(5):
-        terms = [decays[l] * memory_ref[0, l, part] for l in range(3)]
-        m1_ref[part] = terms[0] + terms[1] + terms[2]
-        terms = [decays[l] * terms[l] for l in range(3)]
-        m2_ref[part] = terms[0] + terms[1] + terms[2]
-        terms = [decays[l] * terms[l] for l in range(3)]
-        m3_ref[part] = terms[0] + terms[1] + terms[2]
-    owner_row = owner_row_ref[...]
+        m1_ref[part] = weighted_memory(memory_ref, decays, part, 1)
+
+
+def later_kernel(index_ref, memory_ref, decay_ref, owner_ref, m2_ref, m3_ref, select_ref):
+    decays = [decay_ref[l : l + 1, :] for l in range(3)]
+    for part in range(5):
+        m2_ref[part] = weighted_memory(memory_ref, decays, part, 2)
+        m3_ref[part] = weighted_memory(memory_ref, decays, part, 3)
+    owner = jnp.concatenate([owner_ref[0], owner_ref[1]], axis=1)
+    named = jnp.where(lax.broadcasted_iota(jnp.int32, (16, LANES), 0) == owner, 1.0, 0.0)
     earlier = lax.broadcasted_iota(jnp.int32, (LANES, LANES), 0)
     later = lax.broadcasted_iota(jnp.int32, (LANES, LANES), 1)
-    ahead = (owner_col_ref[...] == owner_row) & (earlier < later) & ((earlier // 64) == (later // 64))
-    rank = jnp.sum(jnp.where(ahead, 1.0, 0.0), axis=0, keepdims=True).astype(jnp.int32)
-    total = select_ref.shape[0]
-    subs = index_ref[2]
-    slots = total // subs
-    slot = lax.broadcasted_iota(jnp.int32, (total, LANES), 0)
-    toward = (slot // slots) ^ index_ref[0]
+    ahead = jnp.where((earlier < later) & ((earlier // 64) == (later // 64)), 1.0, 0.0)
+    rank = jnp.sum(named * dot(named.astype(BF16), ahead.astype(BF16)), axis=0, keepdims=True).astype(jnp.int32)
+    subs = select_ref.shape[0] // LANES
+    slots = 4 * EY * EZ // subs
+    row = lax.broadcasted_iota(jnp.int32, select_ref.shape, 0)
+    toward = (row // LANES) ^ index_ref[0]
     wanted = (lanes_of((1, LANES)) // 64) * (slots // 2) + rank
-    chosen = (owner_row == toward) & (wanted == slot % slots)
+    chosen = (owner == toward) & (wanted == row % slots)
     select_ref[...] = jnp.where(chosen, 1.0, 0.0).astype(BF16)
 
 
@@ -274,10 +293,10 @@
 
 
 def step_kernel(step, *refs):
-    u_ref, lame_ref, mu_ref, m_ref, decay_ref, grad_table, face_table = refs[0:7]
-    older = refs[7 : 7 + step]
-    refs = refs[7 + step :]
-    strain_ref, sigma_ref, first_ref, last_ref = refs[0:4]
+    index_ref, u_ref, lame_ref, mu_ref, m_ref, decay_ref, grad_table, face_table = refs[0:8]
+    older = refs[8 : 8 + step]
+    refs = refs[8 + step :]
+    strain_ref, sigma_ref, odd_ref, even_ref = refs[0:4]
     keep_ref = refs[4] if step < STEPS - 1 else None
     grad_ref = refs[-1]
     grad_ref[...] = dot_six(grad_table, beside(u_ref))
@@ -321,8 +340,14 @@
             for c in range(3):
                 sigma_ref[direction * 128 + rows.start : direction * 128 + rows.stop, c * LANES : (c + 1) * LANES] = values[c]
     faces = dot_six(face_table, sigma_ref[...])
-    first_ref[...] = pack_face(faces[0:32], False)
-    last_ref[...] = pack_face(faces[32:64], True)
+    first, last = pack_face(faces[0:32], False), pack_face(faces[32:64], True)
+    if step < STEPS - 1:
+        even_ring = index_ref[2] == 0
+        odd_ref[...] = jnp.where(even_ring, first, last)
+        even_ref[...] = jnp.where(even_ring, last, first)
+    else:
+        odd_ref[...] = first
+        even_ref[...] = last
 
 
 def rest_kernel(sigma_ref, u_ref, p_ref, scale_ref, force_table, next_ref):
@@ -350,13 +375,13 @@
     delta_ref[...] = jnp.zeros(delta_ref.shape, F32)
     lower = lanes_of((25, LANES)) < 64
     if from_before is not None:
-        packed = from_before[...]
+        packed = from_before
         turned = rolled(packed, 64, 1)
         values = [packed[0:32], turned[0:32], jnp.concatenate([packed[32:48], turned[32:48]], axis=0)]
         for c in range(3):
             delta_ref[c, pl.ds(0, 25, stride=8), :] = jnp.where(lower, values[c][0:25], 0.0)
     if from_after is not None:
-        packed = from_after[...]
+        packed = from_after
         turned = rolled(packed, 64, 1)
         values = [turned[0:32], packed[0:32], jnp.concatenate([turned[32:48], packed[32:48]], axis=0)]
         for c in range(3):
@@ -375,13 +400,15 @@
         u_ref[c, 200:208, :] = jnp.zeros((8, LANES), F32)
 
 
-def update_kernel(before_ref, after_ref, partial_ref, scale_ref, u_ref, low_ref, delta_ref):
-    add_faces(before_ref, after_ref, partial_ref, scale_ref, u_ref, delta_ref)
+def update_kernel(index_ref, odd_ref, even_ref, partial_ref, scale_ref, u_ref, low_ref, delta_ref):
+    even_ring = index_ref[2] == 0
+    odd, even = odd_ref[...], even_ref[...]
+    before, after = jnp.where(even_ring, odd, even), jnp.where(even_ring, even, odd)
+    add_faces(before, after, partial_ref, scale_ref, u_ref, delta_ref)
     low_ref[...] = u_ref[...].astype(BF16)
 
 
-def parts_kernel(index_ref, strain_ref, low_ref, far_ref, lame_ref, mu_ref, select_ref, grad_table, *refs):
-    out_refs, (grad_ref, kernel_ref) = refs[:-2], refs[-2:]
+def kernel_parts(index_ref, strain_ref, low_ref, far_ref, lame_ref, mu_ref, grad_table, grad_ref, kernel_ref):
     forward = jnp.where(index_ref[1] == 0, beside(low_ref), beside(far_ref))
     grad_ref[...] = dot(grad_table[0], forward) + (dot(grad_table[1], forward) + dot(grad_table[2], forward))
     for rows in CHUNKS:
@@ -401,26 +428,59 @@
         )
         kernel_ref[125 + rows.start : 125 + rows.stop, :] = time_step * twice_mu * product
     kernel_ref[250:256, :] = jnp.zeros((6, LANES), F32)
-    outgoing = lax.dot_general(
-        select_ref[...], kernel_ref[...].astype(BF16), (((1,), (1,)), ((), ())), preferred_element_type=F32
-    ).astype(BF16)
-    slots = out_refs[0].shape[0]
+    return kernel_ref[...].astype(BF16)
+
+
+def parts_kernel(
+    index_ref, strain_ref, low_ref, far_ref, lame_ref, mu_ref, grad_table, part_ref, grad_ref, kernel_ref
+):
+    part_ref[...] = kernel_parts(
+        index_ref, strain_ref, low_ref, far_ref, lame_ref, mu_ref, grad_table, grad_ref, kernel_ref
+    )
+
+
+def send_kernel(
+    index_ref, strain_ref, low_ref, far_ref, lame_ref, mu_ref, grad_table, one_ref, two_ref, select_ref, *refs
+):
+    out_refs, (grad_ref, kernel_ref) = refs[:-2], refs[-2:]
+    three = kernel_parts(index_ref, strain_ref, low_ref, far_ref, lame_ref, mu_ref, grad_table, grad_ref, kernel_ref)
+    rows = out_refs[0].shape[0]
+    slots = rows // 2
+    group = lanes_of((rows, LANES)) // slots
+    over_lanes = (((1,), (1,)), ((), ()))
     for k, ref in enumerate(out_refs):
-        ref[...] = outgoing[k * slots : (k + 1) * slots]
+        chosen = select_ref[k * LANES : (k + 1) * LANES, :]
+        total = 0.0
+        for part in (one_ref[...], two_ref[...], three):
+            total = total + lax.dot_general(part, chosen, over_lanes, preferred_element_type=F32)
+        value = total[0:rows]
+        for j in range(1, 256 // rows):
+            value = jnp.where(group == j, total[j * rows : (j + 1) * rows], value)
+        ref[...] = value
 
 
 def sum_kernel(index_ref, *refs):
     in_refs, out_ref = refs[:-1], refs[-1]
-    subs = len(in_refs) // STEPS
-    slots = in_refs[0].shape[0]
-    for k in range(subs):
-        value = in_refs[k][...].astype(F32) + in_refs[subs + k][...].astype(F32) + in_refs[2 * subs + k][...].astype(F32)
-        start = pl.multiple_of((index_ref[0] ^ k) * slots, 16)
-        out_ref[0, pl.ds(start, slots), :] = value[:, 0:250]
+    rows = in_refs[0].shape[0]
+    slots = rows // 2
+    pieces = 256 // rows
+    group = lanes_of((rows, LANES)) // slots
+    blocks = [[jnp.zeros((rows, LANES), F32)] * 2 for _ in range(pieces)]
+    for k, ref in enumerate(in_refs):
+        source = index_ref[0] ^ k
+        spot = source % pieces
+        value = ref[...]
+        for j in range(pieces):
+            moved = pltpu.roll(value, ((spot + pieces - j) % pieces) * slots, 1)
+            for t in range(2):
+                here = (group == spot) & (source // pieces == t)
+                blocks[j][t] = jnp.where(here, moved, blocks[j][t])
+    value = jnp.concatenate([jnp.concatenate(row, axis=1) for row in blocks], axis=0)
+    out_ref[:, 0, :] = value[0:250]
 
 
 def finish_kernel(before_ref, partial_ref, scale_ref, collect_ref, out_ref, u_ref, delta_ref):
-    add_faces(before_ref, None, partial_ref, scale_ref, u_ref, delta_ref)
+    add_faces(before_ref[...], None, partial_ref, scale_ref, u_ref, delta_ref)
     lane = lanes_of((8, LANES))
     sub = lax.broadcasted_iota(jnp.int32, (8, LANES), 0)
     tiles = []
@@ -471,16 +531,22 @@
     return lax.ppermute(value, axis, [(source, (source + steps) % count) for source in range(count)])
 
 
+def swapped(value, axis, first):
+    count = lax.axis_size(axis)
+    pairs = []
+    for source in range(first, count, 2):
+        other = (source + 1) % count
+        pairs += [(source, other), (other, source)]
+    return lax.ppermute(value, axis, pairs)
+
+
 def per_device(disp_now, disp_prev, memory_init, density, lame_lambda, shear_mu, sls_decay, owner_map):
     ring = ("cuts", "sub")
     subs = lax.axis_size("sub")
     groups = lax.axis_size("group")
-    slots = 2 * EY * EZ * 2 // subs
-    index = jnp.stack([lax.axis_index("sub"), lax.axis_index("group"), jnp.int32(subs)]).astype(jnp.int32)
-
-    rim = jnp.concatenate(
-        [disp_now[0, :, 0, :], disp_prev[0, :, 0, :], density[0:1, :], jnp.ones((1, FACE), F32)], axis=0
-    )
+    index = jnp.stack([lax.axis_index("sub"), lax.axis_index("group"), lax.axis_index(ring) % 2]).astype(jnp.int32)
+
+    rim = call(gather_kernel, "gather", shaped(8, FACE), [], disp_now, disp_prev, density)
     rim = passed_along(rim, ring, -1)
 
     grad_table = jnp.asarray(cut_table(GRAD))
@@ -489,66 +555,79 @@
     spread = jnp.asarray(SPREAD, BF16)
     collect = jnp.asarray(COLLECT, BF16)
     mass = jnp.asarray(MASS)
+    memory = jnp.transpose(memory_init, (1, 2, 3, 0, 4))
+    owner = jnp.transpose(owner_map, (0, 2, 1))
 
     state = shaped(3, ROWS, LANES)
     state_low = shaped(3, ROWS, LANES, dtype=BF16)
     scale_shape = shaped(ROWS, LANES)
     five = shaped(5, 125, LANES)
-    u, p, scale, m1, m2, m3, select = call(
-        prologue_kernel, "prologue",
-        [state, state, scale_shape, five, five, five, shaped(subs * slots, LANES, dtype=BF16)],
-        [pltpu.VMEM((8, 56, WINDOW), F32)],
-        index, disp_now, disp_prev, density, memory_init, sls_decay,
-        owner_map.reshape(2 * EY * EZ, 1), owner_map.reshape(1, 2 * EY * EZ), spread, mass,
-        scalars=1, micros=3,
+    part_shape = shaped(256, LANES, dtype=BF16)
+    grad_scratch = pltpu.VMEM((384, 384), F32)
+    part_scratch = [grad_scratch, pltpu.VMEM((256, LANES), F32)]
+    face = shaped(48, LANES)
+    u, p, scale, m1 = call(
+        prologue_kernel, "prologue", [state, state, scale_shape, five], [pltpu.VMEM((8, 56, WINDOW), F32)],
+        disp_now, disp_prev, density, memory, sls_decay, spread, mass, micros=3,
     )
     u, p, scale, low = call(
         rim_kernel, "rim", [state, state, scale_shape, state_low],
         [pltpu.VMEM((8, 8, WINDOW), F32), pltpu.VMEM((ROWS, LANES), F32)],
         rim, u, p, scale, spread, mass,
     )
-    memories = (m1, m2, m3)
+    memories = [m1]
     kept = []
     parts = []
     for step in range(STEPS):
+        outs = [shaped(6, 125, LANES), shaped(384, 384), face, face]
+        if step < STEPS - 1:
+            outs.append(five)
+        results = call(
+            lambda *refs, step=step: step_kernel(step, *refs), "step", outs, [grad_scratch],
+            index, u, lame_lambda, shear_mu, memories[step], sls_decay, grad_table, face_table, *kept, scalars=1,
+        )
+        strain, sigma, odd, even = results[0:4]
+        kept.extend(results[4:])
+        if step < STEPS - 1:
+            odd = swapped(odd, ring, 1)
+            even = swapped(even, ring, 0)
+        else:
+            before = passed_along(even, ring, 1)
         far = None
         for k in range(1, groups):
             moved = passed_along(low, "group", k)
             far = moved if far is None else jnp.where(lax.axis_index("group") == k, moved, far)
-        outs = [shaped(6, 125, LANES), shaped(384, 384), shaped(48, LANES), shaped(48, LANES)]
+        partial = call(rest_kernel, "rest", state, [], sigma, u, p, scale, force_table)
+        shared = (index, strain, low, far, lame_lambda, shear_mu, grad_table)
         if step < STEPS - 1:
-            outs.append(five)
-        results = call(
-            lambda *refs, step=step: step_kernel(step, *refs), "step", outs, [pltpu.VMEM((384, 384), F32)],
-            u, lame_lambda, shear_mu, memories[step], sls_decay, grad_table, face_table, *kept,
-        )
-        strain, sigma, first, last = results[0:4]
-        kept.extend(results[4:])
-        from_before = passed_along(last, ring, 1)
-        if step < STEPS - 1:
-            from_after = passed_along(first, ring, -1)
-        partial = call(rest_kernel, "rest", state, [], sigma, u, p, scale, force_table)
-        sent = call(
-            parts_kernel, "parts", [shaped(slots, WINDOW, dtype=BF16)] * subs,
-            [pltpu.VMEM((384, 384), F32), pltpu.VMEM((256, LANES), F32)],
-            index, strain, low, far, lame_lambda, shear_mu, select, grad_table, scalars=1,
-        )
-        parts.append(sent[0])
-        for k in range(1, subs):
-            parts.append(lax.ppermute(sent[k], "sub", [(j, j ^ k) for j in range(subs)]))
-        p = u
-        if step < STEPS - 1:
+            parts.append(call(parts_kernel, "parts", part_shape, part_scratch, *shared, scalars=1))
+            if step == 0:
+                m2, m3, select = call(
+                    later_kernel, "later", [five, five, shaped(subs * LANES, LANES, dtype=BF16)], [],
+                    index, memory, sls_decay, owner, scalars=1,
+                )
+                memories += [m2, m3]
+                partial, parts[0], select, memories[2] = lax.optimization_barrier((partial, parts[0], select, m3))
+            else:
+                partial, parts[1] = lax.optimization_barrier((partial, parts[1]))
+            p = u
             u, low = call(
                 update_kernel, "update", [state, state_low], [pltpu.VMEM((3, ROWS, LANES), F32)],
-                from_before, from_after, partial, scale,
+                index, odd, even, partial, scale, scalars=1,
             )
+        else:
+            sent = list(call(
+                send_kernel, "send", [shaped(512 // subs, LANES)] * subs, part_scratch, *shared, *parts, select, scalars=1)
+            )
+            for k in range(subs - 1, 0, -1):
+                sent[k] = lax.ppermute(sent[k], "sub", [(j, j ^ k) for j in range(subs)])
     final = call(
         finish_kernel, "finish", shaped(1, 3, 8, FACE),
         [pltpu.VMEM((3, ROWS, LANES), F32), pltpu.VMEM((3, ROWS, LANES), F32)],
-        from_before, partial, scale, collect,
+        before, partial, scale, collect,
     )
-    kernels = call(sum_kernel, "sum", shaped(1, subs * slots, 250), [], index, *parts, scalars=1)
-    return final, kernels
+    kernels = call(sum_kernel, "sum", shaped(250, 1, 256), [], index, *sent, scalars=1)
+    return final, jnp.transpose(kernels, (1, 2, 0))
 
 
 def solution(mesh):

time: 65.7 us -> 55.3 us (0.84)
  starting transfers between devices: 31.5 us -> 17.3 us
  Pallas kernels: 20.2 us -> 22.5 us
  waiting for transfers between devices: 6.3 us -> 8.39 us
  other arithmetic: 0.81 us -> 0.08 us
    ppermute x9 -> x5, starting transfers between devices: 21.1 us -> 7.66 us  [passed_along(): lax.ppermute(value, axis, [(source, (source + steps) % count) for source...]
    pallas_call x15 -> x17, Pallas kernels: 20.2 us -> 22.5 us  [call(): pl.pallas_call(kernel, name=name, out_shape=outs, in_specs=[SMEM] * scala...]
    unnamed x29 -> x32, local copies, waits for them, and re-layouts: 3.98 us -> 5.84 us
    slice x6 -> x0, local copies, waits for them, and re-layouts: 1.31 us -> none  [the longest x2 0.67 us: per_device(): density[0:1, :]]
    ppermute x9 -> x7, waiting for transfers between devices: 1.22 us -> 2.49 us  [the longest x4 2.48 us: swapped(): return lax.ppermute(value, axis, pairs)]
    ppermute x9 -> x7, starting transfers between devices: 10.4 us -> 9.62 us  [the longest x4 6.07 us: swapped(): return lax.ppermute(value, axis, pairs)]
    ppermute x9 -> x5, waiting for transfers between devices: 5.08 us -> 5.9 us  [passed_along(): lax.ppermute(value, axis, [(source, (source + steps) % count) for source...]
    unnamed x1 -> x0, other arithmetic: 0.66 us -> none
  transfers between devices with their start and end apart: 18 -> 12, of which waited for: 3 -> 2; matrix products, arithmetic and copies ran while one was open for 4% -> 0% of each run, Pallas kernels for 24% -> 32%
where the time goes in v1:
time: 55.3 us; the launch traced here: 54.9 us
  Pallas kernels  22.5 us (41%)
  starting transfers between devices  17.3 us (31%)
  waiting for transfers between devices  8.39 us (15%)
  local copies, waits for them, and re-layouts  5.84 us (11%)
  between operations  0.87 us (2%)
    pallas_call x17, Pallas kernels, call(): pl.pallas_call(kernel, name=name, out_shape=outs, in_specs=[SMEM] * scala...  22.5 us
    ppermute x5, starting transfers between devices, passed_along(): lax.ppermute(value, axis, [(source, (source + steps) % count) for source...  7.66 us
    ppermute x4, starting transfers between devices, swapped(): return lax.ppermute(value, axis, pairs)  6.07 us
    ppermute x5, waiting for transfers between devices, passed_along(): lax.ppermute(value, axis, [(source, (source + steps) % count) for source...  5.9 us
    unnamed x32, local copies, waits for them, and re-layouts  5.84 us
    ppermute x3, starting transfers between devices, per_device(): sent[k] = lax.ppermute(sent[k], 'sub', [(j, j ^ k) for j in range(subs)])  3.55 us
    ppermute x4, waiting for transfers between devices, swapped(): return lax.ppermute(value, axis, pairs)  2.48 us
  transfers between devices with their start and end apart: 12, of which 2 were waited for; matrix products, arithmetic and copies ran while one was open for 0% of the time, Pallas kernels for 32%

profile of v1, /device:TPU:0, one launch (start us, length us, event | category | flops | bytes accessed | tf_op | source)
XLA Modules:
  0.0 54.9 jit_solution(6070270491115505934)
XLA Ops:
  0.6 0.9 %copy-done.10 = f32[1,3,8,1089]{3,2,1,0:T(8,128)S(1)} copy-done((f32[1,3,8,1089]{3,2,1,0:T(8,128)S(1)}, f32[1,3,8,1089]{3,2,1,0:T(8,128)}, u32[]{:S(2)}) %copy-start.10) | copy-done | bytes 104568
  1.5 0.9 %copy-done.11 = f32[1,3,8,1089]{3,2,1,0:T(8,128)S(1)} copy-done((f32[1,3,8,1089]{3,2,1,0:T(8,128)S(1)}, f32[1,3,8,1089]{3,2,1,0:T(8,128)}, u32[]{:S(2)}) %copy-start.11) | copy-done | bytes 104568
  3.2 7.0 %collective-permute-start = (f32[8,1089]{1,0:T(8,128)S(1)}, f32[8,1089]{1,0:T(8,128)S(1)}, u32[]{:S(2)}, u32[]{:S(2)}) collective-permute-start(f32[8,1089]{1,0:T(8,128)S(1)} %gather.1), channel_id=1, source_target_pairs={{0,15},{1,0},{2,1},{3,2},{4,3},{5,4},{6,5},{7,6},{8,7},{9,8},{10,9... | collective-permute-start | bytes 104552 | tf_op jit(solution)/shard_map/ppermute | solution.py:531
  10.2 1.2 %copy-done.2 = f32[1,3,5,125,128]{4,0,3,2,1:T(1,128)S(1)} copy-done((f32[1,3,5,125,128]{4,0,3,2,1:T(1,128)S(1)}, f32[1,3,5,125,128]{4,0,3,2,1:T(1,128)}, u32[]{:S(2)}) %copy-start.2) | copy-done | bytes 960024
  11.4 1.2 %copy-done.4 = bf16[256,1664]{1,0:T(8,128)(2,1)S(1)} copy-done((bf16[256,1664]{1,0:T(8,128)(2,1)S(1)}, bf16[256,1664]{1,0:T(8,128)(2,1)}, u32[]{:S(2)}) %copy-start.4) | copy-done | bytes 851992
  12.6 2.1 %prologue.1 = (f32[3,208,128]{2,1,0:T(8,128)S(1)}, f32[3,208,128]{2,1,0:T(8,128)S(1)}, f32[208,128]{1,0:T(8,128)S(1)}, f32[5,125,128]{2,1,0:T(8,128)S(1)}) custom-call(f32[1,3,8,1089]{3,2,1,0:T(8,128)S(1)} %copy-done.10, f32[1,3,8,1089]{3,2,1,0:T(8,128)S(1)} %copy-done.11, f32[8,1089]{1,0:T(8,128)S(1)} %copy-done.13, f32[3,5,125,1,128]{4,3,2,1,0:T(1,128)S(1)} %bitcast.8, ...), custom_call_target="tpu_custom_call" | custom-call | bytes 9000000 | tf_op jit(solution)/shard_map/prologue/pallas_call | solution.py:517
  15.8 2.0 %step.3 = (f32[6,125,128]{2,1,0:T(8,128)S(1)}, f32[384,384]{1,0:T(8,128)S(1)}, f32[48,128]{1,0:T(8,128)S(1)}, f32[48,128]{1,0:T(8,128)S(1)}, f32[5,125,128]{2,1,0:T(8,128)S(1)}) custom-call(s32[3]{0:T(128)S(1)} %pad_add_fusion.refs_0_.index_ref, f32[3,208,128]{2,1,0:T(8,128)S(1)} %get-tuple-element.43.refs_1_.u_ref.p_ref, f32[125,128]{1,0:T(8,128)S(1)} %copy-done.6, ...), custom_call_target="tpu_custom_call" | custom-call | bytes 3000000 | tf_op jit(solution)/shard_map/step/pallas_call | solution.py:517
  17.8 3.2 %collective-permute-start.1 = (f32[48,128]{1,0:T(8,128)S(1)}, f32[48,128]{1,0:T(8,128)S(1)}, u32[]{:S(2)}, u32[]{:S(2)}) collective-permute-start(f32[48,128]{1,0:T(8,128)S(1)} %get-tuple-element.45), channel_id=1, source_target_pairs={{1,2},{2,1},{3,4},{4,3},{5,6},{6,5},{7,8},{8,7},{9,10},{10,9},{11,... | collective-permute-start | bytes 73736 | tf_op jit(solution)/shard_map/ppermute | solution.py:540
  21.6 1.7 %later.1 = (f32[5,125,128]{2,1,0:T(8,128)S(1)}, f32[5,125,128]{2,1,0:T(8,128)S(1)}, bf16[512,128]{1,0:T(8,128)(2,1)S(1)}) custom-call(s32[3]{0:T(128)S(1)} %pad_add_fusion.refs_0_.index_ref, f32[3,5,125,1,128]{4,3,2,1,0:T(1,128)S(1)} %bitcast.9, f32[3,128]{1,0:T(4,128)S(1)} %copy-done.14, s32[2,1,64]{2,1,0:T(1,128)S(1)} %bitcast.10), custom_call_target="tpu_custom_call" | custom-call | bytes 3000000 | tf_op jit(solution)/shard_map/later/pallas_call | solution.py:517
  23.3 1.1 %rest.3.partial_ref = f32[3,208,128]{2,1,0:T(8,128)S(1)} custom-call(f32[384,384]{1,0:T(8,128)S(1)} %get-tuple-element.47.sigma_ref, f32[3,208,128]{2,1,0:T(8,128)S(1)} %get-tuple-element.43.refs_1_.u_ref.p_ref, f32[3,208,128]{2,1,0:T(8,128)S(1)} %get-tuple-element.48.p_ref, f32[208,128]{1,0:T(8,128)S(1)} %get-tuple-element.49.scale_ref, ...), custom_call_target="tpu_custom_call" | custom-call | bytes 3000000 | tf_op jit(solution)/shard_map/rest/pallas_call | solution.py:517
  24.4 1.1 %parts.2.one_ref = bf16[256,128]{1,0:T(8,128)(2,1)S(1)} custom-call(s32[3]{0:T(128)S(1)} %pad_add_fusion.refs_0_.index_ref, f32[6,125,128]{2,1,0:T(8,128)S(1)} %get-tuple-element.50.strain_ref, bf16[3,208,128]{2,1,0:T(8,128)(2,1)S(1)} %get-tuple-element.51.low_ref, bf16[3,208,128]{2,1,0:T(8,128)(2,1)S(1)} %collective-permute-done.3.far_ref, ...), custom_call_target="tpu_custom_call" | custom-call | bytes 3000000 | tf_op jit(solution)/shard_map/parts/pallas_call | solution.py:517
  26.4 2.0 %step.4 = (f32[6,125,128]{2,1,0:T(8,128)S(1)}, f32[384,384]{1,0:T(8,128)S(1)}, f32[48,128]{1,0:T(8,128)S(1)}, f32[48,128]{1,0:T(8,128)S(1)}, f32[5,125,128]{2,1,0:T(8,128)S(1)}) custom-call(s32[3]{0:T(128)S(1)} %pad_add_fusion.refs_0_.index_ref, f32[3,208,128]{2,1,0:T(8,128)S(1)} %get-tuple-element.55.refs_1_.u_ref.p_ref, f32[125,128]{1,0:T(8,128)S(1)} %copy-done.6, ...), custom_call_target="tpu_custom_call" | custom-call | bytes 3000000 | tf_op jit(solution)/shard_map/step/pallas_call | solution.py:517
  28.3 2.9 %collective-permute-start.4 = (f32[48,128]{1,0:T(8,128)S(1)}, f32[48,128]{1,0:T(8,128)S(1)}, u32[]{:S(2)}, u32[]{:S(2)}) collective-permute-start(f32[48,128]{1,0:T(8,128)S(1)} %get-tuple-element.58), channel_id=1, source_target_pairs={{1,2},{2,1},{3,4},{4,3},{5,6},{6,5},{7,8},{8,7},{9,10},{10,9},{11,... | collective-permute-start | bytes 73736 | tf_op jit(solution)/shard_map/ppermute | solution.py:540
  31.2 1.1 %rest.4.partial_ref = f32[3,208,128]{2,1,0:T(8,128)S(1)} custom-call(f32[384,384]{1,0:T(8,128)S(1)} %get-tuple-element.60.sigma_ref, f32[3,208,128]{2,1,0:T(8,128)S(1)} %get-tuple-element.55.refs_1_.u_ref.p_ref, f32[3,208,128]{2,1,0:T(8,128)S(1)} %get-tuple-element.43.refs_1_.u_ref.p_ref, f32[208,128]{1,0:T(8,128)S(1)} %get-tuple-element.49.scale_ref, ...), custom_call_target="tpu_custom_call" | custom-call | bytes 3000000 | tf_op jit(solution)/shard_map/rest/pallas_call | solution.py:517
  32.3 1.1 %parts.3.two_ref = bf16[256,128]{1,0:T(8,128)(2,1)S(1)} custom-call(s32[3]{0:T(128)S(1)} %pad_add_fusion.refs_0_.index_ref, f32[6,125,128]{2,1,0:T(8,128)S(1)} %get-tuple-element.61.strain_ref, bf16[3,208,128]{2,1,0:T(8,128)(2,1)S(1)} %get-tuple-element.62.low_ref, bf16[3,208,128]{2,1,0:T(8,128)(2,1)S(1)} %collective-permute-done.6.far_ref, ...), custom_call_target="tpu_custom_call" | custom-call | bytes 3000000 | tf_op jit(solution)/shard_map/parts/pallas_call | solution.py:517
  33.4 2.5 %collective-permute-done.4.odd_ref = f32[48,128]{1,0:T(8,128)S(1)} collective-permute-done((f32[48,128]{1,0:T(8,128)S(1)}, f32[48,128]{1,0:T(8,128)S(1)}, u32[]{:S(2)}, u32[]{:S(2)}) %collective-permute-start.4) | collective-permute-done | bytes 24608 | tf_op jit(solution)/shard_map/ppermute | solution.py:540
  36.7 2.6 %step.5 = (f32[6,125,128]{2,1,0:T(8,128)S(1)}, f32[384,384]{1,0:T(8,128)S(1)}, f32[48,128]{1,0:T(8,128)}, f32[48,128]{1,0:T(8,128)S(1)}) custom-call(s32[3]{0:T(128)S(1)} %pad_add_fusion.refs_0_.index_ref, f32[3,208,128]{2,1,0:T(8,128)S(1)} %get-tuple-element.64.refs_1_.u_ref, f32[125,128]{1,0:T(8,128)S(1)} %copy-done.6, f32[125,128]{1,0:T(8,128)S(1)} %copy-done.7, ...), custom_call_target="tpu_custom_call" | custom-call | bytes 3000000 | tf_op jit(solution)/shard_map/step/pallas_call | solution.py:517
  39.3 1.3 %send.1 = (f32[128,128]{1,0:T(8,128)S(1)}, f32[128,128]{1,0:T(8,128)S(1)}, f32[128,128]{1,0:T(8,128)S(1)}, f32[128,128]{1,0:T(8,128)S(1)}) custom-call(s32[3]{0:T(128)S(1)} %pad_add_fusion.refs_0_.index_ref, f32[6,125,128]{2,1,0:T(8,128)S(1)} %get-tuple-element.69.strain_ref, bf16[3,208,128]{2,1,0:T(8,128)(2,1)S(1)} %get-tuple-element.70.low_ref, ...), custom_call_target="tpu_custom_call" | custom-call | bytes 3000000 | tf_op jit(solution)/shard_map/send/pallas_call | solution.py:517
  40.7 1.9 %collective-permute-start.11 = (f32[128,128]{1,0:T(8,128)S(1)}, f32[128,128]{1,0:T(8,128)S(1)}, u32[]{:S(2)}, u32[]{:S(2)}) collective-permute-start(f32[128,128]{1,0:T(8,128)S(1)} %get-tuple-element.77), channel_id=1, source_target_pairs={{0,3},{1,2},{2,1},{3,0},{4,7},{5,6},{6,5},{7,4},{8,11},{9,10},{10,... | collective-permute-start | bytes 196616 | tf_op jit(solution)/shard_map/ppermute | solution.py:623
  42.6 1.6 %collective-permute-start.9 = (f32[128,128]{1,0:T(8,128)S(1)}, f32[128,128]{1,0:T(8,128)S(1)}, u32[]{:S(2)}, u32[]{:S(2)}) collective-permute-start(f32[128,128]{1,0:T(8,128)S(1)} %get-tuple-element.75), channel_id=1, source_target_pairs={{0,1},{1,0},{2,3},{3,2},{4,5},{5,4},{6,7},{7,6},{8,9},{9,8},{10,11... | collective-permute-start | bytes 196616 | tf_op jit(solution)/shard_map/ppermute | solution.py:623
  44.6 1.1 %rest.5.partial_ref = f32[3,208,128]{2,1,0:T(8,128)S(1)} custom-call(f32[384,384]{1,0:T(8,128)S(1)} %get-tuple-element.68.sigma_ref, f32[3,208,128]{2,1,0:T(8,128)S(1)} %get-tuple-element.64.refs_1_.u_ref, f32[3,208,128]{2,1,0:T(8,128)S(1)} %get-tuple-element.55.refs_1_.u_ref.p_ref, f32[208,128]{1,0:T(8,128)S(1)} %get-tuple-element.49.scale_ref, ...), custom_call_target="tpu_custom_call" | custom-call | bytes 3000000 | tf_op jit(solution)/shard_map/rest/pallas_call | solution.py:517
  45.7 5.9 %collective-permute-done.7.before_ref = f32[48,128]{1,0:T(8,128)S(1)} collective-permute-done((f32[48,128]{1,0:T(8,128)S(1)}, f32[48,128]{1,0:T(8,128)S(1)}, u32[]{:S(2)}, u32[]{:S(2)}) %collective-permute-start.7) | collective-permute-done | bytes 24608 | tf_op jit(solution)/shard_map/ppermute | solution.py:531
  51.6 1.8 %finish.1 = f32[1,3,8,1089]{3,2,1,0:T(8,128)} custom-call(f32[48,128]{1,0:T(8,128)S(1)} %collective-permute-done.7.before_ref, f32[3,208,128]{2,1,0:T(8,128)S(1)} %rest.5.partial_ref, f32[208,128]{1,0:T(8,128)S(1)} %get-tuple-element.49.scale_ref, bf16[1664,256]{1,0:T(8,128)(2,1)S(1)} %copy-done.9), custom_call_target="tpu_custom_call" | custom-call | bytes 3000000 | tf_op jit(solution)/shard_map/finish/pallas_call | solution.py:517
  53.4 1.5 %sum.1 = f32[250,1,256]{2,1,0:T(1,128)} custom-call(s32[3]{0:T(128)S(1)} %pad_add_fusion.refs_0_.index_ref, f32[128,128]{1,0:T(8,128)S(1)} %get-tuple-element.74.refs_0_, f32[128,128]{1,0:T(8,128)S(1)} %collective-permute-done.9.refs_1_, f32[128,128]{1,0:T(8,128)S(1)} %collective-permute-done.10.refs_2_, f32[128,128]{1,0:T(8,128)S(1)} %collective-permute-done.11.refs_3_), custom_call_target="tpu_custom_call" | custom-call | bytes 3000000 | tf_op jit(solution)/shard_map/sum/pallas_call | solution.py:517
  (50 shorter events, 4.8 us)
Async XLA Ops:
  3.2 7.0 %copy-start.12 = (f32[208,128]{1,0:T(8,128)S(1)}, f32[208,128]{1,0:T(8,128)}, u32[]{:S(2)}) copy-start(f32[208,128]{1,0:T(8,128)} %constant.45.clone.mass_ref) | copy-start | bytes 319492
  3.2 7.0 %copy-start.14 = (f32[3,128]{1,0:T(4,128)S(1)}, f32[3,128]{1,0:T(4,128)}, u32[]{:S(2)}) copy-start(f32[3,128]{1,0:T(4,128)} %refs_5_.5) | copy-start | bytes 4612
  3.2 11.4 %collective-permute-start = (f32[8,1089]{1,0:T(8,128)S(1)}, f32[8,1089]{1,0:T(8,128)S(1)}, u32[]{:S(2)}, u32[]{:S(2)}) collective-permute-start(f32[8,1089]{1,0:T(8,128)S(1)} %gather.1), channel_id=1, source_target_pairs={{0,15},{1,0},{2,1},{3,2},{4,3},{5,4},{6,5},{7,6},{8,7},{9,8},{10,9... | collective-permute-start | bytes 104552 | tf_op jit(solution)/shard_map/ppermute | solution.py:531
  10.2 1.2 %copy-start.2 = (f32[1,3,5,125,128]{4,0,3,2,1:T(1,128)S(1)}, f32[1,3,5,125,128]{4,0,3,2,1:T(1,128)}, u32[]{:S(2)}) copy-start(f32[1,3,5,125,128]{4,0,3,2,1:T(1,128)} %param.16) | copy-start | bytes 2880004
  11.4 1.2 %copy-start.4 = (bf16[256,1664]{1,0:T(8,128)(2,1)S(1)}, bf16[256,1664]{1,0:T(8,128)(2,1)}, u32[]{:S(2)}) copy-start(bf16[256,1664]{1,0:T(8,128)(2,1)} %constant.43.clone.spread_ref) | copy-start | bytes 2555908
  12.6 2.1 %copy-start.5 = (bf16[256,1664]{1,0:T(8,128)(2,1)S(1)}, bf16[256,1664]{1,0:T(8,128)(2,1)}, u32[]{:S(2)}) copy-start(bf16[256,1664]{1,0:T(8,128)(2,1)} %constant.43.clone.spread_ref) | copy-start | bytes 2555908
  14.7 1.1 %copy-start = (bf16[3,384,208]{2,1,0:T(8,128)(2,1)S(1)}, bf16[3,384,208]{2,1,0:T(8,128)(2,1)}, u32[]{:S(2)}) copy-start(bf16[3,384,208]{2,1,0:T(8,128)(2,1)} %constant.40.clone.refs_6_.grad_table) | copy-start | bytes 1437700
  14.7 1.1 %copy-start.6 = (f32[125,128]{1,0:T(8,128)S(1)}, f32[125,128]{1,0:T(8,128)}, u32[]{:S(2)}) copy-start(f32[125,128]{1,0:T(8,128)} %lame_ref.5) | copy-start | bytes 192004
  14.7 1.0 %copy-start.7 = (f32[125,128]{1,0:T(8,128)S(1)}, f32[125,128]{1,0:T(8,128)}, u32[]{:S(2)}) copy-start(f32[125,128]{1,0:T(8,128)} %mu_ref.5) | copy-start | bytes 192004
  14.7 1.1 %copy-start.8 = (bf16[3,64,384]{2,1,0:T(8,128)(2,1)S(1)}, bf16[3,64,384]{2,1,0:T(8,128)(2,1)}, u32[]{:S(2)}) copy-start(bf16[3,64,384]{2,1,0:T(8,128)(2,1)} %constant.42.clone.refs_7_) | copy-start | bytes 442372
  15.4 5.5 %copy-start.3 = (f32[1,3,5,125,128]{4,0,3,2,1:T(1,128)S(1)}, f32[1,3,5,125,128]{4,0,3,2,1:T(1,128)}, u32[]{:S(2)}) copy-start(f32[1,3,5,125,128]{4,0,3,2,1:T(1,128)} %param.16) | copy-start | bytes 2880004
  15.4 9.0 %collective-permute-start.3 = (bf16[3,208,128]{2,1,0:T(8,128)(2,1)S(1)}, bf16[3,208,128]{2,1,0:T(8,128)(2,1)S(1)}, u32[]{:S(2)}, u32[]{:S(2)}) collective-permute-start(bf16[3,208,128]{2,1,0:T(8,128)(2,1)S(1)} %get-tuple-element.51.low_ref), channel_id=1, source_target_pairs={{0,16},{16,0},{1,17},{17,1},{2,18},{18,2},{3,19},{19,3},{4,20},{20... | collective-permute-start | bytes 479240 | tf_op jit(solution)/shard_map/ppermute | solution.py:531
  17.8 7.7 %collective-permute-start.1 = (f32[48,128]{1,0:T(8,128)S(1)}, f32[48,128]{1,0:T(8,128)S(1)}, u32[]{:S(2)}, u32[]{:S(2)}) collective-permute-start(f32[48,128]{1,0:T(8,128)S(1)} %get-tuple-element.45), channel_id=1, source_target_pairs={{1,2},{2,1},{3,4},{4,3},{5,6},{6,5},{7,8},{8,7},{9,10},{10,9},{11,... | collective-permute-start | bytes 73736 | tf_op jit(solution)/shard_map/ppermute | solution.py:540
  20.9 4.6 %collective-permute-start.2 = (f32[48,128]{1,0:T(8,128)S(1)}, f32[48,128]{1,0:T(8,128)S(1)}, u32[]{:S(2)}, u32[]{:S(2)}) collective-permute-start(f32[48,128]{1,0:T(8,128)S(1)} %get-tuple-element.46), channel_id=1, source_target_pairs={{0,1},{1,0},{2,3},{3,2},{4,5},{5,4},{6,7},{7,6},{8,9},{9,8},{10,11... | collective-permute-start | bytes 73736 | tf_op jit(solution)/shard_map/ppermute | solution.py:540
  21.6 1.7 %copy-start.1 = (bf16[3,208,384]{2,1,0:T(8,128)(2,1)S(1)}, bf16[3,208,384]{2,1,0:T(8,128)(2,1)}, u32[]{:S(2)}) copy-start(bf16[3,208,384]{2,1,0:T(8,128)(2,1)} %constant.41.clone.force_table) | copy-start | bytes 1437700
  26.3 6.0 %collective-permute-start.6 = (bf16[3,208,128]{2,1,0:T(8,128)(2,1)S(1)}, bf16[3,208,128]{2,1,0:T(8,128)(2,1)S(1)}, u32[]{:S(2)}, u32[]{:S(2)}) collective-permute-start(bf16[3,208,128]{2,1,0:T(8,128)(2,1)S(1)} %get-tuple-element.62.low_ref), channel_id=1, source_target_pairs={{0,16},{16,0},{1,17},{17,1},{2,18},{18,2},{3,19},{19,3},{4,20},{20... | collective-permute-start | bytes 479240 | tf_op jit(solution)/shard_map/ppermute | solution.py:531
  28.3 7.5 %collective-permute-start.4 = (f32[48,128]{1,0:T(8,128)S(1)}, f32[48,128]{1,0:T(8,128)S(1)}, u32[]{:S(2)}, u32[]{:S(2)}) collective-permute-start(f32[48,128]{1,0:T(8,128)S(1)} %get-tuple-element.58), channel_id=1, source_target_pairs={{1,2},{2,1},{3,4},{4,3},{5,6},{6,5},{7,8},{8,7},{9,10},{10,9},{11,... | collective-permute-start | bytes 73736 | tf_op jit(solution)/shard_map/ppermute | solution.py:540
  31.2 4.6 %collective-permute-start.5 = (f32[48,128]{1,0:T(8,128)S(1)}, f32[48,128]{1,0:T(8,128)S(1)}, u32[]{:S(2)}, u32[]{:S(2)}) collective-permute-start(f32[48,128]{1,0:T(8,128)S(1)} %get-tuple-element.59), channel_id=1, source_target_pairs={{0,1},{1,0},{2,3},{3,2},{4,5},{5,4},{6,7},{7,6},{8,9},{9,8},{10,11... | collective-permute-start | bytes 73736 | tf_op jit(solution)/shard_map/ppermute | solution.py:540
  36.7 2.7 %collective-permute-start.8 = (bf16[3,208,128]{2,1,0:T(8,128)(2,1)S(1)}, bf16[3,208,128]{2,1,0:T(8,128)(2,1)S(1)}, u32[]{:S(2)}, u32[]{:S(2)}) collective-permute-start(bf16[3,208,128]{2,1,0:T(8,128)(2,1)S(1)} %get-tuple-element.70.low_ref), channel_id=1, source_target_pairs={{0,16},{16,0},{1,17},{17,1},{2,18},{18,2},{3,19},{19,3},{4,20},{20... | collective-permute-start | bytes 479240 | tf_op jit(solution)/shard_map/ppermute | solution.py:531
  40.6 12.8 %collective-permute-start.10 = (f32[128,128]{1,0:T(8,128)S(1)}, f32[128,128]{1,0:T(8,128)S(1)}, u32[]{:S(2)}, u32[]{:S(2)}) collective-permute-start(f32[128,128]{1,0:T(8,128)S(1)} %get-tuple-element.76), channel_id=1, source_target_pairs={{0,2},{1,3},{2,0},{3,1},{4,6},{5,7},{6,4},{7,5},{8,10},{9,11},{10,... | collective-permute-start | bytes 196616 | tf_op jit(solution)/shard_map/ppermute | solution.py:623
  40.7 12.7 %collective-permute-start.11 = (f32[128,128]{1,0:T(8,128)S(1)}, f32[128,128]{1,0:T(8,128)S(1)}, u32[]{:S(2)}, u32[]{:S(2)}) collective-permute-start(f32[128,128]{1,0:T(8,128)S(1)} %get-tuple-element.77), channel_id=1, source_target_pairs={{0,3},{1,2},{2,1},{3,0},{4,7},{5,6},{6,5},{7,4},{8,11},{9,10},{10,... | collective-permute-start | bytes 196616 | tf_op jit(solution)/shard_map/ppermute | solution.py:623
  42.6 10.8 %collective-permute-start.9 = (f32[128,128]{1,0:T(8,128)S(1)}, f32[128,128]{1,0:T(8,128)S(1)}, u32[]{:S(2)}, u32[]{:S(2)}) collective-permute-start(f32[128,128]{1,0:T(8,128)S(1)} %get-tuple-element.75), channel_id=1, source_target_pairs={{0,1},{1,0},{2,3},{3,2},{4,5},{5,4},{6,7},{7,6},{8,9},{9,8},{10,11... | collective-permute-start | bytes 196616 | tf_op jit(solution)/shard_map/ppermute | solution.py:623
  44.2 7.4 %collective-permute-start.7 = (f32[48,128]{1,0:T(8,128)S(1)}, f32[48,128]{1,0:T(8,128)S(1)}, u32[]{:S(2)}, u32[]{:S(2)}) collective-permute-start(f32[48,128]{1,0:T(8,128)S(1)} %get-tuple-element.67), channel_id=1, source_target_pairs={{0,1},{1,2},{2,3},{3,4},{4,5},{5,6},{6,7},{7,8},{8,9},{9,10},{10,1... | collective-permute-start | bytes 73736 | tf_op jit(solution)/shard_map/ppermute | solution.py:531
  44.6 7.0 %copy-start.9 = (bf16[1664,256]{1,0:T(8,128)(2,1)S(1)}, bf16[1664,256]{1,0:T(8,128)(2,1)}, u32[]{:S(2)}) copy-start(bf16[1664,256]{1,0:T(8,128)(2,1)} %constant.44.clone.collect_ref) | copy-start | bytes 2555908
  (4 other events, 3.2 us)

commit v2 on v1

--- a/solution.py
+++ b/solution.py
@@ -9,6 +9,7 @@
 from jax.sharding import PartitionSpec as P
 
 STEPS = 3
+PAD = 144
 EY = 8
 EZ = 8
 LANES = 128
@@ -73,7 +74,6 @@
     face = np.zeros((64, 3 * 128))
     face[0:25] = force[0:200:8]
     face[32:57] = force[4:200:8]
-    spread = np.zeros((WINDOW, WIDE), np.float32)
     collect = np.zeros((WIDE, WINDOW), np.float32)
     line = np.zeros(SIDE)
     for e in range(8):
@@ -86,13 +86,12 @@
                 for ez in range(8):
                     column = (b * 5 + d) * 64 + ey * 8 + ez
                     spot = b * SIDE + 4 * ez + d
-                    spread[spot, column] = 1.0
                     if d < 4 or ez == 7:
                         collect[column, spot] = 1.0
                     for slab in range(2):
                         at = (b * 5 + d) * 8
                         mass[at : at + 8, slab * 64 + ey * 8 + ez] = layer * line[4 * ey + b] * line[4 * ez + d]
-    return grad, force, face, spread, collect, mass
+    return grad, force, face, collect, mass
 
 
 def cut_table(table):
@@ -105,7 +104,7 @@
     return np.stack(pieces)
 
 
-GRAD, FORCE, FACES, SPREAD, COLLECT, MASS = make_tables()
+GRAD, FORCE, FACES, COLLECT, MASS = make_tables()
 
 
 def cut(value):
@@ -121,9 +120,21 @@
 
 
 def dot_six(table, value):
+    rows = table.shape[1]
+    stacked = table[...].reshape(3 * rows, table.shape[2])
     high, middle, low = cut(value)
-    small = dot(table[2], high) + dot(table[1], middle) + dot(table[0], low)
-    return dot(table[0], high) + (dot(table[0], middle) + dot(table[1], high) + small)
+    first = dot(stacked, high)
+    second = dot(stacked[0 : 2 * rows], middle)
+    small = first[2 * rows : 3 * rows] + second[rows : 2 * rows] + dot(stacked[0:rows], low)
+    return first[0:rows] + (first[rows : 2 * rows] + second[0:rows] + small)
+
+
+def dot_three(table, value):
+    rows = table.shape[1]
+    stacked = table[0:2].reshape(2 * rows, table.shape[2])
+    high, middle, _ = cut(value)
+    first = dot(stacked, high)
+    return first[0:rows] + (first[rows : 2 * rows] + dot(stacked[0:rows], middle))
 
 
 def lanes_of(shape):
@@ -145,13 +156,15 @@
 
 def to_columns(value, window_ref, spread_ref):
     rows = value.shape[0]
-    high, middle, low = cut(window_rows(value, window_ref))
-    spread = spread_ref[...]
-    wide = dot(high, spread) + dot(middle, spread) + dot(low, spread)
+    pieces = jnp.concatenate(cut(window_rows(value, window_ref)), axis=0)
+    wide = dot(pieces, spread_ref[...])
+    half = EY * rows
     own = (lanes_of((rows, WIDE)) // 8) % 8
-    picked = wide[0:rows]
-    for ey in range(1, EY):
-        picked = jnp.where(own == ey, wide[ey * rows : (ey + 1) * rows], picked)
+    picked = 0.0
+    for ey in range(EY):
+        at = slice(ey * rows, (ey + 1) * rows)
+        value = wide[at] + wide[half : 2 * half][at] + wide[2 * half : 3 * half][at]
+        picked = jnp.where(own == ey, value, picked)
     return picked
 
 
@@ -178,12 +191,21 @@
     return jnp.concatenate([value[0], value[1], value[2]], axis=1)
 
 
-def gather_kernel(now_ref, prev_ref, density_ref, rim_ref):
+def gather_kernel(now_ref, prev_ref, density_ref, rim_ref, now_copy, prev_copy, density_copy, sems):
+    copies = [
+        pltpu.make_async_copy(now_ref.at[0], now_copy, sems.at[0]),
+        pltpu.make_async_copy(prev_ref.at[0], prev_copy, sems.at[1]),
+        pltpu.make_async_copy(density_ref, density_copy, sems.at[2]),
+    ]
+    for copy in copies:
+        copy.start()
+    for copy in copies:
+        copy.wait()
     for c in range(3):
-        rim_ref[c : c + 1, :] = now_ref[0, c, 0:1, :]
-        rim_ref[3 + c : 4 + c, :] = prev_ref[0, c, 0:1, :]
-    rim_ref[6:7, :] = density_ref[0:1, :]
-    rim_ref[7:8, :] = density_ref[0:1, :]
+        rim_ref[c : c + 1, :] = now_copy[c, 0:1, :]
+        rim_ref[3 + c : 4 + c, :] = prev_copy[c, 0:1, :]
+    rim_ref[6:7, :] = density_copy[0:1, :]
+    rim_ref[7:8, :] = density_copy[0:1, :]
 
 
 def weighted_memory(memory_ref, decays, part, power):
@@ -192,13 +214,21 @@
         factor = decays[l]
         for _ in range(power - 1):
             factor = factor * decays[l]
-        value = value + factor * memory_ref[l, part, :, 0, :]
+        value = value + factor * memory_ref[l, part]
     return value
 
 
-def prologue_kernel(
-    now_ref, prev_ref, density_ref, memory_ref, decay_ref, spread_ref, mass_ref, u_ref, p_ref, scale_ref, m1_ref, window_ref
-):
+def spread_table():
+    column = lanes_of((1, WIDE))
+    block = column // 64
+    spot = (block // 5) * SIDE + (block % 5) + 4 * (column % 8)
+    spot = jnp.where(block < 25, spot, WINDOW)
+    return jnp.where(lax.broadcasted_iota(jnp.int32, (WINDOW, WIDE), 0) == spot, 1.0, 0.0).astype(BF16)
+
+
+def prologue_kernel(now_ref, prev_ref, density_ref, memory_ref, decay_ref, mass_ref, *refs):
+    u_ref, p_ref, scale_ref, m1_ref, spread_ref, window_ref = refs[-6:]
+    spread_ref[...] = spread_table()
     rows = jnp.concatenate([now_ref[0].reshape(24, FACE), prev_ref[0].reshape(24, FACE), density_ref[...]], axis=0)
     columns = to_columns(rows, window_ref, spread_ref)
     lane = lanes_of((8, LANES))
@@ -223,7 +253,7 @@
         m1_ref[part] = weighted_memory(memory_ref, decays, part, 1)
 
 
-def later_kernel(index_ref, memory_ref, decay_ref, owner_ref, m2_ref, m3_ref, select_ref):
+def later_kernel(memory_ref, decay_ref, owner_ref, m2_ref, m3_ref, select_ref):
     decays = [decay_ref[l : l + 1, :] for l in range(3)]
     for part in range(5):
         m2_ref[part] = weighted_memory(memory_ref, decays, part, 2)
@@ -237,7 +267,7 @@
     subs = select_ref.shape[0] // LANES
     slots = 4 * EY * EZ // subs
     row = lax.broadcasted_iota(jnp.int32, select_ref.shape, 0)
-    toward = (row // LANES) ^ index_ref[0]
+    toward = (row // LANES) ^ lax.axis_index("sub")
     wanted = (lanes_of((1, LANES)) // 64) * (slots // 2) + rank
     chosen = (owner == toward) & (wanted == row % slots)
     select_ref[...] = jnp.where(chosen, 1.0, 0.0).astype(BF16)
@@ -293,11 +323,11 @@
 
 
 def step_kernel(step, *refs):
-    index_ref, u_ref, lame_ref, mu_ref, m_ref, decay_ref, grad_table, face_table = refs[0:8]
-    older = refs[8 : 8 + step]
-    refs = refs[8 + step :]
-    strain_ref, sigma_ref, odd_ref, even_ref = refs[0:4]
-    keep_ref = refs[4] if step < STEPS - 1 else None
+    u_ref, lame_ref, mu_ref, m_ref, decay_ref, grad_table, face_table = refs[0:7]
+    older = refs[7 : 7 + step]
+    refs = refs[7 + step :]
+    strain_ref, sigma_ref, even_ref = refs[0:3]
+    odd_ref, keep_ref = refs[3:5] if step < STEPS - 1 else (None, None)
     grad_ref = refs[-1]
     grad_ref[...] = dot_six(grad_table, beside(u_ref))
     for block in range(9):
@@ -339,19 +369,19 @@
         for direction, values in enumerate(((xx, xy, xz), (xy, yy, yz), (xz, yz, zz))):
             for c in range(3):
                 sigma_ref[direction * 128 + rows.start : direction * 128 + rows.stop, c * LANES : (c + 1) * LANES] = values[c]
-    faces = dot_six(face_table, sigma_ref[...])
+    faces = dot_three(face_table, sigma_ref[...])
     first, last = pack_face(faces[0:32], False), pack_face(faces[32:64], True)
     if step < STEPS - 1:
-        even_ring = index_ref[2] == 0
+        even_ring = lax.axis_index(("cuts", "sub")) % 2 == 0
         odd_ref[...] = jnp.where(even_ring, first, last)
         even_ref[...] = jnp.where(even_ring, last, first)
     else:
-        odd_ref[...] = first
-        even_ref[...] = last
+        even_ref[0:48, :] = last
+        even_ref[48:, :] = jnp.zeros((even_ref.shape[0] - 48, LANES), F32)
 
 
 def rest_kernel(sigma_ref, u_ref, p_ref, scale_ref, force_table, next_ref):
-    force = dot_six(force_table, sigma_ref[...])
+    force = dot_three(force_table, sigma_ref[...])
     blocks = {}
     for c in range(3):
         for b in range(5):
@@ -400,17 +430,18 @@
         u_ref[c, 200:208, :] = jnp.zeros((8, LANES), F32)
 
 
-def update_kernel(index_ref, odd_ref, even_ref, partial_ref, scale_ref, u_ref, low_ref, delta_ref):
-    even_ring = index_ref[2] == 0
+def update_kernel(odd_ref, even_ref, partial_ref, scale_ref, u_ref, low_ref, delta_ref):
+    even_ring = lax.axis_index(("cuts", "sub")) % 2 == 0
     odd, even = odd_ref[...], even_ref[...]
     before, after = jnp.where(even_ring, odd, even), jnp.where(even_ring, even, odd)
     add_faces(before, after, partial_ref, scale_ref, u_ref, delta_ref)
     low_ref[...] = u_ref[...].astype(BF16)
 
 
-def kernel_parts(index_ref, strain_ref, low_ref, far_ref, lame_ref, mu_ref, grad_table, grad_ref, kernel_ref):
-    forward = jnp.where(index_ref[1] == 0, beside(low_ref), beside(far_ref))
-    grad_ref[...] = dot(grad_table[0], forward) + (dot(grad_table[1], forward) + dot(grad_table[2], forward))
+def kernel_parts(strain_ref, low_ref, far_ref, lame_ref, mu_ref, grad_table, grad_ref, kernel_ref):
+    forward = jnp.where(lax.axis_index("group") == 0, beside(low_ref), beside(far_ref))
+    grads = dot(grad_table[...].reshape(3 * 384, ROWS), forward)
+    grad_ref[...] = grads[0:384] + (grads[384:768] + grads[768:1152])
     for rows in CHUNKS:
         far = strains(grad_ref, rows)
         own = [strain_ref[part, rows, :] for part in range(6)]
@@ -432,18 +463,18 @@
 
 
 def parts_kernel(
-    index_ref, strain_ref, low_ref, far_ref, lame_ref, mu_ref, grad_table, part_ref, grad_ref, kernel_ref
+    strain_ref, low_ref, far_ref, lame_ref, mu_ref, grad_table, part_ref, grad_ref, kernel_ref
 ):
     part_ref[...] = kernel_parts(
-        index_ref, strain_ref, low_ref, far_ref, lame_ref, mu_ref, grad_table, grad_ref, kernel_ref
+        strain_ref, low_ref, far_ref, lame_ref, mu_ref, grad_table, grad_ref, kernel_ref
     )
 
 
 def send_kernel(
-    index_ref, strain_ref, low_ref, far_ref, lame_ref, mu_ref, grad_table, one_ref, two_ref, select_ref, *refs
+    strain_ref, low_ref, far_ref, lame_ref, mu_ref, grad_table, one_ref, two_ref, select_ref, *refs
 ):
     out_refs, (grad_ref, kernel_ref) = refs[:-2], refs[-2:]
-    three = kernel_parts(index_ref, strain_ref, low_ref, far_ref, lame_ref, mu_ref, grad_table, grad_ref, kernel_ref)
+    three = kernel_parts(strain_ref, low_ref, far_ref, lame_ref, mu_ref, grad_table, grad_ref, kernel_ref)
     rows = out_refs[0].shape[0]
     slots = rows // 2
     group = lanes_of((rows, LANES)) // slots
@@ -459,7 +490,7 @@
         ref[...] = value
 
 
-def sum_kernel(index_ref, *refs):
+def sum_kernel(*refs):
     in_refs, out_ref = refs[:-1], refs[-1]
     rows = in_refs[0].shape[0]
     slots = rows // 2
@@ -467,7 +498,7 @@
     group = lanes_of((rows, LANES)) // slots
     blocks = [[jnp.zeros((rows, LANES), F32)] * 2 for _ in range(pieces)]
     for k, ref in enumerate(in_refs):
-        source = index_ref[0] ^ k
+        source = lax.axis_index("sub") ^ k
         spot = source % pieces
         value = ref[...]
         for j in range(pieces):
@@ -480,7 +511,7 @@
 
 
 def finish_kernel(before_ref, partial_ref, scale_ref, collect_ref, out_ref, u_ref, delta_ref):
-    add_faces(before_ref[...], None, partial_ref, scale_ref, u_ref, delta_ref)
+    add_faces(before_ref[0:48], None, partial_ref, scale_ref, u_ref, delta_ref)
     lane = lanes_of((8, LANES))
     sub = lax.broadcasted_iota(jnp.int32, (8, LANES), 0)
     tiles = []
@@ -506,22 +537,22 @@
 
 
 VMEM = pl.BlockSpec(memory_space=pltpu.VMEM)
-SMEM = pl.BlockSpec(memory_space=pltpu.SMEM)
+HBM = pl.BlockSpec(memory_space=pltpu.HBM)
 
 
 def shaped(*shape, dtype=F32):
     return jax.ShapeDtypeStruct(shape, dtype)
 
 
-def call(kernel, name, outs, scratch, *args, scalars=0, micros=1):
+def call(kernel, name, outs, scratch, *args, outside=(), micros=1, room=32 * 1024):
     return pl.pallas_call(
         kernel,
         name=name,
         out_shape=outs,
-        in_specs=[SMEM] * scalars + [VMEM] * (len(args) - scalars),
+        in_specs=[HBM if at in outside else VMEM for at in range(len(args))],
         out_specs=jax.tree.map(lambda _: VMEM, outs),
         scratch_shapes=scratch,
-        compiler_params=pltpu.CompilerParams(vmem_limit_bytes=32 * 1024 * 1024),
+        compiler_params=pltpu.CompilerParams(vmem_limit_bytes=room * 1024),
         cost_estimate=pl.CostEstimate(flops=0, bytes_accessed=micros * 3000000, transcendentals=0),
     )(*args)
 
@@ -540,22 +571,32 @@
     return lax.ppermute(value, axis, pairs)
 
 
+def far_field(low, groups):
+    far = None
+    for k in range(1, groups):
+        moved = passed_along(low, "group", k)
+        far = moved if far is None else jnp.where(lax.axis_index("group") == k, moved, far)
+    return far
+
+
 def per_device(disp_now, disp_prev, memory_init, density, lame_lambda, shear_mu, sls_decay, owner_map):
     ring = ("cuts", "sub")
     subs = lax.axis_size("sub")
     groups = lax.axis_size("group")
-    index = jnp.stack([lax.axis_index("sub"), lax.axis_index("group"), lax.axis_index(ring) % 2]).astype(jnp.int32)
-
-    rim = call(gather_kernel, "gather", shaped(8, FACE), [], disp_now, disp_prev, density)
+
+    rim = call(
+        gather_kernel, "gather", shaped(8, FACE),
+        [pltpu.VMEM((3, 8, FACE), F32)] * 2 + [pltpu.VMEM((8, FACE), F32), pltpu.SemaphoreType.DMA((3,))],
+        disp_now, disp_prev, density, outside=(0, 1, 2), room=54 * 1024 - 120,
+    )
     rim = passed_along(rim, ring, -1)
 
     grad_table = jnp.asarray(cut_table(GRAD))
     force_table = jnp.asarray(cut_table(FORCE))
     face_table = jnp.asarray(cut_table(FACES))
-    spread = jnp.asarray(SPREAD, BF16)
     collect = jnp.asarray(COLLECT, BF16)
     mass = jnp.asarray(MASS)
-    memory = jnp.transpose(memory_init, (1, 2, 3, 0, 4))
+    memory = memory_init[0]
     owner = jnp.transpose(owner_map, (0, 2, 1))
 
     state = shaped(3, ROWS, LANES)
@@ -566,45 +607,47 @@
     grad_scratch = pltpu.VMEM((384, 384), F32)
     part_scratch = [grad_scratch, pltpu.VMEM((256, LANES), F32)]
     face = shaped(48, LANES)
-    u, p, scale, m1 = call(
-        prologue_kernel, "prologue", [state, state, scale_shape, five], [pltpu.VMEM((8, 56, WINDOW), F32)],
-        disp_now, disp_prev, density, memory, sls_decay, spread, mass, micros=3,
+    window_scratch = [pltpu.VMEM((8, 8, WINDOW), F32), pltpu.VMEM((ROWS, LANES), F32)]
+    u, p, scale, m1, spread = call(
+        prologue_kernel, "prologue", [state, state, scale_shape, five, shaped(WINDOW, WIDE, dtype=BF16)],
+        [pltpu.VMEM((8, 56, WINDOW), F32)],
+        disp_now, disp_prev, density, memory, sls_decay, mass, grad_table, face_table, force_table, lame_lambda, shear_mu,
     )
     u, p, scale, low = call(
-        rim_kernel, "rim", [state, state, scale_shape, state_low],
-        [pltpu.VMEM((8, 8, WINDOW), F32), pltpu.VMEM((ROWS, LANES), F32)],
-        rim, u, p, scale, spread, mass,
+        rim_kernel, "rim", [state, state, scale_shape, state_low], window_scratch, rim, u, p, scale, spread, mass
     )
     memories = [m1]
     kept = []
     parts = []
     for step in range(STEPS):
-        outs = [shaped(6, 125, LANES), shaped(384, 384), face, face]
+        if step == STEPS - 1:
+            far = far_field(low, groups)
+        outs = [shaped(6, 125, LANES), shaped(384, 384), face if step < STEPS - 1 else shaped(PAD, LANES)]
         if step < STEPS - 1:
-            outs.append(five)
+            outs += [face, five]
         results = call(
             lambda *refs, step=step: step_kernel(step, *refs), "step", outs, [grad_scratch],
-            index, u, lame_lambda, shear_mu, memories[step], sls_decay, grad_table, face_table, *kept, scalars=1,
+            u, lame_lambda, shear_mu, memories[step], sls_decay, grad_table, face_table, *kept,
         )
-        strain, sigma, odd, even = results[0:4]
-        kept.extend(results[4:])
+        strain, sigma, even = results[0:3]
         if step < STEPS - 1:
+            odd = results[3]
+            kept.append(results[4])
             odd = swapped(odd, ring, 1)
             even = swapped(even, ring, 0)
         else:
             before = passed_along(even, ring, 1)
-        far = None
-        for k in range(1, groups):
-            moved = passed_along(low, "group", k)
-            far = moved if far is None else jnp.where(lax.axis_index("group") == k, moved, far)
         partial = call(rest_kernel, "rest", state, [], sigma, u, p, scale, force_table)
-        shared = (index, strain, low, far, lame_lambda, shear_mu, grad_table)
         if step < STEPS - 1:
-            parts.append(call(parts_kernel, "parts", part_shape, part_scratch, *shared, scalars=1))
+            low, sigma = lax.optimization_barrier((low, sigma))
+            far = far_field(low, groups)
+        shared = (strain, low, far, lame_lambda, shear_mu, grad_table)
+        if step < STEPS - 1:
+            parts.append(call(parts_kernel, "parts", part_shape, part_scratch, *shared))
             if step == 0:
                 m2, m3, select = call(
                     later_kernel, "later", [five, five, shaped(subs * LANES, LANES, dtype=BF16)], [],
-                    index, memory, sls_decay, owner, scalars=1,
+                    memory, sls_decay, owner,
                 )
                 memories += [m2, m3]
                 partial, parts[0], select, memories[2] = lax.optimization_barrier((partial, parts[0], select, m3))
@@ -613,20 +656,20 @@
             p = u
             u, low = call(
                 update_kernel, "update", [state, state_low], [pltpu.VMEM((3, ROWS, LANES), F32)],
-                index, odd, even, partial, scale, scalars=1,
+                odd, even, partial, scale,
             )
         else:
             sent = list(call(
-                send_kernel, "send", [shaped(512 // subs, LANES)] * subs, part_scratch, *shared, *parts, select, scalars=1)
+                send_kernel, "send", [shaped(512 // subs, LANES)] * subs, part_scratch, *shared, *parts, select)
             )
             for k in range(subs - 1, 0, -1):
                 sent[k] = lax.ppermute(sent[k], "sub", [(j, j ^ k) for j in range(subs)])
     final = call(
         finish_kernel, "finish", shaped(1, 3, 8, FACE),
         [pltpu.VMEM((3, ROWS, LANES), F32), pltpu.VMEM((3, ROWS, LANES), F32)],
-        before, partial, scale, collect,
+        before, partial, scale, collect, micros=20,
     )
-    kernels = call(sum_kernel, "sum", shaped(250, 1, 256), [], index, *sent, scalars=1)
+    kernels = call(sum_kernel, "sum", shaped(250, 1, 256), [], *sent)
     return final, jnp.transpose(kernels, (1, 2, 0))
 
 

time: 55.3 us -> 44.2 us (0.80)
  Pallas kernels: 22.5 us -> 14.4 us
  local copies, waits for them, and re-layouts: 5.84 us -> 2.03 us
  starting transfers between devices: 17.3 us -> 20.1 us
  waiting for transfers between devices: 8.39 us -> 6.58 us
    pallas_call x17, Pallas kernels: 22.5 us -> 14.4 us  [call(): pl.pallas_call(kernel, name=name, out_shape=outs, in_specs=[HBM if at in...]
    unnamed x32 -> x25, local copies, waits for them, and re-layouts: 5.84 us -> 2.03 us
    ppermute x5, waiting for transfers between devices: 5.9 us -> 2.46 us  [passed_along(): lax.ppermute(value, axis, [(source, (source + steps) % count) for source...]
    ppermute x4, starting transfers between devices: 6.07 us -> 8.19 us  [swapped(): return lax.ppermute(value, axis, pairs)]
    ppermute x4, waiting for transfers between devices: 2.48 us -> 4.11 us  [swapped(): return lax.ppermute(value, axis, pairs)]
    ppermute x3, starting transfers between devices: 3.55 us -> 4.45 us  [per_device(): sent[k] = lax.ppermute(sent[k], 'sub', [(j, j ^ k) for j in range(subs)])]
  transfers between devices with their start and end apart: 12 -> 12, of which waited for: 2 -> 4; matrix products, arithmetic and copies ran while one was open for 0% -> 3% of each run, Pallas kernels for 32% -> 19%
where the time goes in v2:
time: 44.2 us; the launch traced here: 44 us
  starting transfers between devices  20.1 us (45%)
  Pallas kernels  14.4 us (33%)
  waiting for transfers between devices  6.58 us (15%)
  local copies, waits for them, and re-layouts  2.03 us (5%)
  between operations  0.92 us (2%)
    pallas_call x17, Pallas kernels, call(): pl.pallas_call(kernel, name=name, out_shape=outs, in_specs=[HBM if at in...  14.4 us
    ppermute x4, starting transfers between devices, swapped(): return lax.ppermute(value, axis, pairs)  8.19 us
    ppermute x5, starting transfers between devices, passed_along(): lax.ppermute(value, axis, [(source, (source + steps) % count) for source...  7.5 us
    ppermute x3, starting transfers between devices, per_device(): sent[k] = lax.ppermute(sent[k], 'sub', [(j, j ^ k) for j in range(subs)])  4.45 us
    ppermute x4, waiting for transfers between devices, swapped(): return lax.ppermute(value, axis, pairs)  4.11 us
    ppermute x5, waiting for transfers between devices, passed_along(): lax.ppermute(value, axis, [(source, (source + steps) % count) for source...  2.46 us
    unnamed x25, local copies, waits for them, and re-layouts  2.03 us
  transfers between devices with their start and end apart: 12, of which 4 were waited for; matrix products, arithmetic and copies ran while one was open for 3% of the time, Pallas kernels for 19%

profile of v2, /device:TPU:0, one launch (start us, length us, event | category | flops | bytes accessed | tf_op | source)
XLA Modules:
  0.0 44.0 jit_solution(17428045116631418856)
XLA Ops:
  0.6 1.0 %gather.1 = f32[8,1089]{1,0:T(8,128)S(1)} custom-call(f32[1,3,8,1089]{3,2,1,0:T(8,128)} %now_ref.3, f32[1,3,8,1089]{3,2,1,0:T(8,128)} %prev_ref.3, f32[8,1089]{1,0:T(8,128)} %density_ref.3), custom_call_target="tpu_custom_call" | custom-call | bytes 3000000 | tf_op jit(solution)/shard_map/gather/pallas_call | solution.py:548
  1.7 7.0 %collective-permute-start = (f32[8,1089]{1,0:T(8,128)S(1)}, f32[8,1089]{1,0:T(8,128)S(1)}, u32[]{:S(2)}, u32[]{:S(2)}) collective-permute-start(f32[8,1089]{1,0:T(8,128)S(1)} %gather.1), channel_id=1, source_target_pairs={{0,15},{1,0},{2,1},{3,2},{4,3},{5,4},{6,5},{7,6},{8,7},{9,8},{10,9... | collective-permute-start | bytes 104552 | tf_op jit(solution)/shard_map/ppermute | solution.py:562
  8.7 1.3 %copy.18 = f32[1,3,5,125,128]{4,3,0,2,1:T(8,128)S(1)} copy(f32[1,3,5,125,128]{4,0,3,2,1:T(1,128)} %param.15) | data formatting | bytes 1920000
  10.1 1.7 %prologue.1 = (f32[3,208,128]{2,1,0:T(8,128)S(1)}, f32[3,208,128]{2,1,0:T(8,128)S(1)}, f32[208,128]{1,0:T(8,128)S(1)}, f32[5,125,128]{2,1,0:T(8,128)S(1)}, bf16[256,1664]{1,0:T(8,128)(2,1)S(1)}) custom-call(f32[1,3,8,1089]{3,2,1,0:T(8,128)S(1)} %copy-done.6, f32[1,3,8,1089]{3,2,1,0:T(8,128)S(1)} %copy-done.7, f32[8,1089]{1,0:T(8,128)S(1)} %copy-done.9, ...), custom_call_target="tpu_custom_call" | custom-call | bytes 3000000 | tf_op jit(solution)/shard_map/prologue/pallas_call | solution.py:548
  12.3 1.2 %step.3 = (f32[6,125,128]{2,1,0:T(8,128)S(1)}, f32[384,384]{1,0:T(8,128)S(1)}, f32[48,128]{1,0:T(8,128)S(1)}, f32[48,128]{1,0:T(8,128)S(1)}, f32[5,125,128]{2,1,0:T(8,128)S(1)}) custom-call(f32[3,208,128]{2,1,0:T(8,128)S(1)} %get-tuple-element.47.refs_0_.u_ref.p_ref, f32[125,128]{1,0:T(8,128)S(1)} %copy-done.2, f32[125,128]{1,0:T(8,128)S(1)} %copy-done.3, ...), custom_call_target="tpu_custom_call" | custom-call | bytes 3000000 | tf_op jit(solution)/shard_map/step/pallas_call | solution.py:548
  13.6 4.5 %collective-permute-start.1 = (f32[48,128]{1,0:T(8,128)S(1)}, f32[48,128]{1,0:T(8,128)S(1)}, u32[]{:S(2)}, u32[]{:S(2)}) collective-permute-start(f32[48,128]{1,0:T(8,128)S(1)} %get-tuple-element.49), channel_id=1, source_target_pairs={{1,2},{2,1},{3,4},{4,3},{5,6},{6,5},{7,8},{8,7},{9,10},{10,9},{11,... | collective-permute-start | bytes 73736 | tf_op jit(solution)/shard_map/ppermute | solution.py:571
  18.1 0.7 %copy-done.11 = s32[2,64,1]{1,2,0:T(1,128)S(1)} copy-done((s32[2,64,1]{1,2,0:T(1,128)S(1)}, s32[2,64,1]{1,2,0:T(1,128)}, u32[]{:S(2)}) %copy-start.11) | copy-done | bytes 536
  19.2 0.7 %rest.3.partial_ref = f32[3,208,128]{2,1,0:T(8,128)S(1)} custom-call(f32[384,384]{1,0:T(8,128)S(1)} %get-tuple-element.51.sigma_ref, f32[3,208,128]{2,1,0:T(8,128)S(1)} %get-tuple-element.47.refs_0_.u_ref.p_ref, f32[3,208,128]{2,1,0:T(8,128)S(1)} %get-tuple-element.52.p_ref, f32[208,128]{1,0:T(8,128)S(1)} %get-tuple-element.53.scale_ref, ...), custom_call_target="tpu_custom_call" | custom-call | bytes 3000000 | tf_op jit(solution)/shard_map/rest/pallas_call | solution.py:548
  19.9 0.5 %parts.2.one_ref = bf16[256,128]{1,0:T(8,128)(2,1)S(1)} custom-call(f32[6,125,128]{2,1,0:T(8,128)S(1)} %get-tuple-element.54.strain_ref, bf16[3,208,128]{2,1,0:T(8,128)(2,1)S(1)} %get-tuple-element.56.low_ref, bf16[3,208,128]{2,1,0:T(8,128)(2,1)S(1)} %collective-permute-done.3.far_ref, f32[125,128]{1,0:T(8,128)S(1)} %copy-done.2, f32[125,128]{1,0:T(8,128)S(1)} %copy-done.3, ...), custom_call_target="tpu_custom_call" | custom-call | bytes 3000000 | tf_op jit(solution)/shard_map/parts/pallas_call | solution.py:548
  20.4 0.8 %collective-permute-done.1.odd_ref = f32[48,128]{1,0:T(8,128)S(1)} collective-permute-done((f32[48,128]{1,0:T(8,128)S(1)}, f32[48,128]{1,0:T(8,128)S(1)}, u32[]{:S(2)}, u32[]{:S(2)}) %collective-permute-start.1) | collective-permute-done | bytes 24608 | tf_op jit(solution)/shard_map/ppermute | solution.py:571
  21.2 0.8 %collective-permute-done.2.even_ref = f32[48,128]{1,0:T(8,128)S(1)} collective-permute-done((f32[48,128]{1,0:T(8,128)S(1)}, f32[48,128]{1,0:T(8,128)S(1)}, u32[]{:S(2)}, u32[]{:S(2)}) %collective-permute-start.2) | collective-permute-done | bytes 24608 | tf_op jit(solution)/shard_map/ppermute | solution.py:571
  22.2 1.2 %step.4 = (f32[6,125,128]{2,1,0:T(8,128)S(1)}, f32[384,384]{1,0:T(8,128)S(1)}, f32[48,128]{1,0:T(8,128)S(1)}, f32[48,128]{1,0:T(8,128)S(1)}, f32[5,125,128]{2,1,0:T(8,128)S(1)}) custom-call(f32[3,208,128]{2,1,0:T(8,128)S(1)} %get-tuple-element.60.refs_0_.u_ref.p_ref, f32[125,128]{1,0:T(8,128)S(1)} %copy-done.2, f32[125,128]{1,0:T(8,128)S(1)} %copy-done.3, ...), custom_call_target="tpu_custom_call" | custom-call | bytes 3000000 | tf_op jit(solution)/shard_map/step/pallas_call | solution.py:548
  23.5 3.7 %collective-permute-start.4 = (f32[48,128]{1,0:T(8,128)S(1)}, f32[48,128]{1,0:T(8,128)S(1)}, u32[]{:S(2)}, u32[]{:S(2)}) collective-permute-start(f32[48,128]{1,0:T(8,128)S(1)} %get-tuple-element.63), channel_id=1, source_target_pairs={{1,2},{2,1},{3,4},{4,3},{5,6},{6,5},{7,8},{8,7},{9,10},{10,9},{11,... | collective-permute-start | bytes 73736 | tf_op jit(solution)/shard_map/ppermute | solution.py:571
  27.1 0.7 %rest.4.partial_ref = f32[3,208,128]{2,1,0:T(8,128)S(1)} custom-call(f32[384,384]{1,0:T(8,128)S(1)} %get-tuple-element.65.sigma_ref, f32[3,208,128]{2,1,0:T(8,128)S(1)} %get-tuple-element.60.refs_0_.u_ref.p_ref, f32[3,208,128]{2,1,0:T(8,128)S(1)} %get-tuple-element.47.refs_0_.u_ref.p_ref, f32[208,128]{1,0:T(8,128)S(1)} %get-tuple-element.53.scale_ref, ...), custom_call_target="tpu_custom_call" | custom-call | bytes 3000000 | tf_op jit(solution)/shard_map/rest/pallas_call | solution.py:548
  27.9 0.5 %parts.3.two_ref = bf16[256,128]{1,0:T(8,128)(2,1)S(1)} custom-call(f32[6,125,128]{2,1,0:T(8,128)S(1)} %get-tuple-element.66.strain_ref, bf16[3,208,128]{2,1,0:T(8,128)(2,1)S(1)} %get-tuple-element.68.low_ref, bf16[3,208,128]{2,1,0:T(8,128)(2,1)S(1)} %collective-permute-done.6.far_ref, f32[125,128]{1,0:T(8,128)S(1)} %copy-done.2, f32[125,128]{1,0:T(8,128)S(1)} %copy-done.3, ...), custom_call_target="tpu_custom_call" | custom-call | bytes 3000000 | tf_op jit(solution)/shard_map/parts/pallas_call | solution.py:548
  28.4 2.6 %collective-permute-done.4.odd_ref = f32[48,128]{1,0:T(8,128)S(1)} collective-permute-done((f32[48,128]{1,0:T(8,128)S(1)}, f32[48,128]{1,0:T(8,128)S(1)}, u32[]{:S(2)}, u32[]{:S(2)}) %collective-permute-start.4) | collective-permute-done | bytes 24608 | tf_op jit(solution)/shard_map/ppermute | solution.py:571
  31.3 1.2 %step.5 = (f32[6,125,128]{2,1,0:T(8,128)S(1)}, f32[384,384]{1,0:T(8,128)S(1)}, f32[144,128]{1,0:T(8,128)S(1)}) custom-call(f32[3,208,128]{2,1,0:T(8,128)S(1)} %get-tuple-element.70.refs_0_.u_ref, f32[125,128]{1,0:T(8,128)S(1)} %copy-done.2, f32[125,128]{1,0:T(8,128)S(1)} %copy-done.3, f32[5,125,128]{2,1,0:T(8,128)S(1)} %get-tuple-element.71.refs_3_, ...), custom_call_target="tpu_custom_call" | custom-call | bytes 3000000 | tf_op jit(solution)/shard_map/step/pallas_call | solution.py:548
  32.9 0.8 %send.1 = (f32[128,128]{1,0:T(8,128)S(1)}, f32[128,128]{1,0:T(8,128)S(1)}, f32[128,128]{1,0:T(8,128)S(1)}, f32[128,128]{1,0:T(8,128)S(1)}) custom-call(f32[6,125,128]{2,1,0:T(8,128)S(1)} %get-tuple-element.75.strain_ref, bf16[3,208,128]{2,1,0:T(8,128)(2,1)S(1)} %get-tuple-element.76.low_ref, bf16[3,208,128]{2,1,0:T(8,128)(2,1)S(1)} %collective-permute-done.8.far_ref, ...), custom_call_target="tpu_custom_call" | custom-call | bytes 3000000 | tf_op jit(solution)/shard_map/send/pallas_call | solution.py:548
  33.8 1.6 %collective-permute-start.10 = (f32[128,128]{1,0:T(8,128)S(1)}, f32[128,128]{1,0:T(8,128)S(1)}, u32[]{:S(2)}, u32[]{:S(2)}) collective-permute-start(f32[128,128]{1,0:T(8,128)S(1)} %get-tuple-element.82), channel_id=1, source_target_pairs={{0,2},{1,3},{2,0},{3,1},{4,6},{5,7},{6,4},{7,5},{8,10},{9,11},{10,... | collective-permute-start | bytes 196616 | tf_op jit(solution)/shard_map/ppermute | solution.py:666
  35.4 2.7 %collective-permute-start.11 = (f32[128,128]{1,0:T(8,128)S(1)}, f32[128,128]{1,0:T(8,128)S(1)}, u32[]{:S(2)}, u32[]{:S(2)}) collective-permute-start(f32[128,128]{1,0:T(8,128)S(1)} %get-tuple-element.83), channel_id=1, source_target_pairs={{0,3},{1,2},{2,1},{3,0},{4,7},{5,6},{6,5},{7,4},{8,11},{9,10},{10,... | collective-permute-start | bytes 196616 | tf_op jit(solution)/shard_map/ppermute | solution.py:666
  38.1 0.7 %rest.5.partial_ref = f32[3,208,128]{2,1,0:T(8,128)S(1)} custom-call(f32[384,384]{1,0:T(8,128)S(1)} %get-tuple-element.74.sigma_ref, f32[3,208,128]{2,1,0:T(8,128)S(1)} %get-tuple-element.70.refs_0_.u_ref, f32[3,208,128]{2,1,0:T(8,128)S(1)} %get-tuple-element.60.refs_0_.u_ref.p_ref, f32[208,128]{1,0:T(8,128)S(1)} %get-tuple-element.53.scale_ref, ...), custom_call_target="tpu_custom_call" | custom-call | bytes 3000000 | tf_op jit(solution)/shard_map/rest/pallas_call | solution.py:548
  38.8 2.5 %collective-permute-done.7.before_ref = f32[144,128]{1,0:T(8,128)S(1)} collective-permute-done((f32[144,128]{1,0:T(8,128)S(1)}, f32[144,128]{1,0:T(8,128)S(1)}, u32[]{:S(2)}, u32[]{:S(2)}) %collective-permute-start.7) | collective-permute-done | bytes 73760 | tf_op jit(solution)/shard_map/ppermute | solution.py:562
  41.2 1.8 %finish.1 = f32[1,3,8,1089]{3,2,1,0:T(8,128)} custom-call(f32[144,128]{1,0:T(8,128)S(1)} %collective-permute-done.7.before_ref, f32[3,208,128]{2,1,0:T(8,128)S(1)} %rest.5.partial_ref, f32[208,128]{1,0:T(8,128)S(1)} %get-tuple-element.53.scale_ref, bf16[1664,256]{1,0:T(8,128)(2,1)S(1)} %copy-done.5), custom_call_target="tpu_custom_call" | custom-call | bytes 60000000 | tf_op jit(solution)/shard_map/finish/pallas_call | solution.py:548
  43.1 1.0 %sum.1 = f32[250,1,256]{2,1,0:T(1,128)} custom-call(f32[128,128]{1,0:T(8,128)S(1)} %get-tuple-element.80.refs_0_, f32[128,128]{1,0:T(8,128)S(1)} %collective-permute-done.9.refs_1_, f32[128,128]{1,0:T(8,128)S(1)} %collective-permute-done.10.refs_2_, f32[128,128]{1,0:T(8,128)S(1)} %collective-permute-done.11.refs_3_), custom_call_target="tpu_custom_call" | custom-call | bytes 3000000 | tf_op jit(solution)/shard_map/sum/pallas_call | solution.py:548
  (42 shorter events, 2.2 us)
Async XLA Ops:
  1.6 8.4 %copy-start = (bf16[3,384,208]{2,1,0:T(8,128)(2,1)S(1)}, bf16[3,384,208]{2,1,0:T(8,128)(2,1)}, u32[]{:S(2)}) copy-start(bf16[3,384,208]{2,1,0:T(8,128)(2,1)} %constant.10.clone.refs_0_.refs_5_.grad_table) | copy-start | bytes 1437700
  1.6 8.4 %copy-start.1 = (bf16[3,208,384]{2,1,0:T(8,128)(2,1)S(1)}, bf16[3,208,384]{2,1,0:T(8,128)(2,1)}, u32[]{:S(2)}) copy-start(bf16[3,208,384]{2,1,0:T(8,128)(2,1)} %constant.11.clone.refs_2_.force_table) | copy-start | bytes 1437700
  1.7 8.4 %copy-start.2 = (f32[125,128]{1,0:T(8,128)S(1)}, f32[125,128]{1,0:T(8,128)}, u32[]{:S(2)}) copy-start(f32[125,128]{1,0:T(8,128)} %lame_ref.5) | copy-start | bytes 192004
  1.7 8.4 %copy-start.3 = (f32[125,128]{1,0:T(8,128)S(1)}, f32[125,128]{1,0:T(8,128)}, u32[]{:S(2)}) copy-start(f32[125,128]{1,0:T(8,128)} %mu_ref.5) | copy-start | bytes 192004
  1.7 8.4 %copy-start.4 = (bf16[3,64,384]{2,1,0:T(8,128)(2,1)S(1)}, bf16[3,64,384]{2,1,0:T(8,128)(2,1)}, u32[]{:S(2)}) copy-start(bf16[3,64,384]{2,1,0:T(8,128)(2,1)} %constant.12.clone.refs_1_.refs_6_) | copy-start | bytes 442372
  1.7 8.4 %copy-start.6 = (f32[1,3,8,1089]{3,2,1,0:T(8,128)S(1)}, f32[1,3,8,1089]{3,2,1,0:T(8,128)}, u32[]{:S(2)}) copy-start(f32[1,3,8,1089]{3,2,1,0:T(8,128)} %now_ref.3) | copy-start | bytes 313636
  1.7 8.4 %copy-start.7 = (f32[1,3,8,1089]{3,2,1,0:T(8,128)S(1)}, f32[1,3,8,1089]{3,2,1,0:T(8,128)}, u32[]{:S(2)}) copy-start(f32[1,3,8,1089]{3,2,1,0:T(8,128)} %prev_ref.3) | copy-start | bytes 313636
  1.7 8.4 %copy-start.8 = (f32[208,128]{1,0:T(8,128)S(1)}, f32[208,128]{1,0:T(8,128)}, u32[]{:S(2)}) copy-start(f32[208,128]{1,0:T(8,128)} %constant.14.clone.mass_ref) | copy-start | bytes 319492
  1.7 8.4 %copy-start.9 = (f32[8,1089]{1,0:T(8,128)S(1)}, f32[8,1089]{1,0:T(8,128)}, u32[]{:S(2)}) copy-start(f32[8,1089]{1,0:T(8,128)} %density_ref.3) | copy-start | bytes 104548
  1.7 10.1 %collective-permute-start = (f32[8,1089]{1,0:T(8,128)S(1)}, f32[8,1089]{1,0:T(8,128)S(1)}, u32[]{:S(2)}, u32[]{:S(2)}) collective-permute-start(f32[8,1089]{1,0:T(8,128)S(1)} %gather.1), channel_id=1, source_target_pairs={{0,15},{1,0},{2,1},{3,2},{4,3},{5,4},{6,5},{7,6},{8,7},{9,8},{10,9... | collective-permute-start | bytes 104552 | tf_op jit(solution)/shard_map/ppermute | solution.py:562
  8.7 1.4 %copy-start.10 = (f32[3,128]{1,0:T(4,128)S(1)}, f32[3,128]{1,0:T(4,128)}, u32[]{:S(2)}) copy-start(f32[3,128]{1,0:T(4,128)} %refs_4_.7) | copy-start | bytes 4612
  13.5 6.4 %collective-permute-start.3 = (bf16[3,208,128]{2,1,0:T(8,128)(2,1)S(1)}, bf16[3,208,128]{2,1,0:T(8,128)(2,1)S(1)}, u32[]{:S(2)}, u32[]{:S(2)}) collective-permute-start(bf16[3,208,128]{2,1,0:T(8,128)(2,1)S(1)} %get-tuple-element.56.low_ref), channel_id=1, source_target_pairs={{0,16},{16,0},{1,17},{17,1},{2,18},{18,2},{3,19},{19,3},{4,20},{20... | collective-permute-start | bytes 479240 | tf_op jit(solution)/shard_map/ppermute | solution.py:562
  13.6 7.6 %collective-permute-start.1 = (f32[48,128]{1,0:T(8,128)S(1)}, f32[48,128]{1,0:T(8,128)S(1)}, u32[]{:S(2)}, u32[]{:S(2)}) collective-permute-start(f32[48,128]{1,0:T(8,128)S(1)} %get-tuple-element.49), channel_id=1, source_target_pairs={{1,2},{2,1},{3,4},{4,3},{5,6},{6,5},{7,8},{8,7},{9,10},{10,9},{11,... | collective-permute-start | bytes 73736 | tf_op jit(solution)/shard_map/ppermute | solution.py:571
  18.1 0.7 %copy-start.11 = (s32[2,64,1]{1,2,0:T(1,128)S(1)}, s32[2,64,1]{1,2,0:T(1,128)}, u32[]{:S(2)}) copy-start(s32[2,64,1]{1,2,0:T(1,128)} %param.20) | copy-start | bytes 1540
  18.1 3.8 %collective-permute-start.2 = (f32[48,128]{1,0:T(8,128)S(1)}, f32[48,128]{1,0:T(8,128)S(1)}, u32[]{:S(2)}, u32[]{:S(2)}) collective-permute-start(f32[48,128]{1,0:T(8,128)S(1)} %get-tuple-element.50), channel_id=1, source_target_pairs={{0,1},{1,0},{2,3},{3,2},{4,5},{5,4},{6,7},{7,6},{8,9},{9,8},{10,11... | collective-permute-start | bytes 73736 | tf_op jit(solution)/shard_map/ppermute | solution.py:571
  23.4 4.4 %collective-permute-start.6 = (bf16[3,208,128]{2,1,0:T(8,128)(2,1)S(1)}, bf16[3,208,128]{2,1,0:T(8,128)(2,1)S(1)}, u32[]{:S(2)}, u32[]{:S(2)}) collective-permute-start(bf16[3,208,128]{2,1,0:T(8,128)(2,1)S(1)} %get-tuple-element.68.low_ref), channel_id=1, source_target_pairs={{0,16},{16,0},{1,17},{17,1},{2,18},{18,2},{3,19},{19,3},{4,20},{20... | collective-permute-start | bytes 479240 | tf_op jit(solution)/shard_map/ppermute | solution.py:562
  23.5 7.5 %collective-permute-start.4 = (f32[48,128]{1,0:T(8,128)S(1)}, f32[48,128]{1,0:T(8,128)S(1)}, u32[]{:S(2)}, u32[]{:S(2)}) collective-permute-start(f32[48,128]{1,0:T(8,128)S(1)} %get-tuple-element.63), channel_id=1, source_target_pairs={{1,2},{2,1},{3,4},{4,3},{5,6},{6,5},{7,8},{8,7},{9,10},{10,9},{11,... | collective-permute-start | bytes 73736 | tf_op jit(solution)/shard_map/ppermute | solution.py:571
  27.1 3.8 %collective-permute-start.5 = (f32[48,128]{1,0:T(8,128)S(1)}, f32[48,128]{1,0:T(8,128)S(1)}, u32[]{:S(2)}, u32[]{:S(2)}) collective-permute-start(f32[48,128]{1,0:T(8,128)S(1)} %get-tuple-element.64), channel_id=1, source_target_pairs={{0,1},{1,0},{2,3},{3,2},{4,5},{5,4},{6,7},{7,6},{8,9},{9,8},{10,11... | collective-permute-start | bytes 73736 | tf_op jit(solution)/shard_map/ppermute | solution.py:571
  31.2 1.6 %collective-permute-start.8 = (bf16[3,208,128]{2,1,0:T(8,128)(2,1)S(1)}, bf16[3,208,128]{2,1,0:T(8,128)(2,1)S(1)}, u32[]{:S(2)}, u32[]{:S(2)}) collective-permute-start(bf16[3,208,128]{2,1,0:T(8,128)(2,1)S(1)} %get-tuple-element.76.low_ref), channel_id=1, source_target_pairs={{0,16},{16,0},{1,17},{17,1},{2,18},{18,2},{3,19},{19,3},{4,20},{20... | collective-permute-start | bytes 479240 | tf_op jit(solution)/shard_map/ppermute | solution.py:562
  32.5 8.7 %collective-permute-start.7 = (f32[144,128]{1,0:T(8,128)S(1)}, f32[144,128]{1,0:T(8,128)S(1)}, u32[]{:S(2)}, u32[]{:S(2)}) collective-permute-start(f32[144,128]{1,0:T(8,128)S(1)} %get-tuple-element.73), channel_id=1, source_target_pairs={{0,1},{1,2},{2,3},{3,4},{4,5},{5,6},{6,7},{7,8},{8,9},{9,10},{10,1... | collective-permute-start | bytes 221192 | tf_op jit(solution)/shard_map/ppermute | solution.py:562
  33.6 9.4 %collective-permute-start.9 = (f32[128,128]{1,0:T(8,128)S(1)}, f32[128,128]{1,0:T(8,128)S(1)}, u32[]{:S(2)}, u32[]{:S(2)}) collective-permute-start(f32[128,128]{1,0:T(8,128)S(1)} %get-tuple-element.81), channel_id=1, source_target_pairs={{0,1},{1,0},{2,3},{3,2},{4,5},{5,4},{6,7},{7,6},{8,9},{9,8},{10,11... | collective-permute-start | bytes 196616 | tf_op jit(solution)/shard_map/ppermute | solution.py:666
  33.8 9.3 %collective-permute-start.10 = (f32[128,128]{1,0:T(8,128)S(1)}, f32[128,128]{1,0:T(8,128)S(1)}, u32[]{:S(2)}, u32[]{:S(2)}) collective-permute-start(f32[128,128]{1,0:T(8,128)S(1)} %get-tuple-element.82), channel_id=1, source_target_pairs={{0,2},{1,3},{2,0},{3,1},{4,6},{5,7},{6,4},{7,5},{8,10},{9,11},{10,... | collective-permute-start | bytes 196616 | tf_op jit(solution)/shard_map/ppermute | solution.py:666
  35.4 7.7 %collective-permute-start.11 = (f32[128,128]{1,0:T(8,128)S(1)}, f32[128,128]{1,0:T(8,128)S(1)}, u32[]{:S(2)}, u32[]{:S(2)}) collective-permute-start(f32[128,128]{1,0:T(8,128)S(1)} %get-tuple-element.83), channel_id=1, source_target_pairs={{0,3},{1,2},{2,1},{3,0},{4,7},{5,6},{6,5},{7,4},{8,11},{9,10},{10,... | collective-permute-start | bytes 196616 | tf_op jit(solution)/shard_map/ppermute | solution.py:666
  38.1 3.2 %copy-start.5 = (bf16[1664,256]{1,0:T(8,128)(2,1)S(1)}, bf16[1664,256]{1,0:T(8,128)(2,1)}, u32[]{:S(2)}) copy-start(bf16[1664,256]{1,0:T(8,128)(2,1)} %constant.13.clone.collect_ref) | copy-start | bytes 2555908

commit v3 on v2

--- a/solution.py
+++ b/solution.py
@@ -9,7 +9,7 @@
 from jax.sharding import PartitionSpec as P
 
 STEPS = 3
-PAD = 144
+PAD = 136
 EY = 8
 EZ = 8
 LANES = 128
@@ -58,15 +58,15 @@
 
 def make_tables():
     derivative, weights = gll_tables()
-    grad = np.zeros((3 * 128, ROWS))
+    grad = np.zeros((3 * 128, 128))
     force = np.zeros((ROWS, 3 * 128))
     for a in range(5):
         for b in range(5):
             for d in range(5):
                 for m in range(5):
-                    grad[node(a, b, d), place(m, b, d)] = derivative[a, m]
-                    grad[128 + node(a, b, d), place(a, m, d)] = derivative[b, m]
-                    grad[256 + node(a, b, d), place(a, b, m)] = derivative[d, m]
+                    grad[node(a, b, d), node(m, b, d)] = derivative[a, m]
+                    grad[128 + node(a, b, d), node(a, m, d)] = derivative[b, m]
+                    grad[256 + node(a, b, d), node(a, b, m)] = derivative[d, m]
                     row = place(a, b, d)
                     force[row, node(m, b, d)] = -derivative[m, a] * weights[m] * weights[b] * weights[d]
                     force[row, 128 + node(a, m, d)] = -derivative[m, b] * weights[a] * weights[m] * weights[d]
@@ -74,7 +74,6 @@
     face = np.zeros((64, 3 * 128))
     face[0:25] = force[0:200:8]
     face[32:57] = force[4:200:8]
-    collect = np.zeros((WIDE, WINDOW), np.float32)
     line = np.zeros(SIDE)
     for e in range(8):
         line[4 * e : 4 * e + 5] += weights
@@ -84,14 +83,17 @@
         for d in range(5):
             for ey in range(8):
                 for ez in range(8):
-                    column = (b * 5 + d) * 64 + ey * 8 + ez
-                    spot = b * SIDE + 4 * ez + d
-                    if d < 4 or ez == 7:
-                        collect[column, spot] = 1.0
                     for slab in range(2):
                         at = (b * 5 + d) * 8
                         mass[at : at + 8, slab * 64 + ey * 8 + ez] = layer * line[4 * ey + b] * line[4 * ez + d]
-    return grad, force, face, collect, mass
+    face_mass = (layer[0] * np.outer(line, line)).reshape(1, FACE).astype(np.float32)
+    return grad, force, face, mass, face_mass
+
+
+def side_by_side(table):
+    high, middle, low = cut_table(table)
+    pairs = ((high, middle), (middle, high), (low, high))
+    return np.stack([np.concatenate(pair, axis=1) for pair in pairs])
 
 
 def cut_table(table):
@@ -104,7 +106,7 @@
     return np.stack(pieces)
 
 
-GRAD, FORCE, FACES, COLLECT, MASS = make_tables()
+GRAD, FORCE, FACES, MASS, FACE_MASS = make_tables()
 
 
 def cut(value):
@@ -119,14 +121,21 @@
     return jnp.dot(left, right, preferred_element_type=F32)
 
 
-def dot_six(table, value):
-    rows = table.shape[1]
-    stacked = table[...].reshape(3 * rows, table.shape[2])
-    high, middle, low = cut(value)
-    first = dot(stacked, high)
-    second = dot(stacked[0 : 2 * rows], middle)
-    small = first[2 * rows : 3 * rows] + second[rows : 2 * rows] + dot(stacked[0:rows], low)
-    return first[0:rows] + (first[rows : 2 * rows] + second[0:rows] + small)
+def gradients(table, flat):
+    high, middle, low = cut(flat)
+    first = dot(table[0:2].reshape(768, 256), jnp.concatenate([high, middle], axis=0))
+    return first[0:384] + (first[384:768] + dot(table[2], jnp.concatenate([high, low], axis=0)))
+
+
+def low_gradients(table, low):
+    return dot(table[0], jnp.concatenate([low, low], axis=0)) + dot(table[2, :, 0:128], low)
+
+
+def flatten(u_ref, flat_ref):
+    for c in range(3):
+        flat_ref[c, 120:128, :] = jnp.zeros((8, LANES), F32)
+        for a in range(5):
+            flat_ref[c, 25 * a : 25 * a + 25, :] = u_ref[c, pl.ds(a, 25, stride=8), :]
 
 
 def dot_three(table, value):
@@ -273,7 +282,7 @@
     select_ref[...] = jnp.where(chosen, 1.0, 0.0).astype(BF16)
 
 
-def rim_kernel(rim_ref, u_in, p_in, scale_in, spread_ref, mass_ref, u_ref, p_ref, scale_ref, low_ref, window_ref, rows_ref):
+def rim_kernel(rim_ref, u_in, p_in, scale_in, spread_ref, mass_ref, u_ref, p_ref, scale_ref, flat_ref, low_ref, window_ref, rows_ref):
     columns = to_columns(rim_ref[...], window_ref, spread_ref)
     for pair in range(BLOCKS // 2):
         tile = columns[:, LANES * pair : LANES * pair + LANES]
@@ -289,7 +298,8 @@
         p_ref[c, last, :] = jnp.where(upper, rows_ref[pl.ds(3 + c, 25, stride=8), :], p_ref[c, last, :])
     rim = step_square / (rows_ref[pl.ds(6, 25, stride=8), :] * mass_ref[last, :])
     scale_ref[last, :] = jnp.where(upper, rim, scale_ref[last, :])
-    low_ref[...] = u_ref[...].astype(BF16)
+    flatten(u_ref, flat_ref)
+    low_ref[...] = flat_ref[...].astype(BF16)
 
 
 def strains(grad, rows):
@@ -323,13 +333,13 @@
 
 
 def step_kernel(step, *refs):
-    u_ref, lame_ref, mu_ref, m_ref, decay_ref, grad_table, face_table = refs[0:7]
+    flat_ref, lame_ref, mu_ref, m_ref, decay_ref, grad_table, face_table = refs[0:7]
     older = refs[7 : 7 + step]
     refs = refs[7 + step :]
     strain_ref, sigma_ref, even_ref = refs[0:3]
     odd_ref, keep_ref = refs[3:5] if step < STEPS - 1 else (None, None)
     grad_ref = refs[-1]
-    grad_ref[...] = dot_six(grad_table, beside(u_ref))
+    grad_ref[...] = gradients(grad_table, beside(flat_ref))
     for block in range(9):
         sigma_ref[(block // 3) * 128 + 120 : (block // 3) * 128 + 128, (block % 3) * LANES : (block % 3) * LANES + LANES] = (
             jnp.zeros((8, LANES), F32)
@@ -401,21 +411,17 @@
         next_ref[c, 200:208, :] = jnp.zeros((8, LANES), F32)
 
 
-def add_faces(from_before, from_after, partial_ref, scale_ref, u_ref, delta_ref):
+def add_faces(packed_before, packed_after, partial_ref, scale_ref, u_ref, delta_ref):
     delta_ref[...] = jnp.zeros(delta_ref.shape, F32)
     lower = lanes_of((25, LANES)) < 64
-    if from_before is not None:
-        packed = from_before
-        turned = rolled(packed, 64, 1)
-        values = [packed[0:32], turned[0:32], jnp.concatenate([packed[32:48], turned[32:48]], axis=0)]
-        for c in range(3):
-            delta_ref[c, pl.ds(0, 25, stride=8), :] = jnp.where(lower, values[c][0:25], 0.0)
-    if from_after is not None:
-        packed = from_after
-        turned = rolled(packed, 64, 1)
-        values = [turned[0:32], packed[0:32], jnp.concatenate([turned[32:48], packed[32:48]], axis=0)]
-        for c in range(3):
-            delta_ref[c, pl.ds(4, 25, stride=8), :] = jnp.where(lower, 0.0, values[c][0:25])
+    turned = rolled(packed_before, 64, 1)
+    values = [packed_before[0:32], turned[0:32], jnp.concatenate([packed_before[32:48], turned[32:48]], axis=0)]
+    for c in range(3):
+        delta_ref[c, pl.ds(0, 25, stride=8), :] = jnp.where(lower, values[c][0:25], 0.0)
+    turned = rolled(packed_after, 64, 1)
+    values = [turned[0:32], packed_after[0:32], jnp.concatenate([turned[32:48], packed_after[32:48]], axis=0)]
+    for c in range(3):
+        delta_ref[c, pl.ds(4, 25, stride=8), :] = jnp.where(lower, 0.0, values[c][0:25])
     blocks = {}
     for c in range(3):
         for b in range(5):
@@ -430,18 +436,18 @@
         u_ref[c, 200:208, :] = jnp.zeros((8, LANES), F32)
 
 
-def update_kernel(odd_ref, even_ref, partial_ref, scale_ref, u_ref, low_ref, delta_ref):
+def update_kernel(odd_ref, even_ref, partial_ref, scale_ref, u_ref, flat_ref, low_ref, delta_ref):
     even_ring = lax.axis_index(("cuts", "sub")) % 2 == 0
     odd, even = odd_ref[...], even_ref[...]
     before, after = jnp.where(even_ring, odd, even), jnp.where(even_ring, even, odd)
     add_faces(before, after, partial_ref, scale_ref, u_ref, delta_ref)
-    low_ref[...] = u_ref[...].astype(BF16)
+    flatten(u_ref, flat_ref)
+    low_ref[...] = flat_ref[...].astype(BF16)
 
 
 def kernel_parts(strain_ref, low_ref, far_ref, lame_ref, mu_ref, grad_table, grad_ref, kernel_ref):
     forward = jnp.where(lax.axis_index("group") == 0, beside(low_ref), beside(far_ref))
-    grads = dot(grad_table[...].reshape(3 * 384, ROWS), forward)
-    grad_ref[...] = grads[0:384] + (grads[384:768] + grads[768:1152])
+    grad_ref[...] = low_gradients(grad_table, forward)
     for rows in CHUNKS:
         far = strains(grad_ref, rows)
         own = [strain_ref[part, rows, :] for part in range(6)]
@@ -510,30 +516,59 @@
     out_ref[:, 0, :] = value[0:250]
 
 
-def finish_kernel(before_ref, partial_ref, scale_ref, collect_ref, out_ref, u_ref, delta_ref):
-    add_faces(before_ref[0:48], None, partial_ref, scale_ref, u_ref, delta_ref)
+def to_nodal(columns, spread_ref, nodal_ref):
+    rows = columns.shape[0]
+    own = (lanes_of((rows, WIDE)) // 8) % 8
+    expanded = jnp.concatenate([jnp.where(own == ey, columns, 0.0) for ey in range(EY)], axis=0)
+    over_lanes = (((1,), (1,)), ((), ()))
+    pieces = jnp.concatenate(cut(expanded), axis=0)
+    windows = lax.dot_general(pieces, spread_ref[...], over_lanes, preferred_element_type=F32)
+    half = EY * rows
+    windows = windows[0:half] + windows[half : 2 * half] + windows[2 * half : 3 * half]
+    nodal_ref[...] = jnp.zeros(nodal_ref.shape, F32)
+    for ey in range(EY):
+        at = slice(JUMP * ey, JUMP * ey + 5 * SIDE)
+        nodal_ref[:, at] = nodal_ref[:, at] + windows[ey * rows : (ey + 1) * rows, 0 : 5 * SIDE]
+
+
+def nodal_kernel(partial_ref, spread_ref, nodal_ref):
     lane = lanes_of((8, LANES))
     sub = lax.broadcasted_iota(jnp.int32, (8, LANES), 0)
     tiles = []
     for c in range(3):
         row = []
         for pair in range(BLOCKS // 2):
-            even = u_ref[c, 16 * pair : 16 * pair + 8, :]
-            odd = u_ref[c, 16 * pair + 8 : 16 * pair + 16, :]
+            even = partial_ref[c, 16 * pair : 16 * pair + 8, :]
+            odd = partial_ref[c, 16 * pair + 8 : 16 * pair + 16, :]
             low = jnp.where(sub < 4, even, rolled(rolled(even, 64, 1), 4, 0))
             high = jnp.where(sub < 4, rolled(odd, 64, 1), rolled(odd, 4, 0))
             row.append(jnp.where(lane < 64, low, high))
         tiles.append(jnp.concatenate(row, axis=1))
     columns = jnp.concatenate(tiles, axis=0)
-    own = (lanes_of((24, WIDE)) // 8) % 8
-    spread = jnp.concatenate([jnp.where(own == ey, columns, 0.0) for ey in range(EY)], axis=0)
-    high, middle, low = cut(spread)
-    collect = collect_ref[...]
-    windows = dot(high, collect) + dot(middle, collect) + dot(low, collect)
-    for ey in range(EY):
-        width = JUMP if ey < EY - 1 else JUMP + SIDE
-        for c in range(3):
-            out_ref[0, c, :, JUMP * ey : JUMP * ey + width] = windows[24 * ey + 8 * c : 24 * ey + 8 * c + 8, 0:width]
+    column = lanes_of((24, WIDE))
+    block = column // 64
+    once = ((block % 5 < 4) | (column % 8 == 7)) & ((block // 5 < 4) | ((column // 8) % 8 == 7))
+    to_nodal(jnp.where(once, columns, 0.0), spread_ref, nodal_ref)
+
+
+def finish_kernel(before_ref, nodal_ref, density_ref, face_mass_ref, spread_ref, out_ref, rows_ref, face_ref):
+    packed = before_ref[0:48]
+    turned = rolled(packed, 64, 1)
+    values = [packed[0:32], turned[0:32], jnp.concatenate([packed[32:48], turned[32:48]], axis=0)]
+    rows_ref[...] = jnp.zeros(rows_ref.shape, F32)
+    for c in range(3):
+        rows_ref[pl.ds(c, 25, stride=8), :] = values[c][0:25]
+    lane = lanes_of((8, LANES))
+    tiles = []
+    for pair in range(BLOCKS // 2):
+        even, odd = rows_ref[16 * pair : 16 * pair + 8, :], rows_ref[16 * pair + 8 : 16 * pair + 16, :]
+        tiles.append(jnp.where(lane < 64, even, rolled(odd, 64, 1)))
+    to_nodal(jnp.concatenate(tiles, axis=1), spread_ref, face_ref)
+    scale = step_square / (density_ref[0:1, :] * face_mass_ref[...])
+    first = lax.broadcasted_iota(jnp.int32, (8, FACE), 0) == 0
+    for c in range(3):
+        share = face_ref[c : c + 1, :] * scale
+        out_ref[0, c] = nodal_ref[8 * c : 8 * c + 8, :] + jnp.where(first, share, 0.0)
 
 
 VMEM = pl.BlockSpec(memory_space=pltpu.VMEM)
@@ -591,16 +626,17 @@
     )
     rim = passed_along(rim, ring, -1)
 
-    grad_table = jnp.asarray(cut_table(GRAD))
+    grad_table = jnp.asarray(side_by_side(GRAD))
     force_table = jnp.asarray(cut_table(FORCE))
     face_table = jnp.asarray(cut_table(FACES))
-    collect = jnp.asarray(COLLECT, BF16)
+    face_mass = jnp.asarray(FACE_MASS)
     mass = jnp.asarray(MASS)
     memory = memory_init[0]
     owner = jnp.transpose(owner_map, (0, 2, 1))
 
     state = shaped(3, ROWS, LANES)
-    state_low = shaped(3, ROWS, LANES, dtype=BF16)
+    flat_shape = shaped(3, 128, LANES)
+    low_shape = shaped(3, 128, LANES, dtype=BF16)
     scale_shape = shaped(ROWS, LANES)
     five = shaped(5, 125, LANES)
     part_shape = shaped(256, LANES, dtype=BF16)
@@ -613,8 +649,8 @@
         [pltpu.VMEM((8, 56, WINDOW), F32)],
         disp_now, disp_prev, density, memory, sls_decay, mass, grad_table, face_table, force_table, lame_lambda, shear_mu,
     )
-    u, p, scale, low = call(
-        rim_kernel, "rim", [state, state, scale_shape, state_low], window_scratch, rim, u, p, scale, spread, mass
+    u, p, scale, flat, low = call(
+        rim_kernel, "rim", [state, state, scale_shape, flat_shape, low_shape], window_scratch, rim, u, p, scale, spread, mass
     )
     memories = [m1]
     kept = []
@@ -627,7 +663,7 @@
             outs += [face, five]
         results = call(
             lambda *refs, step=step: step_kernel(step, *refs), "step", outs, [grad_scratch],
-            u, lame_lambda, shear_mu, memories[step], sls_decay, grad_table, face_table, *kept,
+            flat, lame_lambda, shear_mu, memories[step], sls_decay, grad_table, face_table, *kept,
         )
         strain, sigma, even = results[0:3]
         if step < STEPS - 1:
@@ -654,20 +690,20 @@
             else:
                 partial, parts[1] = lax.optimization_barrier((partial, parts[1]))
             p = u
-            u, low = call(
-                update_kernel, "update", [state, state_low], [pltpu.VMEM((3, ROWS, LANES), F32)],
+            u, flat, low = call(
+                update_kernel, "update", [state, flat_shape, low_shape], [pltpu.VMEM((3, ROWS, LANES), F32)],
                 odd, even, partial, scale,
             )
         else:
             sent = list(call(
                 send_kernel, "send", [shaped(512 // subs, LANES)] * subs, part_scratch, *shared, *parts, select)
             )
-            for k in range(subs - 1, 0, -1):
+            for k in [at ^ (at >> 1) for at in range(subs - 1, 0, -1)]:
                 sent[k] = lax.ppermute(sent[k], "sub", [(j, j ^ k) for j in range(subs)])
+    nodal = call(nodal_kernel, "nodal", shaped(24, FACE), [], partial, spread)
     final = call(
-        finish_kernel, "finish", shaped(1, 3, 8, FACE),
-        [pltpu.VMEM((3, ROWS, LANES), F32), pltpu.VMEM((3, ROWS, LANES), F32)],
-        before, partial, scale, collect, micros=20,
+        finish_kernel, "finish", shaped(1, 3, 8, FACE), [pltpu.VMEM((ROWS, LANES), F32), pltpu.VMEM((8, FACE), F32)],
+        before, nodal, density, face_mass, spread,
     )
     kernels = call(sum_kernel, "sum", shaped(250, 1, 256), [], *sent)
     return final, jnp.transpose(kernels, (1, 2, 0))

time: 44.2 us -> 42.8 us (0.968)
  Pallas kernels: 14.4 us -> 13.5 us
  waiting for transfers between devices: 6.58 us -> 5.97 us
    ppermute x5, waiting for transfers between devices: 2.46 us -> 1.61 us  [passed_along(): lax.ppermute(value, axis, [(source, (source + steps) % count) for source...]
    pallas_call x17 -> x18, Pallas kernels: 14.4 us -> 13.5 us  [call(): pl.pallas_call(kernel, name=name, out_shape=outs, in_specs=[HBM if at in...]
  transfers between devices with their start and end apart: 12 -> 12, of which waited for: 4 -> 5; matrix products, arithmetic and copies ran while one was open for 3% -> 3% of each run, Pallas kernels for 19% -> 19%
where the time goes in v3:
time: 42.8 us; the launch traced here: 42.6 us
  starting transfers between devices  20.2 us (47%)
  Pallas kernels  13.5 us (32%)
  waiting for transfers between devices  5.97 us (14%)
  local copies, waits for them, and re-layouts  2.04 us (5%)
  between operations  0.92 us (2%)
    pallas_call x18, Pallas kernels, call(): pl.pallas_call(kernel, name=name, out_shape=outs, in_specs=[HBM if at in...  13.5 us
    ppermute x4, starting transfers between devices, swapped(): return lax.ppermute(value, axis, pairs)  8.2 us
    ppermute x5, starting transfers between devices, passed_along(): lax.ppermute(value, axis, [(source, (source + steps) % count) for source...  7.5 us
    ppermute x3, starting transfers between devices, per_device(): sent[k] = lax.ppermute(sent[k], 'sub', [(j, j ^ k) for j in range(subs)])  4.45 us
    ppermute x4, waiting for transfers between devices, swapped(): return lax.ppermute(value, axis, pairs)  4.35 us
    unnamed x25, local copies, waits for them, and re-layouts  2.04 us
    ppermute x5, waiting for transfers between devices, passed_along(): lax.ppermute(value, axis, [(source, (source + steps) % count) for source...  1.61 us
  transfers between devices with their start and end apart: 12, of which 5 were waited for; matrix products, arithmetic and copies ran while one was open for 3% of the time, Pallas kernels for 19%

profile of v3, /device:TPU:0, one launch (start us, length us, event | category | flops | bytes accessed | tf_op | source)
XLA Modules:
  0.0 42.6 jit_solution(9091838031145707984)
XLA Ops:
  0.6 1.0 %gather.1 = f32[8,1089]{1,0:T(8,128)S(1)} custom-call(f32[1,3,8,1089]{3,2,1,0:T(8,128)} %now_ref.3, f32[1,3,8,1089]{3,2,1,0:T(8,128)} %prev_ref.3, f32[8,1089]{1,0:T(8,128)} %density_ref.5), custom_call_target="tpu_custom_call" | custom-call | bytes 3000000 | tf_op jit(solution)/shard_map/gather/pallas_call | solution.py:583
  1.7 7.0 %collective-permute-start = (f32[8,1089]{1,0:T(8,128)S(1)}, f32[8,1089]{1,0:T(8,128)S(1)}, u32[]{:S(2)}, u32[]{:S(2)}) collective-permute-start(f32[8,1089]{1,0:T(8,128)S(1)} %gather.1), channel_id=1, source_target_pairs={{0,15},{1,0},{2,1},{3,2},{4,3},{5,4},{6,5},{7,6},{8,7},{9,8},{10,9... | collective-permute-start | bytes 104552 | tf_op jit(solution)/shard_map/ppermute | solution.py:597
  8.7 1.3 %copy.18 = f32[1,3,5,125,128]{4,3,0,2,1:T(8,128)S(1)} copy(f32[1,3,5,125,128]{4,0,3,2,1:T(1,128)} %param.15) | data formatting | bytes 1920000
  10.1 1.7 %prologue.1 = (f32[3,208,128]{2,1,0:T(8,128)S(1)}, f32[3,208,128]{2,1,0:T(8,128)S(1)}, f32[208,128]{1,0:T(8,128)S(1)}, f32[5,125,128]{2,1,0:T(8,128)S(1)}, bf16[256,1664]{1,0:T(8,128)(2,1)S(1)}) custom-call(f32[1,3,8,1089]{3,2,1,0:T(8,128)S(1)} %copy-done.5, f32[1,3,8,1089]{3,2,1,0:T(8,128)S(1)} %copy-done.6, f32[8,1089]{1,0:T(8,128)S(1)} %copy-done.8, ...), custom_call_target="tpu_custom_call" | custom-call | bytes 3000000 | tf_op jit(solution)/shard_map/prologue/pallas_call | solution.py:583
  11.8 0.5 %rim.1 = (f32[3,208,128]{2,1,0:T(8,128)S(1)}, f32[3,208,128]{2,1,0:T(8,128)S(1)}, f32[208,128]{1,0:T(8,128)S(1)}, f32[3,128,128]{2,1,0:T(8,128)S(1)}, bf16[3,128,128]{2,1,0:T(8,128)(2,1)S(1)}) custom-call(f32[8,1089]{1,0:T(8,128)S(1)} %collective-permute-done.rim_ref, f32[3,208,128]{2,1,0:T(8,128)S(1)} %get-tuple-element.46.u_in, ...), custom_call_target="tpu_custom_call" | custom-call | bytes 3000000 | tf_op jit(solution)/shard_map/rim/pallas_call | solution.py:583
  12.3 0.9 %step.3 = (f32[6,125,128]{2,1,0:T(8,128)S(1)}, f32[384,384]{1,0:T(8,128)S(1)}, f32[48,128]{1,0:T(8,128)S(1)}, f32[48,128]{1,0:T(8,128)S(1)}, f32[5,125,128]{2,1,0:T(8,128)S(1)}) custom-call(f32[3,128,128]{2,1,0:T(8,128)S(1)} %get-tuple-element.50.refs_0_, f32[125,128]{1,0:T(8,128)S(1)} %copy-done.2, f32[125,128]{1,0:T(8,128)S(1)} %copy-done.3, ...), custom_call_target="tpu_custom_call" | custom-call | bytes 3000000 | tf_op jit(solution)/shard_map/step/pallas_call | solution.py:583
  13.3 4.5 %collective-permute-start.1 = (f32[48,128]{1,0:T(8,128)S(1)}, f32[48,128]{1,0:T(8,128)S(1)}, u32[]{:S(2)}, u32[]{:S(2)}) collective-permute-start(f32[48,128]{1,0:T(8,128)S(1)} %get-tuple-element.52), channel_id=1, source_target_pairs={{1,2},{2,1},{3,4},{4,3},{5,6},{6,5},{7,8},{8,7},{9,10},{10,9},{11,... | collective-permute-start | bytes 73736 | tf_op jit(solution)/shard_map/ppermute | solution.py:606
  17.8 0.7 %copy-done.11 = s32[2,64,1]{1,2,0:T(1,128)S(1)} copy-done((s32[2,64,1]{1,2,0:T(1,128)S(1)}, s32[2,64,1]{1,2,0:T(1,128)}, u32[]{:S(2)}) %copy-start.11) | copy-done | bytes 536
  18.9 0.7 %rest.3.partial_ref = f32[3,208,128]{2,1,0:T(8,128)S(1)} custom-call(f32[384,384]{1,0:T(8,128)S(1)} %get-tuple-element.54.sigma_ref, f32[3,208,128]{2,1,0:T(8,128)S(1)} %get-tuple-element.55.u_ref.p_ref, f32[3,208,128]{2,1,0:T(8,128)S(1)} %get-tuple-element.56.p_ref, f32[208,128]{1,0:T(8,128)S(1)} %get-tuple-element.57.scale_ref, ...), custom_call_target="tpu_custom_call" | custom-call | bytes 3000000 | tf_op jit(solution)/shard_map/rest/pallas_call | solution.py:583
  20.0 0.9 %collective-permute-done.1.odd_ref = f32[48,128]{1,0:T(8,128)S(1)} collective-permute-done((f32[48,128]{1,0:T(8,128)S(1)}, f32[48,128]{1,0:T(8,128)S(1)}, u32[]{:S(2)}, u32[]{:S(2)}) %collective-permute-start.1) | collective-permute-done | bytes 24608 | tf_op jit(solution)/shard_map/ppermute | solution.py:606
  20.9 0.8 %collective-permute-done.2.even_ref = f32[48,128]{1,0:T(8,128)S(1)} collective-permute-done((f32[48,128]{1,0:T(8,128)S(1)}, f32[48,128]{1,0:T(8,128)S(1)}, u32[]{:S(2)}, u32[]{:S(2)}) %collective-permute-start.2) | collective-permute-done | bytes 24608 | tf_op jit(solution)/shard_map/ppermute | solution.py:606
  22.0 0.9 %step.4 = (f32[6,125,128]{2,1,0:T(8,128)S(1)}, f32[384,384]{1,0:T(8,128)S(1)}, f32[48,128]{1,0:T(8,128)S(1)}, f32[48,128]{1,0:T(8,128)S(1)}, f32[5,125,128]{2,1,0:T(8,128)S(1)}) custom-call(f32[3,128,128]{2,1,0:T(8,128)S(1)} %get-tuple-element.64.refs_0_, f32[125,128]{1,0:T(8,128)S(1)} %copy-done.2, f32[125,128]{1,0:T(8,128)S(1)} %copy-done.3, ...), custom_call_target="tpu_custom_call" | custom-call | bytes 3000000 | tf_op jit(solution)/shard_map/step/pallas_call | solution.py:583
  22.9 3.7 %collective-permute-start.4 = (f32[48,128]{1,0:T(8,128)S(1)}, f32[48,128]{1,0:T(8,128)S(1)}, u32[]{:S(2)}, u32[]{:S(2)}) collective-permute-start(f32[48,128]{1,0:T(8,128)S(1)} %get-tuple-element.67), channel_id=1, source_target_pairs={{1,2},{2,1},{3,4},{4,3},{5,6},{6,5},{7,8},{8,7},{9,10},{10,9},{11,... | collective-permute-start | bytes 73736 | tf_op jit(solution)/shard_map/ppermute | solution.py:606
  26.6 0.7 %rest.4.partial_ref = f32[3,208,128]{2,1,0:T(8,128)S(1)} custom-call(f32[384,384]{1,0:T(8,128)S(1)} %get-tuple-element.69.sigma_ref, f32[3,208,128]{2,1,0:T(8,128)S(1)} %get-tuple-element.70.u_ref.p_ref, f32[3,208,128]{2,1,0:T(8,128)S(1)} %get-tuple-element.55.u_ref.p_ref, f32[208,128]{1,0:T(8,128)S(1)} %get-tuple-element.57.scale_ref, ...), custom_call_target="tpu_custom_call" | custom-call | bytes 3000000 | tf_op jit(solution)/shard_map/rest/pallas_call | solution.py:583
  27.7 2.7 %collective-permute-done.4.odd_ref = f32[48,128]{1,0:T(8,128)S(1)} collective-permute-done((f32[48,128]{1,0:T(8,128)S(1)}, f32[48,128]{1,0:T(8,128)S(1)}, u32[]{:S(2)}, u32[]{:S(2)}) %collective-permute-start.4) | collective-permute-done | bytes 24608 | tf_op jit(solution)/shard_map/ppermute | solution.py:606
  30.8 0.9 %step.5 = (f32[6,125,128]{2,1,0:T(8,128)S(1)}, f32[384,384]{1,0:T(8,128)S(1)}, f32[136,128]{1,0:T(8,128)S(1)}) custom-call(f32[3,128,128]{2,1,0:T(8,128)S(1)} %get-tuple-element.75.refs_0_, f32[125,128]{1,0:T(8,128)S(1)} %copy-done.2, f32[125,128]{1,0:T(8,128)S(1)} %copy-done.3, f32[5,125,128]{2,1,0:T(8,128)S(1)} %get-tuple-element.76.refs_3_, ...), custom_call_target="tpu_custom_call" | custom-call | bytes 3000000 | tf_op jit(solution)/shard_map/step/pallas_call | solution.py:583
  32.1 0.7 %send.1 = (f32[128,128]{1,0:T(8,128)S(1)}, f32[128,128]{1,0:T(8,128)S(1)}, f32[128,128]{1,0:T(8,128)S(1)}, f32[128,128]{1,0:T(8,128)S(1)}) custom-call(f32[6,125,128]{2,1,0:T(8,128)S(1)} %get-tuple-element.81.strain_ref, bf16[3,128,128]{2,1,0:T(8,128)(2,1)S(1)} %get-tuple-element.82.low_ref, bf16[3,128,128]{2,1,0:T(8,128)(2,1)S(1)} %collective-permute-done.8.far_ref, ...), custom_call_target="tpu_custom_call" | custom-call | bytes 3000000 | tf_op jit(solution)/shard_map/send/pallas_call | solution.py:583
  33.1 1.4 %collective-permute-start.10 = (f32[128,128]{1,0:T(8,128)S(1)}, f32[128,128]{1,0:T(8,128)S(1)}, u32[]{:S(2)}, u32[]{:S(2)}) collective-permute-start(f32[128,128]{1,0:T(8,128)S(1)} %get-tuple-element.88), channel_id=1, source_target_pairs={{0,2},{1,3},{2,0},{3,1},{4,6},{5,7},{6,4},{7,5},{8,10},{9,11},{10,... | collective-permute-start | bytes 196616 | tf_op jit(solution)/shard_map/ppermute | solution.py:702
  34.4 2.8 %collective-permute-start.11 = (f32[128,128]{1,0:T(8,128)S(1)}, f32[128,128]{1,0:T(8,128)S(1)}, u32[]{:S(2)}, u32[]{:S(2)}) collective-permute-start(f32[128,128]{1,0:T(8,128)S(1)} %get-tuple-element.89), channel_id=1, source_target_pairs={{0,3},{1,2},{2,1},{3,0},{4,7},{5,6},{6,5},{7,4},{8,11},{9,10},{10,... | collective-permute-start | bytes 196616 | tf_op jit(solution)/shard_map/ppermute | solution.py:702
  37.2 0.7 %rest.5.partial_ref = f32[3,208,128]{2,1,0:T(8,128)S(1)} custom-call(f32[384,384]{1,0:T(8,128)S(1)} %get-tuple-element.79.sigma_ref, f32[3,208,128]{2,1,0:T(8,128)S(1)} %get-tuple-element.80.u_ref, f32[3,208,128]{2,1,0:T(8,128)S(1)} %get-tuple-element.70.u_ref.p_ref, f32[208,128]{1,0:T(8,128)S(1)} %get-tuple-element.57.scale_ref, ...), custom_call_target="tpu_custom_call" | custom-call | bytes 3000000 | tf_op jit(solution)/shard_map/rest/pallas_call | solution.py:583
  37.9 0.9 %nodal.1.nodal_ref = f32[24,1089]{1,0:T(8,128)S(1)} custom-call(f32[3,208,128]{2,1,0:T(8,128)S(1)} %rest.5.partial_ref, bf16[256,1664]{1,0:T(8,128)(2,1)S(1)} %get-tuple-element.49.spread_ref), custom_call_target="tpu_custom_call" | custom-call | bytes 3000000 | tf_op jit(solution)/shard_map/nodal/pallas_call | solution.py:583
  38.8 1.5 %collective-permute-done.7.before_ref = f32[136,128]{1,0:T(8,128)S(1)} collective-permute-done((f32[136,128]{1,0:T(8,128)S(1)}, f32[136,128]{1,0:T(8,128)S(1)}, u32[]{:S(2)}, u32[]{:S(2)}) %collective-permute-start.7) | collective-permute-done | bytes 69664 | tf_op jit(solution)/shard_map/ppermute | solution.py:597
  40.3 1.3 %finish.1 = f32[1,3,8,1089]{3,2,1,0:T(8,128)} custom-call(f32[136,128]{1,0:T(8,128)S(1)} %collective-permute-done.7.before_ref, f32[24,1089]{1,0:T(8,128)S(1)} %nodal.1.nodal_ref, f32[8,1089]{1,0:T(8,128)S(1)} %copy-done.8, f32[1,1089]{1,0:T(1,128)S(1)} %copy-done.10, bf16[256,1664]{1,0:T(8,128)(2,1)S(1)} %get-tuple-element.49.spread_ref), custom_call_target="tpu_custom_call" | custom-call | bytes 3000000 | tf_op jit(solution)/shard_map/finish/pallas_call | solution.py:583
  41.6 1.0 %sum.1 = f32[250,1,256]{2,1,0:T(1,128)} custom-call(f32[128,128]{1,0:T(8,128)S(1)} %get-tuple-element.86.refs_0_, f32[128,128]{1,0:T(8,128)S(1)} %collective-permute-done.9.refs_1_, f32[128,128]{1,0:T(8,128)S(1)} %collective-permute-done.10.refs_2_, f32[128,128]{1,0:T(8,128)S(1)} %collective-permute-done.11.refs_3_), custom_call_target="tpu_custom_call" | custom-call | bytes 3000000 | tf_op jit(solution)/shard_map/sum/pallas_call | solution.py:583
  (43 shorter events, 2.8 us)
Async XLA Ops:
  1.6 8.4 %copy-start = (bf16[3,384,256]{2,1,0:T(8,128)(2,1)S(1)}, bf16[3,384,256]{2,1,0:T(8,128)(2,1)}, u32[]{:S(2)}) copy-start(bf16[3,384,256]{2,1,0:T(8,128)(2,1)} %constant.10.clone.refs_0_.refs_5_.grad_table) | copy-start | bytes 1769476
  1.6 8.4 %copy-start.1 = (bf16[3,208,384]{2,1,0:T(8,128)(2,1)S(1)}, bf16[3,208,384]{2,1,0:T(8,128)(2,1)}, u32[]{:S(2)}) copy-start(bf16[3,208,384]{2,1,0:T(8,128)(2,1)} %constant.11.clone.refs_2_.force_table) | copy-start | bytes 1437700
  1.7 8.4 %copy-start.2 = (f32[125,128]{1,0:T(8,128)S(1)}, f32[125,128]{1,0:T(8,128)}, u32[]{:S(2)}) copy-start(f32[125,128]{1,0:T(8,128)} %lame_ref.5) | copy-start | bytes 192004
  1.7 8.4 %copy-start.3 = (f32[125,128]{1,0:T(8,128)S(1)}, f32[125,128]{1,0:T(8,128)}, u32[]{:S(2)}) copy-start(f32[125,128]{1,0:T(8,128)} %mu_ref.5) | copy-start | bytes 192004
  1.7 8.4 %copy-start.4 = (bf16[3,64,384]{2,1,0:T(8,128)(2,1)S(1)}, bf16[3,64,384]{2,1,0:T(8,128)(2,1)}, u32[]{:S(2)}) copy-start(bf16[3,64,384]{2,1,0:T(8,128)(2,1)} %constant.12.clone.refs_1_.refs_6_) | copy-start | bytes 442372
  1.7 8.4 %copy-start.5 = (f32[1,3,8,1089]{3,2,1,0:T(8,128)S(1)}, f32[1,3,8,1089]{3,2,1,0:T(8,128)}, u32[]{:S(2)}) copy-start(f32[1,3,8,1089]{3,2,1,0:T(8,128)} %now_ref.3) | copy-start | bytes 313636
  1.7 8.4 %copy-start.6 = (f32[1,3,8,1089]{3,2,1,0:T(8,128)S(1)}, f32[1,3,8,1089]{3,2,1,0:T(8,128)}, u32[]{:S(2)}) copy-start(f32[1,3,8,1089]{3,2,1,0:T(8,128)} %prev_ref.3) | copy-start | bytes 313636
  1.7 8.4 %copy-start.7 = (f32[208,128]{1,0:T(8,128)S(1)}, f32[208,128]{1,0:T(8,128)}, u32[]{:S(2)}) copy-start(f32[208,128]{1,0:T(8,128)} %constant.14.clone.mass_ref) | copy-start | bytes 319492
  1.7 8.4 %copy-start.8 = (f32[8,1089]{1,0:T(8,128)S(1)}, f32[8,1089]{1,0:T(8,128)}, u32[]{:S(2)}) copy-start(f32[8,1089]{1,0:T(8,128)} %density_ref.5) | copy-start | bytes 104548
  1.7 10.1 %collective-permute-start = (f32[8,1089]{1,0:T(8,128)S(1)}, f32[8,1089]{1,0:T(8,128)S(1)}, u32[]{:S(2)}, u32[]{:S(2)}) collective-permute-start(f32[8,1089]{1,0:T(8,128)S(1)} %gather.1), channel_id=1, source_target_pairs={{0,15},{1,0},{2,1},{3,2},{4,3},{5,4},{6,5},{7,6},{8,7},{9,8},{10,9... | collective-permute-start | bytes 104552 | tf_op jit(solution)/shard_map/ppermute | solution.py:597
  8.7 1.4 %copy-start.9 = (f32[3,128]{1,0:T(4,128)S(1)}, f32[3,128]{1,0:T(4,128)}, u32[]{:S(2)}) copy-start(f32[3,128]{1,0:T(4,128)} %refs_4_.7) | copy-start | bytes 4612
  13.2 6.4 %collective-permute-start.3 = (bf16[3,128,128]{2,1,0:T(8,128)(2,1)S(1)}, bf16[3,128,128]{2,1,0:T(8,128)(2,1)S(1)}, u32[]{:S(2)}, u32[]{:S(2)}) collective-permute-start(bf16[3,128,128]{2,1,0:T(8,128)(2,1)S(1)} %get-tuple-element.60.low_ref), channel_id=1, source_target_pairs={{0,16},{16,0},{1,17},{17,1},{2,18},{18,2},{3,19},{19,3},{4,20},{20... | collective-permute-start | bytes 294920 | tf_op jit(solution)/shard_map/ppermute | solution.py:597
  13.3 7.6 %collective-permute-start.1 = (f32[48,128]{1,0:T(8,128)S(1)}, f32[48,128]{1,0:T(8,128)S(1)}, u32[]{:S(2)}, u32[]{:S(2)}) collective-permute-start(f32[48,128]{1,0:T(8,128)S(1)} %get-tuple-element.52), channel_id=1, source_target_pairs={{1,2},{2,1},{3,4},{4,3},{5,6},{6,5},{7,8},{8,7},{9,10},{10,9},{11,... | collective-permute-start | bytes 73736 | tf_op jit(solution)/shard_map/ppermute | solution.py:606
  17.8 0.7 %copy-start.11 = (s32[2,64,1]{1,2,0:T(1,128)S(1)}, s32[2,64,1]{1,2,0:T(1,128)}, u32[]{:S(2)}) copy-start(s32[2,64,1]{1,2,0:T(1,128)} %param.20) | copy-start | bytes 1540
  17.8 3.8 %collective-permute-start.2 = (f32[48,128]{1,0:T(8,128)S(1)}, f32[48,128]{1,0:T(8,128)S(1)}, u32[]{:S(2)}, u32[]{:S(2)}) collective-permute-start(f32[48,128]{1,0:T(8,128)S(1)} %get-tuple-element.53), channel_id=1, source_target_pairs={{0,1},{1,0},{2,3},{3,2},{4,5},{5,4},{6,7},{7,6},{8,9},{9,8},{10,11... | collective-permute-start | bytes 73736 | tf_op jit(solution)/shard_map/ppermute | solution.py:606
  22.8 4.5 %collective-permute-start.6 = (bf16[3,128,128]{2,1,0:T(8,128)(2,1)S(1)}, bf16[3,128,128]{2,1,0:T(8,128)(2,1)S(1)}, u32[]{:S(2)}, u32[]{:S(2)}) collective-permute-start(bf16[3,128,128]{2,1,0:T(8,128)(2,1)S(1)} %get-tuple-element.73.low_ref), channel_id=1, source_target_pairs={{0,16},{16,0},{1,17},{17,1},{2,18},{18,2},{3,19},{19,3},{4,20},{20... | collective-permute-start | bytes 294920 | tf_op jit(solution)/shard_map/ppermute | solution.py:597
  22.9 7.5 %collective-permute-start.4 = (f32[48,128]{1,0:T(8,128)S(1)}, f32[48,128]{1,0:T(8,128)S(1)}, u32[]{:S(2)}, u32[]{:S(2)}) collective-permute-start(f32[48,128]{1,0:T(8,128)S(1)} %get-tuple-element.67), channel_id=1, source_target_pairs={{1,2},{2,1},{3,4},{4,3},{5,6},{6,5},{7,8},{8,7},{9,10},{10,9},{11,... | collective-permute-start | bytes 73736 | tf_op jit(solution)/shard_map/ppermute | solution.py:606
  26.6 3.8 %collective-permute-start.5 = (f32[48,128]{1,0:T(8,128)S(1)}, f32[48,128]{1,0:T(8,128)S(1)}, u32[]{:S(2)}, u32[]{:S(2)}) collective-permute-start(f32[48,128]{1,0:T(8,128)S(1)} %get-tuple-element.68), channel_id=1, source_target_pairs={{0,1},{1,0},{2,3},{3,2},{4,5},{5,4},{6,7},{7,6},{8,9},{9,8},{10,11... | collective-permute-start | bytes 73736 | tf_op jit(solution)/shard_map/ppermute | solution.py:606
  30.7 1.4 %collective-permute-start.8 = (bf16[3,128,128]{2,1,0:T(8,128)(2,1)S(1)}, bf16[3,128,128]{2,1,0:T(8,128)(2,1)S(1)}, u32[]{:S(2)}, u32[]{:S(2)}) collective-permute-start(bf16[3,128,128]{2,1,0:T(8,128)(2,1)S(1)} %get-tuple-element.82.low_ref), channel_id=1, source_target_pairs={{0,16},{16,0},{1,17},{17,1},{2,18},{18,2},{3,19},{19,3},{4,20},{20... | collective-permute-start | bytes 294920 | tf_op jit(solution)/shard_map/ppermute | solution.py:597
  31.7 8.6 %collective-permute-start.7 = (f32[136,128]{1,0:T(8,128)S(1)}, f32[136,128]{1,0:T(8,128)S(1)}, u32[]{:S(2)}, u32[]{:S(2)}) collective-permute-start(f32[136,128]{1,0:T(8,128)S(1)} %get-tuple-element.78), channel_id=1, source_target_pairs={{0,1},{1,2},{2,3},{3,4},{4,5},{5,6},{6,7},{7,8},{8,9},{9,10},{10,1... | collective-permute-start | bytes 208904 | tf_op jit(solution)/shard_map/ppermute | solution.py:597
  32.7 8.9 %collective-permute-start.9 = (f32[128,128]{1,0:T(8,128)S(1)}, f32[128,128]{1,0:T(8,128)S(1)}, u32[]{:S(2)}, u32[]{:S(2)}) collective-permute-start(f32[128,128]{1,0:T(8,128)S(1)} %get-tuple-element.87), channel_id=1, source_target_pairs={{0,1},{1,0},{2,3},{3,2},{4,5},{5,4},{6,7},{7,6},{8,9},{9,8},{10,11... | collective-permute-start | bytes 196616 | tf_op jit(solution)/shard_map/ppermute | solution.py:702
  33.1 8.5 %collective-permute-start.10 = (f32[128,128]{1,0:T(8,128)S(1)}, f32[128,128]{1,0:T(8,128)S(1)}, u32[]{:S(2)}, u32[]{:S(2)}) collective-permute-start(f32[128,128]{1,0:T(8,128)S(1)} %get-tuple-element.88), channel_id=1, source_target_pairs={{0,2},{1,3},{2,0},{3,1},{4,6},{5,7},{6,4},{7,5},{8,10},{9,11},{10,... | collective-permute-start | bytes 196616 | tf_op jit(solution)/shard_map/ppermute | solution.py:702
  34.4 7.2 %collective-permute-start.11 = (f32[128,128]{1,0:T(8,128)S(1)}, f32[128,128]{1,0:T(8,128)S(1)}, u32[]{:S(2)}, u32[]{:S(2)}) collective-permute-start(f32[128,128]{1,0:T(8,128)S(1)} %get-tuple-element.89), channel_id=1, source_target_pairs={{0,3},{1,2},{2,1},{3,0},{4,7},{5,6},{6,5},{7,4},{8,11},{9,10},{10,... | collective-permute-start | bytes 196616 | tf_op jit(solution)/shard_map/ppermute | solution.py:702
  37.9 2.4 %copy-start.10 = (f32[1,1089]{1,0:T(1,128)S(1)}, f32[1,1089]{1,0:T(1,128)}, u32[]{:S(2)}) copy-start(f32[1,1089]{1,0:T(1,128)} %constant.13.clone.face_mass_ref) | copy-start | bytes 13072

commit v4 on v3

--- a/solution.py
+++ b/solution.py
@@ -56,6 +56,9 @@
     return (b * 5 + d) * 8 + a
 
 
+FACE_ROWS = [slice(0, 128), slice(128, 160), slice(224, 256), slice(256, 288), slice(352, 384)]
+
+
 def make_tables():
     derivative, weights = gll_tables()
     grad = np.zeros((3 * 128, 128))
@@ -71,9 +74,18 @@
                     force[row, node(m, b, d)] = -derivative[m, a] * weights[m] * weights[b] * weights[d]
                     force[row, 128 + node(a, m, d)] = -derivative[m, b] * weights[a] * weights[m] * weights[d]
                     force[row, 256 + node(a, b, m)] = -derivative[m, d] * weights[a] * weights[b] * weights[m]
-    face = np.zeros((64, 3 * 128))
-    face[0:25] = force[0:200:8]
-    face[32:57] = force[4:200:8]
+    full = np.zeros((80, 3 * 128))
+    first_grad, last_grad = np.zeros((3 * 128, 40)), np.zeros((3 * 128, 40))
+    for b in range(5):
+        for d in range(5):
+            full[d * 8 + b] = force[place(0, b, d)]
+            full[40 + d * 8 + b] = force[place(4, b, d)]
+            first_grad[:, d * 8 + b] = grad[:, node(0, b, d)]
+            last_grad[:, d * 8 + b] = grad[:, node(4, b, d)]
+    face = np.concatenate([full[:, rows] for rows in FACE_ROWS], axis=1)
+    first, last = cut_table(first_grad), cut_table(last_grad)
+    share = np.concatenate([first[0], first[0], first[1], last[0], last[0], last[1]], axis=1)
+    rim = np.concatenate([last[0], last[0], last[1], last[1], last[0], last[2]], axis=1)
     line = np.zeros(SIDE)
     for e in range(8):
         line[4 * e : 4 * e + 5] += weights
@@ -87,7 +99,7 @@
                         at = (b * 5 + d) * 8
                         mass[at : at + 8, slab * 64 + ey * 8 + ez] = layer * line[4 * ey + b] * line[4 * ez + d]
     face_mass = (layer[0] * np.outer(line, line)).reshape(1, FACE).astype(np.float32)
-    return grad, force, face, mass, face_mass
+    return grad, force, face, mass, face_mass, share, rim
 
 
 def side_by_side(table):
@@ -106,7 +118,7 @@
     return np.stack(pieces)
 
 
-GRAD, FORCE, FACES, MASS, FACE_MASS = make_tables()
+GRAD, FORCE, FACES, MASS, FACE_MASS, SHARE, RIM = make_tables()
 
 
 def cut(value):
@@ -236,7 +248,8 @@
 
 
 def prologue_kernel(now_ref, prev_ref, density_ref, memory_ref, decay_ref, mass_ref, *refs):
-    u_ref, p_ref, scale_ref, m1_ref, spread_ref, window_ref = refs[-6:]
+    grad_table = refs[0]
+    u_ref, p_ref, scale_ref, m1_ref, spread_ref, flat_ref, grad_ref, window_ref = refs[-8:]
     spread_ref[...] = spread_table()
     rows = jnp.concatenate([now_ref[0].reshape(24, FACE), prev_ref[0].reshape(24, FACE), density_ref[...]], axis=0)
     columns = to_columns(rows, window_ref, spread_ref)
@@ -260,6 +273,11 @@
     decays = [decay_ref[l : l + 1, :] for l in range(3)]
     for part in range(5):
         m1_ref[part] = weighted_memory(memory_ref, decays, part, 1)
+    flatten(u_ref, flat_ref)
+    lower = lanes_of((25, LANES)) < 64
+    for c in range(3):
+        flat_ref[c, 100:125, :] = jnp.where(lower, flat_ref[c, 100:125, :], 0.0)
+    grad_ref[...] = gradients(grad_table, beside(flat_ref))
 
 
 def later_kernel(memory_ref, decay_ref, owner_ref, m2_ref, m3_ref, select_ref):
@@ -282,24 +300,46 @@
     select_ref[...] = jnp.where(chosen, 1.0, 0.0).astype(BF16)
 
 
-def rim_kernel(rim_ref, u_in, p_in, scale_in, spread_ref, mass_ref, u_ref, p_ref, scale_ref, flat_ref, low_ref, window_ref, rows_ref):
+def rim_rows(rim_ref, spread_ref, window_ref, rows_ref):
     columns = to_columns(rim_ref[...], window_ref, spread_ref)
     for pair in range(BLOCKS // 2):
         tile = columns[:, LANES * pair : LANES * pair + LANES]
         rows_ref[16 * pair : 16 * pair + 8, :] = rolled(tile, 64, 1)
         rows_ref[16 * pair + 8 : 16 * pair + 16, :] = tile
-    u_ref[...] = u_in[...]
-    p_ref[...] = p_in[...]
-    scale_ref[...] = scale_in[...]
-    upper = lanes_of((25, LANES)) >= 64
-    last = pl.ds(4, 25, stride=8)
-    for c in range(3):
-        u_ref[c, last, :] = jnp.where(upper, rows_ref[pl.ds(c, 25, stride=8), :], u_ref[c, last, :])
-        p_ref[c, last, :] = jnp.where(upper, rows_ref[pl.ds(3 + c, 25, stride=8), :], p_ref[c, last, :])
-    rim = step_square / (rows_ref[pl.ds(6, 25, stride=8), :] * mass_ref[last, :])
-    scale_ref[last, :] = jnp.where(upper, rim, scale_ref[last, :])
-    flatten(u_ref, flat_ref)
-    low_ref[...] = flat_ref[...].astype(BF16)
+
+
+def unpack_face(here, there):
+    top = lax.broadcasted_iota(jnp.int32, (8, LANES), 0) < 3
+    parts = [[], [], []]
+    for d in range(5):
+        first, second = here[8 * d : 8 * d + 8], there[8 * d : 8 * d + 8]
+        third = jnp.where(top, rolled(first, 3, 0), rolled(second, 6, 0))
+        for part, line in zip(parts, (first, second, third)):
+            part.append(line)
+    return parts
+
+
+def face_shares(odd_ref, even_ref, face_scale_ref):
+    even_ring = lax.axis_index(("cuts", "sub")) % 2 == 0
+    odd, even = odd_ref[...], even_ref[...]
+    lower = (lanes_of((40, LANES)) < 64) == even_ring
+    rows = unpack_face(jnp.where(lower, odd, even), rolled(jnp.where(lower, even, odd), 64, 1))
+    lane = lanes_of((8, LANES))
+    sub = lax.broadcasted_iota(jnp.int32, (8, LANES), 0)
+    ez, ey = lane % 8, (lane // 8) % 8
+    up, down = (sub == 0) & (ey > 0), (sub == 4) & (ey < 7)
+    shares = []
+    for c in range(3):
+        lines = rows[c]
+        first, last = lines[0], lines[4]
+        lines[0] = first + jnp.where(ez > 0, rolled(last, 1, 1), 0.0)
+        lines[4] = last + jnp.where(ez < 7, rolled(first, -1, 1), 0.0)
+        for d in range(5):
+            turned = rolled(lines[d], 4, 0)
+            added = jnp.where(up, rolled(turned, 8, 1), jnp.where(down, rolled(turned, -8, 1), 0.0))
+            lines[d] = face_scale_ref[8 * d : 8 * d + 8, :] * (lines[d] + added)
+        shares.append(lines)
+    return shares
 
 
 def strains(grad, rows):
@@ -316,30 +356,59 @@
     ]
 
 
-CHUNKS = [slice(0, 32), slice(32, 64), slice(64, 96), slice(96, 125)]
+CHUNKS = [slice(row, min(row + 8, 125)) for row in range(0, 125, 8)]
 
 
 def pack_face(face, upper):
-    parts = [face[:, c * LANES : (c + 1) * LANES] for c in range(3)]
-    lower_lane = lanes_of((16, LANES)) < 64
-    lower_lanes = lanes_of((32, LANES)) < 64
-    if upper:
-        first = jnp.where(lower_lanes, rolled(parts[0], 64, 1), parts[1])
-        second = jnp.where(lower_lane, rolled(parts[2][0:16], 64, 1), parts[2][16:32])
+    lane = lanes_of((8, LANES))
+    target = lane < 64 if upper else lane >= 64
+    own = lax.broadcasted_iota(jnp.int32, (8, LANES), 0) < 5
+    lines = []
+    for d in range(5):
+        first, second, third = [face[8 * d : 8 * d + 8, c * LANES : (c + 1) * LANES] for c in range(3)]
+        moved = rolled(jnp.where(own, first, rolled(third, 5, 0)), 64, 1)
+        lines.append(jnp.where(target, moved, jnp.where(own, second, rolled(third, 2, 0))))
+    return jnp.concatenate(lines, axis=0)
+
+
+def step_kernel(step, *refs):
+    lame_ref, mu_ref, m_ref, decay_ref, share_table, face_table, base_ref, flat_in = refs[0:8]
+    arrived = refs[8 : 10 if step == 0 else 11]
+    refs = refs[8 + len(arrived) :]
+    older, refs = refs[:step], refs[step:]
+    strain_ref, sigma_ref, even_ref, low_ref, extra_ref = refs[0:5]
+    odd_ref, keep_ref = refs[5:7] if step < STEPS - 1 else (None, None)
+    grad_ref, flat_ref, window_ref, rim_ref = refs[-4:]
+    flat_ref[...] = flat_in[...]
+    upper = lanes_of((40, 3 * LANES)) % LANES >= 64
+    if step == 0:
+        rim_rows(arrived[0], arrived[1], window_ref, extra_ref)
+        rim_ref[...] = jnp.zeros(rim_ref.shape, F32)
+        for c in range(3):
+            for d in range(5):
+                rim_ref[8 * d : 8 * d + 5, c * LANES : (c + 1) * LANES] = extra_ref[pl.ds(8 * d + c, 5, stride=40), :]
+        high, middle, low = [piece.astype(F32) for piece in cut(jnp.where(upper, rim_ref[...], 0.0))]
+        stacked = [high, middle, high, middle, low, high]
+        at_upper = lanes_of((25, LANES)) >= 64
+        for c in range(3):
+            flat_ref[c, 100:125, :] = jnp.where(at_upper, extra_ref[pl.ds(c, 25, stride=8), :], flat_ref[c, 100:125, :])
     else:
-        first = jnp.where(lower_lanes, parts[0], rolled(parts[1], 64, 1))
-        second = jnp.where(lower_lane, parts[2][0:16], rolled(parts[2][16:32], 64, 1))
-    return jnp.concatenate([first, second], axis=0)
-
-
-def step_kernel(step, *refs):
-    flat_ref, lame_ref, mu_ref, m_ref, decay_ref, grad_table, face_table = refs[0:7]
-    older = refs[7 : 7 + step]
-    refs = refs[7 + step :]
-    strain_ref, sigma_ref, even_ref = refs[0:3]
-    odd_ref, keep_ref = refs[3:5] if step < STEPS - 1 else (None, None)
-    grad_ref = refs[-1]
-    grad_ref[...] = gradients(grad_table, beside(flat_ref))
+        shares = face_shares(*arrived)
+        value = jnp.concatenate([jnp.concatenate(lines, axis=0) for lines in shares], axis=1)
+        high, middle, _ = [piece.astype(F32) for piece in cut(value)]
+        stacked = []
+        for at in (~upper, upper):
+            stacked += [jnp.where(at, high, 0.0), jnp.where(at, middle, 0.0), jnp.where(at, high, 0.0)]
+        at_upper = lanes_of((5, LANES)) >= 64
+        for c in range(3):
+            for d in range(5):
+                extra_ref[c, 8 * d : 8 * d + 8, :] = shares[c][d]
+                share = shares[c][d][0:5]
+                first, last = pl.ds(d, 5, stride=5), pl.ds(100 + d, 5, stride=5)
+                flat_ref[c, first, :] = flat_ref[c, first, :] + jnp.where(at_upper, 0.0, share)
+                flat_ref[c, last, :] = flat_ref[c, last, :] + jnp.where(at_upper, share, 0.0)
+    grad_ref[...] = base_ref[...] + dot(share_table[...], jnp.concatenate(stacked, axis=0).astype(BF16))
+    low_ref[...] = flat_ref[...].astype(BF16)
     for block in range(9):
         sigma_ref[(block // 3) * 128 + 120 : (block // 3) * 128 + 128, (block % 3) * LANES : (block % 3) * LANES + LANES] = (
             jnp.zeros((8, LANES), F32)
@@ -379,18 +448,18 @@
         for direction, values in enumerate(((xx, xy, xz), (xy, yy, yz), (xz, yz, zz))):
             for c in range(3):
                 sigma_ref[direction * 128 + rows.start : direction * 128 + rows.stop, c * LANES : (c + 1) * LANES] = values[c]
-    faces = dot_three(face_table, sigma_ref[...])
-    first, last = pack_face(faces[0:32], False), pack_face(faces[32:64], True)
+    faces = dot_three(face_table, jnp.concatenate([sigma_ref[rows, :] for rows in FACE_ROWS], axis=0))
+    first, last = pack_face(faces[0:40], False), pack_face(faces[40:80], True)
     if step < STEPS - 1:
         even_ring = lax.axis_index(("cuts", "sub")) % 2 == 0
         odd_ref[...] = jnp.where(even_ring, first, last)
         even_ref[...] = jnp.where(even_ring, last, first)
     else:
-        even_ref[0:48, :] = last
-        even_ref[48:, :] = jnp.zeros((even_ref.shape[0] - 48, LANES), F32)
-
-
-def rest_kernel(sigma_ref, u_ref, p_ref, scale_ref, force_table, next_ref):
+        even_ref[0:40, :] = last
+        even_ref[40:, :] = jnp.zeros((even_ref.shape[0] - 40, LANES), F32)
+
+
+def next_state(sigma_ref, force_table, u_ref, p_ref, scale_ref, next_ref):
     force = dot_three(force_table, sigma_ref[...])
     blocks = {}
     for c in range(3):
@@ -411,38 +480,44 @@
         next_ref[c, 200:208, :] = jnp.zeros((8, LANES), F32)
 
 
-def add_faces(packed_before, packed_after, partial_ref, scale_ref, u_ref, delta_ref):
-    delta_ref[...] = jnp.zeros(delta_ref.shape, F32)
-    lower = lanes_of((25, LANES)) < 64
-    turned = rolled(packed_before, 64, 1)
-    values = [packed_before[0:32], turned[0:32], jnp.concatenate([packed_before[32:48], turned[32:48]], axis=0)]
-    for c in range(3):
-        delta_ref[c, pl.ds(0, 25, stride=8), :] = jnp.where(lower, values[c][0:25], 0.0)
-    turned = rolled(packed_after, 64, 1)
-    values = [turned[0:32], packed_after[0:32], jnp.concatenate([turned[32:48], packed_after[32:48]], axis=0)]
-    for c in range(3):
-        delta_ref[c, pl.ds(4, 25, stride=8), :] = jnp.where(lower, 0.0, values[c][0:25])
-    blocks = {}
-    for c in range(3):
-        for b in range(5):
-            for d in range(5):
-                blocks[(c, b, d)] = delta_ref[c, block_rows(b, d), :]
-    blocks = assembled(blocks)
-    for c in range(3):
-        for b in range(5):
-            for d in range(5):
-                at = block_rows(b, d)
-                u_ref[c, at, :] = partial_ref[c, at, :] + scale_ref[at, :] * blocks[(c, b, d)]
-        u_ref[c, 200:208, :] = jnp.zeros((8, LANES), F32)
-
-
-def update_kernel(odd_ref, even_ref, partial_ref, scale_ref, u_ref, flat_ref, low_ref, delta_ref):
-    even_ring = lax.axis_index(("cuts", "sub")) % 2 == 0
-    odd, even = odd_ref[...], even_ref[...]
-    before, after = jnp.where(even_ring, odd, even), jnp.where(even_ring, even, odd)
-    add_faces(before, after, partial_ref, scale_ref, u_ref, delta_ref)
-    flatten(u_ref, flat_ref)
-    low_ref[...] = flat_ref[...].astype(BF16)
+def first_rest_kernel(
+    sigma_ref, force_table, u_in, p_in, scale_in, rows_ref, mass_ref, grad_table,
+    u_ref, scale_ref, next_ref, flat_ref, grad_ref, face_scale_ref, p_ref
+):
+    u_ref[...] = u_in[...]
+    p_ref[...] = p_in[...]
+    scale_ref[...] = scale_in[...]
+    upper = lanes_of((25, LANES)) >= 64
+    last = pl.ds(4, 25, stride=8)
+    for c in range(3):
+        u_ref[c, last, :] = jnp.where(upper, rows_ref[pl.ds(c, 25, stride=8), :], u_ref[c, last, :])
+        p_ref[c, last, :] = jnp.where(upper, rows_ref[pl.ds(3 + c, 25, stride=8), :], p_ref[c, last, :])
+    rim = step_square / (rows_ref[pl.ds(6, 25, stride=8), :] * mass_ref[last, :])
+    scale_ref[last, :] = jnp.where(upper, rim, scale_ref[last, :])
+    face_scale_ref[...] = jnp.zeros(face_scale_ref.shape, F32)
+    lower = lanes_of((5, LANES)) < 64
+    for d in range(5):
+        first, last = pl.ds(8 * d, 5, stride=40), pl.ds(8 * d + 4, 5, stride=40)
+        face_scale_ref[8 * d : 8 * d + 5, :] = jnp.where(lower, scale_ref[first, :], scale_ref[last, :])
+    next_state(sigma_ref, force_table, u_ref, p_ref, scale_ref, next_ref)
+    flatten(next_ref, flat_ref)
+    grad_ref[...] = gradients(grad_table, beside(flat_ref))
+
+
+def rest_kernel(sigma_ref, force_table, partial_ref, delta_ref, p_ref, scale_ref, grad_table, next_ref, u_ref, *refs):
+    u_ref[...] = partial_ref[...]
+    upper = lanes_of((5, LANES)) >= 64
+    for c in range(3):
+        for d in range(5):
+            share = delta_ref[c, 8 * d : 8 * d + 5, :]
+            first, last = pl.ds(8 * d, 5, stride=40), pl.ds(8 * d + 4, 5, stride=40)
+            u_ref[c, first, :] = u_ref[c, first, :] + jnp.where(upper, 0.0, share)
+            u_ref[c, last, :] = u_ref[c, last, :] + jnp.where(upper, share, 0.0)
+    next_state(sigma_ref, force_table, u_ref, p_ref, scale_ref, next_ref)
+    if refs:
+        flat_ref, grad_ref = refs
+        flatten(next_ref, flat_ref)
+        grad_ref[...] = gradients(grad_table, beside(flat_ref))
 
 
 def kernel_parts(strain_ref, low_ref, far_ref, lame_ref, mu_ref, grad_table, grad_ref, kernel_ref):
@@ -468,42 +543,47 @@
     return kernel_ref[...].astype(BF16)
 
 
-def parts_kernel(
-    strain_ref, low_ref, far_ref, lame_ref, mu_ref, grad_table, part_ref, grad_ref, kernel_ref
+def placed(part, select_ref, rows):
+    slots = rows // 2
+    group = lanes_of((rows, LANES)) // slots
+    total = lax.dot_general(part, select_ref[...], (((1,), (1,)), ((), ())), preferred_element_type=F32)
+    blocks = []
+    for k in range(select_ref.shape[0] // LANES):
+        value = total[0:rows, k * LANES : (k + 1) * LANES]
+        for j in range(1, 256 // rows):
+            value = jnp.where(group == j, total[j * rows : (j + 1) * rows, k * LANES : (k + 1) * LANES], value)
+        blocks.append(value)
+    return blocks
+
+
+def parts_kernel(strain_ref, low_ref, far_ref, lame_ref, mu_ref, grad_table, part_ref, grad_ref, kernel_ref):
+    part_ref[...] = kernel_parts(strain_ref, low_ref, far_ref, lame_ref, mu_ref, grad_table, grad_ref, kernel_ref)
+
+
+def both_parts_kernel(
+    strain_ref, low_ref, far_ref, lame_ref, mu_ref, grad_table, one_ref, select_ref, both_ref, grad_ref, kernel_ref
 ):
-    part_ref[...] = kernel_parts(
-        strain_ref, low_ref, far_ref, lame_ref, mu_ref, grad_table, grad_ref, kernel_ref
-    )
-
-
-def send_kernel(
-    strain_ref, low_ref, far_ref, lame_ref, mu_ref, grad_table, one_ref, two_ref, select_ref, *refs
-):
+    two = kernel_parts(strain_ref, low_ref, far_ref, lame_ref, mu_ref, grad_table, grad_ref, kernel_ref)
+    rows = both_ref.shape[1]
+    for k, (first, second) in enumerate(zip(placed(one_ref[...], select_ref, rows), placed(two, select_ref, rows))):
+        both_ref[k] = first + second
+
+
+def send_kernel(strain_ref, low_ref, far_ref, lame_ref, mu_ref, grad_table, both_ref, select_ref, *refs):
     out_refs, (grad_ref, kernel_ref) = refs[:-2], refs[-2:]
     three = kernel_parts(strain_ref, low_ref, far_ref, lame_ref, mu_ref, grad_table, grad_ref, kernel_ref)
-    rows = out_refs[0].shape[0]
-    slots = rows // 2
-    group = lanes_of((rows, LANES)) // slots
-    over_lanes = (((1,), (1,)), ((), ()))
-    for k, ref in enumerate(out_refs):
-        chosen = select_ref[k * LANES : (k + 1) * LANES, :]
-        total = 0.0
-        for part in (one_ref[...], two_ref[...], three):
-            total = total + lax.dot_general(part, chosen, over_lanes, preferred_element_type=F32)
-        value = total[0:rows]
-        for j in range(1, 256 // rows):
-            value = jnp.where(group == j, total[j * rows : (j + 1) * rows], value)
-        ref[...] = value
-
-
-def sum_kernel(*refs):
+    for k, (ref, value) in enumerate(zip(out_refs, placed(three, select_ref, out_refs[0].shape[0]))):
+        ref[...] = both_ref[k] + value
+
+
+def sum_kernel(order, *refs):
     in_refs, out_ref = refs[:-1], refs[-1]
     rows = in_refs[0].shape[0]
     slots = rows // 2
     pieces = 256 // rows
     group = lanes_of((rows, LANES)) // slots
     blocks = [[jnp.zeros((rows, LANES), F32)] * 2 for _ in range(pieces)]
-    for k, ref in enumerate(in_refs):
+    for k, ref in zip(order, in_refs):
         source = lax.axis_index("sub") ^ k
         spot = source % pieces
         value = ref[...]
@@ -552,12 +632,12 @@
 
 
 def finish_kernel(before_ref, nodal_ref, density_ref, face_mass_ref, spread_ref, out_ref, rows_ref, face_ref):
-    packed = before_ref[0:48]
-    turned = rolled(packed, 64, 1)
-    values = [packed[0:32], turned[0:32], jnp.concatenate([packed[32:48], turned[32:48]], axis=0)]
+    packed = before_ref[0:40]
+    values = unpack_face(packed, rolled(packed, 64, 1))
     rows_ref[...] = jnp.zeros(rows_ref.shape, F32)
     for c in range(3):
-        rows_ref[pl.ds(c, 25, stride=8), :] = values[c][0:25]
+        for d in range(5):
+            rows_ref[pl.ds(8 * d + c, 5, stride=40), :] = values[c][d][0:5]
     lane = lanes_of((8, LANES))
     tiles = []
     for pair in range(BLOCKS // 2):
@@ -629,83 +709,94 @@
     grad_table = jnp.asarray(side_by_side(GRAD))
     force_table = jnp.asarray(cut_table(FORCE))
     face_table = jnp.asarray(cut_table(FACES))
+    share_table = jnp.asarray(SHARE)
+    rim_table = jnp.asarray(RIM)
     face_mass = jnp.asarray(FACE_MASS)
     mass = jnp.asarray(MASS)
     memory = memory_init[0]
     owner = jnp.transpose(owner_map, (0, 2, 1))
 
     state = shaped(3, ROWS, LANES)
-    flat_shape = shaped(3, 128, LANES)
-    low_shape = shaped(3, 128, LANES, dtype=BF16)
     scale_shape = shaped(ROWS, LANES)
     five = shaped(5, 125, LANES)
     part_shape = shaped(256, LANES, dtype=BF16)
     grad_scratch = pltpu.VMEM((384, 384), F32)
     part_scratch = [grad_scratch, pltpu.VMEM((256, LANES), F32)]
-    face = shaped(48, LANES)
-    window_scratch = [pltpu.VMEM((8, 8, WINDOW), F32), pltpu.VMEM((ROWS, LANES), F32)]
-    u, p, scale, m1, spread = call(
-        prologue_kernel, "prologue", [state, state, scale_shape, five, shaped(WINDOW, WIDE, dtype=BF16)],
+    face = shaped(40, LANES)
+    grad_shape = shaped(384, 384)
+    flat_shape = shaped(3, 128, LANES)
+    u, p, scale, m1, spread, flat, base = call(
+        prologue_kernel, "prologue", [state, state, scale_shape, five, shaped(WINDOW, WIDE, dtype=BF16), flat_shape, grad_shape],
         [pltpu.VMEM((8, 56, WINDOW), F32)],
-        disp_now, disp_prev, density, memory, sls_decay, mass, grad_table, face_table, force_table, lame_lambda, shear_mu,
+        disp_now, disp_prev, density, memory, sls_decay, mass, grad_table, face_table, force_table, rim_table, share_table, lame_lambda, shear_mu,
     )
-    u, p, scale, flat, low = call(
-        rim_kernel, "rim", [state, state, scale_shape, flat_shape, low_shape], window_scratch, rim, u, p, scale, spread, mass
-    )
+    rows = 512 // subs
     memories = [m1]
     kept = []
-    parts = []
     for step in range(STEPS):
-        if step == STEPS - 1:
-            far = far_field(low, groups)
-        outs = [shaped(6, 125, LANES), shaped(384, 384), face if step < STEPS - 1 else shaped(PAD, LANES)]
-        if step < STEPS - 1:
+        last_step = step == STEPS - 1
+        arrived = (rim, spread) if step == 0 else (odd, even, face_scale)
+        outs = [
+            shaped(6, 125, LANES), shaped(384, 384), shaped(PAD, LANES) if last_step else face,
+            shaped(3, 128, LANES, dtype=BF16), scale_shape if step == 0 else shaped(3, 40, LANES),
+        ]
+        if not last_step:
             outs += [face, five]
         results = call(
-            lambda *refs, step=step: step_kernel(step, *refs), "step", outs, [grad_scratch],
-            flat, lame_lambda, shear_mu, memories[step], sls_decay, grad_table, face_table, *kept,
+            lambda *refs, step=step: step_kernel(step, *refs), "step", outs,
+            [grad_scratch, pltpu.VMEM((3, 128, LANES), F32), pltpu.VMEM((8, 8, WINDOW), F32), pltpu.VMEM((40, 384), F32)],
+            lame_lambda, shear_mu, memories[step], sls_decay, rim_table if step == 0 else share_table, face_table, base, flat, *arrived, *kept,
         )
-        strain, sigma, even = results[0:3]
-        if step < STEPS - 1:
-            odd = results[3]
-            kept.append(results[4])
-            odd = swapped(odd, ring, 1)
+        strain, sigma, even, low, extra = results[0:5]
+        if last_step:
+            before = passed_along(even, ring, 1)
+        else:
+            kept.append(results[6])
+            odd = swapped(results[5], ring, 1)
             even = swapped(even, ring, 0)
-        else:
-            before = passed_along(even, ring, 1)
-        partial = call(rest_kernel, "rest", state, [], sigma, u, p, scale, force_table)
-        if step < STEPS - 1:
-            low, sigma = lax.optimization_barrier((low, sigma))
-            far = far_field(low, groups)
-        shared = (strain, low, far, lame_lambda, shear_mu, grad_table)
-        if step < STEPS - 1:
-            parts.append(call(parts_kernel, "parts", part_shape, part_scratch, *shared))
-            if step == 0:
-                m2, m3, select = call(
-                    later_kernel, "later", [five, five, shaped(subs * LANES, LANES, dtype=BF16)], [],
-                    memory, sls_decay, owner,
-                )
-                memories += [m2, m3]
-                partial, parts[0], select, memories[2] = lax.optimization_barrier((partial, parts[0], select, m3))
-            else:
-                partial, parts[1] = lax.optimization_barrier((partial, parts[1]))
-            p = u
-            u, flat, low = call(
-                update_kernel, "update", [state, flat_shape, low_shape], [pltpu.VMEM((3, ROWS, LANES), F32)],
-                odd, even, partial, scale,
+        far = far_field(low, groups)
+        if step == 0:
+            p, scale, partial, flat, base, face_scale = call(
+                first_rest_kernel, "rest", [state, scale_shape, state, flat_shape, grad_shape, shaped(40, LANES)],
+                [pltpu.VMEM((3, ROWS, LANES), F32)], sigma, force_table, u, p, scale, extra, mass, grad_table,
             )
         else:
-            sent = list(call(
-                send_kernel, "send", [shaped(512 // subs, LANES)] * subs, part_scratch, *shared, *parts, select)
+            results = call(
+                rest_kernel, "rest", [state] if last_step else [state, state, flat_shape, grad_shape],
+                [pltpu.VMEM((3, ROWS, LANES), F32)] if last_step else [], sigma, force_table, partial, extra, p, scale, grad_table,
             )
-            for k in [at ^ (at >> 1) for at in range(subs - 1, 0, -1)]:
+            if last_step:
+                partial = results[0]
+            else:
+                partial, p, flat, base = results
+        shared = (strain, low, far, lame_lambda, shear_mu, grad_table)
+        if step == 0:
+            one = call(parts_kernel, "parts", part_shape, part_scratch, *shared)
+            m2, m3, select = call(
+                later_kernel, "later", [five, five, shaped(subs * LANES, LANES, dtype=BF16)], [], memory, sls_decay, owner
+            )
+            memories += [m2, m3]
+            base, one, select, memories[2] = lax.optimization_barrier((base, one, select, m3))
+        elif not last_step:
+            both = call(
+                both_parts_kernel, "parts", shaped(subs, rows, LANES), part_scratch, *shared, one, select
+            )
+            base, both = lax.optimization_barrier((base, both))
+        else:
+            sent = list(
+                call(send_kernel, "send", [shaped(rows, LANES)] * subs, part_scratch, *shared, both, select)
+            )
+            order = [at ^ (at >> 1) for at in range(subs - 1, -1, -1)]
+            for k in order[:-1]:
                 sent[k] = lax.ppermute(sent[k], "sub", [(j, j ^ k) for j in range(subs)])
     nodal = call(nodal_kernel, "nodal", shaped(24, FACE), [], partial, spread)
     final = call(
         finish_kernel, "finish", shaped(1, 3, 8, FACE), [pltpu.VMEM((ROWS, LANES), F32), pltpu.VMEM((8, FACE), F32)],
         before, nodal, density, face_mass, spread,
     )
-    kernels = call(sum_kernel, "sum", shaped(250, 1, 256), [], *sent)
+    kernels = call(
+        lambda *refs: sum_kernel(order, *refs), "sum", shaped(250, 1, 256), [], *[sent[k] for k in order]
+    )
     return final, jnp.transpose(kernels, (1, 2, 0))
 
 

time: 42.8 us -> 42.8 us (level)
  starting transfers between devices: 20.2 us -> 17.7 us
  Pallas kernels: 13.5 us -> 15 us
  waiting for transfers between devices: 5.97 us -> 6.94 us
    pallas_call x18 -> x15, Pallas kernels: 13.5 us -> 15 us  [call(): pl.pallas_call(kernel, name=name, out_shape=outs, in_specs=[HBM if at in...]
    ppermute x5, waiting for transfers between devices: 1.61 us -> 2.96 us  [passed_along(): lax.ppermute(value, axis, [(source, (source + steps) % count) for source...]
    ppermute x4, starting transfers between devices: 8.2 us -> 6.93 us  [swapped(): return lax.ppermute(value, axis, pairs)]
    ppermute x4, waiting for transfers between devices: 4.35 us -> 3.43 us  [swapped(): return lax.ppermute(value, axis, pairs)]
    ppermute x3, starting transfers between devices: 4.45 us -> 3.55 us  [per_device(): sent[k] = lax.ppermute(sent[k], 'sub', [(j, j ^ k) for j in range(subs)])]
    ppermute x3, waiting for transfers between devices: 0.01 us -> 0.56 us  [per_device(): sent[k] = lax.ppermute(sent[k], 'sub', [(j, j ^ k) for j in range(subs)])]
    unnamed x25 -> x29, local copies, waits for them, and re-layouts: 2.04 us -> 2.04 us
  transfers between devices with their start and end apart: 12 -> 12, of which waited for: 5 -> 5; matrix products, arithmetic and copies ran while one was open for 3% -> 3% of each run, Pallas kernels for 19% -> 22%
where the time goes in v4:
time: 42.8 us; the launch traced here: 42.6 us
  starting transfers between devices  17.7 us (41%)
  Pallas kernels  15 us (35%)
  waiting for transfers between devices  6.94 us (16%)
  local copies, waits for them, and re-layouts  2.04 us (5%)
  between operations  0.96 us (2%)
    pallas_call x15, Pallas kernels, call(): pl.pallas_call(kernel, name=name, out_shape=outs, in_specs=[HBM if at in...  15 us
    ppermute x5, starting transfers between devices, passed_along(): lax.ppermute(value, axis, [(source, (source + steps) % count) for source...  7.21 us
    ppermute x4, starting transfers between devices, swapped(): return lax.ppermute(value, axis, pairs)  6.93 us
    ppermute x3, starting transfers between devices, per_device(): sent[k] = lax.ppermute(sent[k], 'sub', [(j, j ^ k) for j in range(subs)])  3.55 us
    ppermute x4, waiting for transfers between devices, swapped(): return lax.ppermute(value, axis, pairs)  3.43 us
    ppermute x5, waiting for transfers between devices, passed_along(): lax.ppermute(value, axis, [(source, (source + steps) % count) for source...  2.96 us
    unnamed x29, local copies, waits for them, and re-layouts  2.04 us
  transfers between devices with their start and end apart: 12, of which 5 were waited for; matrix products, arithmetic and copies ran while one was open for 3% of the time, Pallas kernels for 22%

profile of v4, /device:TPU:0, one launch (start us, length us, event | category | flops | bytes accessed | tf_op | source)
XLA Modules:
  0.0 42.6 jit_solution(11974847470071617635)
XLA Ops:
  0.7 1.0 %gather.1 = f32[8,1089]{1,0:T(8,128)S(1)} custom-call(f32[1,3,8,1089]{3,2,1,0:T(8,128)} %now_ref.3, f32[1,3,8,1089]{3,2,1,0:T(8,128)} %prev_ref.3, f32[8,1089]{1,0:T(8,128)} %density_ref.5), custom_call_target="tpu_custom_call" | custom-call | bytes 3000000 | tf_op jit(solution)/shard_map/gather/pallas_call | solution.py:663
  1.8 7.0 %collective-permute-start = (f32[8,1089]{1,0:T(8,128)S(1)}, f32[8,1089]{1,0:T(8,128)S(1)}, u32[]{:S(2)}, u32[]{:S(2)}) collective-permute-start(f32[8,1089]{1,0:T(8,128)S(1)} %gather.1), channel_id=1, source_target_pairs={{0,15},{1,0},{2,1},{3,2},{4,3},{5,4},{6,5},{7,6},{8,7},{9,8},{10,9... | collective-permute-start | bytes 104552 | tf_op jit(solution)/shard_map/ppermute | solution.py:677
  8.8 1.3 %copy.20 = f32[1,3,5,125,128]{4,3,0,2,1:T(8,128)S(1)} copy(f32[1,3,5,125,128]{4,0,3,2,1:T(1,128)} %param.17) | data formatting | bytes 1920000
  10.2 2.7 %prologue.1 = (f32[3,208,128]{2,1,0:T(8,128)S(1)}, f32[3,208,128]{2,1,0:T(8,128)S(1)}, f32[208,128]{1,0:T(8,128)S(1)}, f32[5,125,128]{2,1,0:T(8,128)S(1)}, bf16[...) custom-call(f32[1,3,8,1089]{3,2,1,0:T(8,128)S(1)} %copy-done.7, ...), custom_call_target="tpu_custom_call" | custom-call | bytes 3000000 | tf_op jit(solution)/shard_map/prologue/pallas_call | solution.py:663
  12.9 1.2 %step.3 = (f32[6,125,128]{2,1,0:T(8,128)S(1)}, f32[384,384]{1,0:T(8,128)S(1)}, f32[40,128]{1,0:T(8,128)S(1)}, bf16[3,128,128]{2,1,0:T(8,128)(2,1)S(1)}, f32[208,...) custom-call(f32[125,128]{1,0:T(8,128)S(1)} %copy-done.2, f32[125,128]{1,0:T(8,128)S(1)} %copy-done.3, ...), custom_call_target="tpu_custom_call" | custom-call | bytes 3000000 | tf_op jit(solution)/shard_map/step/pallas_call | solution.py:663
  14.2 3.5 %collective-permute-start.2 = (f32[40,128]{1,0:T(8,128)S(1)}, f32[40,128]{1,0:T(8,128)S(1)}, u32[]{:S(2)}, u32[]{:S(2)}) collective-permute-start(f32[40,128]{1,0:T(8,128)S(1)} %get-tuple-element.69), channel_id=1, source_target_pairs={{1,2},{2,1},{3,4},{4,3},{5,6},{6,5},{7,8},{8,7},{9,10},{10,9},{11,... | collective-permute-start | bytes 61448 | tf_op jit(solution)/shard_map/ppermute | solution.py:686
  17.7 0.7 %copy-done.13 = s32[2,64,1]{1,2,0:T(1,128)S(1)} copy-done((s32[2,64,1]{1,2,0:T(1,128)S(1)}, s32[2,64,1]{1,2,0:T(1,128)}, u32[]{:S(2)}) %copy-start.13) | copy-done | bytes 536
  18.7 1.2 %rest.3 = (f32[3,208,128]{2,1,0:T(8,128)S(1)}, f32[208,128]{1,0:T(8,128)S(1)}, f32[3,208,128]{2,1,0:T(8,128)S(1)}, f32[3,128,128]{2,1,0:T(8,128)S(1)}, f32[384,384]{1,0:T(8,128)S(1)}, /*index=5*/f32[40,128]{1,0:T(8,128)S(1)}) custom-call(f32[384,384]{1,0:T(8,128)S(1)} %get-tuple-element.55.sigma_ref, bf16[3,208,384]{2,1,0:T(8,128)(2,1)S(1)} %copy-done.1, ...), custom_call_target="tpu_custom_call" | custom-call | bytes 3000000 | tf_op jit(solution)/shard_map/rest/pallas_call | solution.py:663
  20.4 1.3 %collective-permute-done.2.refs_8_ = f32[40,128]{1,0:T(8,128)S(1)} collective-permute-done((f32[40,128]{1,0:T(8,128)S(1)}, f32[40,128]{1,0:T(8,128)S(1)}, u32[]{:S(2)}, u32[]{:S(2)}) %collective-permute-start.2) | collective-permute-done | bytes 20512 | tf_op jit(solution)/shard_map/ppermute | solution.py:686
  21.7 0.9 %step.4 = (f32[6,125,128]{2,1,0:T(8,128)S(1)}, f32[384,384]{1,0:T(8,128)S(1)}, f32[40,128]{1,0:T(8,128)S(1)}, bf16[3,128,128]{2,1,0:T(8,128)(2,1)S(1)}, f32[3,40...) custom-call(f32[125,128]{1,0:T(8,128)S(1)} %copy-done.2, f32[125,128]{1,0:T(8,128)S(1)} %copy-done.3, ...), custom_call_target="tpu_custom_call" | custom-call | bytes 3000000 | tf_op jit(solution)/shard_map/step/pallas_call | solution.py:663
  22.6 3.5 %collective-permute-start.5 = (f32[40,128]{1,0:T(8,128)S(1)}, f32[40,128]{1,0:T(8,128)S(1)}, u32[]{:S(2)}, u32[]{:S(2)}) collective-permute-start(f32[40,128]{1,0:T(8,128)S(1)} %get-tuple-element.85), channel_id=1, source_target_pairs={{1,2},{2,1},{3,4},{4,3},{5,6},{6,5},{7,8},{8,7},{9,10},{10,9},{11,... | collective-permute-start | bytes 61448 | tf_op jit(solution)/shard_map/ppermute | solution.py:686
  26.1 1.2 %rest.4 = (f32[3,208,128]{2,1,0:T(8,128)S(1)}, f32[3,208,128]{2,1,0:T(8,128)S(1)}, f32[3,128,128]{2,1,0:T(8,128)S(1)}, f32[384,384]{1,0:T(8,128)S(1)}) custom-call(f32[384,384]{1,0:T(8,128)S(1)} %get-tuple-element.73.sigma_ref, bf16[3,208,384]{2,1,0:T(8,128)(2,1)S(1)} %copy-done.1, f32[3,208,128]{2,1,0:T(8,128)S(1)} %get-tuple-element.74.partial_ref, ...), custom_call_target="tpu_custom_call" | custom-call | bytes 3000000 | tf_op jit(solution)/shard_map/rest/pallas_call | solution.py:663
  27.3 0.6 %parts.3.both_ref = f32[4,128,128]{2,1,0:T(8,128)S(1)} custom-call(f32[6,125,128]{2,1,0:T(8,128)S(1)} %get-tuple-element.79.strain_ref, bf16[3,128,128]{2,1,0:T(8,128)(2,1)S(1)} %get-tuple-element.80.low_ref, bf16[3,128,128]{2,1,0:T(8,128)(2,1)S(1)} %collective-permute-done.4.far_ref, f32[125,128]{1,0:T(8,128)S(1)} %copy-done.2, f32[125,128]{1,0:T(8,128)S(1)} %copy-done.3, ...), custom_call_target="tpu_custom_call" | custom-call | bytes 3000000 | tf_op jit(solution)/shard_map/parts/pallas_call | solution.py:663
  27.9 2.1 %collective-permute-done.5.refs_8_ = f32[40,128]{1,0:T(8,128)S(1)} collective-permute-done((f32[40,128]{1,0:T(8,128)S(1)}, f32[40,128]{1,0:T(8,128)S(1)}, u32[]{:S(2)}, u32[]{:S(2)}) %collective-permute-start.5) | collective-permute-done | bytes 20512 | tf_op jit(solution)/shard_map/ppermute | solution.py:686
  30.1 0.9 %step.5 = (f32[6,125,128]{2,1,0:T(8,128)S(1)}, f32[384,384]{1,0:T(8,128)S(1)}, f32[136,128]{1,0:T(8,128)S(1)}, bf16[3,128,128]{2,1,0:T(8,128)(2,1)S(1)}, f32[3,40,128]{2,1,0:T(8,128)S(1)}) custom-call(f32[125,128]{1,0:T(8,128)S(1)} %copy-done.2, f32[125,128]{1,0:T(8,128)S(1)} %copy-done.3, f32[5,125,128]{2,1,0:T(8,128)S(1)} %get-tuple-element.65.refs_2_, ...), custom_call_target="tpu_custom_call" | custom-call | bytes 3000000 | tf_op jit(solution)/shard_map/step/pallas_call | solution.py:663
  31.1 1.2 %collective-permute-done.8.far_ref = bf16[3,128,128]{2,1,0:T(8,128)(2,1)S(1)} collective-permute-done((bf16[3,128,128]{2,1,0:T(8,128)(2,1)S(1)}, bf16[3,128,128]{2,1,0:T(8,128)(2,1)S(1)}, u32[]{:S(2)}, u32[]{:S(2)}) %collective-permute-start.8) | collective-permute-done | bytes 98336 | tf_op jit(solution)/shard_map/ppermute | solution.py:677
  32.3 0.6 %send.1 = (f32[128,128]{1,0:T(8,128)S(1)}, f32[128,128]{1,0:T(8,128)S(1)}, f32[128,128]{1,0:T(8,128)S(1)}, f32[128,128]{1,0:T(8,128)S(1)}) custom-call(f32[6,125,128]{2,1,0:T(8,128)S(1)} %get-tuple-element.93.strain_ref, bf16[3,128,128]{2,1,0:T(8,128)(2,1)S(1)} %get-tuple-element.94.low_ref, bf16[3,128,128]{2,1,0:T(8,128)(2,1)S(1)} %collective-permute-done.8.far_ref, ...), custom_call_target="tpu_custom_call" | custom-call | bytes 3000000 | tf_op jit(solution)/shard_map/send/pallas_call | solution.py:663
  33.0 2.4 %collective-permute-start.10 = (f32[128,128]{1,0:T(8,128)S(1)}, f32[128,128]{1,0:T(8,128)S(1)}, u32[]{:S(2)}, u32[]{:S(2)}) collective-permute-start(f32[128,128]{1,0:T(8,128)S(1)} %get-tuple-element.97), channel_id=1, source_target_pairs={{0,3},{1,2},{2,1},{3,0},{4,7},{5,6},{6,5},{7,4},{8,11},{9,10},{10,... | collective-permute-start | bytes 196616 | tf_op jit(solution)/shard_map/ppermute | solution.py:791
  35.3 1.1 %collective-permute-start.11 = (f32[128,128]{1,0:T(8,128)S(1)}, f32[128,128]{1,0:T(8,128)S(1)}, u32[]{:S(2)}, u32[]{:S(2)}) collective-permute-start(f32[128,128]{1,0:T(8,128)S(1)} %get-tuple-element.98), channel_id=1, source_target_pairs={{0,1},{1,0},{2,3},{3,2},{4,5},{5,4},{6,7},{7,6},{8,9},{9,8},{10,11... | collective-permute-start | bytes 196616 | tf_op jit(solution)/shard_map/ppermute | solution.py:791
  36.5 0.7 %rest.5.partial_ref = f32[3,208,128]{2,1,0:T(8,128)S(1)} custom-call(f32[384,384]{1,0:T(8,128)S(1)} %get-tuple-element.89.sigma_ref, bf16[3,208,384]{2,1,0:T(8,128)(2,1)S(1)} %copy-done.1, f32[3,208,128]{2,1,0:T(8,128)S(1)} %get-tuple-element.90.partial_ref, f32[3,40,128]{2,1,0:T(8,128)S(1)} %get-tuple-element.91.delta_ref, ...), custom_call_target="tpu_custom_call" | custom-call | bytes 3000000 | tf_op jit(solution)/shard_map/rest/pallas_call | solution.py:663
  37.2 0.8 %nodal.1.nodal_ref = f32[24,1089]{1,0:T(8,128)S(1)} custom-call(f32[3,208,128]{2,1,0:T(8,128)S(1)} %rest.5.partial_ref, bf16[256,1664]{1,0:T(8,128)(2,1)S(1)} %get-tuple-element.54.refs_9_.spread_ref), custom_call_target="tpu_custom_call" | custom-call | bytes 3000000 | tf_op jit(solution)/shard_map/nodal/pallas_call | solution.py:663
  38.0 1.7 %collective-permute-done.7.before_ref = f32[136,128]{1,0:T(8,128)S(1)} collective-permute-done((f32[136,128]{1,0:T(8,128)S(1)}, f32[136,128]{1,0:T(8,128)S(1)}, u32[]{:S(2)}, u32[]{:S(2)}) %collective-permute-start.7) | collective-permute-done | bytes 69664 | tf_op jit(solution)/shard_map/ppermute | solution.py:677
  39.8 1.3 %finish.1 = f32[1,3,8,1089]{3,2,1,0:T(8,128)} custom-call(f32[136,128]{1,0:T(8,128)S(1)} %collective-permute-done.7.before_ref, f32[24,1089]{1,0:T(8,128)S(1)} %nodal.1.nodal_ref, f32[8,1089]{1,0:T(8,128)S(1)} %copy-done.10, f32[1,1089]{1,0:T(1,128)S(1)} %copy-done.12, bf16[256,1664]{1,0:T(8,128)(2,1)S(1)} %get-tuple-element.54.refs_9_.spread_ref), custom_call_target="tpu_custom_call" | custom-call | bytes 3000000 | tf_op jit(solution)/shard_map/finish/pallas_call | solution.py:663
  41.6 1.0 %sum.1 = f32[250,1,256]{2,1,0:T(1,128)} custom-call(f32[128,128]{1,0:T(8,128)S(1)} %collective-permute-done.9.refs_0_, f32[128,128]{1,0:T(8,128)S(1)} %collective-permute-done.10.refs_1_, f32[128,128]{1,0:T(8,128)S(1)} %collective-permute-done.11.refs_2_, f32[128,128]{1,0:T(8,128)S(1)} %get-tuple-element.99.refs_3_), custom_call_target="tpu_custom_call" | custom-call | bytes 3000000 | tf_op jit(solution)/shard_map/sum/pallas_call | solution.py:663
  (44 shorter events, 1.7 us)
Async XLA Ops:
  0.6 9.5 %copy-start.9 = (f32[208,128]{1,0:T(8,128)S(1)}, f32[208,128]{1,0:T(8,128)}, u32[]{:S(2)}) copy-start(f32[208,128]{1,0:T(8,128)} %constant.20.clone.mass_ref) | copy-start | bytes 319492
  0.6 9.5 %copy-start.10 = (f32[8,1089]{1,0:T(8,128)S(1)}, f32[8,1089]{1,0:T(8,128)}, u32[]{:S(2)}) copy-start(f32[8,1089]{1,0:T(8,128)} %density_ref.5) | copy-start | bytes 104548
  1.7 8.4 %copy-start = (bf16[3,384,256]{2,1,0:T(8,128)(2,1)S(1)}, bf16[3,384,256]{2,1,0:T(8,128)(2,1)}, u32[]{:S(2)}) copy-start(bf16[3,384,256]{2,1,0:T(8,128)(2,1)} %constant.14.clone.refs_0_.grad_table) | copy-start | bytes 1769476
  1.7 8.4 %copy-start.1 = (bf16[3,208,384]{2,1,0:T(8,128)(2,1)S(1)}, bf16[3,208,384]{2,1,0:T(8,128)(2,1)}, u32[]{:S(2)}) copy-start(bf16[3,208,384]{2,1,0:T(8,128)(2,1)} %constant.15.clone.refs_2_.force_table) | copy-start | bytes 1437700
  1.7 8.4 %copy-start.2 = (f32[125,128]{1,0:T(8,128)S(1)}, f32[125,128]{1,0:T(8,128)}, u32[]{:S(2)}) copy-start(f32[125,128]{1,0:T(8,128)} %lame_ref.5) | copy-start | bytes 192004
  1.7 8.4 %copy-start.3 = (f32[125,128]{1,0:T(8,128)S(1)}, f32[125,128]{1,0:T(8,128)}, u32[]{:S(2)}) copy-start(f32[125,128]{1,0:T(8,128)} %mu_ref.5) | copy-start | bytes 192004
  1.7 8.4 %copy-start.4 = (bf16[3,80,256]{2,1,0:T(8,128)(2,1)S(1)}, bf16[3,80,256]{2,1,0:T(8,128)(2,1)}, u32[]{:S(2)}) copy-start(bf16[3,80,256]{2,1,0:T(8,128)(2,1)} %constant.16.clone.refs_1_.refs_5_) | copy-start | bytes 368644
  1.7 8.4 %copy-start.5 = (bf16[384,240]{1,0:T(8,128)(2,1)S(1)}, bf16[384,240]{1,0:T(8,128)(2,1)}, u32[]{:S(2)}) copy-start(bf16[384,240]{1,0:T(8,128)(2,1)} %constant.17.clone.refs_4_) | copy-start | bytes 552964
  1.8 8.4 %copy-start.6 = (bf16[384,240]{1,0:T(8,128)(2,1)S(1)}, bf16[384,240]{1,0:T(8,128)(2,1)}, u32[]{:S(2)}) copy-start(bf16[384,240]{1,0:T(8,128)(2,1)} %constant.18.clone.refs_3_.refs_4_) | copy-start | bytes 552964
  1.8 8.4 %copy-start.7 = (f32[1,3,8,1089]{3,2,1,0:T(8,128)S(1)}, f32[1,3,8,1089]{3,2,1,0:T(8,128)}, u32[]{:S(2)}) copy-start(f32[1,3,8,1089]{3,2,1,0:T(8,128)} %now_ref.3) | copy-start | bytes 313636
  1.8 8.4 %copy-start.8 = (f32[1,3,8,1089]{3,2,1,0:T(8,128)S(1)}, f32[1,3,8,1089]{3,2,1,0:T(8,128)}, u32[]{:S(2)}) copy-start(f32[1,3,8,1089]{3,2,1,0:T(8,128)} %prev_ref.3) | copy-start | bytes 313636
  1.8 11.1 %collective-permute-start = (f32[8,1089]{1,0:T(8,128)S(1)}, f32[8,1089]{1,0:T(8,128)S(1)}, u32[]{:S(2)}, u32[]{:S(2)}) collective-permute-start(f32[8,1089]{1,0:T(8,128)S(1)} %gather.1), channel_id=1, source_target_pairs={{0,15},{1,0},{2,1},{3,2},{4,3},{5,4},{6,5},{7,6},{8,7},{9,8},{10,9... | collective-permute-start | bytes 104552 | tf_op jit(solution)/shard_map/ppermute | solution.py:677
  14.1 5.8 %collective-permute-start.1 = (bf16[3,128,128]{2,1,0:T(8,128)(2,1)S(1)}, bf16[3,128,128]{2,1,0:T(8,128)(2,1)S(1)}, u32[]{:S(2)}, u32[]{:S(2)}) collective-permute-start(bf16[3,128,128]{2,1,0:T(8,128)(2,1)S(1)} %get-tuple-element.62.low_ref), channel_id=1, source_target_pairs={{0,16},{16,0},{1,17},{17,1},{2,18},{18,2},{3,19},{19,3},{4,20},{20... | collective-permute-start | bytes 294920 | tf_op jit(solution)/shard_map/ppermute | solution.py:677
  14.2 7.4 %collective-permute-start.2 = (f32[40,128]{1,0:T(8,128)S(1)}, f32[40,128]{1,0:T(8,128)S(1)}, u32[]{:S(2)}, u32[]{:S(2)}) collective-permute-start(f32[40,128]{1,0:T(8,128)S(1)} %get-tuple-element.69), channel_id=1, source_target_pairs={{1,2},{2,1},{3,4},{4,3},{5,6},{6,5},{7,8},{8,7},{9,10},{10,9},{11,... | collective-permute-start | bytes 61448 | tf_op jit(solution)/shard_map/ppermute | solution.py:686
  17.7 4.0 %collective-permute-start.3 = (f32[40,128]{1,0:T(8,128)S(1)}, f32[40,128]{1,0:T(8,128)S(1)}, u32[]{:S(2)}, u32[]{:S(2)}) collective-permute-start(f32[40,128]{1,0:T(8,128)S(1)} %get-tuple-element.70), channel_id=1, source_target_pairs={{0,1},{1,0},{2,3},{3,2},{4,5},{5,4},{6,7},{7,6},{8,9},{9,8},{10,11... | collective-permute-start | bytes 61448 | tf_op jit(solution)/shard_map/ppermute | solution.py:686
  22.6 4.8 %collective-permute-start.4 = (bf16[3,128,128]{2,1,0:T(8,128)(2,1)S(1)}, bf16[3,128,128]{2,1,0:T(8,128)(2,1)S(1)}, u32[]{:S(2)}, u32[]{:S(2)}) collective-permute-start(bf16[3,128,128]{2,1,0:T(8,128)(2,1)S(1)} %get-tuple-element.80.low_ref), channel_id=1, source_target_pairs={{0,16},{16,0},{1,17},{17,1},{2,18},{18,2},{3,19},{19,3},{4,20},{20... | collective-permute-start | bytes 294920 | tf_op jit(solution)/shard_map/ppermute | solution.py:677
  22.6 7.4 %collective-permute-start.5 = (f32[40,128]{1,0:T(8,128)S(1)}, f32[40,128]{1,0:T(8,128)S(1)}, u32[]{:S(2)}, u32[]{:S(2)}) collective-permute-start(f32[40,128]{1,0:T(8,128)S(1)} %get-tuple-element.85), channel_id=1, source_target_pairs={{1,2},{2,1},{3,4},{4,3},{5,6},{6,5},{7,8},{8,7},{9,10},{10,9},{11,... | collective-permute-start | bytes 61448 | tf_op jit(solution)/shard_map/ppermute | solution.py:686
  26.1 4.0 %collective-permute-start.6 = (f32[40,128]{1,0:T(8,128)S(1)}, f32[40,128]{1,0:T(8,128)S(1)}, u32[]{:S(2)}, u32[]{:S(2)}) collective-permute-start(f32[40,128]{1,0:T(8,128)S(1)} %get-tuple-element.86), channel_id=1, source_target_pairs={{0,1},{1,0},{2,3},{3,2},{4,5},{5,4},{6,7},{7,6},{8,9},{9,8},{10,11... | collective-permute-start | bytes 61448 | tf_op jit(solution)/shard_map/ppermute | solution.py:686
  31.0 1.3 %collective-permute-start.8 = (bf16[3,128,128]{2,1,0:T(8,128)(2,1)S(1)}, bf16[3,128,128]{2,1,0:T(8,128)(2,1)S(1)}, u32[]{:S(2)}, u32[]{:S(2)}) collective-permute-start(bf16[3,128,128]{2,1,0:T(8,128)(2,1)S(1)} %get-tuple-element.94.low_ref), channel_id=1, source_target_pairs={{0,16},{16,0},{1,17},{17,1},{2,18},{18,2},{3,19},{19,3},{4,20},{20... | collective-permute-start | bytes 294920 | tf_op jit(solution)/shard_map/ppermute | solution.py:677
  31.0 8.7 %collective-permute-start.7 = (f32[136,128]{1,0:T(8,128)S(1)}, f32[136,128]{1,0:T(8,128)S(1)}, u32[]{:S(2)}, u32[]{:S(2)}) collective-permute-start(f32[136,128]{1,0:T(8,128)S(1)} %get-tuple-element.88), channel_id=1, source_target_pairs={{0,1},{1,2},{2,3},{3,4},{4,5},{5,6},{6,7},{7,8},{8,9},{9,10},{10,1... | collective-permute-start | bytes 208904 | tf_op jit(solution)/shard_map/ppermute | solution.py:677
  32.9 8.2 %collective-permute-start.9 = (f32[128,128]{1,0:T(8,128)S(1)}, f32[128,128]{1,0:T(8,128)S(1)}, u32[]{:S(2)}, u32[]{:S(2)}) collective-permute-start(f32[128,128]{1,0:T(8,128)S(1)} %get-tuple-element.96), channel_id=1, source_target_pairs={{0,2},{1,3},{2,0},{3,1},{4,6},{5,7},{6,4},{7,5},{8,10},{9,11},{10,... | collective-permute-start | bytes 196616 | tf_op jit(solution)/shard_map/ppermute | solution.py:791
  33.0 8.1 %collective-permute-start.10 = (f32[128,128]{1,0:T(8,128)S(1)}, f32[128,128]{1,0:T(8,128)S(1)}, u32[]{:S(2)}, u32[]{:S(2)}) collective-permute-start(f32[128,128]{1,0:T(8,128)S(1)} %get-tuple-element.97), channel_id=1, source_target_pairs={{0,3},{1,2},{2,1},{3,0},{4,7},{5,6},{6,5},{7,4},{8,11},{9,10},{10,... | collective-permute-start | bytes 196616 | tf_op jit(solution)/shard_map/ppermute | solution.py:791
  35.3 6.3 %collective-permute-start.11 = (f32[128,128]{1,0:T(8,128)S(1)}, f32[128,128]{1,0:T(8,128)S(1)}, u32[]{:S(2)}, u32[]{:S(2)}) collective-permute-start(f32[128,128]{1,0:T(8,128)S(1)} %get-tuple-element.98), channel_id=1, source_target_pairs={{0,1},{1,0},{2,3},{3,2},{4,5},{5,4},{6,7},{7,6},{8,9},{9,8},{10,11... | collective-permute-start | bytes 196616 | tf_op jit(solution)/shard_map/ppermute | solution.py:791
  37.2 2.6 %copy-start.12 = (f32[1,1089]{1,0:T(1,128)S(1)}, f32[1,1089]{1,0:T(1,128)}, u32[]{:S(2)}) copy-start(f32[1,1089]{1,0:T(1,128)} %constant.19.clone.face_mass_ref) | copy-start | bytes 13072
  (2 other events, 2.1 us)

commit v5 on v4

--- a/solution.py
+++ b/solution.py
@@ -9,7 +9,6 @@
 from jax.sharding import PartitionSpec as P
 
 STEPS = 3
-PAD = 136
 EY = 8
 EZ = 8
 LANES = 128
@@ -371,18 +370,37 @@
     return jnp.concatenate(lines, axis=0)
 
 
+def add_shares(shares, flat_ref):
+    upper = lanes_of((5, LANES)) >= 64
+    for c in range(3):
+        for d in range(5):
+            first, last = pl.ds(d, 5, stride=5), pl.ds(100 + d, 5, stride=5)
+            flat_ref[c, first, :] = flat_ref[c, first, :] + jnp.where(upper, 0.0, shares[c][d][0:5])
+            flat_ref[c, last, :] = flat_ref[c, last, :] + jnp.where(upper, shares[c][d][0:5], 0.0)
+
+
+def shares_kernel(odd_ref, even_ref, face_scale_ref, flat_in, delta_ref, low_ref, flat_ref):
+    shares = face_shares(odd_ref, even_ref, face_scale_ref)
+    for c in range(3):
+        delta_ref[c] = jnp.concatenate(shares[c], axis=0)
+    flat_ref[...] = flat_in[...]
+    add_shares(shares, flat_ref)
+    low_ref[...] = flat_ref[...].astype(BF16)
+
+
 def step_kernel(step, *refs):
-    lame_ref, mu_ref, m_ref, decay_ref, share_table, face_table, base_ref, flat_in = refs[0:8]
-    arrived = refs[8 : 10 if step == 0 else 11]
-    refs = refs[8 + len(arrived) :]
+    lame_ref, mu_ref, m_ref, decay_ref, share_table, face_table, base_ref = refs[0:7]
+    arrived = refs[7 : 7 + (3, 4, 1)[step]]
+    refs = refs[7 + len(arrived) :]
     older, refs = refs[:step], refs[step:]
-    strain_ref, sigma_ref, even_ref, low_ref, extra_ref = refs[0:5]
-    odd_ref, keep_ref = refs[5:7] if step < STEPS - 1 else (None, None)
+    strain_ref, sigma_ref, even_ref = refs[0:3]
+    if step < STEPS - 1:
+        odd_ref, keep_ref, low_ref, extra_ref = refs[3:7]
     grad_ref, flat_ref, window_ref, rim_ref = refs[-4:]
-    flat_ref[...] = flat_in[...]
     upper = lanes_of((40, 3 * LANES)) % LANES >= 64
     if step == 0:
-        rim_rows(arrived[0], arrived[1], window_ref, extra_ref)
+        flat_ref[...] = arrived[0][...]
+        rim_rows(arrived[1], arrived[2], window_ref, extra_ref)
         rim_ref[...] = jnp.zeros(rim_ref.shape, F32)
         for c in range(3):
             for d in range(5):
@@ -393,22 +411,22 @@
         for c in range(3):
             flat_ref[c, 100:125, :] = jnp.where(at_upper, extra_ref[pl.ds(c, 25, stride=8), :], flat_ref[c, 100:125, :])
     else:
-        shares = face_shares(*arrived)
-        value = jnp.concatenate([jnp.concatenate(lines, axis=0) for lines in shares], axis=1)
+        if step == STEPS - 1:
+            value = jnp.concatenate([arrived[0][c] for c in range(3)], axis=1)
+        else:
+            shares = face_shares(*arrived[1:4])
+            value = jnp.concatenate([jnp.concatenate(lines, axis=0) for lines in shares], axis=1)
+            for c in range(3):
+                extra_ref[c] = value[:, c * LANES : (c + 1) * LANES]
+            flat_ref[...] = arrived[0][...]
+            add_shares(shares, flat_ref)
         high, middle, _ = [piece.astype(F32) for piece in cut(value)]
         stacked = []
         for at in (~upper, upper):
             stacked += [jnp.where(at, high, 0.0), jnp.where(at, middle, 0.0), jnp.where(at, high, 0.0)]
-        at_upper = lanes_of((5, LANES)) >= 64
-        for c in range(3):
-            for d in range(5):
-                extra_ref[c, 8 * d : 8 * d + 8, :] = shares[c][d]
-                share = shares[c][d][0:5]
-                first, last = pl.ds(d, 5, stride=5), pl.ds(100 + d, 5, stride=5)
-                flat_ref[c, first, :] = flat_ref[c, first, :] + jnp.where(at_upper, 0.0, share)
-                flat_ref[c, last, :] = flat_ref[c, last, :] + jnp.where(at_upper, share, 0.0)
     grad_ref[...] = base_ref[...] + dot(share_table[...], jnp.concatenate(stacked, axis=0).astype(BF16))
-    low_ref[...] = flat_ref[...].astype(BF16)
+    if step < STEPS - 1:
+        low_ref[...] = flat_ref[...].astype(BF16)
     for block in range(9):
         sigma_ref[(block // 3) * 128 + 120 : (block // 3) * 128 + 128, (block % 3) * LANES : (block % 3) * LANES + LANES] = (
             jnp.zeros((8, LANES), F32)
@@ -436,7 +454,7 @@
             for back in range(step):
                 value = value + factors[back + 1] * older[step - 1 - back][part, rows, :]
             relax.append(value)
-            if keep_ref is not None:
+            if step < STEPS - 1:
                 keep_ref[part, rows, :] = fresh[part]
         bulk = lame * trace
         xx = bulk + pulls[0] - relax[0]
@@ -455,8 +473,7 @@
         odd_ref[...] = jnp.where(even_ring, first, last)
         even_ref[...] = jnp.where(even_ring, last, first)
     else:
-        even_ref[0:40, :] = last
-        even_ref[40:, :] = jnp.zeros((even_ref.shape[0] - 40, LANES), F32)
+        even_ref[...] = last
 
 
 def next_state(sigma_ref, force_table, u_ref, p_ref, scale_ref, next_ref):
@@ -632,7 +649,7 @@
 
 
 def finish_kernel(before_ref, nodal_ref, density_ref, face_mass_ref, spread_ref, out_ref, rows_ref, face_ref):
-    packed = before_ref[0:40]
+    packed = before_ref[...]
     values = unpack_face(packed, rolled(packed, 64, 1))
     rows_ref[...] = jnp.zeros(rows_ref.shape, F32)
     for c in range(3):
@@ -659,7 +676,7 @@
     return jax.ShapeDtypeStruct(shape, dtype)
 
 
-def call(kernel, name, outs, scratch, *args, outside=(), micros=1, room=32 * 1024):
+def call(kernel, name, outs, scratch, *args, outside=(), flops=0, room=32 * 1024):
     return pl.pallas_call(
         kernel,
         name=name,
@@ -668,7 +685,7 @@
         out_specs=jax.tree.map(lambda _: VMEM, outs),
         scratch_shapes=scratch,
         compiler_params=pltpu.CompilerParams(vmem_limit_bytes=room * 1024),
-        cost_estimate=pl.CostEstimate(flops=0, bytes_accessed=micros * 3000000, transcendentals=0),
+        cost_estimate=pl.CostEstimate(flops=flops, bytes_accessed=3000000, transcendentals=0),
     )(*args)
 
 
@@ -735,26 +752,33 @@
     kept = []
     for step in range(STEPS):
         last_step = step == STEPS - 1
-        arrived = (rim, spread) if step == 0 else (odd, even, face_scale)
-        outs = [
-            shaped(6, 125, LANES), shaped(384, 384), shaped(PAD, LANES) if last_step else face,
-            shaped(3, 128, LANES, dtype=BF16), scale_shape if step == 0 else shaped(3, 40, LANES),
-        ]
+        low_shape = shaped(3, 128, LANES, dtype=BF16)
+        if last_step:
+            extra, low = call(
+                shares_kernel, "shares", [shaped(3, 40, LANES), low_shape], [pltpu.VMEM((3, 128, LANES), F32)],
+                odd, even, face_scale, flat,
+            )
+            far = far_field(low, groups)
+            arrived = (extra,)
+        else:
+            arrived = (flat, rim, spread) if step == 0 else (flat, odd, even, face_scale)
+        outs = [shaped(6, 125, LANES), grad_shape, face]
         if not last_step:
-            outs += [face, five]
+            outs += [face, five, low_shape, scale_shape if step == 0 else shaped(3, 40, LANES)]
         results = call(
             lambda *refs, step=step: step_kernel(step, *refs), "step", outs,
             [grad_scratch, pltpu.VMEM((3, 128, LANES), F32), pltpu.VMEM((8, 8, WINDOW), F32), pltpu.VMEM((40, 384), F32)],
-            lame_lambda, shear_mu, memories[step], sls_decay, rim_table if step == 0 else share_table, face_table, base, flat, *arrived, *kept,
+            lame_lambda, shear_mu, memories[step], sls_decay, rim_table if step == 0 else share_table, face_table, base, *arrived, *kept,
         )
-        strain, sigma, even, low, extra = results[0:5]
+        strain, sigma, even = results[0:3]
         if last_step:
             before = passed_along(even, ring, 1)
         else:
-            kept.append(results[6])
-            odd = swapped(results[5], ring, 1)
+            odd, keep, low, extra = results[3:7]
+            kept.append(keep)
+            odd = swapped(odd, ring, 1)
             even = swapped(even, ring, 0)
-        far = far_field(low, groups)
+            far = far_field(low, groups)
         if step == 0:
             p, scale, partial, flat, base, face_scale = call(
                 first_rest_kernel, "rest", [state, scale_shape, state, flat_shape, grad_shape, shaped(40, LANES)],
@@ -781,7 +805,7 @@
             both = call(
                 both_parts_kernel, "parts", shaped(subs, rows, LANES), part_scratch, *shared, one, select
             )
-            base, both = lax.optimization_barrier((base, both))
+            base, flat, both = lax.optimization_barrier((base, flat, both))
         else:
             sent = list(
                 call(send_kernel, "send", [shaped(rows, LANES)] * subs, part_scratch, *shared, both, select)
@@ -792,7 +816,7 @@
     nodal = call(nodal_kernel, "nodal", shaped(24, FACE), [], partial, spread)
     final = call(
         finish_kernel, "finish", shaped(1, 3, 8, FACE), [pltpu.VMEM((ROWS, LANES), F32), pltpu.VMEM((8, FACE), F32)],
-        before, nodal, density, face_mass, spread,
+        before, nodal, density, face_mass, spread, flops=550000000,
     )
     kernels = call(
         lambda *refs: sum_kernel(order, *refs), "sum", shaped(250, 1, 256), [], *[sent[k] for k in order]

time: 42.8 us -> 42.2 us (0.986)
  waiting for transfers between devices: 6.94 us -> 6.32 us
    ppermute x5, waiting for transfers between devices: 2.96 us -> 1.71 us  [passed_along(): lax.ppermute(value, axis, [(source, (source + steps) % count) for source...]
    ppermute x3, waiting for transfers between devices: 0.56 us -> 1.18 us  [per_device(): sent[k] = lax.ppermute(sent[k], 'sub', [(j, j ^ k) for j in range(subs)])]
    pallas_call x15 -> x16, Pallas kernels: 15 us -> 14.9 us  [call(): pl.pallas_call(kernel, name=name, out_shape=outs, in_specs=[HBM if at in...]
  transfers between devices with their start and end apart: 12 -> 12, of which waited for: 5 -> 5; matrix products, arithmetic and copies ran while one was open for 3% -> 3% of each run, Pallas kernels for 22% -> 24%
where the time goes in v5:
time: 42.2 us; the launch traced here: 42 us
  starting transfers between devices  17.7 us (42%)
  Pallas kernels  14.9 us (35%)
  waiting for transfers between devices  6.32 us (15%)
  local copies, waits for them, and re-layouts  2.05 us (5%)
  between operations  0.96 us (2%)
    pallas_call x16, Pallas kernels, call(): pl.pallas_call(kernel, name=name, out_shape=outs, in_specs=[HBM if at in...  14.9 us
    ppermute x5, starting transfers between devices, passed_along(): lax.ppermute(value, axis, [(source, (source + steps) % count) for source...  7.23 us
    ppermute x4, starting transfers between devices, swapped(): return lax.ppermute(value, axis, pairs)  6.94 us
    ppermute x3, starting transfers between devices, per_device(): sent[k] = lax.ppermute(sent[k], 'sub', [(j, j ^ k) for j in range(subs)])  3.55 us
    ppermute x4, waiting for transfers between devices, swapped(): return lax.ppermute(value, axis, pairs)  3.42 us
    unnamed x29, local copies, waits for them, and re-layouts  2.05 us
    ppermute x5, waiting for transfers between devices, passed_along(): lax.ppermute(value, axis, [(source, (source + steps) % count) for source...  1.71 us
    ppermute x3, waiting for transfers between devices, per_device(): sent[k] = lax.ppermute(sent[k], 'sub', [(j, j ^ k) for j in range(subs)])  1.18 us
  transfers between devices with their start and end apart: 12, of which 5 were waited for; matrix products, arithmetic and copies ran while one was open for 3% of the time, Pallas kernels for 24%

profile of v5, /device:TPU:0, one launch (start us, length us, event | category | flops | bytes accessed | tf_op | source)
XLA Modules:
  0.0 42.0 jit_solution(9953777867969443912)
XLA Ops:
  0.7 1.0 %gather.1 = f32[8,1089]{1,0:T(8,128)S(1)} custom-call(f32[1,3,8,1089]{3,2,1,0:T(8,128)} %now_ref.3, f32[1,3,8,1089]{3,2,1,0:T(8,128)} %prev_ref.3, f32[8,1089]{1,0:T(8,128)} %density_ref.5), custom_call_target="tpu_custom_call" | custom-call | bytes 3000000 | tf_op jit(solution)/shard_map/gather/pallas_call | solution.py:680
  1.8 7.0 %collective-permute-start = (f32[8,1089]{1,0:T(8,128)S(1)}, f32[8,1089]{1,0:T(8,128)S(1)}, u32[]{:S(2)}, u32[]{:S(2)}) collective-permute-start(f32[8,1089]{1,0:T(8,128)S(1)} %gather.1), channel_id=1, source_target_pairs={{0,15},{1,0},{2,1},{3,2},{4,3},{5,4},{6,5},{7,6},{8,7},{9,8},{10,9... | collective-permute-start | bytes 104552 | tf_op jit(solution)/shard_map/ppermute | solution.py:694
  8.8 1.3 %copy.20 = f32[1,3,5,125,128]{4,3,0,2,1:T(8,128)S(1)} copy(f32[1,3,5,125,128]{4,0,3,2,1:T(1,128)} %param.17) | data formatting | bytes 1920000
  10.2 2.7 %prologue.1 = (f32[3,208,128]{2,1,0:T(8,128)S(1)}, f32[3,208,128]{2,1,0:T(8,128)S(1)}, f32[208,128]{1,0:T(8,128)S(1)}, f32[5,125,128]{2,1,0:T(8,128)S(1)}, bf16[...) custom-call(f32[1,3,8,1089]{3,2,1,0:T(8,128)S(1)} %copy-done.7, ...), custom_call_target="tpu_custom_call" | custom-call | bytes 3000000 | tf_op jit(solution)/shard_map/prologue/pallas_call | solution.py:680
  12.9 1.2 %step.3 = (f32[6,125,128]{2,1,0:T(8,128)S(1)}, f32[384,384]{1,0:T(8,128)S(1)}, f32[40,128]{1,0:T(8,128)S(1)}, f32[40,128]{1,0:T(8,128)S(1)}, f32[5,125,128]{2,1,...) custom-call(f32[125,128]{1,0:T(8,128)S(1)} %copy-done.2, f32[125,128]{1,0:T(8,128)S(1)} %copy-done.3, ...), custom_call_target="tpu_custom_call" | custom-call | bytes 3000000 | tf_op jit(solution)/shard_map/step/pallas_call | solution.py:680
  14.2 3.5 %collective-permute-start.2 = (f32[40,128]{1,0:T(8,128)S(1)}, f32[40,128]{1,0:T(8,128)S(1)}, u32[]{:S(2)}, u32[]{:S(2)}) collective-permute-start(f32[40,128]{1,0:T(8,128)S(1)} %get-tuple-element.70), channel_id=1, source_target_pairs={{1,2},{2,1},{3,4},{4,3},{5,6},{6,5},{7,8},{8,7},{9,10},{10,9},{11,... | collective-permute-start | bytes 61448 | tf_op jit(solution)/shard_map/ppermute | solution.py:703
  17.7 0.7 %copy-done.12 = s32[2,64,1]{1,2,0:T(1,128)S(1)} copy-done((s32[2,64,1]{1,2,0:T(1,128)S(1)}, s32[2,64,1]{1,2,0:T(1,128)}, u32[]{:S(2)}) %copy-start.12) | copy-done | bytes 536
  18.7 1.2 %rest.3 = (f32[3,208,128]{2,1,0:T(8,128)S(1)}, f32[208,128]{1,0:T(8,128)S(1)}, f32[3,208,128]{2,1,0:T(8,128)S(1)}, f32[3,128,128]{2,1,0:T(8,128)S(1)}, f32[384,384]{1,0:T(8,128)S(1)}, /*index=5*/f32[40,128]{1,0:T(8,128)S(1)}) custom-call(f32[384,384]{1,0:T(8,128)S(1)} %get-tuple-element.56.sigma_ref, bf16[3,208,384]{2,1,0:T(8,128)(2,1)S(1)} %copy-done.1, ...), custom_call_target="tpu_custom_call" | custom-call | bytes 3000000 | tf_op jit(solution)/shard_map/rest/pallas_call | solution.py:680
  20.4 1.3 %collective-permute-done.2.refs_8_ = f32[40,128]{1,0:T(8,128)S(1)} collective-permute-done((f32[40,128]{1,0:T(8,128)S(1)}, f32[40,128]{1,0:T(8,128)S(1)}, u32[]{:S(2)}, u32[]{:S(2)}) %collective-permute-start.2) | collective-permute-done | bytes 20512 | tf_op jit(solution)/shard_map/ppermute | solution.py:703
  21.7 0.9 %step.4 = (f32[6,125,128]{2,1,0:T(8,128)S(1)}, f32[384,384]{1,0:T(8,128)S(1)}, f32[40,128]{1,0:T(8,128)S(1)}, f32[40,128]{1,0:T(8,128)S(1)}, f32[5,125,128]{2,1,...) custom-call(f32[125,128]{1,0:T(8,128)S(1)} %copy-done.2, f32[125,128]{1,0:T(8,128)S(1)} %copy-done.3, ...), custom_call_target="tpu_custom_call" | custom-call | bytes 3000000 | tf_op jit(solution)/shard_map/step/pallas_call | solution.py:680
  22.6 3.5 %collective-permute-start.5 = (f32[40,128]{1,0:T(8,128)S(1)}, f32[40,128]{1,0:T(8,128)S(1)}, u32[]{:S(2)}, u32[]{:S(2)}) collective-permute-start(f32[40,128]{1,0:T(8,128)S(1)} %get-tuple-element.86), channel_id=1, source_target_pairs={{1,2},{2,1},{3,4},{4,3},{5,6},{6,5},{7,8},{8,7},{9,10},{10,9},{11,... | collective-permute-start | bytes 61448 | tf_op jit(solution)/shard_map/ppermute | solution.py:703
  26.1 1.2 %rest.4 = (f32[3,208,128]{2,1,0:T(8,128)S(1)}, f32[3,208,128]{2,1,0:T(8,128)S(1)}, f32[3,128,128]{2,1,0:T(8,128)S(1)}, f32[384,384]{1,0:T(8,128)S(1)}) custom-call(f32[384,384]{1,0:T(8,128)S(1)} %get-tuple-element.74.sigma_ref, bf16[3,208,384]{2,1,0:T(8,128)(2,1)S(1)} %copy-done.1, f32[3,208,128]{2,1,0:T(8,128)S(1)} %get-tuple-element.75.partial_ref, ...), custom_call_target="tpu_custom_call" | custom-call | bytes 3000000 | tf_op jit(solution)/shard_map/rest/pallas_call | solution.py:680
  27.3 0.6 %parts.3.both_ref = f32[4,128,128]{2,1,0:T(8,128)S(1)} custom-call(f32[6,125,128]{2,1,0:T(8,128)S(1)} %get-tuple-element.81.strain_ref, bf16[3,128,128]{2,1,0:T(8,128)(2,1)S(1)} %get-tuple-element.82.low_ref, bf16[3,128,128]{2,1,0:T(8,128)(2,1)S(1)} %collective-permute-done.4.far_ref, f32[125,128]{1,0:T(8,128)S(1)} %copy-done.2, f32[125,128]{1,0:T(8,128)S(1)} %copy-done.3, ...), custom_call_target="tpu_custom_call" | custom-call | bytes 3000000 | tf_op jit(solution)/shard_map/parts/pallas_call | solution.py:680
  27.9 2.1 %collective-permute-done.5.odd_ref = f32[40,128]{1,0:T(8,128)S(1)} collective-permute-done((f32[40,128]{1,0:T(8,128)S(1)}, f32[40,128]{1,0:T(8,128)S(1)}, u32[]{:S(2)}, u32[]{:S(2)}) %collective-permute-start.5) | collective-permute-done | bytes 20512 | tf_op jit(solution)/shard_map/ppermute | solution.py:703
  30.4 0.7 %step.5 = (f32[6,125,128]{2,1,0:T(8,128)S(1)}, f32[384,384]{1,0:T(8,128)S(1)}, f32[40,128]{1,0:T(8,128)S(1)}) custom-call(f32[125,128]{1,0:T(8,128)S(1)} %copy-done.2, f32[125,128]{1,0:T(8,128)S(1)} %copy-done.3, f32[5,125,128]{2,1,0:T(8,128)S(1)} %get-tuple-element.66.refs_2_, f32[3,128]{1,0:T(4,128)S(1)} %copy-done.11, bf16[384,240]{1,0:T(8,128)(2,1)S(1)} %copy-done.5, ...), custom_call_target="tpu_custom_call" | custom-call | bytes 3000000 | tf_op jit(solution)/shard_map/step/pallas_call | solution.py:680
  31.1 0.6 %collective-permute-done.8.far_ref = bf16[3,128,128]{2,1,0:T(8,128)(2,1)S(1)} collective-permute-done((bf16[3,128,128]{2,1,0:T(8,128)(2,1)S(1)}, bf16[3,128,128]{2,1,0:T(8,128)(2,1)S(1)}, u32[]{:S(2)}, u32[]{:S(2)}) %collective-permute-start.8) | collective-permute-done | bytes 98336 | tf_op jit(solution)/shard_map/ppermute | solution.py:694
  32.4 2.4 %collective-permute-start.10 = (f32[128,128]{1,0:T(8,128)S(1)}, f32[128,128]{1,0:T(8,128)S(1)}, u32[]{:S(2)}, u32[]{:S(2)}) collective-permute-start(f32[128,128]{1,0:T(8,128)S(1)} %get-tuple-element.99), channel_id=1, source_target_pairs={{0,3},{1,2},{2,1},{3,0},{4,7},{5,6},{6,5},{7,4},{8,11},{9,10},{10,... | collective-permute-start | bytes 196616 | tf_op jit(solution)/shard_map/ppermute | solution.py:815
  34.7 1.1 %collective-permute-start.11 = (f32[128,128]{1,0:T(8,128)S(1)}, f32[128,128]{1,0:T(8,128)S(1)}, u32[]{:S(2)}, u32[]{:S(2)}) collective-permute-start(f32[128,128]{1,0:T(8,128)S(1)} %get-tuple-element.100), channel_id=1, source_target_pairs={{0,1},{1,0},{2,3},{3,2},{4,5},{5,4},{6,7},{7,6},{8,9},{9,8},{10,11... | collective-permute-start | bytes 196616 | tf_op jit(solution)/shard_map/ppermute | solution.py:815
  35.8 0.7 %rest.5.partial_ref = f32[3,208,128]{2,1,0:T(8,128)S(1)} custom-call(f32[384,384]{1,0:T(8,128)S(1)} %get-tuple-element.92.sigma_ref, bf16[3,208,384]{2,1,0:T(8,128)(2,1)S(1)} %copy-done.1, f32[3,208,128]{2,1,0:T(8,128)S(1)} %get-tuple-element.93.partial_ref, f32[3,40,128]{2,1,0:T(8,128)S(1)} %get-tuple-element.89.refs_7_.delta_ref, ...), custom_call_target="tpu_custom_call" | custom-call | bytes 3000000 | tf_op jit(solution)/shard_map/rest/pallas_call | solution.py:680
  36.6 0.8 %nodal.1.nodal_ref = f32[24,1089]{1,0:T(8,128)S(1)} custom-call(f32[3,208,128]{2,1,0:T(8,128)S(1)} %rest.5.partial_ref, bf16[256,1664]{1,0:T(8,128)(2,1)S(1)} %get-tuple-element.55.refs_9_.spread_ref), custom_call_target="tpu_custom_call" | custom-call | bytes 3000000 | tf_op jit(solution)/shard_map/nodal/pallas_call | solution.py:680
  37.4 1.1 %collective-permute-done.7.before_ref = f32[40,128]{1,0:T(8,128)S(1)} collective-permute-done((f32[40,128]{1,0:T(8,128)S(1)}, f32[40,128]{1,0:T(8,128)S(1)}, u32[]{:S(2)}, u32[]{:S(2)}) %collective-permute-start.7) | collective-permute-done | bytes 20512 | tf_op jit(solution)/shard_map/ppermute | solution.py:694
  38.5 1.3 %finish.1 = f32[1,3,8,1089]{3,2,1,0:T(8,128)} custom-call(f32[40,128]{1,0:T(8,128)S(1)} %collective-permute-done.7.before_ref, f32[24,1089]{1,0:T(8,128)S(1)} %nodal.1.nodal_ref, f32[8,1089]{1,0:T(8,128)S(1)} %copy-done.10, f32[1,1089]{1,0:T(1,128)S(1)} %copy-done.13, bf16[256,1664]{1,0:T(8,128)(2,1)S(1)} %get-tuple-element.55.refs_9_.spread_ref), custom_call_target="tpu_custom_call" | custom-call | flops 550000000 | bytes 3000000 | tf_op jit(solution)/shard_map/finish/pallas_call | solution.py:680
  39.8 1.2 %collective-permute-done.11.refs_2_ = f32[128,128]{1,0:T(8,128)S(1)} collective-permute-done((f32[128,128]{1,0:T(8,128)S(1)}, f32[128,128]{1,0:T(8,128)S(1)}, u32[]{:S(2)}, u32[]{:S(2)}) %collective-permute-start.11) | collective-permute-done | bytes 65568 | tf_op jit(solution)/shard_map/ppermute | solution.py:815
  41.0 1.0 %sum.1 = f32[250,1,256]{2,1,0:T(1,128)} custom-call(f32[128,128]{1,0:T(8,128)S(1)} %collective-permute-done.9.refs_0_, f32[128,128]{1,0:T(8,128)S(1)} %collective-permute-done.10.refs_1_, f32[128,128]{1,0:T(8,128)S(1)} %collective-permute-done.11.refs_2_, f32[128,128]{1,0:T(8,128)S(1)} %get-tuple-element.101.refs_3_), custom_call_target="tpu_custom_call" | custom-call | bytes 3000000 | tf_op jit(solution)/shard_map/sum/pallas_call | solution.py:680
  (45 shorter events, 2.0 us)
Async XLA Ops:
  0.6 9.5 %copy-start.9 = (f32[208,128]{1,0:T(8,128)S(1)}, f32[208,128]{1,0:T(8,128)}, u32[]{:S(2)}) copy-start(f32[208,128]{1,0:T(8,128)} %constant.20.clone.mass_ref) | copy-start | bytes 319492
  0.6 9.5 %copy-start.10 = (f32[8,1089]{1,0:T(8,128)S(1)}, f32[8,1089]{1,0:T(8,128)}, u32[]{:S(2)}) copy-start(f32[8,1089]{1,0:T(8,128)} %density_ref.5) | copy-start | bytes 104548
  1.7 8.4 %copy-start = (bf16[3,384,256]{2,1,0:T(8,128)(2,1)S(1)}, bf16[3,384,256]{2,1,0:T(8,128)(2,1)}, u32[]{:S(2)}) copy-start(bf16[3,384,256]{2,1,0:T(8,128)(2,1)} %constant.14.clone.refs_0_.grad_table) | copy-start | bytes 1769476
  1.7 8.4 %copy-start.1 = (bf16[3,208,384]{2,1,0:T(8,128)(2,1)S(1)}, bf16[3,208,384]{2,1,0:T(8,128)(2,1)}, u32[]{:S(2)}) copy-start(bf16[3,208,384]{2,1,0:T(8,128)(2,1)} %constant.15.clone.refs_2_.force_table) | copy-start | bytes 1437700
  1.7 8.4 %copy-start.2 = (f32[125,128]{1,0:T(8,128)S(1)}, f32[125,128]{1,0:T(8,128)}, u32[]{:S(2)}) copy-start(f32[125,128]{1,0:T(8,128)} %lame_ref.5) | copy-start | bytes 192004
  1.7 8.4 %copy-start.3 = (f32[125,128]{1,0:T(8,128)S(1)}, f32[125,128]{1,0:T(8,128)}, u32[]{:S(2)}) copy-start(f32[125,128]{1,0:T(8,128)} %mu_ref.5) | copy-start | bytes 192004
  1.7 8.4 %copy-start.4 = (bf16[3,80,256]{2,1,0:T(8,128)(2,1)S(1)}, bf16[3,80,256]{2,1,0:T(8,128)(2,1)}, u32[]{:S(2)}) copy-start(bf16[3,80,256]{2,1,0:T(8,128)(2,1)} %constant.16.clone.refs_1_.refs_5_) | copy-start | bytes 368644
  1.7 8.4 %copy-start.5 = (bf16[384,240]{1,0:T(8,128)(2,1)S(1)}, bf16[384,240]{1,0:T(8,128)(2,1)}, u32[]{:S(2)}) copy-start(bf16[384,240]{1,0:T(8,128)(2,1)} %constant.17.clone.refs_4_) | copy-start | bytes 552964
  1.8 8.4 %copy-start.6 = (bf16[384,240]{1,0:T(8,128)(2,1)S(1)}, bf16[384,240]{1,0:T(8,128)(2,1)}, u32[]{:S(2)}) copy-start(bf16[384,240]{1,0:T(8,128)(2,1)} %constant.18.clone.refs_3_.refs_4_) | copy-start | bytes 552964
  1.8 8.4 %copy-start.7 = (f32[1,3,8,1089]{3,2,1,0:T(8,128)S(1)}, f32[1,3,8,1089]{3,2,1,0:T(8,128)}, u32[]{:S(2)}) copy-start(f32[1,3,8,1089]{3,2,1,0:T(8,128)} %now_ref.3) | copy-start | bytes 313636
  1.8 8.4 %copy-start.8 = (f32[1,3,8,1089]{3,2,1,0:T(8,128)S(1)}, f32[1,3,8,1089]{3,2,1,0:T(8,128)}, u32[]{:S(2)}) copy-start(f32[1,3,8,1089]{3,2,1,0:T(8,128)} %prev_ref.3) | copy-start | bytes 313636
  1.8 11.1 %collective-permute-start = (f32[8,1089]{1,0:T(8,128)S(1)}, f32[8,1089]{1,0:T(8,128)S(1)}, u32[]{:S(2)}, u32[]{:S(2)}) collective-permute-start(f32[8,1089]{1,0:T(8,128)S(1)} %gather.1), channel_id=1, source_target_pairs={{0,15},{1,0},{2,1},{3,2},{4,3},{5,4},{6,5},{7,6},{8,7},{9,8},{10,9... | collective-permute-start | bytes 104552 | tf_op jit(solution)/shard_map/ppermute | solution.py:694
  14.1 5.8 %collective-permute-start.1 = (bf16[3,128,128]{2,1,0:T(8,128)(2,1)S(1)}, bf16[3,128,128]{2,1,0:T(8,128)(2,1)S(1)}, u32[]{:S(2)}, u32[]{:S(2)}) collective-permute-start(bf16[3,128,128]{2,1,0:T(8,128)(2,1)S(1)} %get-tuple-element.63.low_ref), channel_id=1, source_target_pairs={{0,16},{16,0},{1,17},{17,1},{2,18},{18,2},{3,19},{19,3},{4,20},{20... | collective-permute-start | bytes 294920 | tf_op jit(solution)/shard_map/ppermute | solution.py:694
  14.2 7.4 %collective-permute-start.2 = (f32[40,128]{1,0:T(8,128)S(1)}, f32[40,128]{1,0:T(8,128)S(1)}, u32[]{:S(2)}, u32[]{:S(2)}) collective-permute-start(f32[40,128]{1,0:T(8,128)S(1)} %get-tuple-element.70), channel_id=1, source_target_pairs={{1,2},{2,1},{3,4},{4,3},{5,6},{6,5},{7,8},{8,7},{9,10},{10,9},{11,... | collective-permute-start | bytes 61448 | tf_op jit(solution)/shard_map/ppermute | solution.py:703
  17.7 4.0 %collective-permute-start.3 = (f32[40,128]{1,0:T(8,128)S(1)}, f32[40,128]{1,0:T(8,128)S(1)}, u32[]{:S(2)}, u32[]{:S(2)}) collective-permute-start(f32[40,128]{1,0:T(8,128)S(1)} %get-tuple-element.71), channel_id=1, source_target_pairs={{0,1},{1,0},{2,3},{3,2},{4,5},{5,4},{6,7},{7,6},{8,9},{9,8},{10,11... | collective-permute-start | bytes 61448 | tf_op jit(solution)/shard_map/ppermute | solution.py:703
  22.6 4.8 %collective-permute-start.4 = (bf16[3,128,128]{2,1,0:T(8,128)(2,1)S(1)}, bf16[3,128,128]{2,1,0:T(8,128)(2,1)S(1)}, u32[]{:S(2)}, u32[]{:S(2)}) collective-permute-start(bf16[3,128,128]{2,1,0:T(8,128)(2,1)S(1)} %get-tuple-element.82.low_ref), channel_id=1, source_target_pairs={{0,16},{16,0},{1,17},{17,1},{2,18},{18,2},{3,19},{19,3},{4,20},{20... | collective-permute-start | bytes 294920 | tf_op jit(solution)/shard_map/ppermute | solution.py:694
  22.6 7.4 %collective-permute-start.5 = (f32[40,128]{1,0:T(8,128)S(1)}, f32[40,128]{1,0:T(8,128)S(1)}, u32[]{:S(2)}, u32[]{:S(2)}) collective-permute-start(f32[40,128]{1,0:T(8,128)S(1)} %get-tuple-element.86), channel_id=1, source_target_pairs={{1,2},{2,1},{3,4},{4,3},{5,6},{6,5},{7,8},{8,7},{9,10},{10,9},{11,... | collective-permute-start | bytes 61448 | tf_op jit(solution)/shard_map/ppermute | solution.py:703
  26.1 4.0 %collective-permute-start.6 = (f32[40,128]{1,0:T(8,128)S(1)}, f32[40,128]{1,0:T(8,128)S(1)}, u32[]{:S(2)}, u32[]{:S(2)}) collective-permute-start(f32[40,128]{1,0:T(8,128)S(1)} %get-tuple-element.87), channel_id=1, source_target_pairs={{0,1},{1,0},{2,3},{3,2},{4,5},{5,4},{6,7},{7,6},{8,9},{9,8},{10,11... | collective-permute-start | bytes 61448 | tf_op jit(solution)/shard_map/ppermute | solution.py:703
  30.3 1.4 %collective-permute-start.8 = (bf16[3,128,128]{2,1,0:T(8,128)(2,1)S(1)}, bf16[3,128,128]{2,1,0:T(8,128)(2,1)S(1)}, u32[]{:S(2)}, u32[]{:S(2)}) collective-permute-start(bf16[3,128,128]{2,1,0:T(8,128)(2,1)S(1)} %get-tuple-element.96.low_ref), channel_id=1, source_target_pairs={{0,16},{16,0},{1,17},{17,1},{2,18},{18,2},{3,19},{19,3},{4,20},{20... | collective-permute-start | bytes 294920 | tf_op jit(solution)/shard_map/ppermute | solution.py:694
  31.1 7.4 %collective-permute-start.7 = (f32[40,128]{1,0:T(8,128)S(1)}, f32[40,128]{1,0:T(8,128)S(1)}, u32[]{:S(2)}, u32[]{:S(2)}) collective-permute-start(f32[40,128]{1,0:T(8,128)S(1)} %get-tuple-element.91), channel_id=1, source_target_pairs={{0,1},{1,2},{2,3},{3,4},{4,5},{5,6},{6,7},{7,8},{8,9},{9,10},{10,1... | collective-permute-start | bytes 61448 | tf_op jit(solution)/shard_map/ppermute | solution.py:694
  32.3 7.6 %collective-permute-start.9 = (f32[128,128]{1,0:T(8,128)S(1)}, f32[128,128]{1,0:T(8,128)S(1)}, u32[]{:S(2)}, u32[]{:S(2)}) collective-permute-start(f32[128,128]{1,0:T(8,128)S(1)} %get-tuple-element.98), channel_id=1, source_target_pairs={{0,2},{1,3},{2,0},{3,1},{4,6},{5,7},{6,4},{7,5},{8,10},{9,11},{10,... | collective-permute-start | bytes 196616 | tf_op jit(solution)/shard_map/ppermute | solution.py:815
  32.4 7.5 %collective-permute-start.10 = (f32[128,128]{1,0:T(8,128)S(1)}, f32[128,128]{1,0:T(8,128)S(1)}, u32[]{:S(2)}, u32[]{:S(2)}) collective-permute-start(f32[128,128]{1,0:T(8,128)S(1)} %get-tuple-element.99), channel_id=1, source_target_pairs={{0,3},{1,2},{2,1},{3,0},{4,7},{5,6},{6,5},{7,4},{8,11},{9,10},{10,... | collective-permute-start | bytes 196616 | tf_op jit(solution)/shard_map/ppermute | solution.py:815
  34.7 6.3 %collective-permute-start.11 = (f32[128,128]{1,0:T(8,128)S(1)}, f32[128,128]{1,0:T(8,128)S(1)}, u32[]{:S(2)}, u32[]{:S(2)}) collective-permute-start(f32[128,128]{1,0:T(8,128)S(1)} %get-tuple-element.100), channel_id=1, source_target_pairs={{0,1},{1,0},{2,3},{3,2},{4,5},{5,4},{6,7},{7,6},{8,9},{9,8},{10,11... | collective-permute-start | bytes 196616 | tf_op jit(solution)/shard_map/ppermute | solution.py:815
  36.5 2.0 %copy-start.13 = (f32[1,1089]{1,0:T(1,128)S(1)}, f32[1,1089]{1,0:T(1,128)}, u32[]{:S(2)}) copy-start(f32[1,1089]{1,0:T(1,128)} %constant.19.clone.face_mass_ref) | copy-start | bytes 13072
  (2 other events, 2.1 us)

commit v6 on v5

--- a/solution.py
+++ b/solution.py
@@ -560,12 +560,14 @@
     return kernel_ref[...].astype(BF16)
 
 
-def placed(part, select_ref, rows):
+def placed(pieces, select, rows):
     slots = rows // 2
     group = lanes_of((rows, LANES)) // slots
-    total = lax.dot_general(part, select_ref[...], (((1,), (1,)), ((), ())), preferred_element_type=F32)
+    total = 0.0
+    for piece in pieces:
+        total = total + lax.dot_general(piece, select, (((1,), (1,)), ((), ())), preferred_element_type=F32)
     blocks = []
-    for k in range(select_ref.shape[0] // LANES):
+    for k in range(select.shape[0] // LANES):
         value = total[0:rows, k * LANES : (k + 1) * LANES]
         for j in range(1, 256 // rows):
             value = jnp.where(group == j, total[j * rows : (j + 1) * rows, k * LANES : (k + 1) * LANES], value)
@@ -573,24 +575,43 @@
     return blocks
 
 
+def group_scale(mantissa, exponent):
+    return mantissa * jnp.exp2(exponent) * (1.0 / (4096.0 * 32767.0))
+
+
 def parts_kernel(strain_ref, low_ref, far_ref, lame_ref, mu_ref, grad_table, part_ref, grad_ref, kernel_ref):
     part_ref[...] = kernel_parts(strain_ref, low_ref, far_ref, lame_ref, mu_ref, grad_table, grad_ref, kernel_ref)
 
 
-def both_parts_kernel(
-    strain_ref, low_ref, far_ref, lame_ref, mu_ref, grad_table, one_ref, select_ref, both_ref, grad_ref, kernel_ref
-):
+def both_parts_kernel(strain_ref, low_ref, far_ref, lame_ref, mu_ref, grad_table, one_ref, both_ref, grad_ref, kernel_ref):
     two = kernel_parts(strain_ref, low_ref, far_ref, lame_ref, mu_ref, grad_table, grad_ref, kernel_ref)
-    rows = both_ref.shape[1]
-    for k, (first, second) in enumerate(zip(placed(one_ref[...], select_ref, rows), placed(two, select_ref, rows))):
-        both_ref[k] = first + second
-
-
-def send_kernel(strain_ref, low_ref, far_ref, lame_ref, mu_ref, grad_table, both_ref, select_ref, *refs):
+    both_ref[...] = one_ref[...].astype(F32) + two.astype(F32)
+
+
+def send_kernel(strain_ref, low_ref, far_ref, lame_ref, mu_ref, grad_table, both_ref, select_ref, total_ref, *refs):
     out_refs, (grad_ref, kernel_ref) = refs[:-2], refs[-2:]
     three = kernel_parts(strain_ref, low_ref, far_ref, lame_ref, mu_ref, grad_table, grad_ref, kernel_ref)
-    for k, (ref, value) in enumerate(zip(out_refs, placed(three, select_ref, out_refs[0].shape[0]))):
-        ref[...] = both_ref[k] + value
+    kernel_ref[...] = both_ref[...] + three.astype(F32)
+    total_ref[...] = kernel_ref[...]
+    for k in range(2):
+        rows = slice(125 * k, 125 * k + 125)
+        value = kernel_ref[rows, :]
+        largest = jnp.maximum(jnp.max(jnp.abs(value), axis=0, keepdims=True), 1e-33)
+        exponent = jnp.floor(jnp.log2(largest))
+        mantissa = jnp.floor(largest * jnp.exp2(-exponent) * 4096.0) + 2.0
+        kernel_ref[rows, :] = jnp.floor(value * (1.0 / group_scale(mantissa, exponent)) + 0.5)
+        kernel_ref[250 + 2 * k : 251 + 2 * k, :] = mantissa
+        kernel_ref[251 + 2 * k : 252 + 2 * k, :] = exponent
+    high, middle, _ = cut(kernel_ref[...])
+    for ref, value in zip(out_refs, placed((high, middle), select_ref[LANES:, :], out_refs[0].shape[0])):
+        ref[...] = value.astype(jnp.int32).astype(jnp.int16)
+
+
+def own_kernel(total_ref, select_ref, own_ref):
+    row = lax.broadcasted_iota(jnp.int32, (256, LANES), 0)
+    unit = jnp.where((row == 250) | (row == 252), 4096.0 * 32767.0, 0.0)
+    value = jnp.where(row < 250, total_ref[...], unit)
+    own_ref[...] = placed(cut(value), select_ref[0:LANES, :], own_ref.shape[0])[0]
 
 
 def sum_kernel(order, *refs):
@@ -603,13 +624,16 @@
     for k, ref in zip(order, in_refs):
         source = lax.axis_index("sub") ^ k
         spot = source % pieces
-        value = ref[...]
+        value = ref[...].astype(jnp.int32).astype(F32) if k > 0 else ref[...]
         for j in range(pieces):
             moved = pltpu.roll(value, ((spot + pieces - j) % pieces) * slots, 1)
             for t in range(2):
                 here = (group == spot) & (source // pieces == t)
                 blocks[j][t] = jnp.where(here, moved, blocks[j][t])
     value = jnp.concatenate([jnp.concatenate(row, axis=1) for row in blocks], axis=0)
+    first, second = [group_scale(value[row : row + 1], value[row + 1 : row + 2]) for row in (250, 252)]
+    row = lax.broadcasted_iota(jnp.int32, (256, 256), 0)
+    value = value * jnp.where(row < 125, first, second)
     out_ref[:, 0, :] = value[0:250]
 
 
@@ -803,23 +827,24 @@
             base, one, select, memories[2] = lax.optimization_barrier((base, one, select, m3))
         elif not last_step:
             both = call(
-                both_parts_kernel, "parts", shaped(subs, rows, LANES), part_scratch, *shared, one, select
+                both_parts_kernel, "parts", shaped(256, LANES), part_scratch, *shared, one
             )
             base, flat, both = lax.optimization_barrier((base, flat, both))
         else:
-            sent = list(
-                call(send_kernel, "send", [shaped(rows, LANES)] * subs, part_scratch, *shared, both, select)
+            total, *blocks = call(
+                send_kernel, "send", [shaped(256, LANES)] + [shaped(rows, LANES, dtype=jnp.int16)] * (subs - 1),
+                part_scratch, *shared, both, select,
             )
-            order = [at ^ (at >> 1) for at in range(subs - 1, -1, -1)]
-            for k in order[:-1]:
-                sent[k] = lax.ppermute(sent[k], "sub", [(j, j ^ k) for j in range(subs)])
+            order = [*range(subs - 1, 0, -1), 0]
+            sent = [lax.ppermute(blocks[k - 1], "sub", [(j, j ^ k) for j in range(subs)]) for k in order[:-1]]
+            sent.append(call(own_kernel, "own", shaped(rows, LANES), [], total, select))
     nodal = call(nodal_kernel, "nodal", shaped(24, FACE), [], partial, spread)
     final = call(
         finish_kernel, "finish", shaped(1, 3, 8, FACE), [pltpu.VMEM((ROWS, LANES), F32), pltpu.VMEM((8, FACE), F32)],
-        before, nodal, density, face_mass, spread, flops=550000000,
+        before, nodal, density, face_mass, spread, flops=250000000,
     )
     kernels = call(
-        lambda *refs: sum_kernel(order, *refs), "sum", shaped(250, 1, 256), [], *[sent[k] for k in order]
+        lambda *refs: sum_kernel(order, *refs), "sum", shaped(250, 1, 256), [], *sent
     )
     return final, jnp.transpose(kernels, (1, 2, 0))
 

time: 42.2 us -> 41.2 us (0.976)
  waiting for transfers between devices: 6.32 us -> 4.18 us
  starting transfers between devices: 17.7 us -> 18.6 us
    ppermute x3, waiting for transfers between devices: 1.18 us -> 0.01 us  [per_device(): lax.ppermute(blocks[k - 1], 'sub', [(j, j ^ k) for j in range(subs)])]
    ppermute x5, waiting for transfers between devices: 1.71 us -> 0.59 us  [passed_along(): lax.ppermute(value, axis, [(source, (source + steps) % count) for source...]
    ppermute x3, starting transfers between devices: 3.55 us -> 4.45 us  [per_device(): lax.ppermute(blocks[k - 1], 'sub', [(j, j ^ k) for j in range(subs)])]
    pallas_call x16 -> x17, Pallas kernels: 14.9 us -> 15.1 us  [call(): pl.pallas_call(kernel, name=name, out_shape=outs, in_specs=[HBM if at in...]
  transfers between devices with their start and end apart: 12 -> 12, of which waited for: 5 -> 3; matrix products, arithmetic and copies ran while one was open for 3% -> 3% of each run, Pallas kernels for 24% -> 25%
where the time goes in v6:
time: 41.2 us; the launch traced here: 41 us
  starting transfers between devices  18.6 us (45%)
  Pallas kernels  15.1 us (37%)
  waiting for transfers between devices  4.18 us (10%)
  local copies, waits for them, and re-layouts  2.05 us (5%)
  between operations  0.98 us (2%)
    pallas_call x17, Pallas kernels, call(): pl.pallas_call(kernel, name=name, out_shape=outs, in_specs=[HBM if at in...  15.1 us
    ppermute x5, starting transfers between devices, passed_along(): lax.ppermute(value, axis, [(source, (source + steps) % count) for source...  7.23 us
    ppermute x4, starting transfers between devices, swapped(): return lax.ppermute(value, axis, pairs)  6.95 us
    ppermute x3, starting transfers between devices, per_device(): lax.ppermute(blocks[k - 1], 'sub', [(j, j ^ k) for j in range(subs)])  4.45 us
    ppermute x4, waiting for transfers between devices, swapped(): return lax.ppermute(value, axis, pairs)  3.58 us
    unnamed x29, local copies, waits for them, and re-layouts  2.05 us
  transfers between devices with their start and end apart: 12, of which 3 were waited for; matrix products, arithmetic and copies ran while one was open for 3% of the time, Pallas kernels for 25%

profile of v6, /device:TPU:0, one launch (start us, length us, event | category | flops | bytes accessed | tf_op | source)
XLA Modules:
  0.0 41.0 jit_solution(11018444197397422927)
XLA Ops:
  0.7 1.0 %gather.1 = f32[8,1089]{1,0:T(8,128)S(1)} custom-call(f32[1,3,8,1089]{3,2,1,0:T(8,128)} %now_ref.3, f32[1,3,8,1089]{3,2,1,0:T(8,128)} %prev_ref.3, f32[8,1089]{1,0:T(8,128)} %density_ref.5), custom_call_target="tpu_custom_call" | custom-call | bytes 3000000 | tf_op jit(solution)/shard_map/gather/pallas_call | solution.py:704
  1.8 7.0 %collective-permute-start = (f32[8,1089]{1,0:T(8,128)S(1)}, f32[8,1089]{1,0:T(8,128)S(1)}, u32[]{:S(2)}, u32[]{:S(2)}) collective-permute-start(f32[8,1089]{1,0:T(8,128)S(1)} %gather.1), channel_id=1, source_target_pairs={{0,15},{1,0},{2,1},{3,2},{4,3},{5,4},{6,5},{7,6},{8,7},{9,8},{10,9... | collective-permute-start | bytes 104552 | tf_op jit(solution)/shard_map/ppermute | solution.py:718
  8.8 1.3 %copy.20 = f32[1,3,5,125,128]{4,3,0,2,1:T(8,128)S(1)} copy(f32[1,3,5,125,128]{4,0,3,2,1:T(1,128)} %param.17) | data formatting | bytes 1920000
  10.2 2.7 %prologue.1 = (f32[3,208,128]{2,1,0:T(8,128)S(1)}, f32[3,208,128]{2,1,0:T(8,128)S(1)}, f32[208,128]{1,0:T(8,128)S(1)}, f32[5,125,128]{2,1,0:T(8,128)S(1)}, bf16[...) custom-call(f32[1,3,8,1089]{3,2,1,0:T(8,128)S(1)} %copy-done.7, ...), custom_call_target="tpu_custom_call" | custom-call | bytes 3000000 | tf_op jit(solution)/shard_map/prologue/pallas_call | solution.py:704
  12.9 1.2 %step.3 = (f32[6,125,128]{2,1,0:T(8,128)S(1)}, f32[384,384]{1,0:T(8,128)S(1)}, f32[40,128]{1,0:T(8,128)S(1)}, f32[40,128]{1,0:T(8,128)S(1)}, f32[5,125,128]{2,1,...) custom-call(f32[125,128]{1,0:T(8,128)S(1)} %copy-done.2, f32[125,128]{1,0:T(8,128)S(1)} %copy-done.3, ...), custom_call_target="tpu_custom_call" | custom-call | bytes 3000000 | tf_op jit(solution)/shard_map/step/pallas_call | solution.py:704
  14.2 3.5 %collective-permute-start.2 = (f32[40,128]{1,0:T(8,128)S(1)}, f32[40,128]{1,0:T(8,128)S(1)}, u32[]{:S(2)}, u32[]{:S(2)}) collective-permute-start(f32[40,128]{1,0:T(8,128)S(1)} %get-tuple-element.70), channel_id=1, source_target_pairs={{1,2},{2,1},{3,4},{4,3},{5,6},{6,5},{7,8},{8,7},{9,10},{10,9},{11,... | collective-permute-start | bytes 61448 | tf_op jit(solution)/shard_map/ppermute | solution.py:727
  17.7 0.7 %copy-done.13 = s32[2,64,1]{1,2,0:T(1,128)S(1)} copy-done((s32[2,64,1]{1,2,0:T(1,128)S(1)}, s32[2,64,1]{1,2,0:T(1,128)}, u32[]{:S(2)}) %copy-start.13) | copy-done | bytes 536
  18.7 1.2 %rest.3 = (f32[3,208,128]{2,1,0:T(8,128)S(1)}, f32[208,128]{1,0:T(8,128)S(1)}, f32[3,208,128]{2,1,0:T(8,128)S(1)}, f32[3,128,128]{2,1,0:T(8,128)S(1)}, f32[384,384]{1,0:T(8,128)S(1)}, /*index=5*/f32[40,128]{1,0:T(8,128)S(1)}) custom-call(f32[384,384]{1,0:T(8,128)S(1)} %get-tuple-element.56.sigma_ref, bf16[3,208,384]{2,1,0:T(8,128)(2,1)S(1)} %copy-done.1, ...), custom_call_target="tpu_custom_call" | custom-call | bytes 3000000 | tf_op jit(solution)/shard_map/rest/pallas_call | solution.py:704
  20.4 1.3 %collective-permute-done.2.refs_8_ = f32[40,128]{1,0:T(8,128)S(1)} collective-permute-done((f32[40,128]{1,0:T(8,128)S(1)}, f32[40,128]{1,0:T(8,128)S(1)}, u32[]{:S(2)}, u32[]{:S(2)}) %collective-permute-start.2) | collective-permute-done | bytes 20512 | tf_op jit(solution)/shard_map/ppermute | solution.py:727
  21.6 0.9 %step.4 = (f32[6,125,128]{2,1,0:T(8,128)S(1)}, f32[384,384]{1,0:T(8,128)S(1)}, f32[40,128]{1,0:T(8,128)S(1)}, f32[40,128]{1,0:T(8,128)S(1)}, f32[5,125,128]{2,1,...) custom-call(f32[125,128]{1,0:T(8,128)S(1)} %copy-done.2, f32[125,128]{1,0:T(8,128)S(1)} %copy-done.3, ...), custom_call_target="tpu_custom_call" | custom-call | bytes 3000000 | tf_op jit(solution)/shard_map/step/pallas_call | solution.py:704
  22.6 3.5 %collective-permute-start.5 = (f32[40,128]{1,0:T(8,128)S(1)}, f32[40,128]{1,0:T(8,128)S(1)}, u32[]{:S(2)}, u32[]{:S(2)}) collective-permute-start(f32[40,128]{1,0:T(8,128)S(1)} %get-tuple-element.85), channel_id=1, source_target_pairs={{1,2},{2,1},{3,4},{4,3},{5,6},{6,5},{7,8},{8,7},{9,10},{10,9},{11,... | collective-permute-start | bytes 61448 | tf_op jit(solution)/shard_map/ppermute | solution.py:727
  26.1 1.2 %rest.4 = (f32[3,208,128]{2,1,0:T(8,128)S(1)}, f32[3,208,128]{2,1,0:T(8,128)S(1)}, f32[3,128,128]{2,1,0:T(8,128)S(1)}, f32[384,384]{1,0:T(8,128)S(1)}) custom-call(f32[384,384]{1,0:T(8,128)S(1)} %get-tuple-element.74.sigma_ref, bf16[3,208,384]{2,1,0:T(8,128)(2,1)S(1)} %copy-done.1, f32[3,208,128]{2,1,0:T(8,128)S(1)} %get-tuple-element.75.partial_ref, ...), custom_call_target="tpu_custom_call" | custom-call | bytes 3000000 | tf_op jit(solution)/shard_map/rest/pallas_call | solution.py:704
  27.3 0.4 %parts.3.both_ref = f32[256,128]{1,0:T(8,128)S(1)} custom-call(f32[6,125,128]{2,1,0:T(8,128)S(1)} %get-tuple-element.81.strain_ref, bf16[3,128,128]{2,1,0:T(8,128)(2,1)S(1)} %get-tuple-element.82.low_ref, bf16[3,128,128]{2,1,0:T(8,128)(2,1)S(1)} %collective-permute-done.4.far_ref, f32[125,128]{1,0:T(8,128)S(1)} %copy-done.2, f32[125,128]{1,0:T(8,128)S(1)} %copy-done.3, ...), custom_call_target="tpu_custom_call" | custom-call | bytes 3000000 | tf_op jit(solution)/shard_map/parts/pallas_call | solution.py:704
  27.8 2.3 %collective-permute-done.5.odd_ref = f32[40,128]{1,0:T(8,128)S(1)} collective-permute-done((f32[40,128]{1,0:T(8,128)S(1)}, f32[40,128]{1,0:T(8,128)S(1)}, u32[]{:S(2)}, u32[]{:S(2)}) %collective-permute-start.5) | collective-permute-done | bytes 20512 | tf_op jit(solution)/shard_map/ppermute | solution.py:727
  30.4 0.7 %step.5 = (f32[6,125,128]{2,1,0:T(8,128)S(1)}, f32[384,384]{1,0:T(8,128)S(1)}, f32[40,128]{1,0:T(8,128)S(1)}) custom-call(f32[125,128]{1,0:T(8,128)S(1)} %copy-done.2, f32[125,128]{1,0:T(8,128)S(1)} %copy-done.3, f32[5,125,128]{2,1,0:T(8,128)S(1)} %get-tuple-element.66.refs_2_, f32[3,128]{1,0:T(4,128)S(1)} %copy-done.11, bf16[384,240]{1,0:T(8,128)(2,1)S(1)} %copy-done.5, ...), custom_call_target="tpu_custom_call" | custom-call | bytes 3000000 | tf_op jit(solution)/shard_map/step/pallas_call | solution.py:704
  31.1 0.6 %collective-permute-done.8.far_ref = bf16[3,128,128]{2,1,0:T(8,128)(2,1)S(1)} collective-permute-done((bf16[3,128,128]{2,1,0:T(8,128)(2,1)S(1)}, bf16[3,128,128]{2,1,0:T(8,128)(2,1)S(1)}, u32[]{:S(2)}, u32[]{:S(2)}) %collective-permute-start.8) | collective-permute-done | bytes 98336 | tf_op jit(solution)/shard_map/ppermute | solution.py:718
  31.7 0.7 %send.1 = (f32[256,128]{1,0:T(8,128)S(1)}, s16[128,128]{1,0:T(8,128)(2,1)S(1)}, s16[128,128]{1,0:T(8,128)(2,1)S(1)}, s16[128,128]{1,0:T(8,128)(2,1)S(1)}) custom-call(f32[6,125,128]{2,1,0:T(8,128)S(1)} %get-tuple-element.94.strain_ref, bf16[3,128,128]{2,1,0:T(8,128)(2,1)S(1)} %get-tuple-element.95.low_ref, ...), custom_call_target="tpu_custom_call" | custom-call | bytes 3000000 | tf_op jit(solution)/shard_map/send/pallas_call | solution.py:704
  32.4 0.5 %collective-permute-start.9 = (s16[128,128]{1,0:T(8,128)(2,1)S(1)}, s16[128,128]{1,0:T(8,128)(2,1)S(1)}, u32[]{:S(2)}, u32[]{:S(2)}) collective-permute-start(s16[128,128]{1,0:T(8,128)(2,1)S(1)} %get-tuple-element.98), channel_id=1, source_target_pairs={{0,3},{1,2},{2,1},{3,0},{4,7},{5,6},{6,5},{7,4},{8,11},{9,10},{10,... | collective-permute-start | bytes 98312 | tf_op jit(solution)/shard_map/ppermute | solution.py:839
  32.9 1.0 %collective-permute-start.10 = (s16[128,128]{1,0:T(8,128)(2,1)S(1)}, s16[128,128]{1,0:T(8,128)(2,1)S(1)}, u32[]{:S(2)}, u32[]{:S(2)}) collective-permute-start(s16[128,128]{1,0:T(8,128)(2,1)S(1)} %get-tuple-element.99), channel_id=1, source_target_pairs={{0,2},{1,3},{2,0},{3,1},{4,6},{5,7},{6,4},{7,5},{8,10},{9,11},{10,... | collective-permute-start | bytes 98312 | tf_op jit(solution)/shard_map/ppermute | solution.py:839
  34.0 2.9 %collective-permute-start.11 = (s16[128,128]{1,0:T(8,128)(2,1)S(1)}, s16[128,128]{1,0:T(8,128)(2,1)S(1)}, u32[]{:S(2)}, u32[]{:S(2)}) collective-permute-start(s16[128,128]{1,0:T(8,128)(2,1)S(1)} %get-tuple-element.100), channel_id=1, source_target_pairs={{0,1},{1,0},{2,3},{3,2},{4,5},{5,4},{6,7},{7,6},{8,9},{9,8},{10,11... | collective-permute-start | bytes 98312 | tf_op jit(solution)/shard_map/ppermute | solution.py:839
  36.9 0.7 %rest.5.partial_ref = f32[3,208,128]{2,1,0:T(8,128)S(1)} custom-call(f32[384,384]{1,0:T(8,128)S(1)} %get-tuple-element.91.sigma_ref, bf16[3,208,384]{2,1,0:T(8,128)(2,1)S(1)} %copy-done.1, f32[3,208,128]{2,1,0:T(8,128)S(1)} %get-tuple-element.92.partial_ref, f32[3,40,128]{2,1,0:T(8,128)S(1)} %get-tuple-element.88.refs_7_.delta_ref, ...), custom_call_target="tpu_custom_call" | custom-call | bytes 3000000 | tf_op jit(solution)/shard_map/rest/pallas_call | solution.py:704
  37.6 0.8 %nodal.1.nodal_ref = f32[24,1089]{1,0:T(8,128)S(1)} custom-call(f32[3,208,128]{2,1,0:T(8,128)S(1)} %rest.5.partial_ref, bf16[256,1664]{1,0:T(8,128)(2,1)S(1)} %get-tuple-element.55.refs_9_.spread_ref), custom_call_target="tpu_custom_call" | custom-call | bytes 3000000 | tf_op jit(solution)/shard_map/nodal/pallas_call | solution.py:704
  38.5 1.3 %finish.1 = f32[1,3,8,1089]{3,2,1,0:T(8,128)} custom-call(f32[40,128]{1,0:T(8,128)S(1)} %collective-permute-done.7.before_ref, f32[24,1089]{1,0:T(8,128)S(1)} %nodal.1.nodal_ref, f32[8,1089]{1,0:T(8,128)S(1)} %copy-done.10, f32[1,1089]{1,0:T(1,128)S(1)} %copy-done.12, bf16[256,1664]{1,0:T(8,128)(2,1)S(1)} %get-tuple-element.55.refs_9_.spread_ref), custom_call_target="tpu_custom_call" | custom-call | flops 250000000 | bytes 3000000 | tf_op jit(solution)/shard_map/finish/pallas_call | solution.py:704
  40.0 1.0 %sum.1 = f32[250,1,256]{2,1,0:T(1,128)} custom-call(s16[128,128]{1,0:T(8,128)(2,1)S(1)} %collective-permute-done.9.refs_0_, s16[128,128]{1,0:T(8,128)(2,1)S(1)} %collective-permute-done.10.refs_1_, s16[128,128]{1,0:T(8,128)(2,1)S(1)} %collective-permute-done.11.refs_2_, f32[128,128]{1,0:T(8,128)S(1)} %own.1.refs_3_), custom_call_target="tpu_custom_call" | custom-call | bytes 3000000 | tf_op jit(solution)/shard_map/sum/pallas_call | solution.py:704
  (46 shorter events, 1.6 us)
Async XLA Ops:
  0.6 9.5 %copy-start.9 = (f32[208,128]{1,0:T(8,128)S(1)}, f32[208,128]{1,0:T(8,128)}, u32[]{:S(2)}) copy-start(f32[208,128]{1,0:T(8,128)} %constant.20.clone.mass_ref) | copy-start | bytes 319492
  0.6 9.5 %copy-start.10 = (f32[8,1089]{1,0:T(8,128)S(1)}, f32[8,1089]{1,0:T(8,128)}, u32[]{:S(2)}) copy-start(f32[8,1089]{1,0:T(8,128)} %density_ref.5) | copy-start | bytes 104548
  1.7 8.4 %copy-start = (bf16[3,384,256]{2,1,0:T(8,128)(2,1)S(1)}, bf16[3,384,256]{2,1,0:T(8,128)(2,1)}, u32[]{:S(2)}) copy-start(bf16[3,384,256]{2,1,0:T(8,128)(2,1)} %constant.14.clone.refs_0_.grad_table) | copy-start | bytes 1769476
  1.7 8.4 %copy-start.1 = (bf16[3,208,384]{2,1,0:T(8,128)(2,1)S(1)}, bf16[3,208,384]{2,1,0:T(8,128)(2,1)}, u32[]{:S(2)}) copy-start(bf16[3,208,384]{2,1,0:T(8,128)(2,1)} %constant.15.clone.refs_2_.force_table) | copy-start | bytes 1437700
  1.7 8.4 %copy-start.2 = (f32[125,128]{1,0:T(8,128)S(1)}, f32[125,128]{1,0:T(8,128)}, u32[]{:S(2)}) copy-start(f32[125,128]{1,0:T(8,128)} %lame_ref.5) | copy-start | bytes 192004
  1.7 8.4 %copy-start.3 = (f32[125,128]{1,0:T(8,128)S(1)}, f32[125,128]{1,0:T(8,128)}, u32[]{:S(2)}) copy-start(f32[125,128]{1,0:T(8,128)} %mu_ref.5) | copy-start | bytes 192004
  1.7 8.4 %copy-start.4 = (bf16[3,80,256]{2,1,0:T(8,128)(2,1)S(1)}, bf16[3,80,256]{2,1,0:T(8,128)(2,1)}, u32[]{:S(2)}) copy-start(bf16[3,80,256]{2,1,0:T(8,128)(2,1)} %constant.16.clone.refs_1_.refs_5_) | copy-start | bytes 368644
  1.7 8.4 %copy-start.5 = (bf16[384,240]{1,0:T(8,128)(2,1)S(1)}, bf16[384,240]{1,0:T(8,128)(2,1)}, u32[]{:S(2)}) copy-start(bf16[384,240]{1,0:T(8,128)(2,1)} %constant.17.clone.refs_4_) | copy-start | bytes 552964
  1.8 8.4 %copy-start.6 = (bf16[384,240]{1,0:T(8,128)(2,1)S(1)}, bf16[384,240]{1,0:T(8,128)(2,1)}, u32[]{:S(2)}) copy-start(bf16[384,240]{1,0:T(8,128)(2,1)} %constant.18.clone.refs_3_.refs_4_) | copy-start | bytes 552964
  1.8 8.4 %copy-start.7 = (f32[1,3,8,1089]{3,2,1,0:T(8,128)S(1)}, f32[1,3,8,1089]{3,2,1,0:T(8,128)}, u32[]{:S(2)}) copy-start(f32[1,3,8,1089]{3,2,1,0:T(8,128)} %now_ref.3) | copy-start | bytes 313636
  1.8 8.4 %copy-start.8 = (f32[1,3,8,1089]{3,2,1,0:T(8,128)S(1)}, f32[1,3,8,1089]{3,2,1,0:T(8,128)}, u32[]{:S(2)}) copy-start(f32[1,3,8,1089]{3,2,1,0:T(8,128)} %prev_ref.3) | copy-start | bytes 313636
  1.8 11.1 %collective-permute-start = (f32[8,1089]{1,0:T(8,128)S(1)}, f32[8,1089]{1,0:T(8,128)S(1)}, u32[]{:S(2)}, u32[]{:S(2)}) collective-permute-start(f32[8,1089]{1,0:T(8,128)S(1)} %gather.1), channel_id=1, source_target_pairs={{0,15},{1,0},{2,1},{3,2},{4,3},{5,4},{6,5},{7,6},{8,7},{9,8},{10,9... | collective-permute-start | bytes 104552 | tf_op jit(solution)/shard_map/ppermute | solution.py:718
  8.8 1.4 %copy-start.11 = (f32[3,128]{1,0:T(4,128)S(1)}, f32[3,128]{1,0:T(4,128)}, u32[]{:S(2)}) copy-start(f32[3,128]{1,0:T(4,128)} %refs_3_.6) | copy-start | bytes 4612
  14.1 5.8 %collective-permute-start.1 = (bf16[3,128,128]{2,1,0:T(8,128)(2,1)S(1)}, bf16[3,128,128]{2,1,0:T(8,128)(2,1)S(1)}, u32[]{:S(2)}, u32[]{:S(2)}) collective-permute-start(bf16[3,128,128]{2,1,0:T(8,128)(2,1)S(1)} %get-tuple-element.63.low_ref), channel_id=1, source_target_pairs={{0,16},{16,0},{1,17},{17,1},{2,18},{18,2},{3,19},{19,3},{4,20},{20... | collective-permute-start | bytes 294920 | tf_op jit(solution)/shard_map/ppermute | solution.py:718
  14.2 7.4 %collective-permute-start.2 = (f32[40,128]{1,0:T(8,128)S(1)}, f32[40,128]{1,0:T(8,128)S(1)}, u32[]{:S(2)}, u32[]{:S(2)}) collective-permute-start(f32[40,128]{1,0:T(8,128)S(1)} %get-tuple-element.70), channel_id=1, source_target_pairs={{1,2},{2,1},{3,4},{4,3},{5,6},{6,5},{7,8},{8,7},{9,10},{10,9},{11,... | collective-permute-start | bytes 61448 | tf_op jit(solution)/shard_map/ppermute | solution.py:727
  17.7 4.0 %collective-permute-start.3 = (f32[40,128]{1,0:T(8,128)S(1)}, f32[40,128]{1,0:T(8,128)S(1)}, u32[]{:S(2)}, u32[]{:S(2)}) collective-permute-start(f32[40,128]{1,0:T(8,128)S(1)} %get-tuple-element.71), channel_id=1, source_target_pairs={{0,1},{1,0},{2,3},{3,2},{4,5},{5,4},{6,7},{7,6},{8,9},{9,8},{10,11... | collective-permute-start | bytes 61448 | tf_op jit(solution)/shard_map/ppermute | solution.py:727
  22.6 4.8 %collective-permute-start.4 = (bf16[3,128,128]{2,1,0:T(8,128)(2,1)S(1)}, bf16[3,128,128]{2,1,0:T(8,128)(2,1)S(1)}, u32[]{:S(2)}, u32[]{:S(2)}) collective-permute-start(bf16[3,128,128]{2,1,0:T(8,128)(2,1)S(1)} %get-tuple-element.82.low_ref), channel_id=1, source_target_pairs={{0,16},{16,0},{1,17},{17,1},{2,18},{18,2},{3,19},{19,3},{4,20},{20... | collective-permute-start | bytes 294920 | tf_op jit(solution)/shard_map/ppermute | solution.py:718
  22.6 7.4 %collective-permute-start.5 = (f32[40,128]{1,0:T(8,128)S(1)}, f32[40,128]{1,0:T(8,128)S(1)}, u32[]{:S(2)}, u32[]{:S(2)}) collective-permute-start(f32[40,128]{1,0:T(8,128)S(1)} %get-tuple-element.85), channel_id=1, source_target_pairs={{1,2},{2,1},{3,4},{4,3},{5,6},{6,5},{7,8},{8,7},{9,10},{10,9},{11,... | collective-permute-start | bytes 61448 | tf_op jit(solution)/shard_map/ppermute | solution.py:727
  26.1 4.0 %collective-permute-start.6 = (f32[40,128]{1,0:T(8,128)S(1)}, f32[40,128]{1,0:T(8,128)S(1)}, u32[]{:S(2)}, u32[]{:S(2)}) collective-permute-start(f32[40,128]{1,0:T(8,128)S(1)} %get-tuple-element.86), channel_id=1, source_target_pairs={{0,1},{1,0},{2,3},{3,2},{4,5},{5,4},{6,7},{7,6},{8,9},{9,8},{10,11... | collective-permute-start | bytes 61448 | tf_op jit(solution)/shard_map/ppermute | solution.py:727
  30.3 1.4 %collective-permute-start.8 = (bf16[3,128,128]{2,1,0:T(8,128)(2,1)S(1)}, bf16[3,128,128]{2,1,0:T(8,128)(2,1)S(1)}, u32[]{:S(2)}, u32[]{:S(2)}) collective-permute-start(bf16[3,128,128]{2,1,0:T(8,128)(2,1)S(1)} %get-tuple-element.95.low_ref), channel_id=1, source_target_pairs={{0,16},{16,0},{1,17},{17,1},{2,18},{18,2},{3,19},{19,3},{4,20},{20... | collective-permute-start | bytes 294920 | tf_op jit(solution)/shard_map/ppermute | solution.py:718
  31.1 7.4 %collective-permute-start.7 = (f32[40,128]{1,0:T(8,128)S(1)}, f32[40,128]{1,0:T(8,128)S(1)}, u32[]{:S(2)}, u32[]{:S(2)}) collective-permute-start(f32[40,128]{1,0:T(8,128)S(1)} %get-tuple-element.90), channel_id=1, source_target_pairs={{0,1},{1,2},{2,3},{3,4},{4,5},{5,6},{6,7},{7,8},{8,9},{9,10},{10,1... | collective-permute-start | bytes 61448 | tf_op jit(solution)/shard_map/ppermute | solution.py:718
  32.4 7.6 %collective-permute-start.9 = (s16[128,128]{1,0:T(8,128)(2,1)S(1)}, s16[128,128]{1,0:T(8,128)(2,1)S(1)}, u32[]{:S(2)}, u32[]{:S(2)}) collective-permute-start(s16[128,128]{1,0:T(8,128)(2,1)S(1)} %get-tuple-element.98), channel_id=1, source_target_pairs={{0,3},{1,2},{2,1},{3,0},{4,7},{5,6},{6,5},{7,4},{8,11},{9,10},{10,... | collective-permute-start | bytes 98312 | tf_op jit(solution)/shard_map/ppermute | solution.py:839
  32.9 7.1 %collective-permute-start.10 = (s16[128,128]{1,0:T(8,128)(2,1)S(1)}, s16[128,128]{1,0:T(8,128)(2,1)S(1)}, u32[]{:S(2)}, u32[]{:S(2)}) collective-permute-start(s16[128,128]{1,0:T(8,128)(2,1)S(1)} %get-tuple-element.99), channel_id=1, source_target_pairs={{0,2},{1,3},{2,0},{3,1},{4,6},{5,7},{6,4},{7,5},{8,10},{9,11},{10,... | collective-permute-start | bytes 98312 | tf_op jit(solution)/shard_map/ppermute | solution.py:839
  34.0 6.0 %collective-permute-start.11 = (s16[128,128]{1,0:T(8,128)(2,1)S(1)}, s16[128,128]{1,0:T(8,128)(2,1)S(1)}, u32[]{:S(2)}, u32[]{:S(2)}) collective-permute-start(s16[128,128]{1,0:T(8,128)(2,1)S(1)} %get-tuple-element.100), channel_id=1, source_target_pairs={{0,1},{1,0},{2,3},{3,2},{4,5},{5,4},{6,7},{7,6},{8,9},{9,8},{10,11... | collective-permute-start | bytes 98312 | tf_op jit(solution)/shard_map/ppermute | solution.py:839
  (2 other events, 1.6 us)

commit v7 on v6

--- a/solution.py
+++ b/solution.py
@@ -18,6 +18,7 @@
 ROWS = 8 * BLOCKS
 WIDE = 64 * BLOCKS
 JUMP = 4 * SIDE
+WIDE_FACE = 1152
 WINDOW = 256
 
 time_step = 0.03
@@ -97,8 +98,7 @@
                     for slab in range(2):
                         at = (b * 5 + d) * 8
                         mass[at : at + 8, slab * 64 + ey * 8 + ez] = layer * line[4 * ey + b] * line[4 * ez + d]
-    face_mass = (layer[0] * np.outer(line, line)).reshape(1, FACE).astype(np.float32)
-    return grad, force, face, mass, face_mass, share, rim
+    return grad, force, face, mass, share, rim
 
 
 def side_by_side(table):
@@ -117,7 +117,41 @@
     return np.stack(pieces)
 
 
-GRAD, FORCE, FACES, MASS, FACE_MASS, SHARE, RIM = make_tables()
+GRAD, FORCE, FACES, MASS, SHARE, RIM = make_tables()
+
+
+def make_gathers():
+    columns = np.zeros((BLOCKS // 2, LANES), np.int32)
+    for b in range(5):
+        for d in range(5):
+            block = b * 5 + d
+            for ey in range(8):
+                for ez in range(8):
+                    columns[block // 2, (block % 2) * 64 + ey * 8 + ez] = (4 * ey + b) * SIDE + 4 * ez + d
+    nodes = np.zeros((WIDE_FACE // LANES, LANES), np.int32)
+    for y in range(SIDE):
+        for z in range(SIDE):
+            ey, ez = min(y // 4, 7), min(z // 4, 7)
+            block = (y - 4 * ey) * 5 + z - 4 * ez
+            spot = y * SIDE + z
+            nodes[spot // LANES, spot % LANES] = (block // 2) * LANES + (block % 2) * 64 + ey * 8 + ez
+    return columns, nodes
+
+
+COLUMN_LANES, NODE_LANES = make_gathers()
+
+
+def gathered(tiles, table, table_ref):
+    results = []
+    for row in range(table.shape[0]):
+        spots = jnp.broadcast_to(table_ref[row : row + 1, :], (8, LANES))
+        tile_of, lane_of = spots // LANES, spots % LANES
+        value = jnp.zeros((8, LANES), F32)
+        for at in sorted(set((table[row] // LANES).tolist())):
+            moved = jnp.take_along_axis(tiles[at], lane_of, axis=1, mode="promise_in_bounds")
+            value = jnp.where(tile_of == at, moved, value)
+        results.append(value)
+    return results
 
 
 def cut(value):
@@ -221,11 +255,12 @@
         copy.start()
     for copy in copies:
         copy.wait()
-    for c in range(3):
-        rim_ref[c : c + 1, :] = now_copy[c, 0:1, :]
-        rim_ref[3 + c : 4 + c, :] = prev_copy[c, 0:1, :]
-    rim_ref[6:7, :] = density_copy[0:1, :]
-    rim_ref[7:8, :] = density_copy[0:1, :]
+    rim_ref[:, 1024:] = jnp.zeros((8, WIDE_FACE - 1024), F32)
+    for c in range(3):
+        rim_ref[c : c + 1, 0:FACE] = now_copy[c, 0:1, :]
+        rim_ref[3 + c : 4 + c, 0:FACE] = prev_copy[c, 0:1, :]
+    rim_ref[6:7, 0:FACE] = density_copy[0:1, :]
+    rim_ref[7:8, 0:FACE] = density_copy[0:1, :]
 
 
 def weighted_memory(memory_ref, decays, part, power):
@@ -299,10 +334,9 @@
     select_ref[...] = jnp.where(chosen, 1.0, 0.0).astype(BF16)
 
 
-def rim_rows(rim_ref, spread_ref, window_ref, rows_ref):
-    columns = to_columns(rim_ref[...], window_ref, spread_ref)
-    for pair in range(BLOCKS // 2):
-        tile = columns[:, LANES * pair : LANES * pair + LANES]
+def rim_rows(rim_ref, lanes_ref, rows_ref):
+    tiles = [rim_ref[:, at : at + LANES] for at in range(0, WIDE_FACE, LANES)]
+    for pair, tile in enumerate(gathered(tiles, COLUMN_LANES, lanes_ref)):
         rows_ref[16 * pair : 16 * pair + 8, :] = rolled(tile, 64, 1)
         rows_ref[16 * pair + 8 : 16 * pair + 16, :] = tile
 
@@ -323,22 +357,23 @@
     odd, even = odd_ref[...], even_ref[...]
     lower = (lanes_of((40, LANES)) < 64) == even_ring
     rows = unpack_face(jnp.where(lower, odd, even), rolled(jnp.where(lower, even, odd), 64, 1))
+    return [assembled_lines(lines, face_scale_ref) for lines in rows]
+
+
+def assembled_lines(lines, face_scale_ref):
     lane = lanes_of((8, LANES))
     sub = lax.broadcasted_iota(jnp.int32, (8, LANES), 0)
     ez, ey = lane % 8, (lane // 8) % 8
     up, down = (sub == 0) & (ey > 0), (sub == 4) & (ey < 7)
-    shares = []
-    for c in range(3):
-        lines = rows[c]
-        first, last = lines[0], lines[4]
-        lines[0] = first + jnp.where(ez > 0, rolled(last, 1, 1), 0.0)
-        lines[4] = last + jnp.where(ez < 7, rolled(first, -1, 1), 0.0)
-        for d in range(5):
-            turned = rolled(lines[d], 4, 0)
-            added = jnp.where(up, rolled(turned, 8, 1), jnp.where(down, rolled(turned, -8, 1), 0.0))
-            lines[d] = face_scale_ref[8 * d : 8 * d + 8, :] * (lines[d] + added)
-        shares.append(lines)
-    return shares
+    first, last = lines[0], lines[4]
+    lines = list(lines)
+    lines[0] = first + jnp.where(ez > 0, rolled(last, 1, 1), 0.0)
+    lines[4] = last + jnp.where(ez < 7, rolled(first, -1, 1), 0.0)
+    for d in range(5):
+        turned = rolled(lines[d], 4, 0)
+        added = jnp.where(up, rolled(turned, 8, 1), jnp.where(down, rolled(turned, -8, 1), 0.0))
+        lines[d] = face_scale_ref[8 * d : 8 * d + 8, :] * (lines[d] + added)
+    return lines
 
 
 def strains(grad, rows):
@@ -396,11 +431,11 @@
     strain_ref, sigma_ref, even_ref = refs[0:3]
     if step < STEPS - 1:
         odd_ref, keep_ref, low_ref, extra_ref = refs[3:7]
-    grad_ref, flat_ref, window_ref, rim_ref = refs[-4:]
+    grad_ref, flat_ref, rim_ref = refs[-3:]
     upper = lanes_of((40, 3 * LANES)) % LANES >= 64
     if step == 0:
         flat_ref[...] = arrived[0][...]
-        rim_rows(arrived[1], arrived[2], window_ref, extra_ref)
+        rim_rows(arrived[1], arrived[2], extra_ref)
         rim_ref[...] = jnp.zeros(rim_ref.shape, F32)
         for c in range(3):
             for d in range(5):
@@ -672,24 +707,24 @@
     to_nodal(jnp.where(once, columns, 0.0), spread_ref, nodal_ref)
 
 
-def finish_kernel(before_ref, nodal_ref, density_ref, face_mass_ref, spread_ref, out_ref, rows_ref, face_ref):
+def finish_kernel(before_ref, nodal_ref, face_scale_ref, lanes_ref, out_ref, rows_ref, face_ref):
     packed = before_ref[...]
     values = unpack_face(packed, rolled(packed, 64, 1))
     rows_ref[...] = jnp.zeros(rows_ref.shape, F32)
     for c in range(3):
+        lines = assembled_lines(values[c], face_scale_ref)
         for d in range(5):
-            rows_ref[pl.ds(8 * d + c, 5, stride=40), :] = values[c][d][0:5]
+            rows_ref[pl.ds(8 * d + c, 5, stride=40), :] = lines[d][0:5]
     lane = lanes_of((8, LANES))
     tiles = []
     for pair in range(BLOCKS // 2):
         even, odd = rows_ref[16 * pair : 16 * pair + 8, :], rows_ref[16 * pair + 8 : 16 * pair + 16, :]
         tiles.append(jnp.where(lane < 64, even, rolled(odd, 64, 1)))
-    to_nodal(jnp.concatenate(tiles, axis=1), spread_ref, face_ref)
-    scale = step_square / (density_ref[0:1, :] * face_mass_ref[...])
+    for at, tile in enumerate(gathered(tiles, NODE_LANES, lanes_ref)):
+        face_ref[:, LANES * at : LANES * at + LANES] = tile
     first = lax.broadcasted_iota(jnp.int32, (8, FACE), 0) == 0
     for c in range(3):
-        share = face_ref[c : c + 1, :] * scale
-        out_ref[0, c] = nodal_ref[8 * c : 8 * c + 8, :] + jnp.where(first, share, 0.0)
+        out_ref[0, c] = nodal_ref[8 * c : 8 * c + 8, :] + jnp.where(first, face_ref[c : c + 1, 0:FACE], 0.0)
 
 
 VMEM = pl.BlockSpec(memory_space=pltpu.VMEM)
@@ -741,7 +776,7 @@
     groups = lax.axis_size("group")
 
     rim = call(
-        gather_kernel, "gather", shaped(8, FACE),
+        gather_kernel, "gather", shaped(8, WIDE_FACE),
         [pltpu.VMEM((3, 8, FACE), F32)] * 2 + [pltpu.VMEM((8, FACE), F32), pltpu.SemaphoreType.DMA((3,))],
         disp_now, disp_prev, density, outside=(0, 1, 2), room=54 * 1024 - 120,
     )
@@ -752,7 +787,8 @@
     face_table = jnp.asarray(cut_table(FACES))
     share_table = jnp.asarray(SHARE)
     rim_table = jnp.asarray(RIM)
-    face_mass = jnp.asarray(FACE_MASS)
+    column_lanes = jnp.asarray(COLUMN_LANES)
+    node_lanes = jnp.asarray(NODE_LANES)
     mass = jnp.asarray(MASS)
     memory = memory_init[0]
     owner = jnp.transpose(owner_map, (0, 2, 1))
@@ -785,13 +821,13 @@
             far = far_field(low, groups)
             arrived = (extra,)
         else:
-            arrived = (flat, rim, spread) if step == 0 else (flat, odd, even, face_scale)
+            arrived = (flat, rim, column_lanes) if step == 0 else (flat, odd, even, face_scale)
         outs = [shaped(6, 125, LANES), grad_shape, face]
         if not last_step:
             outs += [face, five, low_shape, scale_shape if step == 0 else shaped(3, 40, LANES)]
         results = call(
             lambda *refs, step=step: step_kernel(step, *refs), "step", outs,
-            [grad_scratch, pltpu.VMEM((3, 128, LANES), F32), pltpu.VMEM((8, 8, WINDOW), F32), pltpu.VMEM((40, 384), F32)],
+            [grad_scratch, pltpu.VMEM((3, 128, LANES), F32), pltpu.VMEM((40, 384), F32)],
             lame_lambda, shear_mu, memories[step], sls_decay, rim_table if step == 0 else share_table, face_table, base, *arrived, *kept,
         )
         strain, sigma, even = results[0:3]
@@ -840,8 +876,8 @@
             sent.append(call(own_kernel, "own", shaped(rows, LANES), [], total, select))
     nodal = call(nodal_kernel, "nodal", shaped(24, FACE), [], partial, spread)
     final = call(
-        finish_kernel, "finish", shaped(1, 3, 8, FACE), [pltpu.VMEM((ROWS, LANES), F32), pltpu.VMEM((8, FACE), F32)],
-        before, nodal, density, face_mass, spread, flops=250000000,
+        finish_kernel, "finish", shaped(1, 3, 8, FACE), [pltpu.VMEM((ROWS, LANES), F32), pltpu.VMEM((8, WIDE_FACE), F32)],
+        before, nodal, face_scale, node_lanes, flops=250000000,
     )
     kernels = call(
         lambda *refs: sum_kernel(order, *refs), "sum", shaped(250, 1, 256), [], *sent

time: 41.2 us -> 41 us (level)
    unnamed x29 -> x31, local copies, waits for them, and re-layouts: 2.05 us -> 2.05 us
where the time goes in v7:
time: 41 us; the launch traced here: 40.8 us
  starting transfers between devices  18.6 us (45%)
  Pallas kernels  15 us (37%)
  waiting for transfers between devices  4.23 us (10%)
  local copies, waits for them, and re-layouts  2.05 us (5%)
  between operations  1.01 us (2%)
    pallas_call x17, Pallas kernels, call(): pl.pallas_call(kernel, name=name, out_shape=outs, in_specs=[HBM if at in...  15 us
    ppermute x5, starting transfers between devices, passed_along(): lax.ppermute(value, axis, [(source, (source + steps) % count) for source...  7.2 us
    ppermute x4, starting transfers between devices, swapped(): return lax.ppermute(value, axis, pairs)  6.89 us
    ppermute x3, starting transfers between devices, per_device(): lax.ppermute(blocks[k - 1], 'sub', [(j, j ^ k) for j in range(subs)])  4.45 us
    ppermute x4, waiting for transfers between devices, swapped(): return lax.ppermute(value, axis, pairs)  3.62 us
    unnamed x31, local copies, waits for them, and re-layouts  2.05 us
  transfers between devices with their start and end apart: 12, of which 3 were waited for; matrix products, arithmetic and copies ran while one was open for 3% of the time, Pallas kernels for 25%

profile of v7, /device:TPU:0, one launch (start us, length us, event | category | flops | bytes accessed | tf_op | source)
XLA Modules:
  0.0 40.8 jit_solution(9362062844859042865)
XLA Ops:
  0.7 1.0 %gather.1 = f32[8,1152]{1,0:T(8,128)S(1)} custom-call(f32[1,3,8,1089]{3,2,1,0:T(8,128)} %now_ref.3, f32[1,3,8,1089]{3,2,1,0:T(8,128)} %prev_ref.3, f32[8,1089]{1,0:T(8,128)} %density_ref.3), custom_call_target="tpu_custom_call" | custom-call | bytes 3000000 | tf_op jit(solution)/shard_map/gather/pallas_call | solution.py:739
  1.8 7.0 %collective-permute-start = (f32[8,1152]{1,0:T(8,128)S(1)}, f32[8,1152]{1,0:T(8,128)S(1)}, u32[]{:S(2)}, u32[]{:S(2)}) collective-permute-start(f32[8,1152]{1,0:T(8,128)S(1)} %gather.1), channel_id=1, source_target_pairs={{0,15},{1,0},{2,1},{3,2},{4,3},{5,4},{6,5},{7,6},{8,7},{9,8},{10,9... | collective-permute-start | bytes 110600 | tf_op jit(solution)/shard_map/ppermute | solution.py:753
  8.8 1.3 %copy.21 = f32[1,3,5,125,128]{4,3,0,2,1:T(8,128)S(1)} copy(f32[1,3,5,125,128]{4,0,3,2,1:T(1,128)} %param.18) | data formatting | bytes 1920000
  10.2 2.7 %prologue.1 = (f32[3,208,128]{2,1,0:T(8,128)S(1)}, f32[3,208,128]{2,1,0:T(8,128)S(1)}, f32[208,128]{1,0:T(8,128)S(1)}, f32[5,125,128]{2,1,0:T(8,128)S(1)}, bf16[...) custom-call(f32[1,3,8,1089]{3,2,1,0:T(8,128)S(1)} %copy-done.7, ...), custom_call_target="tpu_custom_call" | custom-call | bytes 3000000 | tf_op jit(solution)/shard_map/prologue/pallas_call | solution.py:739
  12.9 1.1 %step.3 = (f32[6,125,128]{2,1,0:T(8,128)S(1)}, f32[384,384]{1,0:T(8,128)S(1)}, f32[40,128]{1,0:T(8,128)S(1)}, f32[40,128]{1,0:T(8,128)S(1)}, f32[5,125,128]{2,1,...) custom-call(f32[125,128]{1,0:T(8,128)S(1)} %copy-done.2, f32[125,128]{1,0:T(8,128)S(1)} %copy-done.3, ...), custom_call_target="tpu_custom_call" | custom-call | bytes 3000000 | tf_op jit(solution)/shard_map/step/pallas_call | solution.py:739
  14.1 3.4 %collective-permute-start.2 = (f32[40,128]{1,0:T(8,128)S(1)}, f32[40,128]{1,0:T(8,128)S(1)}, u32[]{:S(2)}, u32[]{:S(2)}) collective-permute-start(f32[40,128]{1,0:T(8,128)S(1)} %get-tuple-element.69), channel_id=1, source_target_pairs={{1,2},{2,1},{3,4},{4,3},{5,6},{6,5},{7,8},{8,7},{9,10},{10,9},{11,... | collective-permute-start | bytes 61448 | tf_op jit(solution)/shard_map/ppermute | solution.py:762
  17.6 0.7 %copy-done.13 = s32[2,64,1]{1,2,0:T(1,128)S(1)} copy-done((s32[2,64,1]{1,2,0:T(1,128)S(1)}, s32[2,64,1]{1,2,0:T(1,128)}, u32[]{:S(2)}) %copy-start.13) | copy-done | bytes 536
  18.6 1.2 %rest.3 = (f32[3,208,128]{2,1,0:T(8,128)S(1)}, f32[208,128]{1,0:T(8,128)S(1)}, f32[3,208,128]{2,1,0:T(8,128)S(1)}, f32[3,128,128]{2,1,0:T(8,128)S(1)}, f32[384,384]{1,0:T(8,128)S(1)}, /*index=5*/f32[40,128]{1,0:T(8,128)S(1)}) custom-call(f32[384,384]{1,0:T(8,128)S(1)} %get-tuple-element.55.sigma_ref, bf16[3,208,384]{2,1,0:T(8,128)(2,1)S(1)} %copy-done.1, ...), custom_call_target="tpu_custom_call" | custom-call | bytes 3000000 | tf_op jit(solution)/shard_map/rest/pallas_call | solution.py:739
  20.3 1.3 %collective-permute-done.2.refs_8_ = f32[40,128]{1,0:T(8,128)S(1)} collective-permute-done((f32[40,128]{1,0:T(8,128)S(1)}, f32[40,128]{1,0:T(8,128)S(1)}, u32[]{:S(2)}, u32[]{:S(2)}) %collective-permute-start.2) | collective-permute-done | bytes 20512 | tf_op jit(solution)/shard_map/ppermute | solution.py:762
  21.6 0.9 %step.4 = (f32[6,125,128]{2,1,0:T(8,128)S(1)}, f32[384,384]{1,0:T(8,128)S(1)}, f32[40,128]{1,0:T(8,128)S(1)}, f32[40,128]{1,0:T(8,128)S(1)}, f32[5,125,128]{2,1,...) custom-call(f32[125,128]{1,0:T(8,128)S(1)} %copy-done.2, f32[125,128]{1,0:T(8,128)S(1)} %copy-done.3, ...), custom_call_target="tpu_custom_call" | custom-call | bytes 3000000 | tf_op jit(solution)/shard_map/step/pallas_call | solution.py:739
  22.6 3.4 %collective-permute-start.5 = (f32[40,128]{1,0:T(8,128)S(1)}, f32[40,128]{1,0:T(8,128)S(1)}, u32[]{:S(2)}, u32[]{:S(2)}) collective-permute-start(f32[40,128]{1,0:T(8,128)S(1)} %get-tuple-element.84), channel_id=1, source_target_pairs={{1,2},{2,1},{3,4},{4,3},{5,6},{6,5},{7,8},{8,7},{9,10},{10,9},{11,... | collective-permute-start | bytes 61448 | tf_op jit(solution)/shard_map/ppermute | solution.py:762
  26.0 1.2 %rest.4 = (f32[3,208,128]{2,1,0:T(8,128)S(1)}, f32[3,208,128]{2,1,0:T(8,128)S(1)}, f32[3,128,128]{2,1,0:T(8,128)S(1)}, f32[384,384]{1,0:T(8,128)S(1)}) custom-call(f32[384,384]{1,0:T(8,128)S(1)} %get-tuple-element.73.sigma_ref, bf16[3,208,384]{2,1,0:T(8,128)(2,1)S(1)} %copy-done.1, f32[3,208,128]{2,1,0:T(8,128)S(1)} %get-tuple-element.74.partial_ref, ...), custom_call_target="tpu_custom_call" | custom-call | bytes 3000000 | tf_op jit(solution)/shard_map/rest/pallas_call | solution.py:739
  27.2 0.4 %parts.3.both_ref = f32[256,128]{1,0:T(8,128)S(1)} custom-call(f32[6,125,128]{2,1,0:T(8,128)S(1)} %get-tuple-element.80.strain_ref, bf16[3,128,128]{2,1,0:T(8,128)(2,1)S(1)} %get-tuple-element.81.low_ref, bf16[3,128,128]{2,1,0:T(8,128)(2,1)S(1)} %collective-permute-done.4.far_ref, f32[125,128]{1,0:T(8,128)S(1)} %copy-done.2, f32[125,128]{1,0:T(8,128)S(1)} %copy-done.3, ...), custom_call_target="tpu_custom_call" | custom-call | bytes 3000000 | tf_op jit(solution)/shard_map/parts/pallas_call | solution.py:739
  27.7 2.3 %collective-permute-done.5.odd_ref = f32[40,128]{1,0:T(8,128)S(1)} collective-permute-done((f32[40,128]{1,0:T(8,128)S(1)}, f32[40,128]{1,0:T(8,128)S(1)}, u32[]{:S(2)}, u32[]{:S(2)}) %collective-permute-start.5) | collective-permute-done | bytes 20512 | tf_op jit(solution)/shard_map/ppermute | solution.py:762
  30.3 0.7 %step.5 = (f32[6,125,128]{2,1,0:T(8,128)S(1)}, f32[384,384]{1,0:T(8,128)S(1)}, f32[40,128]{1,0:T(8,128)S(1)}) custom-call(f32[125,128]{1,0:T(8,128)S(1)} %copy-done.2, f32[125,128]{1,0:T(8,128)S(1)} %copy-done.3, f32[5,125,128]{2,1,0:T(8,128)S(1)} %get-tuple-element.65.refs_2_, f32[3,128]{1,0:T(4,128)S(1)} %copy-done.11, bf16[384,240]{1,0:T(8,128)(2,1)S(1)} %copy-done.5, ...), custom_call_target="tpu_custom_call" | custom-call | bytes 3000000 | tf_op jit(solution)/shard_map/step/pallas_call | solution.py:739
  31.0 0.6 %collective-permute-done.8.far_ref = bf16[3,128,128]{2,1,0:T(8,128)(2,1)S(1)} collective-permute-done((bf16[3,128,128]{2,1,0:T(8,128)(2,1)S(1)}, bf16[3,128,128]{2,1,0:T(8,128)(2,1)S(1)}, u32[]{:S(2)}, u32[]{:S(2)}) %collective-permute-start.8) | collective-permute-done | bytes 98336 | tf_op jit(solution)/shard_map/ppermute | solution.py:753
  31.6 0.7 %send.1 = (f32[256,128]{1,0:T(8,128)S(1)}, s16[128,128]{1,0:T(8,128)(2,1)S(1)}, s16[128,128]{1,0:T(8,128)(2,1)S(1)}, s16[128,128]{1,0:T(8,128)(2,1)S(1)}) custom-call(f32[6,125,128]{2,1,0:T(8,128)S(1)} %get-tuple-element.94.strain_ref, bf16[3,128,128]{2,1,0:T(8,128)(2,1)S(1)} %get-tuple-element.95.low_ref, ...), custom_call_target="tpu_custom_call" | custom-call | bytes 3000000 | tf_op jit(solution)/shard_map/send/pallas_call | solution.py:739
  32.3 0.5 %collective-permute-start.9 = (s16[128,128]{1,0:T(8,128)(2,1)S(1)}, s16[128,128]{1,0:T(8,128)(2,1)S(1)}, u32[]{:S(2)}, u32[]{:S(2)}) collective-permute-start(s16[128,128]{1,0:T(8,128)(2,1)S(1)} %get-tuple-element.98), channel_id=1, source_target_pairs={{0,3},{1,2},{2,1},{3,0},{4,7},{5,6},{6,5},{7,4},{8,11},{9,10},{10,... | collective-permute-start | bytes 98312 | tf_op jit(solution)/shard_map/ppermute | solution.py:875
  32.9 1.0 %collective-permute-start.10 = (s16[128,128]{1,0:T(8,128)(2,1)S(1)}, s16[128,128]{1,0:T(8,128)(2,1)S(1)}, u32[]{:S(2)}, u32[]{:S(2)}) collective-permute-start(s16[128,128]{1,0:T(8,128)(2,1)S(1)} %get-tuple-element.99), channel_id=1, source_target_pairs={{0,2},{1,3},{2,0},{3,1},{4,6},{5,7},{6,4},{7,5},{8,10},{9,11},{10,... | collective-permute-start | bytes 98312 | tf_op jit(solution)/shard_map/ppermute | solution.py:875
  33.9 2.9 %collective-permute-start.11 = (s16[128,128]{1,0:T(8,128)(2,1)S(1)}, s16[128,128]{1,0:T(8,128)(2,1)S(1)}, u32[]{:S(2)}, u32[]{:S(2)}) collective-permute-start(s16[128,128]{1,0:T(8,128)(2,1)S(1)} %get-tuple-element.100), channel_id=1, source_target_pairs={{0,1},{1,0},{2,3},{3,2},{4,5},{5,4},{6,7},{7,6},{8,9},{9,8},{10,11... | collective-permute-start | bytes 98312 | tf_op jit(solution)/shard_map/ppermute | solution.py:875
  36.8 0.7 %rest.5.partial_ref = f32[3,208,128]{2,1,0:T(8,128)S(1)} custom-call(f32[384,384]{1,0:T(8,128)S(1)} %get-tuple-element.90.sigma_ref, bf16[3,208,384]{2,1,0:T(8,128)(2,1)S(1)} %copy-done.1, f32[3,208,128]{2,1,0:T(8,128)S(1)} %get-tuple-element.91.partial_ref, f32[3,40,128]{2,1,0:T(8,128)S(1)} %get-tuple-element.87.refs_7_.delta_ref, ...), custom_call_target="tpu_custom_call" | custom-call | bytes 3000000 | tf_op jit(solution)/shard_map/rest/pallas_call | solution.py:739
  37.5 0.9 %nodal.1.nodal_ref = f32[24,1089]{1,0:T(8,128)S(1)} custom-call(f32[3,208,128]{2,1,0:T(8,128)S(1)} %rest.5.partial_ref, bf16[256,1664]{1,0:T(8,128)(2,1)S(1)} %get-tuple-element.93.spread_ref), custom_call_target="tpu_custom_call" | custom-call | bytes 3000000 | tf_op jit(solution)/shard_map/nodal/pallas_call | solution.py:739
  38.4 1.2 %finish.1 = f32[1,3,8,1089]{3,2,1,0:T(8,128)} custom-call(f32[40,128]{1,0:T(8,128)S(1)} %collective-permute-done.7.before_ref, f32[24,1089]{1,0:T(8,128)S(1)} %nodal.1.nodal_ref, f32[40,128]{1,0:T(8,128)S(1)} %get-tuple-element.71.refs_10_.face_scale_ref, s32[9,128]{1,0:T(8,128)S(1)} %copy-done.14), custom_call_target="tpu_custom_call" | custom-call | flops 250000000 | bytes 3000000 | tf_op jit(solution)/shard_map/finish/pallas_call | solution.py:739
  39.8 1.0 %sum.1 = f32[250,1,256]{2,1,0:T(1,128)} custom-call(s16[128,128]{1,0:T(8,128)(2,1)S(1)} %collective-permute-done.9.refs_0_, s16[128,128]{1,0:T(8,128)(2,1)S(1)} %collective-permute-done.10.refs_1_, s16[128,128]{1,0:T(8,128)(2,1)S(1)} %collective-permute-done.11.refs_2_, f32[128,128]{1,0:T(8,128)S(1)} %own.1.refs_3_), custom_call_target="tpu_custom_call" | custom-call | bytes 3000000 | tf_op jit(solution)/shard_map/sum/pallas_call | solution.py:739
  (48 shorter events, 1.6 us)
Async XLA Ops:
  0.6 9.5 %copy-start.9 = (f32[208,128]{1,0:T(8,128)S(1)}, f32[208,128]{1,0:T(8,128)}, u32[]{:S(2)}) copy-start(f32[208,128]{1,0:T(8,128)} %constant.23.clone.mass_ref) | copy-start | bytes 319492
  0.6 9.5 %copy-start.10 = (f32[8,1089]{1,0:T(8,128)S(1)}, f32[8,1089]{1,0:T(8,128)}, u32[]{:S(2)}) copy-start(f32[8,1089]{1,0:T(8,128)} %density_ref.3) | copy-start | bytes 104548
  1.7 8.4 %copy-start = (bf16[3,384,256]{2,1,0:T(8,128)(2,1)S(1)}, bf16[3,384,256]{2,1,0:T(8,128)(2,1)}, u32[]{:S(2)}) copy-start(bf16[3,384,256]{2,1,0:T(8,128)(2,1)} %constant.16.clone.refs_0_.grad_table) | copy-start | bytes 1769476
  1.7 8.4 %copy-start.1 = (bf16[3,208,384]{2,1,0:T(8,128)(2,1)S(1)}, bf16[3,208,384]{2,1,0:T(8,128)(2,1)}, u32[]{:S(2)}) copy-start(bf16[3,208,384]{2,1,0:T(8,128)(2,1)} %constant.17.clone.refs_2_.force_table) | copy-start | bytes 1437700
  1.7 8.4 %copy-start.2 = (f32[125,128]{1,0:T(8,128)S(1)}, f32[125,128]{1,0:T(8,128)}, u32[]{:S(2)}) copy-start(f32[125,128]{1,0:T(8,128)} %lame_ref.5) | copy-start | bytes 192004
  1.7 8.4 %copy-start.3 = (f32[125,128]{1,0:T(8,128)S(1)}, f32[125,128]{1,0:T(8,128)}, u32[]{:S(2)}) copy-start(f32[125,128]{1,0:T(8,128)} %mu_ref.5) | copy-start | bytes 192004
  1.7 8.4 %copy-start.4 = (bf16[3,80,256]{2,1,0:T(8,128)(2,1)S(1)}, bf16[3,80,256]{2,1,0:T(8,128)(2,1)}, u32[]{:S(2)}) copy-start(bf16[3,80,256]{2,1,0:T(8,128)(2,1)} %constant.18.clone.refs_1_.refs_5_) | copy-start | bytes 368644
  1.7 8.4 %copy-start.5 = (bf16[384,240]{1,0:T(8,128)(2,1)S(1)}, bf16[384,240]{1,0:T(8,128)(2,1)}, u32[]{:S(2)}) copy-start(bf16[384,240]{1,0:T(8,128)(2,1)} %constant.19.clone.refs_4_) | copy-start | bytes 552964
  1.8 8.4 %copy-start.6 = (bf16[384,240]{1,0:T(8,128)(2,1)S(1)}, bf16[384,240]{1,0:T(8,128)(2,1)}, u32[]{:S(2)}) copy-start(bf16[384,240]{1,0:T(8,128)(2,1)} %constant.20.clone.refs_3_.refs_4_) | copy-start | bytes 552964
  1.8 8.4 %copy-start.7 = (f32[1,3,8,1089]{3,2,1,0:T(8,128)S(1)}, f32[1,3,8,1089]{3,2,1,0:T(8,128)}, u32[]{:S(2)}) copy-start(f32[1,3,8,1089]{3,2,1,0:T(8,128)} %now_ref.3) | copy-start | bytes 313636
  1.8 8.4 %copy-start.8 = (f32[1,3,8,1089]{3,2,1,0:T(8,128)S(1)}, f32[1,3,8,1089]{3,2,1,0:T(8,128)}, u32[]{:S(2)}) copy-start(f32[1,3,8,1089]{3,2,1,0:T(8,128)} %prev_ref.3) | copy-start | bytes 313636
  1.8 11.1 %collective-permute-start = (f32[8,1152]{1,0:T(8,128)S(1)}, f32[8,1152]{1,0:T(8,128)S(1)}, u32[]{:S(2)}, u32[]{:S(2)}) collective-permute-start(f32[8,1152]{1,0:T(8,128)S(1)} %gather.1), channel_id=1, source_target_pairs={{0,15},{1,0},{2,1},{3,2},{4,3},{5,4},{6,5},{7,6},{8,7},{9,8},{10,9... | collective-permute-start | bytes 110600 | tf_op jit(solution)/shard_map/ppermute | solution.py:753
  10.2 2.7 %copy-start.12 = (s32[13,128]{1,0:T(8,128)S(1)}, s32[13,128]{1,0:T(8,128)}, u32[]{:S(2)}) copy-start(s32[13,128]{1,0:T(8,128)} %constant.21.clone.refs_9_) | copy-start | bytes 19972
  14.0 5.8 %collective-permute-start.1 = (bf16[3,128,128]{2,1,0:T(8,128)(2,1)S(1)}, bf16[3,128,128]{2,1,0:T(8,128)(2,1)S(1)}, u32[]{:S(2)}, u32[]{:S(2)}) collective-permute-start(bf16[3,128,128]{2,1,0:T(8,128)(2,1)S(1)} %get-tuple-element.62.low_ref), channel_id=1, source_target_pairs={{0,16},{16,0},{1,17},{17,1},{2,18},{18,2},{3,19},{19,3},{4,20},{20... | collective-permute-start | bytes 294920 | tf_op jit(solution)/shard_map/ppermute | solution.py:753
  14.1 7.4 %collective-permute-start.2 = (f32[40,128]{1,0:T(8,128)S(1)}, f32[40,128]{1,0:T(8,128)S(1)}, u32[]{:S(2)}, u32[]{:S(2)}) collective-permute-start(f32[40,128]{1,0:T(8,128)S(1)} %get-tuple-element.69), channel_id=1, source_target_pairs={{1,2},{2,1},{3,4},{4,3},{5,6},{6,5},{7,8},{8,7},{9,10},{10,9},{11,... | collective-permute-start | bytes 61448 | tf_op jit(solution)/shard_map/ppermute | solution.py:762
  17.6 4.0 %collective-permute-start.3 = (f32[40,128]{1,0:T(8,128)S(1)}, f32[40,128]{1,0:T(8,128)S(1)}, u32[]{:S(2)}, u32[]{:S(2)}) collective-permute-start(f32[40,128]{1,0:T(8,128)S(1)} %get-tuple-element.70), channel_id=1, source_target_pairs={{0,1},{1,0},{2,3},{3,2},{4,5},{5,4},{6,7},{7,6},{8,9},{9,8},{10,11... | collective-permute-start | bytes 61448 | tf_op jit(solution)/shard_map/ppermute | solution.py:762
  22.5 4.8 %collective-permute-start.4 = (bf16[3,128,128]{2,1,0:T(8,128)(2,1)S(1)}, bf16[3,128,128]{2,1,0:T(8,128)(2,1)S(1)}, u32[]{:S(2)}, u32[]{:S(2)}) collective-permute-start(bf16[3,128,128]{2,1,0:T(8,128)(2,1)S(1)} %get-tuple-element.81.low_ref), channel_id=1, source_target_pairs={{0,16},{16,0},{1,17},{17,1},{2,18},{18,2},{3,19},{19,3},{4,20},{20... | collective-permute-start | bytes 294920 | tf_op jit(solution)/shard_map/ppermute | solution.py:753
  22.6 7.4 %collective-permute-start.5 = (f32[40,128]{1,0:T(8,128)S(1)}, f32[40,128]{1,0:T(8,128)S(1)}, u32[]{:S(2)}, u32[]{:S(2)}) collective-permute-start(f32[40,128]{1,0:T(8,128)S(1)} %get-tuple-element.84), channel_id=1, source_target_pairs={{1,2},{2,1},{3,4},{4,3},{5,6},{6,5},{7,8},{8,7},{9,10},{10,9},{11,... | collective-permute-start | bytes 61448 | tf_op jit(solution)/shard_map/ppermute | solution.py:762
  26.0 4.0 %collective-permute-start.6 = (f32[40,128]{1,0:T(8,128)S(1)}, f32[40,128]{1,0:T(8,128)S(1)}, u32[]{:S(2)}, u32[]{:S(2)}) collective-permute-start(f32[40,128]{1,0:T(8,128)S(1)} %get-tuple-element.85), channel_id=1, source_target_pairs={{0,1},{1,0},{2,3},{3,2},{4,5},{5,4},{6,7},{7,6},{8,9},{9,8},{10,11... | collective-permute-start | bytes 61448 | tf_op jit(solution)/shard_map/ppermute | solution.py:762
  30.2 1.4 %collective-permute-start.8 = (bf16[3,128,128]{2,1,0:T(8,128)(2,1)S(1)}, bf16[3,128,128]{2,1,0:T(8,128)(2,1)S(1)}, u32[]{:S(2)}, u32[]{:S(2)}) collective-permute-start(bf16[3,128,128]{2,1,0:T(8,128)(2,1)S(1)} %get-tuple-element.95.low_ref), channel_id=1, source_target_pairs={{0,16},{16,0},{1,17},{17,1},{2,18},{18,2},{3,19},{19,3},{4,20},{20... | collective-permute-start | bytes 294920 | tf_op jit(solution)/shard_map/ppermute | solution.py:753
  31.0 7.4 %collective-permute-start.7 = (f32[40,128]{1,0:T(8,128)S(1)}, f32[40,128]{1,0:T(8,128)S(1)}, u32[]{:S(2)}, u32[]{:S(2)}) collective-permute-start(f32[40,128]{1,0:T(8,128)S(1)} %get-tuple-element.89), channel_id=1, source_target_pairs={{0,1},{1,2},{2,3},{3,4},{4,5},{5,6},{6,7},{7,8},{8,9},{9,10},{10,1... | collective-permute-start | bytes 61448 | tf_op jit(solution)/shard_map/ppermute | solution.py:753
  32.3 7.5 %collective-permute-start.9 = (s16[128,128]{1,0:T(8,128)(2,1)S(1)}, s16[128,128]{1,0:T(8,128)(2,1)S(1)}, u32[]{:S(2)}, u32[]{:S(2)}) collective-permute-start(s16[128,128]{1,0:T(8,128)(2,1)S(1)} %get-tuple-element.98), channel_id=1, source_target_pairs={{0,3},{1,2},{2,1},{3,0},{4,7},{5,6},{6,5},{7,4},{8,11},{9,10},{10,... | collective-permute-start | bytes 98312 | tf_op jit(solution)/shard_map/ppermute | solution.py:875
  32.9 7.0 %collective-permute-start.10 = (s16[128,128]{1,0:T(8,128)(2,1)S(1)}, s16[128,128]{1,0:T(8,128)(2,1)S(1)}, u32[]{:S(2)}, u32[]{:S(2)}) collective-permute-start(s16[128,128]{1,0:T(8,128)(2,1)S(1)} %get-tuple-element.99), channel_id=1, source_target_pairs={{0,2},{1,3},{2,0},{3,1},{4,6},{5,7},{6,4},{7,5},{8,10},{9,11},{10,... | collective-permute-start | bytes 98312 | tf_op jit(solution)/shard_map/ppermute | solution.py:875
  33.9 6.0 %collective-permute-start.11 = (s16[128,128]{1,0:T(8,128)(2,1)S(1)}, s16[128,128]{1,0:T(8,128)(2,1)S(1)}, u32[]{:S(2)}, u32[]{:S(2)}) collective-permute-start(s16[128,128]{1,0:T(8,128)(2,1)S(1)} %get-tuple-element.100), channel_id=1, source_target_pairs={{0,1},{1,0},{2,3},{3,2},{4,5},{5,4},{6,7},{7,6},{8,9},{9,8},{10,11... | collective-permute-start | bytes 98312 | tf_op jit(solution)/shard_map/ppermute | solution.py:875
  (3 other events, 3.0 us)

commit v8 on v7

--- a/solution.py
+++ b/solution.py
@@ -341,6 +341,24 @@
         rows_ref[16 * pair + 8 : 16 * pair + 16, :] = tile
 
 
+def rim_displacement(rim_ref, lanes_ref, rows_ref):
+    sub = lax.broadcasted_iota(jnp.int32, (8, LANES), 0)
+    tiles = [rim_ref[:, at : at + LANES] for at in range(0, WIDE_FACE, LANES)]
+    tiles.append(tiles[-1])
+    pairs = [jnp.where(sub < 3, tiles[at], rolled(tiles[at + 1], 3, 0)) for at in range(0, len(tiles), 2)]
+    second = jnp.where(sub < 3, 0, 1)
+    for row in range(BLOCKS // 2):
+        spots = jnp.broadcast_to(lanes_ref[row : row + 1, :], (8, LANES))
+        tile_of, lane_of = spots // LANES, spots % LANES
+        value = jnp.zeros((8, LANES), F32)
+        for at in sorted(set((COLUMN_LANES[row] // (2 * LANES)).tolist())):
+            moved = jnp.take_along_axis(pairs[at], lane_of, axis=1, mode="promise_in_bounds")
+            value = jnp.where(tile_of == 2 * at + second, moved, value)
+        tile = jnp.where(tile_of % 2 == 0, value, rolled(value, -3, 0))
+        rows_ref[16 * row : 16 * row + 8, :] = rolled(tile, 64, 1)
+        rows_ref[16 * row + 8 : 16 * row + 16, :] = tile
+
+
 def unpack_face(here, there):
     top = lax.broadcasted_iota(jnp.int32, (8, LANES), 0) < 3
     parts = [[], [], []]
@@ -430,21 +448,21 @@
     older, refs = refs[:step], refs[step:]
     strain_ref, sigma_ref, even_ref = refs[0:3]
     if step < STEPS - 1:
-        odd_ref, keep_ref, low_ref, extra_ref = refs[3:7]
-    grad_ref, flat_ref, rim_ref = refs[-3:]
+        odd_ref, keep_ref, low_ref = refs[3:6]
+    grad_ref, flat_ref, rim_ref, rows_ref = refs[-4:]
     upper = lanes_of((40, 3 * LANES)) % LANES >= 64
     if step == 0:
         flat_ref[...] = arrived[0][...]
-        rim_rows(arrived[1], arrived[2], extra_ref)
+        rim_displacement(arrived[1], arrived[2], rows_ref)
         rim_ref[...] = jnp.zeros(rim_ref.shape, F32)
         for c in range(3):
             for d in range(5):
-                rim_ref[8 * d : 8 * d + 5, c * LANES : (c + 1) * LANES] = extra_ref[pl.ds(8 * d + c, 5, stride=40), :]
+                rim_ref[8 * d : 8 * d + 5, c * LANES : (c + 1) * LANES] = rows_ref[pl.ds(8 * d + c, 5, stride=40), :]
         high, middle, low = [piece.astype(F32) for piece in cut(jnp.where(upper, rim_ref[...], 0.0))]
         stacked = [high, middle, high, middle, low, high]
         at_upper = lanes_of((25, LANES)) >= 64
         for c in range(3):
-            flat_ref[c, 100:125, :] = jnp.where(at_upper, extra_ref[pl.ds(c, 25, stride=8), :], flat_ref[c, 100:125, :])
+            flat_ref[c, 100:125, :] = jnp.where(at_upper, rows_ref[pl.ds(c, 25, stride=8), :], flat_ref[c, 100:125, :])
     else:
         if step == STEPS - 1:
             value = jnp.concatenate([arrived[0][c] for c in range(3)], axis=1)
@@ -452,7 +470,7 @@
             shares = face_shares(*arrived[1:4])
             value = jnp.concatenate([jnp.concatenate(lines, axis=0) for lines in shares], axis=1)
             for c in range(3):
-                extra_ref[c] = value[:, c * LANES : (c + 1) * LANES]
+                refs[6][c] = value[:, c * LANES : (c + 1) * LANES]
             flat_ref[...] = arrived[0][...]
             add_shares(shares, flat_ref)
         high, middle, _ = [piece.astype(F32) for piece in cut(value)]
@@ -533,9 +551,10 @@
 
 
 def first_rest_kernel(
-    sigma_ref, force_table, u_in, p_in, scale_in, rows_ref, mass_ref, grad_table,
-    u_ref, scale_ref, next_ref, flat_ref, grad_ref, face_scale_ref, p_ref
+    sigma_ref, force_table, u_in, p_in, scale_in, rim_ref, lanes_ref, mass_ref, grad_table,
+    u_ref, scale_ref, next_ref, flat_ref, grad_ref, face_scale_ref, p_ref, rows_ref
 ):
+    rim_rows(rim_ref, lanes_ref, rows_ref)
     u_ref[...] = u_in[...]
     p_ref[...] = p_in[...]
     scale_ref[...] = scale_in[...]
@@ -824,17 +843,20 @@
             arrived = (flat, rim, column_lanes) if step == 0 else (flat, odd, even, face_scale)
         outs = [shaped(6, 125, LANES), grad_shape, face]
         if not last_step:
-            outs += [face, five, low_shape, scale_shape if step == 0 else shaped(3, 40, LANES)]
+            outs += [face, five, low_shape]
+        if step == 1:
+            outs.append(shaped(3, 40, LANES))
         results = call(
             lambda *refs, step=step: step_kernel(step, *refs), "step", outs,
-            [grad_scratch, pltpu.VMEM((3, 128, LANES), F32), pltpu.VMEM((40, 384), F32)],
+            [grad_scratch, pltpu.VMEM((3, 128, LANES), F32), pltpu.VMEM((40, 384), F32), pltpu.VMEM((ROWS, LANES), F32)],
             lame_lambda, shear_mu, memories[step], sls_decay, rim_table if step == 0 else share_table, face_table, base, *arrived, *kept,
         )
         strain, sigma, even = results[0:3]
         if last_step:
             before = passed_along(even, ring, 1)
         else:
-            odd, keep, low, extra = results[3:7]
+            odd, keep, low = results[3:6]
+            extra = results[6] if step == 1 else None
             kept.append(keep)
             odd = swapped(odd, ring, 1)
             even = swapped(even, ring, 0)
@@ -842,7 +864,8 @@
         if step == 0:
             p, scale, partial, flat, base, face_scale = call(
                 first_rest_kernel, "rest", [state, scale_shape, state, flat_shape, grad_shape, shaped(40, LANES)],
-                [pltpu.VMEM((3, ROWS, LANES), F32)], sigma, force_table, u, p, scale, extra, mass, grad_table,
+                [pltpu.VMEM((3, ROWS, LANES), F32), pltpu.VMEM((ROWS, LANES), F32)],
+                sigma, force_table, u, p, scale, rim, column_lanes, mass, grad_table,
             )
         else:
             results = call(

time: 41 us -> 40.8 us (level)
  no operation moved by 1% of the time
where the time goes in v8:
time: 40.8 us; the launch traced here: 40.7 us
  starting transfers between devices  18.6 us (46%)
  Pallas kernels  14.8 us (36%)
  waiting for transfers between devices  4.23 us (10%)
  local copies, waits for them, and re-layouts  2.05 us (5%)
  between operations  1 us (2%)
    pallas_call x17, Pallas kernels, call(): pl.pallas_call(kernel, name=name, out_shape=outs, in_specs=[HBM if at in...  14.8 us
    ppermute x5, starting transfers between devices, passed_along(): lax.ppermute(value, axis, [(source, (source + steps) % count) for source...  7.21 us
    ppermute x4, starting transfers between devices, swapped(): return lax.ppermute(value, axis, pairs)  6.91 us
    ppermute x3, starting transfers between devices, per_device(): lax.ppermute(blocks[k - 1], 'sub', [(j, j ^ k) for j in range(subs)])  4.45 us
    ppermute x4, waiting for transfers between devices, swapped(): return lax.ppermute(value, axis, pairs)  3.62 us
    unnamed x31, local copies, waits for them, and re-layouts  2.05 us
  transfers between devices with their start and end apart: 12, of which 3 were waited for; matrix products, arithmetic and copies ran while one was open for 3% of the time, Pallas kernels for 25%

profile of v8, /device:TPU:0, one launch (start us, length us, event | category | flops | bytes accessed | tf_op | source)
XLA Modules:
  0.0 40.7 jit_solution(7156351705055698654)
XLA Ops:
  0.7 1.0 %gather.1 = f32[8,1152]{1,0:T(8,128)S(1)} custom-call(f32[1,3,8,1089]{3,2,1,0:T(8,128)} %now_ref.3, f32[1,3,8,1089]{3,2,1,0:T(8,128)} %prev_ref.3, f32[8,1089]{1,0:T(8,128)} %density_ref.3), custom_call_target="tpu_custom_call" | custom-call | bytes 3000000 | tf_op jit(solution)/shard_map/gather/pallas_call | solution.py:758
  1.8 7.0 %collective-permute-start = (f32[8,1152]{1,0:T(8,128)S(1)}, f32[8,1152]{1,0:T(8,128)S(1)}, u32[]{:S(2)}, u32[]{:S(2)}) collective-permute-start(f32[8,1152]{1,0:T(8,128)S(1)} %gather.1), channel_id=1, source_target_pairs={{0,15},{1,0},{2,1},{3,2},{4,3},{5,4},{6,5},{7,6},{8,7},{9,8},{10,9... | collective-permute-start | bytes 110600 | tf_op jit(solution)/shard_map/ppermute | solution.py:772
  8.8 1.3 %copy.21 = f32[1,3,5,125,128]{4,3,0,2,1:T(8,128)S(1)} copy(f32[1,3,5,125,128]{4,0,3,2,1:T(1,128)} %param.18) | data formatting | bytes 1920000
  10.2 2.7 %prologue.1 = (f32[3,208,128]{2,1,0:T(8,128)S(1)}, f32[3,208,128]{2,1,0:T(8,128)S(1)}, f32[208,128]{1,0:T(8,128)S(1)}, f32[5,125,128]{2,1,0:T(8,128)S(1)}, bf16[...) custom-call(f32[1,3,8,1089]{3,2,1,0:T(8,128)S(1)} %copy-done.7, ...), custom_call_target="tpu_custom_call" | custom-call | bytes 3000000 | tf_op jit(solution)/shard_map/prologue/pallas_call | solution.py:758
  12.9 0.9 %step.3 = (f32[6,125,128]{2,1,0:T(8,128)S(1)}, f32[384,384]{1,0:T(8,128)S(1)}, f32[40,128]{1,0:T(8,128)S(1)}, f32[40,128]{1,0:T(8,128)S(1)}, f32[5,125,128]{2,1,...) custom-call(f32[125,128]{1,0:T(8,128)S(1)} %copy-done.2, f32[125,128]{1,0:T(8,128)S(1)} %copy-done.3, ...), custom_call_target="tpu_custom_call" | custom-call | bytes 3000000 | tf_op jit(solution)/shard_map/step/pallas_call | solution.py:758
  14.0 3.5 %collective-permute-start.2 = (f32[40,128]{1,0:T(8,128)S(1)}, f32[40,128]{1,0:T(8,128)S(1)}, u32[]{:S(2)}, u32[]{:S(2)}) collective-permute-start(f32[40,128]{1,0:T(8,128)S(1)} %get-tuple-element.67), channel_id=1, source_target_pairs={{1,2},{2,1},{3,4},{4,3},{5,6},{6,5},{7,8},{8,7},{9,10},{10,9},{11,... | collective-permute-start | bytes 61448 | tf_op jit(solution)/shard_map/ppermute | solution.py:781
  17.4 0.7 %copy-done.13 = s32[2,64,1]{1,2,0:T(1,128)S(1)} copy-done((s32[2,64,1]{1,2,0:T(1,128)S(1)}, s32[2,64,1]{1,2,0:T(1,128)}, u32[]{:S(2)}) %copy-start.13) | copy-done | bytes 536
  18.5 1.2 %rest.3 = (f32[3,208,128]{2,1,0:T(8,128)S(1)}, f32[208,128]{1,0:T(8,128)S(1)}, f32[3,208,128]{2,1,0:T(8,128)S(1)}, f32[3,128,128]{2,1,0:T(8,128)S(1)}, f32[384,384]{1,0:T(8,128)S(1)}, /*index=5*/f32[40,128]{1,0:T(8,128)S(1)}) custom-call(f32[384,384]{1,0:T(8,128)S(1)} %get-tuple-element.54.sigma_ref, bf16[3,208,384]{2,1,0:T(8,128)(2,1)S(1)} %copy-done.1, ...), custom_call_target="tpu_custom_call" | custom-call | bytes 3000000 | tf_op jit(solution)/shard_map/rest/pallas_call | solution.py:758
  20.1 1.3 %collective-permute-done.2.refs_8_ = f32[40,128]{1,0:T(8,128)S(1)} collective-permute-done((f32[40,128]{1,0:T(8,128)S(1)}, f32[40,128]{1,0:T(8,128)S(1)}, u32[]{:S(2)}, u32[]{:S(2)}) %collective-permute-start.2) | collective-permute-done | bytes 20512 | tf_op jit(solution)/shard_map/ppermute | solution.py:781
  21.4 0.9 %step.4 = (f32[6,125,128]{2,1,0:T(8,128)S(1)}, f32[384,384]{1,0:T(8,128)S(1)}, f32[40,128]{1,0:T(8,128)S(1)}, f32[40,128]{1,0:T(8,128)S(1)}, f32[5,125,128]{2,1,...) custom-call(f32[125,128]{1,0:T(8,128)S(1)} %copy-done.2, f32[125,128]{1,0:T(8,128)S(1)} %copy-done.3, ...), custom_call_target="tpu_custom_call" | custom-call | bytes 3000000 | tf_op jit(solution)/shard_map/step/pallas_call | solution.py:758
  22.4 3.5 %collective-permute-start.5 = (f32[40,128]{1,0:T(8,128)S(1)}, f32[40,128]{1,0:T(8,128)S(1)}, u32[]{:S(2)}, u32[]{:S(2)}) collective-permute-start(f32[40,128]{1,0:T(8,128)S(1)} %get-tuple-element.82), channel_id=1, source_target_pairs={{1,2},{2,1},{3,4},{4,3},{5,6},{6,5},{7,8},{8,7},{9,10},{10,9},{11,... | collective-permute-start | bytes 61448 | tf_op jit(solution)/shard_map/ppermute | solution.py:781
  25.9 1.2 %rest.4 = (f32[3,208,128]{2,1,0:T(8,128)S(1)}, f32[3,208,128]{2,1,0:T(8,128)S(1)}, f32[3,128,128]{2,1,0:T(8,128)S(1)}, f32[384,384]{1,0:T(8,128)S(1)}) custom-call(f32[384,384]{1,0:T(8,128)S(1)} %get-tuple-element.71.sigma_ref, bf16[3,208,384]{2,1,0:T(8,128)(2,1)S(1)} %copy-done.1, f32[3,208,128]{2,1,0:T(8,128)S(1)} %get-tuple-element.72.partial_ref, ...), custom_call_target="tpu_custom_call" | custom-call | bytes 3000000 | tf_op jit(solution)/shard_map/rest/pallas_call | solution.py:758
  27.1 0.4 %parts.3.both_ref = f32[256,128]{1,0:T(8,128)S(1)} custom-call(f32[6,125,128]{2,1,0:T(8,128)S(1)} %get-tuple-element.78.strain_ref, bf16[3,128,128]{2,1,0:T(8,128)(2,1)S(1)} %get-tuple-element.79.low_ref, bf16[3,128,128]{2,1,0:T(8,128)(2,1)S(1)} %collective-permute-done.4.far_ref, f32[125,128]{1,0:T(8,128)S(1)} %copy-done.2, f32[125,128]{1,0:T(8,128)S(1)} %copy-done.3, ...), custom_call_target="tpu_custom_call" | custom-call | bytes 3000000 | tf_op jit(solution)/shard_map/parts/pallas_call | solution.py:758
  27.5 2.3 %collective-permute-done.5.odd_ref = f32[40,128]{1,0:T(8,128)S(1)} collective-permute-done((f32[40,128]{1,0:T(8,128)S(1)}, f32[40,128]{1,0:T(8,128)S(1)}, u32[]{:S(2)}, u32[]{:S(2)}) %collective-permute-start.5) | collective-permute-done | bytes 20512 | tf_op jit(solution)/shard_map/ppermute | solution.py:781
  30.2 0.7 %step.5 = (f32[6,125,128]{2,1,0:T(8,128)S(1)}, f32[384,384]{1,0:T(8,128)S(1)}, f32[40,128]{1,0:T(8,128)S(1)}) custom-call(f32[125,128]{1,0:T(8,128)S(1)} %copy-done.2, f32[125,128]{1,0:T(8,128)S(1)} %copy-done.3, f32[5,125,128]{2,1,0:T(8,128)S(1)} %get-tuple-element.63.refs_2_, f32[3,128]{1,0:T(4,128)S(1)} %copy-done.11, bf16[384,240]{1,0:T(8,128)(2,1)S(1)} %copy-done.5, ...), custom_call_target="tpu_custom_call" | custom-call | bytes 3000000 | tf_op jit(solution)/shard_map/step/pallas_call | solution.py:758
  30.9 0.6 %collective-permute-done.8.far_ref = bf16[3,128,128]{2,1,0:T(8,128)(2,1)S(1)} collective-permute-done((bf16[3,128,128]{2,1,0:T(8,128)(2,1)S(1)}, bf16[3,128,128]{2,1,0:T(8,128)(2,1)S(1)}, u32[]{:S(2)}, u32[]{:S(2)}) %collective-permute-start.8) | collective-permute-done | bytes 98336 | tf_op jit(solution)/shard_map/ppermute | solution.py:772
  31.5 0.7 %send.1 = (f32[256,128]{1,0:T(8,128)S(1)}, s16[128,128]{1,0:T(8,128)(2,1)S(1)}, s16[128,128]{1,0:T(8,128)(2,1)S(1)}, s16[128,128]{1,0:T(8,128)(2,1)S(1)}) custom-call(f32[6,125,128]{2,1,0:T(8,128)S(1)} %get-tuple-element.92.strain_ref, bf16[3,128,128]{2,1,0:T(8,128)(2,1)S(1)} %get-tuple-element.93.low_ref, ...), custom_call_target="tpu_custom_call" | custom-call | bytes 3000000 | tf_op jit(solution)/shard_map/send/pallas_call | solution.py:758
  32.2 0.5 %collective-permute-start.9 = (s16[128,128]{1,0:T(8,128)(2,1)S(1)}, s16[128,128]{1,0:T(8,128)(2,1)S(1)}, u32[]{:S(2)}, u32[]{:S(2)}) collective-permute-start(s16[128,128]{1,0:T(8,128)(2,1)S(1)} %get-tuple-element.96), channel_id=1, source_target_pairs={{0,3},{1,2},{2,1},{3,0},{4,7},{5,6},{6,5},{7,4},{8,11},{9,10},{10,... | collective-permute-start | bytes 98312 | tf_op jit(solution)/shard_map/ppermute | solution.py:898
  32.7 1.0 %collective-permute-start.10 = (s16[128,128]{1,0:T(8,128)(2,1)S(1)}, s16[128,128]{1,0:T(8,128)(2,1)S(1)}, u32[]{:S(2)}, u32[]{:S(2)}) collective-permute-start(s16[128,128]{1,0:T(8,128)(2,1)S(1)} %get-tuple-element.97), channel_id=1, source_target_pairs={{0,2},{1,3},{2,0},{3,1},{4,6},{5,7},{6,4},{7,5},{8,10},{9,11},{10,... | collective-permute-start | bytes 98312 | tf_op jit(solution)/shard_map/ppermute | solution.py:898
  33.7 2.9 %collective-permute-start.11 = (s16[128,128]{1,0:T(8,128)(2,1)S(1)}, s16[128,128]{1,0:T(8,128)(2,1)S(1)}, u32[]{:S(2)}, u32[]{:S(2)}) collective-permute-start(s16[128,128]{1,0:T(8,128)(2,1)S(1)} %get-tuple-element.98), channel_id=1, source_target_pairs={{0,1},{1,0},{2,3},{3,2},{4,5},{5,4},{6,7},{7,6},{8,9},{9,8},{10,11... | collective-permute-start | bytes 98312 | tf_op jit(solution)/shard_map/ppermute | solution.py:898
  36.6 0.7 %rest.5.partial_ref = f32[3,208,128]{2,1,0:T(8,128)S(1)} custom-call(f32[384,384]{1,0:T(8,128)S(1)} %get-tuple-element.88.sigma_ref, bf16[3,208,384]{2,1,0:T(8,128)(2,1)S(1)} %copy-done.1, f32[3,208,128]{2,1,0:T(8,128)S(1)} %get-tuple-element.89.partial_ref, f32[3,40,128]{2,1,0:T(8,128)S(1)} %get-tuple-element.85.refs_7_.delta_ref, ...), custom_call_target="tpu_custom_call" | custom-call | bytes 3000000 | tf_op jit(solution)/shard_map/rest/pallas_call | solution.py:758
  37.4 0.9 %nodal.1.nodal_ref = f32[24,1089]{1,0:T(8,128)S(1)} custom-call(f32[3,208,128]{2,1,0:T(8,128)S(1)} %rest.5.partial_ref, bf16[256,1664]{1,0:T(8,128)(2,1)S(1)} %get-tuple-element.91.spread_ref), custom_call_target="tpu_custom_call" | custom-call | bytes 3000000 | tf_op jit(solution)/shard_map/nodal/pallas_call | solution.py:758
  38.3 1.2 %finish.1 = f32[1,3,8,1089]{3,2,1,0:T(8,128)} custom-call(f32[40,128]{1,0:T(8,128)S(1)} %collective-permute-done.7.before_ref, f32[24,1089]{1,0:T(8,128)S(1)} %nodal.1.nodal_ref, f32[40,128]{1,0:T(8,128)S(1)} %get-tuple-element.69.refs_10_.face_scale_ref, s32[9,128]{1,0:T(8,128)S(1)} %copy-done.14), custom_call_target="tpu_custom_call" | custom-call | flops 250000000 | bytes 3000000 | tf_op jit(solution)/shard_map/finish/pallas_call | solution.py:758
  39.7 1.0 %sum.1 = f32[250,1,256]{2,1,0:T(1,128)} custom-call(s16[128,128]{1,0:T(8,128)(2,1)S(1)} %collective-permute-done.9.refs_0_, s16[128,128]{1,0:T(8,128)(2,1)S(1)} %collective-permute-done.10.refs_1_, s16[128,128]{1,0:T(8,128)(2,1)S(1)} %collective-permute-done.11.refs_2_, f32[128,128]{1,0:T(8,128)S(1)} %own.1.refs_3_), custom_call_target="tpu_custom_call" | custom-call | bytes 3000000 | tf_op jit(solution)/shard_map/sum/pallas_call | solution.py:758
  (48 shorter events, 1.6 us)
Async XLA Ops:
  0.6 9.5 %copy-start.9 = (f32[208,128]{1,0:T(8,128)S(1)}, f32[208,128]{1,0:T(8,128)}, u32[]{:S(2)}) copy-start(f32[208,128]{1,0:T(8,128)} %constant.23.clone.mass_ref) | copy-start | bytes 319492
  0.6 9.5 %copy-start.10 = (f32[8,1089]{1,0:T(8,128)S(1)}, f32[8,1089]{1,0:T(8,128)}, u32[]{:S(2)}) copy-start(f32[8,1089]{1,0:T(8,128)} %density_ref.3) | copy-start | bytes 104548
  1.7 8.4 %copy-start = (bf16[3,384,256]{2,1,0:T(8,128)(2,1)S(1)}, bf16[3,384,256]{2,1,0:T(8,128)(2,1)}, u32[]{:S(2)}) copy-start(bf16[3,384,256]{2,1,0:T(8,128)(2,1)} %constant.16.clone.refs_0_.grad_table) | copy-start | bytes 1769476
  1.7 8.4 %copy-start.1 = (bf16[3,208,384]{2,1,0:T(8,128)(2,1)S(1)}, bf16[3,208,384]{2,1,0:T(8,128)(2,1)}, u32[]{:S(2)}) copy-start(bf16[3,208,384]{2,1,0:T(8,128)(2,1)} %constant.17.clone.refs_2_.force_table) | copy-start | bytes 1437700
  1.7 8.4 %copy-start.2 = (f32[125,128]{1,0:T(8,128)S(1)}, f32[125,128]{1,0:T(8,128)}, u32[]{:S(2)}) copy-start(f32[125,128]{1,0:T(8,128)} %lame_ref.5) | copy-start | bytes 192004
  1.7 8.4 %copy-start.3 = (f32[125,128]{1,0:T(8,128)S(1)}, f32[125,128]{1,0:T(8,128)}, u32[]{:S(2)}) copy-start(f32[125,128]{1,0:T(8,128)} %mu_ref.5) | copy-start | bytes 192004
  1.7 8.4 %copy-start.4 = (bf16[3,80,256]{2,1,0:T(8,128)(2,1)S(1)}, bf16[3,80,256]{2,1,0:T(8,128)(2,1)}, u32[]{:S(2)}) copy-start(bf16[3,80,256]{2,1,0:T(8,128)(2,1)} %constant.18.clone.refs_1_.refs_5_) | copy-start | bytes 368644
  1.7 8.4 %copy-start.5 = (bf16[384,240]{1,0:T(8,128)(2,1)S(1)}, bf16[384,240]{1,0:T(8,128)(2,1)}, u32[]{:S(2)}) copy-start(bf16[384,240]{1,0:T(8,128)(2,1)} %constant.19.clone.refs_4_) | copy-start | bytes 552964
  1.8 8.4 %copy-start.6 = (bf16[384,240]{1,0:T(8,128)(2,1)S(1)}, bf16[384,240]{1,0:T(8,128)(2,1)}, u32[]{:S(2)}) copy-start(bf16[384,240]{1,0:T(8,128)(2,1)} %constant.20.clone.refs_3_.refs_4_) | copy-start | bytes 552964
  1.8 8.4 %copy-start.7 = (f32[1,3,8,1089]{3,2,1,0:T(8,128)S(1)}, f32[1,3,8,1089]{3,2,1,0:T(8,128)}, u32[]{:S(2)}) copy-start(f32[1,3,8,1089]{3,2,1,0:T(8,128)} %now_ref.3) | copy-start | bytes 313636
  1.8 8.4 %copy-start.8 = (f32[1,3,8,1089]{3,2,1,0:T(8,128)S(1)}, f32[1,3,8,1089]{3,2,1,0:T(8,128)}, u32[]{:S(2)}) copy-start(f32[1,3,8,1089]{3,2,1,0:T(8,128)} %prev_ref.3) | copy-start | bytes 313636
  1.8 11.1 %collective-permute-start = (f32[8,1152]{1,0:T(8,128)S(1)}, f32[8,1152]{1,0:T(8,128)S(1)}, u32[]{:S(2)}, u32[]{:S(2)}) collective-permute-start(f32[8,1152]{1,0:T(8,128)S(1)} %gather.1), channel_id=1, source_target_pairs={{0,15},{1,0},{2,1},{3,2},{4,3},{5,4},{6,5},{7,6},{8,7},{9,8},{10,9... | collective-permute-start | bytes 110600 | tf_op jit(solution)/shard_map/ppermute | solution.py:772
  10.2 2.7 %copy-start.12 = (s32[13,128]{1,0:T(8,128)S(1)}, s32[13,128]{1,0:T(8,128)}, u32[]{:S(2)}) copy-start(s32[13,128]{1,0:T(8,128)} %constant.21.clone.refs_9_.lanes_ref) | copy-start | bytes 19972
  13.9 5.8 %collective-permute-start.1 = (bf16[3,128,128]{2,1,0:T(8,128)(2,1)S(1)}, bf16[3,128,128]{2,1,0:T(8,128)(2,1)S(1)}, u32[]{:S(2)}, u32[]{:S(2)}) collective-permute-start(bf16[3,128,128]{2,1,0:T(8,128)(2,1)S(1)} %get-tuple-element.60.low_ref), channel_id=1, source_target_pairs={{0,16},{16,0},{1,17},{17,1},{2,18},{18,2},{3,19},{19,3},{4,20},{20... | collective-permute-start | bytes 294920 | tf_op jit(solution)/shard_map/ppermute | solution.py:772
  14.0 7.4 %collective-permute-start.2 = (f32[40,128]{1,0:T(8,128)S(1)}, f32[40,128]{1,0:T(8,128)S(1)}, u32[]{:S(2)}, u32[]{:S(2)}) collective-permute-start(f32[40,128]{1,0:T(8,128)S(1)} %get-tuple-element.67), channel_id=1, source_target_pairs={{1,2},{2,1},{3,4},{4,3},{5,6},{6,5},{7,8},{8,7},{9,10},{10,9},{11,... | collective-permute-start | bytes 61448 | tf_op jit(solution)/shard_map/ppermute | solution.py:781
  17.4 4.0 %collective-permute-start.3 = (f32[40,128]{1,0:T(8,128)S(1)}, f32[40,128]{1,0:T(8,128)S(1)}, u32[]{:S(2)}, u32[]{:S(2)}) collective-permute-start(f32[40,128]{1,0:T(8,128)S(1)} %get-tuple-element.68), channel_id=1, source_target_pairs={{0,1},{1,0},{2,3},{3,2},{4,5},{5,4},{6,7},{7,6},{8,9},{9,8},{10,11... | collective-permute-start | bytes 61448 | tf_op jit(solution)/shard_map/ppermute | solution.py:781
  22.3 4.8 %collective-permute-start.4 = (bf16[3,128,128]{2,1,0:T(8,128)(2,1)S(1)}, bf16[3,128,128]{2,1,0:T(8,128)(2,1)S(1)}, u32[]{:S(2)}, u32[]{:S(2)}) collective-permute-start(bf16[3,128,128]{2,1,0:T(8,128)(2,1)S(1)} %get-tuple-element.79.low_ref), channel_id=1, source_target_pairs={{0,16},{16,0},{1,17},{17,1},{2,18},{18,2},{3,19},{19,3},{4,20},{20... | collective-permute-start | bytes 294920 | tf_op jit(solution)/shard_map/ppermute | solution.py:772
  22.4 7.4 %collective-permute-start.5 = (f32[40,128]{1,0:T(8,128)S(1)}, f32[40,128]{1,0:T(8,128)S(1)}, u32[]{:S(2)}, u32[]{:S(2)}) collective-permute-start(f32[40,128]{1,0:T(8,128)S(1)} %get-tuple-element.82), channel_id=1, source_target_pairs={{1,2},{2,1},{3,4},{4,3},{5,6},{6,5},{7,8},{8,7},{9,10},{10,9},{11,... | collective-permute-start | bytes 61448 | tf_op jit(solution)/shard_map/ppermute | solution.py:781
  25.9 4.0 %collective-permute-start.6 = (f32[40,128]{1,0:T(8,128)S(1)}, f32[40,128]{1,0:T(8,128)S(1)}, u32[]{:S(2)}, u32[]{:S(2)}) collective-permute-start(f32[40,128]{1,0:T(8,128)S(1)} %get-tuple-element.83), channel_id=1, source_target_pairs={{0,1},{1,0},{2,3},{3,2},{4,5},{5,4},{6,7},{7,6},{8,9},{9,8},{10,11... | collective-permute-start | bytes 61448 | tf_op jit(solution)/shard_map/ppermute | solution.py:781
  30.1 1.4 %collective-permute-start.8 = (bf16[3,128,128]{2,1,0:T(8,128)(2,1)S(1)}, bf16[3,128,128]{2,1,0:T(8,128)(2,1)S(1)}, u32[]{:S(2)}, u32[]{:S(2)}) collective-permute-start(bf16[3,128,128]{2,1,0:T(8,128)(2,1)S(1)} %get-tuple-element.93.low_ref), channel_id=1, source_target_pairs={{0,16},{16,0},{1,17},{17,1},{2,18},{18,2},{3,19},{19,3},{4,20},{20... | collective-permute-start | bytes 294920 | tf_op jit(solution)/shard_map/ppermute | solution.py:772
  30.9 7.4 %collective-permute-start.7 = (f32[40,128]{1,0:T(8,128)S(1)}, f32[40,128]{1,0:T(8,128)S(1)}, u32[]{:S(2)}, u32[]{:S(2)}) collective-permute-start(f32[40,128]{1,0:T(8,128)S(1)} %get-tuple-element.87), channel_id=1, source_target_pairs={{0,1},{1,2},{2,3},{3,4},{4,5},{5,6},{6,7},{7,8},{8,9},{9,10},{10,1... | collective-permute-start | bytes 61448 | tf_op jit(solution)/shard_map/ppermute | solution.py:772
  32.2 7.5 %collective-permute-start.9 = (s16[128,128]{1,0:T(8,128)(2,1)S(1)}, s16[128,128]{1,0:T(8,128)(2,1)S(1)}, u32[]{:S(2)}, u32[]{:S(2)}) collective-permute-start(s16[128,128]{1,0:T(8,128)(2,1)S(1)} %get-tuple-element.96), channel_id=1, source_target_pairs={{0,3},{1,2},{2,1},{3,0},{4,7},{5,6},{6,5},{7,4},{8,11},{9,10},{10,... | collective-permute-start | bytes 98312 | tf_op jit(solution)/shard_map/ppermute | solution.py:898
  32.7 7.0 %collective-permute-start.10 = (s16[128,128]{1,0:T(8,128)(2,1)S(1)}, s16[128,128]{1,0:T(8,128)(2,1)S(1)}, u32[]{:S(2)}, u32[]{:S(2)}) collective-permute-start(s16[128,128]{1,0:T(8,128)(2,1)S(1)} %get-tuple-element.97), channel_id=1, source_target_pairs={{0,2},{1,3},{2,0},{3,1},{4,6},{5,7},{6,4},{7,5},{8,10},{9,11},{10,... | collective-permute-start | bytes 98312 | tf_op jit(solution)/shard_map/ppermute | solution.py:898
  33.7 5.9 %collective-permute-start.11 = (s16[128,128]{1,0:T(8,128)(2,1)S(1)}, s16[128,128]{1,0:T(8,128)(2,1)S(1)}, u32[]{:S(2)}, u32[]{:S(2)}) collective-permute-start(s16[128,128]{1,0:T(8,128)(2,1)S(1)} %get-tuple-element.98), channel_id=1, source_target_pairs={{0,1},{1,0},{2,3},{3,2},{4,5},{5,4},{6,7},{7,6},{8,9},{9,8},{10,11... | collective-permute-start | bytes 98312 | tf_op jit(solution)/shard_map/ppermute | solution.py:898
  (3 other events, 3.0 us)

commit v9 on v8

--- a/solution.py
+++ b/solution.py
@@ -16,6 +16,8 @@
 FACE = SIDE * SIDE
 BLOCKS = 26
 ROWS = 8 * BLOCKS
+TALL = 320
+FLAT = 144
 WIDE = 64 * BLOCKS
 JUMP = 4 * SIDE
 WIDE_FACE = 1152
@@ -90,7 +92,7 @@
     for e in range(8):
         line[4 * e : 4 * e + 5] += weights
     layer = np.array([2 * weights[0], weights[1], weights[2], weights[3], 2 * weights[0], 1.0, 1.0, 1.0])
-    mass = np.ones((ROWS, LANES), np.float32)
+    mass = np.ones((TALL, LANES), np.float32)
     for b in range(5):
         for d in range(5):
             for ey in range(8):
@@ -436,9 +438,9 @@
     shares = face_shares(odd_ref, even_ref, face_scale_ref)
     for c in range(3):
         delta_ref[c] = jnp.concatenate(shares[c], axis=0)
-    flat_ref[...] = flat_in[...]
+    flat_ref[:, 0:128, :] = flat_in[...]
     add_shares(shares, flat_ref)
-    low_ref[...] = flat_ref[...].astype(BF16)
+    low_ref[...] = flat_ref[:, 0:128, :].astype(BF16)
 
 
 def step_kernel(step, *refs):
@@ -452,7 +454,7 @@
     grad_ref, flat_ref, rim_ref, rows_ref = refs[-4:]
     upper = lanes_of((40, 3 * LANES)) % LANES >= 64
     if step == 0:
-        flat_ref[...] = arrived[0][...]
+        flat_ref[:, 0:128, :] = arrived[0][...]
         rim_displacement(arrived[1], arrived[2], rows_ref)
         rim_ref[...] = jnp.zeros(rim_ref.shape, F32)
         for c in range(3):
@@ -471,7 +473,7 @@
             value = jnp.concatenate([jnp.concatenate(lines, axis=0) for lines in shares], axis=1)
             for c in range(3):
                 refs[6][c] = value[:, c * LANES : (c + 1) * LANES]
-            flat_ref[...] = arrived[0][...]
+            flat_ref[:, 0:128, :] = arrived[0][...]
             add_shares(shares, flat_ref)
         high, middle, _ = [piece.astype(F32) for piece in cut(value)]
         stacked = []
@@ -479,7 +481,7 @@
             stacked += [jnp.where(at, high, 0.0), jnp.where(at, middle, 0.0), jnp.where(at, high, 0.0)]
     grad_ref[...] = base_ref[...] + dot(share_table[...], jnp.concatenate(stacked, axis=0).astype(BF16))
     if step < STEPS - 1:
-        low_ref[...] = flat_ref[...].astype(BF16)
+        low_ref[...] = flat_ref[:, 0:128, :].astype(BF16)
     for block in range(9):
         sigma_ref[(block // 3) * 128 + 120 : (block // 3) * 128 + 128, (block % 3) * LANES : (block % 3) * LANES + LANES] = (
             jnp.zeros((8, LANES), F32)
@@ -555,9 +557,9 @@
     u_ref, scale_ref, next_ref, flat_ref, grad_ref, face_scale_ref, p_ref, rows_ref
 ):
     rim_rows(rim_ref, lanes_ref, rows_ref)
-    u_ref[...] = u_in[...]
-    p_ref[...] = p_in[...]
-    scale_ref[...] = scale_in[...]
+    u_ref[:, 0:ROWS, :] = u_in[:, 0:ROWS, :]
+    p_ref[:, 0:ROWS, :] = p_in[:, 0:ROWS, :]
+    scale_ref[0:ROWS, :] = scale_in[0:ROWS, :]
     upper = lanes_of((25, LANES)) >= 64
     last = pl.ds(4, 25, stride=8)
     for c in range(3):
@@ -576,7 +578,7 @@
 
 
 def rest_kernel(sigma_ref, force_table, partial_ref, delta_ref, p_ref, scale_ref, grad_table, next_ref, u_ref, *refs):
-    u_ref[...] = partial_ref[...]
+    u_ref[:, 0:ROWS, :] = partial_ref[:, 0:ROWS, :]
     upper = lanes_of((5, LANES)) >= 64
     for c in range(3):
         for d in range(5):
@@ -812,8 +814,8 @@
     memory = memory_init[0]
     owner = jnp.transpose(owner_map, (0, 2, 1))
 
-    state = shaped(3, ROWS, LANES)
-    scale_shape = shaped(ROWS, LANES)
+    state = shaped(3, TALL, LANES)
+    scale_shape = shaped(TALL, LANES)
     five = shaped(5, 125, LANES)
     part_shape = shaped(256, LANES, dtype=BF16)
     grad_scratch = pltpu.VMEM((384, 384), F32)
@@ -834,7 +836,7 @@
         low_shape = shaped(3, 128, LANES, dtype=BF16)
         if last_step:
             extra, low = call(
-                shares_kernel, "shares", [shaped(3, 40, LANES), low_shape], [pltpu.VMEM((3, 128, LANES), F32)],
+                shares_kernel, "shares", [shaped(3, 40, LANES), low_shape], [pltpu.VMEM((3, FLAT, LANES), F32)],
                 odd, even, face_scale, flat,
             )
             far = far_field(low, groups)
@@ -848,7 +850,7 @@
             outs.append(shaped(3, 40, LANES))
         results = call(
             lambda *refs, step=step: step_kernel(step, *refs), "step", outs,
-            [grad_scratch, pltpu.VMEM((3, 128, LANES), F32), pltpu.VMEM((40, 384), F32), pltpu.VMEM((ROWS, LANES), F32)],
+            [grad_scratch, pltpu.VMEM((3, FLAT, LANES), F32), pltpu.VMEM((40, 384), F32), pltpu.VMEM((TALL, LANES), F32)],
             lame_lambda, shear_mu, memories[step], sls_decay, rim_table if step == 0 else share_table, face_table, base, *arrived, *kept,
         )
         strain, sigma, even = results[0:3]
@@ -864,13 +866,13 @@
         if step == 0:
             p, scale, partial, flat, base, face_scale = call(
                 first_rest_kernel, "rest", [state, scale_shape, state, flat_shape, grad_shape, shaped(40, LANES)],
-                [pltpu.VMEM((3, ROWS, LANES), F32), pltpu.VMEM((ROWS, LANES), F32)],
+                [pltpu.VMEM((3, TALL, LANES), F32), pltpu.VMEM((TALL, LANES), F32)],
                 sigma, force_table, u, p, scale, rim, column_lanes, mass, grad_table,
             )
         else:
             results = call(
                 rest_kernel, "rest", [state] if last_step else [state, state, flat_shape, grad_shape],
-                [pltpu.VMEM((3, ROWS, LANES), F32)] if last_step else [], sigma, force_table, partial, extra, p, scale, grad_table,
+                [pltpu.VMEM((3, TALL, LANES), F32)] if last_step else [], sigma, force_table, partial, extra, p, scale, grad_table,
             )
             if last_step:
                 partial = results[0]
@@ -899,7 +901,7 @@
             sent.append(call(own_kernel, "own", shaped(rows, LANES), [], total, select))
     nodal = call(nodal_kernel, "nodal", shaped(24, FACE), [], partial, spread)
     final = call(
-        finish_kernel, "finish", shaped(1, 3, 8, FACE), [pltpu.VMEM((ROWS, LANES), F32), pltpu.VMEM((8, WIDE_FACE), F32)],
+        finish_kernel, "finish", shaped(1, 3, 8, FACE), [pltpu.VMEM((TALL, LANES), F32), pltpu.VMEM((8, WIDE_FACE), F32)],
         before, nodal, face_scale, node_lanes, flops=250000000,
     )
     kernels = call(

time: 40.8 us -> 40.8 us (level)
  no operation moved by 1% of the time
where the time goes in v9:
time: 40.8 us; the launch traced here: 40.7 us
  starting transfers between devices  18.6 us (46%)
  Pallas kernels  14.8 us (36%)
  waiting for transfers between devices  4.24 us (10%)
  local copies, waits for them, and re-layouts  2.05 us (5%)
  between operations  1.01 us (2%)
    pallas_call x17, Pallas kernels, call(): pl.pallas_call(kernel, name=name, out_shape=outs, in_specs=[HBM if at in...  14.8 us
    ppermute x5, starting transfers between devices, passed_along(): lax.ppermute(value, axis, [(source, (source + steps) % count) for source...  7.2 us
    ppermute x4, starting transfers between devices, swapped(): return lax.ppermute(value, axis, pairs)  6.9 us
    ppermute x3, starting transfers between devices, per_device(): lax.ppermute(blocks[k - 1], 'sub', [(j, j ^ k) for j in range(subs)])  4.45 us
    ppermute x4, waiting for transfers between devices, swapped(): return lax.ppermute(value, axis, pairs)  3.62 us
    unnamed x31, local copies, waits for them, and re-layouts  2.05 us
  transfers between devices with their start and end apart: 12, of which 3 were waited for; matrix products, arithmetic and copies ran while one was open for 3% of the time, Pallas kernels for 25%

profile of v9, /device:TPU:0, one launch (start us, length us, event | category | flops | bytes accessed | tf_op | source)
XLA Modules:
  0.0 40.7 jit_solution(7569663732553842248)
XLA Ops:
  0.6 1.0 %gather.1 = f32[8,1152]{1,0:T(8,128)S(1)} custom-call(f32[1,3,8,1089]{3,2,1,0:T(8,128)} %now_ref.3, f32[1,3,8,1089]{3,2,1,0:T(8,128)} %prev_ref.3, f32[8,1089]{1,0:T(8,128)} %density_ref.3), custom_call_target="tpu_custom_call" | custom-call | bytes 3000000 | tf_op jit(solution)/shard_map/gather/pallas_call | solution.py:760
  1.8 7.0 %collective-permute-start = (f32[8,1152]{1,0:T(8,128)S(1)}, f32[8,1152]{1,0:T(8,128)S(1)}, u32[]{:S(2)}, u32[]{:S(2)}) collective-permute-start(f32[8,1152]{1,0:T(8,128)S(1)} %gather.1), channel_id=1, source_target_pairs={{0,15},{1,0},{2,1},{3,2},{4,3},{5,4},{6,5},{7,6},{8,7},{9,8},{10,9... | collective-permute-start | bytes 110600 | tf_op jit(solution)/shard_map/ppermute | solution.py:774
  8.8 1.3 %copy.21 = f32[1,3,5,125,128]{4,3,0,2,1:T(8,128)S(1)} copy(f32[1,3,5,125,128]{4,0,3,2,1:T(1,128)} %param.18) | data formatting | bytes 1920000
  10.2 2.7 %prologue.1 = (f32[3,320,128]{2,1,0:T(8,128)S(1)}, f32[3,320,128]{2,1,0:T(8,128)S(1)}, f32[320,128]{1,0:T(8,128)S(1)}, f32[5,125,128]{2,1,0:T(8,128)S(1)}, bf16[...) custom-call(f32[1,3,8,1089]{3,2,1,0:T(8,128)S(1)} %copy-done.8, ...), custom_call_target="tpu_custom_call" | custom-call | bytes 3000000 | tf_op jit(solution)/shard_map/prologue/pallas_call | solution.py:760
  13.0 0.9 %step.3 = (f32[6,125,128]{2,1,0:T(8,128)S(1)}, f32[384,384]{1,0:T(8,128)S(1)}, f32[40,128]{1,0:T(8,128)S(1)}, f32[40,128]{1,0:T(8,128)S(1)}, f32[5,125,128]{2,1,...) custom-call(f32[125,128]{1,0:T(8,128)S(1)} %copy-done.2, f32[125,128]{1,0:T(8,128)S(1)} %copy-done.3, ...), custom_call_target="tpu_custom_call" | custom-call | bytes 3000000 | tf_op jit(solution)/shard_map/step/pallas_call | solution.py:760
  14.0 3.4 %collective-permute-start.2 = (f32[40,128]{1,0:T(8,128)S(1)}, f32[40,128]{1,0:T(8,128)S(1)}, u32[]{:S(2)}, u32[]{:S(2)}) collective-permute-start(f32[40,128]{1,0:T(8,128)S(1)} %get-tuple-element.67), channel_id=1, source_target_pairs={{1,2},{2,1},{3,4},{4,3},{5,6},{6,5},{7,8},{8,7},{9,10},{10,9},{11,... | collective-permute-start | bytes 61448 | tf_op jit(solution)/shard_map/ppermute | solution.py:783
  17.4 0.7 %copy-done.13 = s32[2,64,1]{1,2,0:T(1,128)S(1)} copy-done((s32[2,64,1]{1,2,0:T(1,128)S(1)}, s32[2,64,1]{1,2,0:T(1,128)}, u32[]{:S(2)}) %copy-start.13) | copy-done | bytes 536
  18.5 1.2 %rest.3 = (f32[3,320,128]{2,1,0:T(8,128)S(1)}, f32[320,128]{1,0:T(8,128)S(1)}, f32[3,320,128]{2,1,0:T(8,128)S(1)}, f32[3,128,128]{2,1,0:T(8,128)S(1)}, f32[384,384]{1,0:T(8,128)S(1)}, /*index=5*/f32[40,128]{1,0:T(8,128)S(1)}) custom-call(f32[384,384]{1,0:T(8,128)S(1)} %get-tuple-element.54.sigma_ref, bf16[3,208,384]{2,1,0:T(8,128)(2,1)S(1)} %copy-done.1, ...), custom_call_target="tpu_custom_call" | custom-call | bytes 3000000 | tf_op jit(solution)/shard_map/rest/pallas_call | solution.py:760
  20.1 1.3 %collective-permute-done.2.refs_8_ = f32[40,128]{1,0:T(8,128)S(1)} collective-permute-done((f32[40,128]{1,0:T(8,128)S(1)}, f32[40,128]{1,0:T(8,128)S(1)}, u32[]{:S(2)}, u32[]{:S(2)}) %collective-permute-start.2) | collective-permute-done | bytes 20512 | tf_op jit(solution)/shard_map/ppermute | solution.py:783
  21.4 0.9 %step.4 = (f32[6,125,128]{2,1,0:T(8,128)S(1)}, f32[384,384]{1,0:T(8,128)S(1)}, f32[40,128]{1,0:T(8,128)S(1)}, f32[40,128]{1,0:T(8,128)S(1)}, f32[5,125,128]{2,1,...) custom-call(f32[125,128]{1,0:T(8,128)S(1)} %copy-done.2, f32[125,128]{1,0:T(8,128)S(1)} %copy-done.3, ...), custom_call_target="tpu_custom_call" | custom-call | bytes 3000000 | tf_op jit(solution)/shard_map/step/pallas_call | solution.py:760
  22.4 3.4 %collective-permute-start.5 = (f32[40,128]{1,0:T(8,128)S(1)}, f32[40,128]{1,0:T(8,128)S(1)}, u32[]{:S(2)}, u32[]{:S(2)}) collective-permute-start(f32[40,128]{1,0:T(8,128)S(1)} %get-tuple-element.82), channel_id=1, source_target_pairs={{1,2},{2,1},{3,4},{4,3},{5,6},{6,5},{7,8},{8,7},{9,10},{10,9},{11,... | collective-permute-start | bytes 61448 | tf_op jit(solution)/shard_map/ppermute | solution.py:783
  25.9 1.2 %rest.4 = (f32[3,320,128]{2,1,0:T(8,128)S(1)}, f32[3,320,128]{2,1,0:T(8,128)S(1)}, f32[3,128,128]{2,1,0:T(8,128)S(1)}, f32[384,384]{1,0:T(8,128)S(1)}) custom-call(f32[384,384]{1,0:T(8,128)S(1)} %get-tuple-element.71.sigma_ref, bf16[3,208,384]{2,1,0:T(8,128)(2,1)S(1)} %copy-done.1, f32[3,320,128]{2,1,0:T(8,128)S(1)} %get-tuple-element.72.partial_ref, ...), custom_call_target="tpu_custom_call" | custom-call | bytes 3000000 | tf_op jit(solution)/shard_map/rest/pallas_call | solution.py:760
  27.1 0.4 %parts.3.both_ref = f32[256,128]{1,0:T(8,128)S(1)} custom-call(f32[6,125,128]{2,1,0:T(8,128)S(1)} %get-tuple-element.78.strain_ref, bf16[3,128,128]{2,1,0:T(8,128)(2,1)S(1)} %get-tuple-element.79.low_ref, bf16[3,128,128]{2,1,0:T(8,128)(2,1)S(1)} %collective-permute-done.4.far_ref, f32[125,128]{1,0:T(8,128)S(1)} %copy-done.2, f32[125,128]{1,0:T(8,128)S(1)} %copy-done.3, ...), custom_call_target="tpu_custom_call" | custom-call | bytes 3000000 | tf_op jit(solution)/shard_map/parts/pallas_call | solution.py:760
  27.5 2.3 %collective-permute-done.5.odd_ref = f32[40,128]{1,0:T(8,128)S(1)} collective-permute-done((f32[40,128]{1,0:T(8,128)S(1)}, f32[40,128]{1,0:T(8,128)S(1)}, u32[]{:S(2)}, u32[]{:S(2)}) %collective-permute-start.5) | collective-permute-done | bytes 20512 | tf_op jit(solution)/shard_map/ppermute | solution.py:783
  30.2 0.7 %step.5 = (f32[6,125,128]{2,1,0:T(8,128)S(1)}, f32[384,384]{1,0:T(8,128)S(1)}, f32[40,128]{1,0:T(8,128)S(1)}) custom-call(f32[125,128]{1,0:T(8,128)S(1)} %copy-done.2, f32[125,128]{1,0:T(8,128)S(1)} %copy-done.3, f32[5,125,128]{2,1,0:T(8,128)S(1)} %get-tuple-element.63.refs_2_, f32[3,128]{1,0:T(4,128)S(1)} %copy-done.11, bf16[384,240]{1,0:T(8,128)(2,1)S(1)} %copy-done.5, ...), custom_call_target="tpu_custom_call" | custom-call | bytes 3000000 | tf_op jit(solution)/shard_map/step/pallas_call | solution.py:760
  30.9 0.6 %collective-permute-done.8.far_ref = bf16[3,128,128]{2,1,0:T(8,128)(2,1)S(1)} collective-permute-done((bf16[3,128,128]{2,1,0:T(8,128)(2,1)S(1)}, bf16[3,128,128]{2,1,0:T(8,128)(2,1)S(1)}, u32[]{:S(2)}, u32[]{:S(2)}) %collective-permute-start.8) | collective-permute-done | bytes 98336 | tf_op jit(solution)/shard_map/ppermute | solution.py:774
  31.5 0.7 %send.1 = (f32[256,128]{1,0:T(8,128)S(1)}, s16[128,128]{1,0:T(8,128)(2,1)S(1)}, s16[128,128]{1,0:T(8,128)(2,1)S(1)}, s16[128,128]{1,0:T(8,128)(2,1)S(1)}) custom-call(f32[6,125,128]{2,1,0:T(8,128)S(1)} %get-tuple-element.92.strain_ref, bf16[3,128,128]{2,1,0:T(8,128)(2,1)S(1)} %get-tuple-element.93.low_ref, ...), custom_call_target="tpu_custom_call" | custom-call | bytes 3000000 | tf_op jit(solution)/shard_map/send/pallas_call | solution.py:760
  32.2 0.5 %collective-permute-start.9 = (s16[128,128]{1,0:T(8,128)(2,1)S(1)}, s16[128,128]{1,0:T(8,128)(2,1)S(1)}, u32[]{:S(2)}, u32[]{:S(2)}) collective-permute-start(s16[128,128]{1,0:T(8,128)(2,1)S(1)} %get-tuple-element.96), channel_id=1, source_target_pairs={{0,3},{1,2},{2,1},{3,0},{4,7},{5,6},{6,5},{7,4},{8,11},{9,10},{10,... | collective-permute-start | bytes 98312 | tf_op jit(solution)/shard_map/ppermute | solution.py:900
  32.7 1.0 %collective-permute-start.10 = (s16[128,128]{1,0:T(8,128)(2,1)S(1)}, s16[128,128]{1,0:T(8,128)(2,1)S(1)}, u32[]{:S(2)}, u32[]{:S(2)}) collective-permute-start(s16[128,128]{1,0:T(8,128)(2,1)S(1)} %get-tuple-element.97), channel_id=1, source_target_pairs={{0,2},{1,3},{2,0},{3,1},{4,6},{5,7},{6,4},{7,5},{8,10},{9,11},{10,... | collective-permute-start | bytes 98312 | tf_op jit(solution)/shard_map/ppermute | solution.py:900
  33.7 2.9 %collective-permute-start.11 = (s16[128,128]{1,0:T(8,128)(2,1)S(1)}, s16[128,128]{1,0:T(8,128)(2,1)S(1)}, u32[]{:S(2)}, u32[]{:S(2)}) collective-permute-start(s16[128,128]{1,0:T(8,128)(2,1)S(1)} %get-tuple-element.98), channel_id=1, source_target_pairs={{0,1},{1,0},{2,3},{3,2},{4,5},{5,4},{6,7},{7,6},{8,9},{9,8},{10,11... | collective-permute-start | bytes 98312 | tf_op jit(solution)/shard_map/ppermute | solution.py:900
  36.6 0.7 %rest.5.partial_ref = f32[3,320,128]{2,1,0:T(8,128)S(1)} custom-call(f32[384,384]{1,0:T(8,128)S(1)} %get-tuple-element.88.sigma_ref, bf16[3,208,384]{2,1,0:T(8,128)(2,1)S(1)} %copy-done.1, f32[3,320,128]{2,1,0:T(8,128)S(1)} %get-tuple-element.89.partial_ref, f32[3,40,128]{2,1,0:T(8,128)S(1)} %get-tuple-element.85.refs_7_.delta_ref, ...), custom_call_target="tpu_custom_call" | custom-call | bytes 3000000 | tf_op jit(solution)/shard_map/rest/pallas_call | solution.py:760
  37.4 0.9 %nodal.1.nodal_ref = f32[24,1089]{1,0:T(8,128)S(1)} custom-call(f32[3,320,128]{2,1,0:T(8,128)S(1)} %rest.5.partial_ref, bf16[256,1664]{1,0:T(8,128)(2,1)S(1)} %get-tuple-element.91.spread_ref), custom_call_target="tpu_custom_call" | custom-call | bytes 3000000 | tf_op jit(solution)/shard_map/nodal/pallas_call | solution.py:760
  38.3 1.2 %finish.1 = f32[1,3,8,1089]{3,2,1,0:T(8,128)} custom-call(f32[40,128]{1,0:T(8,128)S(1)} %collective-permute-done.7.before_ref, f32[24,1089]{1,0:T(8,128)S(1)} %nodal.1.nodal_ref, f32[40,128]{1,0:T(8,128)S(1)} %get-tuple-element.69.refs_10_.face_scale_ref, s32[9,128]{1,0:T(8,128)S(1)} %copy-done.14), custom_call_target="tpu_custom_call" | custom-call | flops 250000000 | bytes 3000000 | tf_op jit(solution)/shard_map/finish/pallas_call | solution.py:760
  39.7 1.0 %sum.1 = f32[250,1,256]{2,1,0:T(1,128)} custom-call(s16[128,128]{1,0:T(8,128)(2,1)S(1)} %collective-permute-done.9.refs_0_, s16[128,128]{1,0:T(8,128)(2,1)S(1)} %collective-permute-done.10.refs_1_, s16[128,128]{1,0:T(8,128)(2,1)S(1)} %collective-permute-done.11.refs_2_, f32[128,128]{1,0:T(8,128)S(1)} %own.1.refs_3_), custom_call_target="tpu_custom_call" | custom-call | bytes 3000000 | tf_op jit(solution)/shard_map/sum/pallas_call | solution.py:760
  (48 shorter events, 1.6 us)
Async XLA Ops:
  0.6 9.5 %copy-start.8 = (f32[1,3,8,1089]{3,2,1,0:T(8,128)S(1)}, f32[1,3,8,1089]{3,2,1,0:T(8,128)}, u32[]{:S(2)}) copy-start(f32[1,3,8,1089]{3,2,1,0:T(8,128)} %now_ref.3) | copy-start | bytes 313636
  0.6 9.5 %copy-start.9 = (f32[1,3,8,1089]{3,2,1,0:T(8,128)S(1)}, f32[1,3,8,1089]{3,2,1,0:T(8,128)}, u32[]{:S(2)}) copy-start(f32[1,3,8,1089]{3,2,1,0:T(8,128)} %prev_ref.3) | copy-start | bytes 313636
  1.7 8.4 %copy-start = (bf16[3,384,256]{2,1,0:T(8,128)(2,1)S(1)}, bf16[3,384,256]{2,1,0:T(8,128)(2,1)}, u32[]{:S(2)}) copy-start(bf16[3,384,256]{2,1,0:T(8,128)(2,1)} %constant.16.clone.refs_0_.grad_table) | copy-start | bytes 1769476
  1.7 8.4 %copy-start.1 = (bf16[3,208,384]{2,1,0:T(8,128)(2,1)S(1)}, bf16[3,208,384]{2,1,0:T(8,128)(2,1)}, u32[]{:S(2)}) copy-start(bf16[3,208,384]{2,1,0:T(8,128)(2,1)} %constant.17.clone.refs_2_.force_table) | copy-start | bytes 1437700
  1.7 8.4 %copy-start.2 = (f32[125,128]{1,0:T(8,128)S(1)}, f32[125,128]{1,0:T(8,128)}, u32[]{:S(2)}) copy-start(f32[125,128]{1,0:T(8,128)} %lame_ref.5) | copy-start | bytes 192004
  1.7 8.4 %copy-start.3 = (f32[125,128]{1,0:T(8,128)S(1)}, f32[125,128]{1,0:T(8,128)}, u32[]{:S(2)}) copy-start(f32[125,128]{1,0:T(8,128)} %mu_ref.5) | copy-start | bytes 192004
  1.7 8.4 %copy-start.4 = (bf16[3,80,256]{2,1,0:T(8,128)(2,1)S(1)}, bf16[3,80,256]{2,1,0:T(8,128)(2,1)}, u32[]{:S(2)}) copy-start(bf16[3,80,256]{2,1,0:T(8,128)(2,1)} %constant.18.clone.refs_1_.refs_5_) | copy-start | bytes 368644
  1.7 8.4 %copy-start.5 = (bf16[384,240]{1,0:T(8,128)(2,1)S(1)}, bf16[384,240]{1,0:T(8,128)(2,1)}, u32[]{:S(2)}) copy-start(bf16[384,240]{1,0:T(8,128)(2,1)} %constant.19.clone.refs_4_) | copy-start | bytes 552964
  1.8 8.4 %copy-start.6 = (bf16[384,240]{1,0:T(8,128)(2,1)S(1)}, bf16[384,240]{1,0:T(8,128)(2,1)}, u32[]{:S(2)}) copy-start(bf16[384,240]{1,0:T(8,128)(2,1)} %constant.20.clone.refs_3_.refs_4_) | copy-start | bytes 552964
  1.8 8.4 %copy-start.7 = (f32[320,128]{1,0:T(8,128)S(1)}, f32[320,128]{1,0:T(8,128)}, u32[]{:S(2)}) copy-start(f32[320,128]{1,0:T(8,128)} %constant.23.clone.mass_ref) | copy-start | bytes 491524
  1.8 8.4 %copy-start.10 = (f32[8,1089]{1,0:T(8,128)S(1)}, f32[8,1089]{1,0:T(8,128)}, u32[]{:S(2)}) copy-start(f32[8,1089]{1,0:T(8,128)} %density_ref.3) | copy-start | bytes 104548
  1.8 11.1 %collective-permute-start = (f32[8,1152]{1,0:T(8,128)S(1)}, f32[8,1152]{1,0:T(8,128)S(1)}, u32[]{:S(2)}, u32[]{:S(2)}) collective-permute-start(f32[8,1152]{1,0:T(8,128)S(1)} %gather.1), channel_id=1, source_target_pairs={{0,15},{1,0},{2,1},{3,2},{4,3},{5,4},{6,5},{7,6},{8,7},{9,8},{10,9... | collective-permute-start | bytes 110600 | tf_op jit(solution)/shard_map/ppermute | solution.py:774
  10.2 2.7 %copy-start.12 = (s32[13,128]{1,0:T(8,128)S(1)}, s32[13,128]{1,0:T(8,128)}, u32[]{:S(2)}) copy-start(s32[13,128]{1,0:T(8,128)} %constant.21.clone.refs_9_.lanes_ref) | copy-start | bytes 19972
  13.9 5.8 %collective-permute-start.1 = (bf16[3,128,128]{2,1,0:T(8,128)(2,1)S(1)}, bf16[3,128,128]{2,1,0:T(8,128)(2,1)S(1)}, u32[]{:S(2)}, u32[]{:S(2)}) collective-permute-start(bf16[3,128,128]{2,1,0:T(8,128)(2,1)S(1)} %get-tuple-element.60.low_ref), channel_id=1, source_target_pairs={{0,16},{16,0},{1,17},{17,1},{2,18},{18,2},{3,19},{19,3},{4,20},{20... | collective-permute-start | bytes 294920 | tf_op jit(solution)/shard_map/ppermute | solution.py:774
  14.0 7.4 %collective-permute-start.2 = (f32[40,128]{1,0:T(8,128)S(1)}, f32[40,128]{1,0:T(8,128)S(1)}, u32[]{:S(2)}, u32[]{:S(2)}) collective-permute-start(f32[40,128]{1,0:T(8,128)S(1)} %get-tuple-element.67), channel_id=1, source_target_pairs={{1,2},{2,1},{3,4},{4,3},{5,6},{6,5},{7,8},{8,7},{9,10},{10,9},{11,... | collective-permute-start | bytes 61448 | tf_op jit(solution)/shard_map/ppermute | solution.py:783
  17.4 4.0 %collective-permute-start.3 = (f32[40,128]{1,0:T(8,128)S(1)}, f32[40,128]{1,0:T(8,128)S(1)}, u32[]{:S(2)}, u32[]{:S(2)}) collective-permute-start(f32[40,128]{1,0:T(8,128)S(1)} %get-tuple-element.68), channel_id=1, source_target_pairs={{0,1},{1,0},{2,3},{3,2},{4,5},{5,4},{6,7},{7,6},{8,9},{9,8},{10,11... | collective-permute-start | bytes 61448 | tf_op jit(solution)/shard_map/ppermute | solution.py:783
  22.3 4.8 %collective-permute-start.4 = (bf16[3,128,128]{2,1,0:T(8,128)(2,1)S(1)}, bf16[3,128,128]{2,1,0:T(8,128)(2,1)S(1)}, u32[]{:S(2)}, u32[]{:S(2)}) collective-permute-start(bf16[3,128,128]{2,1,0:T(8,128)(2,1)S(1)} %get-tuple-element.79.low_ref), channel_id=1, source_target_pairs={{0,16},{16,0},{1,17},{17,1},{2,18},{18,2},{3,19},{19,3},{4,20},{20... | collective-permute-start | bytes 294920 | tf_op jit(solution)/shard_map/ppermute | solution.py:774
  22.4 7.4 %collective-permute-start.5 = (f32[40,128]{1,0:T(8,128)S(1)}, f32[40,128]{1,0:T(8,128)S(1)}, u32[]{:S(2)}, u32[]{:S(2)}) collective-permute-start(f32[40,128]{1,0:T(8,128)S(1)} %get-tuple-element.82), channel_id=1, source_target_pairs={{1,2},{2,1},{3,4},{4,3},{5,6},{6,5},{7,8},{8,7},{9,10},{10,9},{11,... | collective-permute-start | bytes 61448 | tf_op jit(solution)/shard_map/ppermute | solution.py:783
  25.9 4.0 %collective-permute-start.6 = (f32[40,128]{1,0:T(8,128)S(1)}, f32[40,128]{1,0:T(8,128)S(1)}, u32[]{:S(2)}, u32[]{:S(2)}) collective-permute-start(f32[40,128]{1,0:T(8,128)S(1)} %get-tuple-element.83), channel_id=1, source_target_pairs={{0,1},{1,0},{2,3},{3,2},{4,5},{5,4},{6,7},{7,6},{8,9},{9,8},{10,11... | collective-permute-start | bytes 61448 | tf_op jit(solution)/shard_map/ppermute | solution.py:783
  30.1 1.4 %collective-permute-start.8 = (bf16[3,128,128]{2,1,0:T(8,128)(2,1)S(1)}, bf16[3,128,128]{2,1,0:T(8,128)(2,1)S(1)}, u32[]{:S(2)}, u32[]{:S(2)}) collective-permute-start(bf16[3,128,128]{2,1,0:T(8,128)(2,1)S(1)} %get-tuple-element.93.low_ref), channel_id=1, source_target_pairs={{0,16},{16,0},{1,17},{17,1},{2,18},{18,2},{3,19},{19,3},{4,20},{20... | collective-permute-start | bytes 294920 | tf_op jit(solution)/shard_map/ppermute | solution.py:774
  30.9 7.4 %collective-permute-start.7 = (f32[40,128]{1,0:T(8,128)S(1)}, f32[40,128]{1,0:T(8,128)S(1)}, u32[]{:S(2)}, u32[]{:S(2)}) collective-permute-start(f32[40,128]{1,0:T(8,128)S(1)} %get-tuple-element.87), channel_id=1, source_target_pairs={{0,1},{1,2},{2,3},{3,4},{4,5},{5,6},{6,7},{7,8},{8,9},{9,10},{10,1... | collective-permute-start | bytes 61448 | tf_op jit(solution)/shard_map/ppermute | solution.py:774
  32.2 7.5 %collective-permute-start.9 = (s16[128,128]{1,0:T(8,128)(2,1)S(1)}, s16[128,128]{1,0:T(8,128)(2,1)S(1)}, u32[]{:S(2)}, u32[]{:S(2)}) collective-permute-start(s16[128,128]{1,0:T(8,128)(2,1)S(1)} %get-tuple-element.96), channel_id=1, source_target_pairs={{0,3},{1,2},{2,1},{3,0},{4,7},{5,6},{6,5},{7,4},{8,11},{9,10},{10,... | collective-permute-start | bytes 98312 | tf_op jit(solution)/shard_map/ppermute | solution.py:900
  32.7 7.0 %collective-permute-start.10 = (s16[128,128]{1,0:T(8,128)(2,1)S(1)}, s16[128,128]{1,0:T(8,128)(2,1)S(1)}, u32[]{:S(2)}, u32[]{:S(2)}) collective-permute-start(s16[128,128]{1,0:T(8,128)(2,1)S(1)} %get-tuple-element.97), channel_id=1, source_target_pairs={{0,2},{1,3},{2,0},{3,1},{4,6},{5,7},{6,4},{7,5},{8,10},{9,11},{10,... | collective-permute-start | bytes 98312 | tf_op jit(solution)/shard_map/ppermute | solution.py:900
  33.7 5.9 %collective-permute-start.11 = (s16[128,128]{1,0:T(8,128)(2,1)S(1)}, s16[128,128]{1,0:T(8,128)(2,1)S(1)}, u32[]{:S(2)}, u32[]{:S(2)}) collective-permute-start(s16[128,128]{1,0:T(8,128)(2,1)S(1)} %get-tuple-element.98), channel_id=1, source_target_pairs={{0,1},{1,0},{2,3},{3,2},{4,5},{5,4},{6,7},{7,6},{8,9},{9,8},{10,11... | collective-permute-start | bytes 98312 | tf_op jit(solution)/shard_map/ppermute | solution.py:900
  (3 other events, 3.0 us)

commit v10 on v9

--- a/solution.py
+++ b/solution.py
@@ -671,26 +671,37 @@
 
 
 def sum_kernel(order, *refs):
-    in_refs, out_ref = refs[:-1], refs[-1]
+    in_refs, (out_ref, rows_ref, sems) = refs[:-3], refs[-3:]
     rows = in_refs[0].shape[0]
     slots = rows // 2
     pieces = 256 // rows
     group = lanes_of((rows, LANES)) // slots
-    blocks = [[jnp.zeros((rows, LANES), F32)] * 2 for _ in range(pieces)]
-    for k, ref in zip(order, in_refs):
-        source = lax.axis_index("sub") ^ k
-        spot = source % pieces
-        value = ref[...].astype(jnp.int32).astype(F32) if k > 0 else ref[...]
-        for j in range(pieces):
+    sources = [lax.axis_index("sub") ^ k for k in order]
+    values = [ref[...].astype(jnp.int32).astype(F32) if k > 0 else ref[...] for k, ref in zip(order, in_refs)]
+    scales = None
+    copies = []
+    for j in range(pieces - 1, -1, -1):
+        halves = [jnp.zeros((rows, LANES), F32)] * 2
+        for source, value in zip(sources, values):
+            spot = source % pieces
             moved = pltpu.roll(value, ((spot + pieces - j) % pieces) * slots, 1)
             for t in range(2):
-                here = (group == spot) & (source // pieces == t)
-                blocks[j][t] = jnp.where(here, moved, blocks[j][t])
-    value = jnp.concatenate([jnp.concatenate(row, axis=1) for row in blocks], axis=0)
-    first, second = [group_scale(value[row : row + 1], value[row + 1 : row + 2]) for row in (250, 252)]
-    row = lax.broadcasted_iota(jnp.int32, (256, 256), 0)
-    value = value * jnp.where(row < 125, first, second)
-    out_ref[:, 0, :] = value[0:250]
+                halves[t] = jnp.where((group == spot) & (source // pieces == t), moved, halves[t])
+        value = jnp.concatenate(halves, axis=1)
+        if scales is None:
+            at = 250 - j * rows
+            scales = [group_scale(value[row : row + 1], value[row + 1 : row + 2]) for row in (at, at + 2)]
+        row = lax.broadcasted_iota(jnp.int32, (rows, 256), 0) + j * rows
+        value = value * jnp.where(row < 125, scales[0], scales[1])
+        for start in range(0, rows, 64):
+            first, last = j * rows + start, min(j * rows + start + 64, 250)
+            rows_ref[first:last, 0, :] = value[start : start + last - first]
+            at = pl.ds(first, last - first)
+            copy = pltpu.make_async_copy(rows_ref.at[at], out_ref.at[at], sems.at[len(copies)])
+            copy.start()
+            copies.append(copy)
+    for copy in copies:
+        copy.wait()
 
 
 def to_nodal(columns, spread_ref, nodal_ref):
@@ -756,13 +767,13 @@
     return jax.ShapeDtypeStruct(shape, dtype)
 
 
-def call(kernel, name, outs, scratch, *args, outside=(), flops=0, room=32 * 1024):
+def call(kernel, name, outs, scratch, *args, outside=(), written_outside=False, flops=0, room=32 * 1024):
     return pl.pallas_call(
         kernel,
         name=name,
         out_shape=outs,
         in_specs=[HBM if at in outside else VMEM for at in range(len(args))],
-        out_specs=jax.tree.map(lambda _: VMEM, outs),
+        out_specs=jax.tree.map(lambda _: HBM if written_outside else VMEM, outs),
         scratch_shapes=scratch,
         compiler_params=pltpu.CompilerParams(vmem_limit_bytes=room * 1024),
         cost_estimate=pl.CostEstimate(flops=flops, bytes_accessed=3000000, transcendentals=0),
@@ -905,7 +916,8 @@
         before, nodal, face_scale, node_lanes, flops=250000000,
     )
     kernels = call(
-        lambda *refs: sum_kernel(order, *refs), "sum", shaped(250, 1, 256), [], *sent
+        lambda *refs: sum_kernel(order, *refs), "sum", shaped(250, 1, 256),
+        [pltpu.VMEM((250, 1, 256), F32), pltpu.SemaphoreType.DMA((4,))], *sent, written_outside=True,
     )
     return final, jnp.transpose(kernels, (1, 2, 0))
 

time: 40.8 us -> 40.8 us (level)
  no operation moved by 1% of the time
where the time goes in v10:
time: 40.8 us; the launch traced here: 40.6 us
  starting transfers between devices  18.6 us (46%)
  Pallas kernels  14.8 us (36%)
  waiting for transfers between devices  4.24 us (10%)
  local copies, waits for them, and re-layouts  2.05 us (5%)
  between operations  1.01 us (2%)
    pallas_call x17, Pallas kernels, call(): pl.pallas_call(kernel, name=name, out_shape=outs, in_specs=[HBM if at in...  14.8 us
    ppermute x5, starting transfers between devices, passed_along(): lax.ppermute(value, axis, [(source, (source + steps) % count) for source...  7.2 us
    ppermute x4, starting transfers between devices, swapped(): return lax.ppermute(value, axis, pairs)  6.9 us
    ppermute x3, starting transfers between devices, per_device(): lax.ppermute(blocks[k - 1], 'sub', [(j, j ^ k) for j in range(subs)])  4.45 us
    ppermute x4, waiting for transfers between devices, swapped(): return lax.ppermute(value, axis, pairs)  3.62 us
    unnamed x31, local copies, waits for them, and re-layouts  2.05 us
  transfers between devices with their start and end apart: 12, of which 3 were waited for; matrix products, arithmetic and copies ran while one was open for 3% of the time, Pallas kernels for 25%

profile of v10, /device:TPU:0, one launch (start us, length us, event | category | flops | bytes accessed | tf_op | source)
XLA Modules:
  0.0 40.6 jit_solution(18160282741194415774)
XLA Ops:
  0.6 1.0 %gather.1 = f32[8,1152]{1,0:T(8,128)S(1)} custom-call(f32[1,3,8,1089]{3,2,1,0:T(8,128)} %now_ref.3, f32[1,3,8,1089]{3,2,1,0:T(8,128)} %prev_ref.3, f32[8,1089]{1,0:T(8,128)} %density_ref.3), custom_call_target="tpu_custom_call" | custom-call | bytes 3000000 | tf_op jit(solution)/shard_map/gather/pallas_call | solution.py:771
  1.8 7.0 %collective-permute-start = (f32[8,1152]{1,0:T(8,128)S(1)}, f32[8,1152]{1,0:T(8,128)S(1)}, u32[]{:S(2)}, u32[]{:S(2)}) collective-permute-start(f32[8,1152]{1,0:T(8,128)S(1)} %gather.1), channel_id=1, source_target_pairs={{0,15},{1,0},{2,1},{3,2},{4,3},{5,4},{6,5},{7,6},{8,7},{9,8},{10,9... | collective-permute-start | bytes 110600 | tf_op jit(solution)/shard_map/ppermute | solution.py:785
  8.8 1.3 %copy.21 = f32[1,3,5,125,128]{4,3,0,2,1:T(8,128)S(1)} copy(f32[1,3,5,125,128]{4,0,3,2,1:T(1,128)} %param.18) | data formatting | bytes 1920000
  10.2 2.7 %prologue.1 = (f32[3,320,128]{2,1,0:T(8,128)S(1)}, f32[3,320,128]{2,1,0:T(8,128)S(1)}, f32[320,128]{1,0:T(8,128)S(1)}, f32[5,125,128]{2,1,0:T(8,128)S(1)}, bf16[...) custom-call(f32[1,3,8,1089]{3,2,1,0:T(8,128)S(1)} %copy-done.8, ...), custom_call_target="tpu_custom_call" | custom-call | bytes 3000000 | tf_op jit(solution)/shard_map/prologue/pallas_call | solution.py:771
  13.0 0.9 %step.3 = (f32[6,125,128]{2,1,0:T(8,128)S(1)}, f32[384,384]{1,0:T(8,128)S(1)}, f32[40,128]{1,0:T(8,128)S(1)}, f32[40,128]{1,0:T(8,128)S(1)}, f32[5,125,128]{2,1,...) custom-call(f32[125,128]{1,0:T(8,128)S(1)} %copy-done.2, f32[125,128]{1,0:T(8,128)S(1)} %copy-done.3, ...), custom_call_target="tpu_custom_call" | custom-call | bytes 3000000 | tf_op jit(solution)/shard_map/step/pallas_call | solution.py:771
  14.0 3.4 %collective-permute-start.2 = (f32[40,128]{1,0:T(8,128)S(1)}, f32[40,128]{1,0:T(8,128)S(1)}, u32[]{:S(2)}, u32[]{:S(2)}) collective-permute-start(f32[40,128]{1,0:T(8,128)S(1)} %get-tuple-element.67), channel_id=1, source_target_pairs={{1,2},{2,1},{3,4},{4,3},{5,6},{6,5},{7,8},{8,7},{9,10},{10,9},{11,... | collective-permute-start | bytes 61448 | tf_op jit(solution)/shard_map/ppermute | solution.py:794
  17.4 0.7 %copy-done.13 = s32[2,64,1]{1,2,0:T(1,128)S(1)} copy-done((s32[2,64,1]{1,2,0:T(1,128)S(1)}, s32[2,64,1]{1,2,0:T(1,128)}, u32[]{:S(2)}) %copy-start.13) | copy-done | bytes 536
  18.5 1.2 %rest.3 = (f32[3,320,128]{2,1,0:T(8,128)S(1)}, f32[320,128]{1,0:T(8,128)S(1)}, f32[3,320,128]{2,1,0:T(8,128)S(1)}, f32[3,128,128]{2,1,0:T(8,128)S(1)}, f32[384,384]{1,0:T(8,128)S(1)}, /*index=5*/f32[40,128]{1,0:T(8,128)S(1)}) custom-call(f32[384,384]{1,0:T(8,128)S(1)} %get-tuple-element.54.sigma_ref, bf16[3,208,384]{2,1,0:T(8,128)(2,1)S(1)} %copy-done.1, ...), custom_call_target="tpu_custom_call" | custom-call | bytes 3000000 | tf_op jit(solution)/shard_map/rest/pallas_call | solution.py:771
  20.1 1.3 %collective-permute-done.2.refs_8_ = f32[40,128]{1,0:T(8,128)S(1)} collective-permute-done((f32[40,128]{1,0:T(8,128)S(1)}, f32[40,128]{1,0:T(8,128)S(1)}, u32[]{:S(2)}, u32[]{:S(2)}) %collective-permute-start.2) | collective-permute-done | bytes 20512 | tf_op jit(solution)/shard_map/ppermute | solution.py:794
  21.4 0.9 %step.4 = (f32[6,125,128]{2,1,0:T(8,128)S(1)}, f32[384,384]{1,0:T(8,128)S(1)}, f32[40,128]{1,0:T(8,128)S(1)}, f32[40,128]{1,0:T(8,128)S(1)}, f32[5,125,128]{2,1,...) custom-call(f32[125,128]{1,0:T(8,128)S(1)} %copy-done.2, f32[125,128]{1,0:T(8,128)S(1)} %copy-done.3, ...), custom_call_target="tpu_custom_call" | custom-call | bytes 3000000 | tf_op jit(solution)/shard_map/step/pallas_call | solution.py:771
  22.4 3.4 %collective-permute-start.5 = (f32[40,128]{1,0:T(8,128)S(1)}, f32[40,128]{1,0:T(8,128)S(1)}, u32[]{:S(2)}, u32[]{:S(2)}) collective-permute-start(f32[40,128]{1,0:T(8,128)S(1)} %get-tuple-element.82), channel_id=1, source_target_pairs={{1,2},{2,1},{3,4},{4,3},{5,6},{6,5},{7,8},{8,7},{9,10},{10,9},{11,... | collective-permute-start | bytes 61448 | tf_op jit(solution)/shard_map/ppermute | solution.py:794
  25.9 1.2 %rest.4 = (f32[3,320,128]{2,1,0:T(8,128)S(1)}, f32[3,320,128]{2,1,0:T(8,128)S(1)}, f32[3,128,128]{2,1,0:T(8,128)S(1)}, f32[384,384]{1,0:T(8,128)S(1)}) custom-call(f32[384,384]{1,0:T(8,128)S(1)} %get-tuple-element.71.sigma_ref, bf16[3,208,384]{2,1,0:T(8,128)(2,1)S(1)} %copy-done.1, f32[3,320,128]{2,1,0:T(8,128)S(1)} %get-tuple-element.72.partial_ref, ...), custom_call_target="tpu_custom_call" | custom-call | bytes 3000000 | tf_op jit(solution)/shard_map/rest/pallas_call | solution.py:771
  27.1 0.4 %parts.3.both_ref = f32[256,128]{1,0:T(8,128)S(1)} custom-call(f32[6,125,128]{2,1,0:T(8,128)S(1)} %get-tuple-element.78.strain_ref, bf16[3,128,128]{2,1,0:T(8,128)(2,1)S(1)} %get-tuple-element.79.low_ref, bf16[3,128,128]{2,1,0:T(8,128)(2,1)S(1)} %collective-permute-done.4.far_ref, f32[125,128]{1,0:T(8,128)S(1)} %copy-done.2, f32[125,128]{1,0:T(8,128)S(1)} %copy-done.3, ...), custom_call_target="tpu_custom_call" | custom-call | bytes 3000000 | tf_op jit(solution)/shard_map/parts/pallas_call | solution.py:771
  27.5 2.3 %collective-permute-done.5.odd_ref = f32[40,128]{1,0:T(8,128)S(1)} collective-permute-done((f32[40,128]{1,0:T(8,128)S(1)}, f32[40,128]{1,0:T(8,128)S(1)}, u32[]{:S(2)}, u32[]{:S(2)}) %collective-permute-start.5) | collective-permute-done | bytes 20512 | tf_op jit(solution)/shard_map/ppermute | solution.py:794
  30.2 0.7 %step.5 = (f32[6,125,128]{2,1,0:T(8,128)S(1)}, f32[384,384]{1,0:T(8,128)S(1)}, f32[40,128]{1,0:T(8,128)S(1)}) custom-call(f32[125,128]{1,0:T(8,128)S(1)} %copy-done.2, f32[125,128]{1,0:T(8,128)S(1)} %copy-done.3, f32[5,125,128]{2,1,0:T(8,128)S(1)} %get-tuple-element.63.refs_2_, f32[3,128]{1,0:T(4,128)S(1)} %copy-done.11, bf16[384,240]{1,0:T(8,128)(2,1)S(1)} %copy-done.5, ...), custom_call_target="tpu_custom_call" | custom-call | bytes 3000000 | tf_op jit(solution)/shard_map/step/pallas_call | solution.py:771
  30.9 0.6 %collective-permute-done.8.far_ref = bf16[3,128,128]{2,1,0:T(8,128)(2,1)S(1)} collective-permute-done((bf16[3,128,128]{2,1,0:T(8,128)(2,1)S(1)}, bf16[3,128,128]{2,1,0:T(8,128)(2,1)S(1)}, u32[]{:S(2)}, u32[]{:S(2)}) %collective-permute-start.8) | collective-permute-done | bytes 98336 | tf_op jit(solution)/shard_map/ppermute | solution.py:785
  31.5 0.7 %send.1 = (f32[256,128]{1,0:T(8,128)S(1)}, s16[128,128]{1,0:T(8,128)(2,1)S(1)}, s16[128,128]{1,0:T(8,128)(2,1)S(1)}, s16[128,128]{1,0:T(8,128)(2,1)S(1)}) custom-call(f32[6,125,128]{2,1,0:T(8,128)S(1)} %get-tuple-element.92.strain_ref, bf16[3,128,128]{2,1,0:T(8,128)(2,1)S(1)} %get-tuple-element.93.low_ref, ...), custom_call_target="tpu_custom_call" | custom-call | bytes 3000000 | tf_op jit(solution)/shard_map/send/pallas_call | solution.py:771
  32.2 0.5 %collective-permute-start.9 = (s16[128,128]{1,0:T(8,128)(2,1)S(1)}, s16[128,128]{1,0:T(8,128)(2,1)S(1)}, u32[]{:S(2)}, u32[]{:S(2)}) collective-permute-start(s16[128,128]{1,0:T(8,128)(2,1)S(1)} %get-tuple-element.96), channel_id=1, source_target_pairs={{0,3},{1,2},{2,1},{3,0},{4,7},{5,6},{6,5},{7,4},{8,11},{9,10},{10,... | collective-permute-start | bytes 98312 | tf_op jit(solution)/shard_map/ppermute | solution.py:911
  32.7 1.0 %collective-permute-start.10 = (s16[128,128]{1,0:T(8,128)(2,1)S(1)}, s16[128,128]{1,0:T(8,128)(2,1)S(1)}, u32[]{:S(2)}, u32[]{:S(2)}) collective-permute-start(s16[128,128]{1,0:T(8,128)(2,1)S(1)} %get-tuple-element.97), channel_id=1, source_target_pairs={{0,2},{1,3},{2,0},{3,1},{4,6},{5,7},{6,4},{7,5},{8,10},{9,11},{10,... | collective-permute-start | bytes 98312 | tf_op jit(solution)/shard_map/ppermute | solution.py:911
  33.7 2.9 %collective-permute-start.11 = (s16[128,128]{1,0:T(8,128)(2,1)S(1)}, s16[128,128]{1,0:T(8,128)(2,1)S(1)}, u32[]{:S(2)}, u32[]{:S(2)}) collective-permute-start(s16[128,128]{1,0:T(8,128)(2,1)S(1)} %get-tuple-element.98), channel_id=1, source_target_pairs={{0,1},{1,0},{2,3},{3,2},{4,5},{5,4},{6,7},{7,6},{8,9},{9,8},{10,11... | collective-permute-start | bytes 98312 | tf_op jit(solution)/shard_map/ppermute | solution.py:911
  36.6 0.7 %rest.5.partial_ref = f32[3,320,128]{2,1,0:T(8,128)S(1)} custom-call(f32[384,384]{1,0:T(8,128)S(1)} %get-tuple-element.88.sigma_ref, bf16[3,208,384]{2,1,0:T(8,128)(2,1)S(1)} %copy-done.1, f32[3,320,128]{2,1,0:T(8,128)S(1)} %get-tuple-element.89.partial_ref, f32[3,40,128]{2,1,0:T(8,128)S(1)} %get-tuple-element.85.refs_7_.delta_ref, ...), custom_call_target="tpu_custom_call" | custom-call | bytes 3000000 | tf_op jit(solution)/shard_map/rest/pallas_call | solution.py:771
  37.4 0.9 %nodal.1.nodal_ref = f32[24,1089]{1,0:T(8,128)S(1)} custom-call(f32[3,320,128]{2,1,0:T(8,128)S(1)} %rest.5.partial_ref, bf16[256,1664]{1,0:T(8,128)(2,1)S(1)} %get-tuple-element.91.spread_ref), custom_call_target="tpu_custom_call" | custom-call | bytes 3000000 | tf_op jit(solution)/shard_map/nodal/pallas_call | solution.py:771
  38.3 1.2 %finish.1 = f32[1,3,8,1089]{3,2,1,0:T(8,128)} custom-call(f32[40,128]{1,0:T(8,128)S(1)} %collective-permute-done.7.before_ref, f32[24,1089]{1,0:T(8,128)S(1)} %nodal.1.nodal_ref, f32[40,128]{1,0:T(8,128)S(1)} %get-tuple-element.69.refs_10_.face_scale_ref, s32[9,128]{1,0:T(8,128)S(1)} %copy-done.14), custom_call_target="tpu_custom_call" | custom-call | flops 250000000 | bytes 3000000 | tf_op jit(solution)/shard_map/finish/pallas_call | solution.py:771
  39.7 0.9 %sum.1 = f32[250,1,256]{2,1,0:T(1,128)} custom-call(s16[128,128]{1,0:T(8,128)(2,1)S(1)} %collective-permute-done.9.refs_0_, s16[128,128]{1,0:T(8,128)(2,1)S(1)} %collective-permute-done.10.refs_1_, s16[128,128]{1,0:T(8,128)(2,1)S(1)} %collective-permute-done.11.refs_2_, f32[128,128]{1,0:T(8,128)S(1)} %own.1.refs_3_), custom_call_target="tpu_custom_call" | custom-call | bytes 3000000 | tf_op jit(solution)/shard_map/sum/pallas_call | solution.py:771
  (48 shorter events, 1.6 us)
Async XLA Ops:
  0.6 9.5 %copy-start.8 = (f32[1,3,8,1089]{3,2,1,0:T(8,128)S(1)}, f32[1,3,8,1089]{3,2,1,0:T(8,128)}, u32[]{:S(2)}) copy-start(f32[1,3,8,1089]{3,2,1,0:T(8,128)} %now_ref.3) | copy-start | bytes 313636
  0.6 9.5 %copy-start.9 = (f32[1,3,8,1089]{3,2,1,0:T(8,128)S(1)}, f32[1,3,8,1089]{3,2,1,0:T(8,128)}, u32[]{:S(2)}) copy-start(f32[1,3,8,1089]{3,2,1,0:T(8,128)} %prev_ref.3) | copy-start | bytes 313636
  1.7 8.4 %copy-start = (bf16[3,384,256]{2,1,0:T(8,128)(2,1)S(1)}, bf16[3,384,256]{2,1,0:T(8,128)(2,1)}, u32[]{:S(2)}) copy-start(bf16[3,384,256]{2,1,0:T(8,128)(2,1)} %constant.16.clone.refs_0_.grad_table) | copy-start | bytes 1769476
  1.7 8.4 %copy-start.1 = (bf16[3,208,384]{2,1,0:T(8,128)(2,1)S(1)}, bf16[3,208,384]{2,1,0:T(8,128)(2,1)}, u32[]{:S(2)}) copy-start(bf16[3,208,384]{2,1,0:T(8,128)(2,1)} %constant.17.clone.refs_2_.force_table) | copy-start | bytes 1437700
  1.7 8.4 %copy-start.2 = (f32[125,128]{1,0:T(8,128)S(1)}, f32[125,128]{1,0:T(8,128)}, u32[]{:S(2)}) copy-start(f32[125,128]{1,0:T(8,128)} %lame_ref.5) | copy-start | bytes 192004
  1.7 8.4 %copy-start.3 = (f32[125,128]{1,0:T(8,128)S(1)}, f32[125,128]{1,0:T(8,128)}, u32[]{:S(2)}) copy-start(f32[125,128]{1,0:T(8,128)} %mu_ref.5) | copy-start | bytes 192004
  1.7 8.4 %copy-start.4 = (bf16[3,80,256]{2,1,0:T(8,128)(2,1)S(1)}, bf16[3,80,256]{2,1,0:T(8,128)(2,1)}, u32[]{:S(2)}) copy-start(bf16[3,80,256]{2,1,0:T(8,128)(2,1)} %constant.18.clone.refs_1_.refs_5_) | copy-start | bytes 368644
  1.7 8.4 %copy-start.5 = (bf16[384,240]{1,0:T(8,128)(2,1)S(1)}, bf16[384,240]{1,0:T(8,128)(2,1)}, u32[]{:S(2)}) copy-start(bf16[384,240]{1,0:T(8,128)(2,1)} %constant.19.clone.refs_4_) | copy-start | bytes 552964
  1.8 8.4 %copy-start.6 = (bf16[384,240]{1,0:T(8,128)(2,1)S(1)}, bf16[384,240]{1,0:T(8,128)(2,1)}, u32[]{:S(2)}) copy-start(bf16[384,240]{1,0:T(8,128)(2,1)} %constant.20.clone.refs_3_.refs_4_) | copy-start | bytes 552964
  1.8 8.4 %copy-start.7 = (f32[320,128]{1,0:T(8,128)S(1)}, f32[320,128]{1,0:T(8,128)}, u32[]{:S(2)}) copy-start(f32[320,128]{1,0:T(8,128)} %constant.23.clone.mass_ref) | copy-start | bytes 491524
  1.8 8.4 %copy-start.10 = (f32[8,1089]{1,0:T(8,128)S(1)}, f32[8,1089]{1,0:T(8,128)}, u32[]{:S(2)}) copy-start(f32[8,1089]{1,0:T(8,128)} %density_ref.3) | copy-start | bytes 104548
  1.8 11.1 %collective-permute-start = (f32[8,1152]{1,0:T(8,128)S(1)}, f32[8,1152]{1,0:T(8,128)S(1)}, u32[]{:S(2)}, u32[]{:S(2)}) collective-permute-start(f32[8,1152]{1,0:T(8,128)S(1)} %gather.1), channel_id=1, source_target_pairs={{0,15},{1,0},{2,1},{3,2},{4,3},{5,4},{6,5},{7,6},{8,7},{9,8},{10,9... | collective-permute-start | bytes 110600 | tf_op jit(solution)/shard_map/ppermute | solution.py:785
  10.2 2.7 %copy-start.12 = (s32[13,128]{1,0:T(8,128)S(1)}, s32[13,128]{1,0:T(8,128)}, u32[]{:S(2)}) copy-start(s32[13,128]{1,0:T(8,128)} %constant.21.clone.refs_9_.lanes_ref) | copy-start | bytes 19972
  13.9 5.8 %collective-permute-start.1 = (bf16[3,128,128]{2,1,0:T(8,128)(2,1)S(1)}, bf16[3,128,128]{2,1,0:T(8,128)(2,1)S(1)}, u32[]{:S(2)}, u32[]{:S(2)}) collective-permute-start(bf16[3,128,128]{2,1,0:T(8,128)(2,1)S(1)} %get-tuple-element.60.low_ref), channel_id=1, source_target_pairs={{0,16},{16,0},{1,17},{17,1},{2,18},{18,2},{3,19},{19,3},{4,20},{20... | collective-permute-start | bytes 294920 | tf_op jit(solution)/shard_map/ppermute | solution.py:785
  14.0 7.4 %collective-permute-start.2 = (f32[40,128]{1,0:T(8,128)S(1)}, f32[40,128]{1,0:T(8,128)S(1)}, u32[]{:S(2)}, u32[]{:S(2)}) collective-permute-start(f32[40,128]{1,0:T(8,128)S(1)} %get-tuple-element.67), channel_id=1, source_target_pairs={{1,2},{2,1},{3,4},{4,3},{5,6},{6,5},{7,8},{8,7},{9,10},{10,9},{11,... | collective-permute-start | bytes 61448 | tf_op jit(solution)/shard_map/ppermute | solution.py:794
  17.4 4.0 %collective-permute-start.3 = (f32[40,128]{1,0:T(8,128)S(1)}, f32[40,128]{1,0:T(8,128)S(1)}, u32[]{:S(2)}, u32[]{:S(2)}) collective-permute-start(f32[40,128]{1,0:T(8,128)S(1)} %get-tuple-element.68), channel_id=1, source_target_pairs={{0,1},{1,0},{2,3},{3,2},{4,5},{5,4},{6,7},{7,6},{8,9},{9,8},{10,11... | collective-permute-start | bytes 61448 | tf_op jit(solution)/shard_map/ppermute | solution.py:794
  22.3 4.8 %collective-permute-start.4 = (bf16[3,128,128]{2,1,0:T(8,128)(2,1)S(1)}, bf16[3,128,128]{2,1,0:T(8,128)(2,1)S(1)}, u32[]{:S(2)}, u32[]{:S(2)}) collective-permute-start(bf16[3,128,128]{2,1,0:T(8,128)(2,1)S(1)} %get-tuple-element.79.low_ref), channel_id=1, source_target_pairs={{0,16},{16,0},{1,17},{17,1},{2,18},{18,2},{3,19},{19,3},{4,20},{20... | collective-permute-start | bytes 294920 | tf_op jit(solution)/shard_map/ppermute | solution.py:785
  22.4 7.4 %collective-permute-start.5 = (f32[40,128]{1,0:T(8,128)S(1)}, f32[40,128]{1,0:T(8,128)S(1)}, u32[]{:S(2)}, u32[]{:S(2)}) collective-permute-start(f32[40,128]{1,0:T(8,128)S(1)} %get-tuple-element.82), channel_id=1, source_target_pairs={{1,2},{2,1},{3,4},{4,3},{5,6},{6,5},{7,8},{8,7},{9,10},{10,9},{11,... | collective-permute-start | bytes 61448 | tf_op jit(solution)/shard_map/ppermute | solution.py:794
  25.9 4.0 %collective-permute-start.6 = (f32[40,128]{1,0:T(8,128)S(1)}, f32[40,128]{1,0:T(8,128)S(1)}, u32[]{:S(2)}, u32[]{:S(2)}) collective-permute-start(f32[40,128]{1,0:T(8,128)S(1)} %get-tuple-element.83), channel_id=1, source_target_pairs={{0,1},{1,0},{2,3},{3,2},{4,5},{5,4},{6,7},{7,6},{8,9},{9,8},{10,11... | collective-permute-start | bytes 61448 | tf_op jit(solution)/shard_map/ppermute | solution.py:794
  30.1 1.4 %collective-permute-start.8 = (bf16[3,128,128]{2,1,0:T(8,128)(2,1)S(1)}, bf16[3,128,128]{2,1,0:T(8,128)(2,1)S(1)}, u32[]{:S(2)}, u32[]{:S(2)}) collective-permute-start(bf16[3,128,128]{2,1,0:T(8,128)(2,1)S(1)} %get-tuple-element.93.low_ref), channel_id=1, source_target_pairs={{0,16},{16,0},{1,17},{17,1},{2,18},{18,2},{3,19},{19,3},{4,20},{20... | collective-permute-start | bytes 294920 | tf_op jit(solution)/shard_map/ppermute | solution.py:785
  30.9 7.4 %collective-permute-start.7 = (f32[40,128]{1,0:T(8,128)S(1)}, f32[40,128]{1,0:T(8,128)S(1)}, u32[]{:S(2)}, u32[]{:S(2)}) collective-permute-start(f32[40,128]{1,0:T(8,128)S(1)} %get-tuple-element.87), channel_id=1, source_target_pairs={{0,1},{1,2},{2,3},{3,4},{4,5},{5,6},{6,7},{7,8},{8,9},{9,10},{10,1... | collective-permute-start | bytes 61448 | tf_op jit(solution)/shard_map/ppermute | solution.py:785
  32.2 7.5 %collective-permute-start.9 = (s16[128,128]{1,0:T(8,128)(2,1)S(1)}, s16[128,128]{1,0:T(8,128)(2,1)S(1)}, u32[]{:S(2)}, u32[]{:S(2)}) collective-permute-start(s16[128,128]{1,0:T(8,128)(2,1)S(1)} %get-tuple-element.96), channel_id=1, source_target_pairs={{0,3},{1,2},{2,1},{3,0},{4,7},{5,6},{6,5},{7,4},{8,11},{9,10},{10,... | collective-permute-start | bytes 98312 | tf_op jit(solution)/shard_map/ppermute | solution.py:911
  32.7 7.0 %collective-permute-start.10 = (s16[128,128]{1,0:T(8,128)(2,1)S(1)}, s16[128,128]{1,0:T(8,128)(2,1)S(1)}, u32[]{:S(2)}, u32[]{:S(2)}) collective-permute-start(s16[128,128]{1,0:T(8,128)(2,1)S(1)} %get-tuple-element.97), channel_id=1, source_target_pairs={{0,2},{1,3},{2,0},{3,1},{4,6},{5,7},{6,4},{7,5},{8,10},{9,11},{10,... | collective-permute-start | bytes 98312 | tf_op jit(solution)/shard_map/ppermute | solution.py:911
  33.7 5.9 %collective-permute-start.11 = (s16[128,128]{1,0:T(8,128)(2,1)S(1)}, s16[128,128]{1,0:T(8,128)(2,1)S(1)}, u32[]{:S(2)}, u32[]{:S(2)}) collective-permute-start(s16[128,128]{1,0:T(8,128)(2,1)S(1)} %get-tuple-element.98), channel_id=1, source_target_pairs={{0,1},{1,0},{2,3},{3,2},{4,5},{5,4},{6,7},{7,6},{8,9},{9,8},{10,11... | collective-permute-start | bytes 98312 | tf_op jit(solution)/shard_map/ppermute | solution.py:911
  (3 other events, 3.0 us)
